TPU v7x, 32 devices: a whole 2x2x4 slice. The times are simulated.
32 devices in a mesh: dp: 8 (over z, y), tensor: 4 (over x, core).
Axes of the slice: x: 2, y: 2, z: 4, core: 2. Of those that a mesh axis runs over, the one named last changes fastest.
Arguments:
- tokens_in: bfloat16 [8192, 1024], P(('dp', 'tensor')), may hold values from -6 to 6
- grad_out: bfloat16 [8192, 1024], P(('dp', 'tensor')), may hold values from -6 to 6
- scene_offsets: int32 [4], replicated, may hold values from 0 to 8064, as said below
- input_gain: float32 [1024], replicated, may hold values from 0.25 to 1.75
- weight_zx: bfloat16 [2, 1024, 2048], P(None, None, 'tensor'), may hold values from -0.1875 to 0.1875
- weight_bc: bfloat16 [2, 1024, 128], replicated, may hold values from -0.1875 to 0.1875
- weight_step: bfloat16 [1024, 32], P(None, 'tensor'), may hold values from -0.1875 to 0.1875
- conv_inner: float32 [4, 2048], P(None, 'tensor'), may hold values from -0.5 to 0.5
- conv_inner_bias: float32 [2048], P('tensor'), may hold values from -0.5 to 0.5
- conv_bc: float32 [2, 4, 128], replicated, may hold values from -0.5 to 0.5
- conv_bc_bias: float32 [2, 128], replicated, may hold values from -0.5 to 0.5
- step_bias: float32 [32], P('tensor'), may hold values from -6 to -2
- decay_log: float32 [32], P('tensor'), may hold values from -4 to 2.75
- skip_weight: float32 [32], P('tensor'), may hold values from 0.5 to 2
- norm_gain: float32 [2048], P('tensor'), may hold values from 0.25 to 1.75
- weight_out: bfloat16 [2048, 1024], P('tensor'), may hold values from -0.125 to 0.125
Outputs:
- layer_out: bfloat16 [8192, 1024], P(('dp', 'tensor'))
- grad_tokens: float32 [8192, 1024], P(('dp', 'tensor'))
- grad_input_gain: float32 [1024], replicated
- grad_weight_zx: float32 [2, 1024, 2048], P(None, None, 'tensor')
- grad_weight_bc: float32 [2, 1024, 128], replicated
- grad_weight_step: float32 [1024, 32], P(None, 'tensor')
- grad_conv_inner: float32 [4, 2048], P(None, 'tensor')
- grad_conv_inner_bias: float32 [2048], P('tensor')
- grad_conv_bc: float32 [2, 4, 128], replicated
- grad_conv_bc_bias: float32 [2, 128], replicated
- grad_step_bias: float32 [32], P('tensor')
- grad_decay_log: float32 [32], P('tensor')
- grad_skip_weight: float32 [32], P('tensor')
- grad_norm_gain: float32 [2048], P('tensor')
- grad_weight_out: float32 [2048, 1024], P('tensor')
Inputs may be any that keep to these rules, and one draw needn't show every extreme that they name: `scene_offsets`: scene starts in rising order; the first is 0, each is a multiple of 128, and every scene has 128 positions or more.
All inputs are finite; a program needn't handle non-finite values.
Results may differ from a plain program's by a relative error of at most 0.014.
Values may be sent and summed in bfloat16 or wider, within the bound.
No kernel may reach another device: no remote copies, remote signals or barrier semaphores. Data moves between devices by JAX's collectives and lax.ppermute only.
A program may use at most 128 MiB of HBM per device.

v0:
```python
import jax
import jax.numpy as jnp
from jax import lax
from jax.sharding import PartitionSpec as P

KERNEL = 4
STRETCH = 128
DI = 2048


EPS = 1e-05
HIGH = lax.Precision.HIGHEST


def shifted(block, axis, distance):
    devices = range(lax.axis_size(axis))
    route = [(i - distance, i) for i in devices if i - distance in devices]
    return lax.ppermute(block, axis, route)


def entering(part, axis, combine, identity, reverse):
    count = lax.axis_size(axis)
    place = lax.axis_index(axis)
    ahead = count - 1 - place if reverse else place
    gathered = jax.tree.map(lambda a: lax.all_gather(a, axis), part)
    state = jax.tree.map(lambda a, e: jnp.zeros_like(a) + jnp.asarray(e, a.dtype), part, identity)

    def one(hop, state):
        source = count - 1 - hop if reverse else hop
        return combine(
            state, jax.tree.map(lambda a: lax.dynamic_index_in_dim(a, source, 0, False), gathered)
        )

    return lax.fori_loop(0, ahead, one, state)


def silu_slope(values):
    sigma = jax.nn.sigmoid(values)
    return sigma * (1.0 + values * (1.0 - sigma))


def stretch_starts(first_pos, count, offsets):
    heads_pos = first_pos + jnp.arange(count, dtype=jnp.int32) * STRETCH
    return jnp.any(heads_pos[:, None] == offsets[None, :], axis=1)


def tap_masks(first_pos, length, offsets):
    position = first_pos + jnp.arange(length, dtype=jnp.int32)
    opening = jnp.any((position // STRETCH * STRETCH)[:, None] == offsets[None, :], axis=1)
    inside = position % STRETCH
    return [1.0 - (opening & (inside < delay)).astype(jnp.float32) for delay in range(KERNEL)]


def convolve(padded, kernel, bias, masks):
    length = padded.shape[0] - (KERNEL - 1)
    total = jnp.zeros((length, padded.shape[1]), jnp.float32) + bias[None, :]
    for delay in range(KERNEL):
        column = KERNEL - 1 - delay
        total = (
            total
            + kernel[column][None, :] * padded[column : column + length] * masks[delay][:, None]
        )
    return total


def ssd_block(inner, bvals, cvals, steps, logdec, starts, state):
    length, heads, width = inner.shape
    count = length // STRETCH
    inner_c = inner.reshape(count, STRETCH, heads, width)
    bvals_c = bvals.reshape(count, STRETCH, -1)
    cvals_c = cvals.reshape(count, STRETCH, -1)
    steps_c = steps.reshape(count, STRETCH, heads)
    cumul = jnp.cumsum(logdec.reshape(count, STRETCH, heads), axis=1)
    scores = jnp.einsum("cln,csn->cls", cvals_c, bvals_c, precision=HIGH)
    lower = (jnp.arange(STRETCH)[:, None] >= jnp.arange(STRETCH)[None, :])[None, :, :, None]
    gaps = cumul[:, :, None, :] - cumul[:, None, :, :]
    decay = jnp.exp(jnp.where(lower, gaps, -jnp.inf))
    mixing = scores[:, :, :, None] * decay * steps_c[:, None, :, :]
    within = jnp.einsum("clsh,cshp->clhp", mixing, inner_c, precision=HIGH)
    totals = cumul[:, -1, :]
    weights = jnp.exp(totals[:, None, :] - cumul) * steps_c
    local = jnp.einsum("clh,cln,clhp->chpn", weights, bvals_c, inner_c, precision=HIGH)
    ends = jnp.cumsum(totals, axis=0)
    begins = ends - totals
    marks = jnp.cumsum(starts.astype(jnp.int32))
    order = jnp.arange(count)
    linked = (order[:, None] > order[None, :]) & (marks[:, None] == marks[None, :])
    carried = jnp.exp(
        jnp.where(linked[:, :, None], begins[:, None, :] - ends[None, :, :], -jnp.inf)
    )
    fresh = (marks == 0).astype(jnp.float32)
    entry = jnp.exp(begins) * fresh[:, None]
    opening = (
        jnp.einsum("cdh,dhpn->chpn", carried, local, precision=HIGH)
        + entry[:, :, None, None] * state[None]
    )
    across = jnp.exp(cumul)[..., None] * jnp.einsum(
        "cln,chpn->clhp", cvals_c, opening, precision=HIGH
    )
    outputs = (within + across).reshape(length, heads, width)
    tail = (marks == marks[-1]).astype(jnp.float32)
    keep_end = jnp.exp(ends[-1]) * fresh[-1]
    final = keep_end[:, None, None] * state + jnp.einsum(
        "dh,dhpn->hpn", jnp.exp(ends[-1][None, :] - ends) * tail[:, None], local, precision=HIGH
    )
    return (outputs, final)


def inflow(logdec, starts):
    count = starts.shape[0]
    cumul = jnp.cumsum(logdec.reshape(count, STRETCH, -1), axis=1)
    totals = cumul[:, -1, :]
    begins = jnp.cumsum(totals, axis=0) - totals
    fresh = (jnp.cumsum(starts.astype(jnp.int32)) == 0).astype(jnp.float32)
    return (jnp.exp(begins[:, None, :] + cumul) * fresh[:, None, None]).reshape(-1, cumul.shape[2])


def chain_join(earlier, later):
    return (earlier[0] * later[0], later[0][..., None, None] * earlier[1] + later[1])


def on_device(
    tokens_in,
    grad_out,
    scene_offsets,
    input_gain,
    weight_zx,
    weight_bc,
    weight_step,
    conv_inner,
    conv_inner_bias,
    conv_bc,
    conv_bc_bias,
    step_bias,
    decay_log,
    skip_weight,
    norm_gain,
    weight_out,
):
    share = tokens_in.shape[0]
    group = lax.axis_size("tensor")
    tokens = share * group
    heads = step_bias.shape[0]
    local_width = norm_gain.shape[0]
    head_dim = local_width // heads
    states_n = weight_bc.shape[2]
    count = tokens // STRETCH
    first_pos = lax.axis_index("dp") * tokens
    rows_in = tokens_in.astype(jnp.float32)
    rstd = lax.rsqrt(jnp.mean(rows_in * rows_in, axis=1, keepdims=True) + EPS)
    unit = rows_in * rstd
    normed = (unit * input_gain).astype(jnp.bfloat16)
    normed_all = lax.all_gather(normed, "tensor", axis=0, tiled=True)
    weight_cat = jnp.concatenate([weight_zx[0], weight_zx[1], weight_bc[0], weight_bc[1]], axis=1)
    projected = jnp.dot(normed_all, weight_cat, preferred_element_type=jnp.float32).astype(
        jnp.bfloat16
    )
    step_raw = jnp.dot(normed_all, weight_step, preferred_element_type=jnp.float32).astype(
        jnp.bfloat16
    )
    gate_raw = projected[:, :local_width].astype(jnp.float32)
    conv_cat = projected[:, local_width:]
    rim = shifted(conv_cat[tokens - (KERNEL - 1) :], "dp", 1)
    padded = jnp.concatenate([rim, conv_cat], axis=0).astype(jnp.float32)
    kernel = jnp.concatenate([conv_inner, conv_bc[0], conv_bc[1]], axis=1)
    bias = jnp.concatenate([conv_inner_bias, conv_bc_bias[0], conv_bc_bias[1]])
    starts = stretch_starts(first_pos, count, scene_offsets)
    masks = tap_masks(first_pos, tokens, scene_offsets)
    pre_act = convolve(padded, kernel, bias, masks)
    act = jax.nn.silu(pre_act)
    inner = act[:, :local_width].reshape(tokens, heads, head_dim)
    bvals = act[:, local_width : local_width + states_n]
    cvals = act[:, local_width + states_n :]
    step_in = step_raw.astype(jnp.float32) + step_bias
    steps = jax.nn.softplus(step_in)
    rates = -jnp.exp(decay_log)
    logdec = steps * rates
    zero_state = jnp.zeros((heads, head_dim, states_n), jnp.float32)
    own_ssd, own_end = ssd_block(inner, bvals, cvals, steps, logdec, starts, zero_state)
    reach = inflow(logdec, starts)
    through = reach[-1]
    incoming = entering(
        (through, own_end),
        "dp",
        chain_join,
        (jnp.ones_like(through), jnp.zeros_like(own_end)),
        False,
    )[1]
    ssd_out = own_ssd + reach[:, :, None] * jnp.einsum(
        "tn,hpn->thp", cvals, incoming, precision=HIGH
    )
    mixed = (ssd_out + skip_weight[None, :, None] * inner).reshape(tokens, local_width)
    gate = jax.nn.silu(gate_raw)
    gated = mixed * gate
    square_sum = lax.psum(jnp.sum(gated * gated, axis=1), "tensor")
    scale = lax.rsqrt(square_sum / DI + EPS)
    normout = (gated * scale[:, None] * norm_gain).astype(jnp.bfloat16)
    branch_out = lax.psum_scatter(
        jnp.dot(normout, weight_out, preferred_element_type=jnp.float32),
        "tensor",
        scatter_dimension=0,
        tiled=True,
    )
    layer_out = (rows_in + branch_out).astype(jnp.bfloat16)
    cot_all = lax.all_gather(grad_out, "tensor", axis=0, tiled=True)
    grad_normout = (
        jnp.einsum("td,ed->te", cot_all, weight_out, preferred_element_type=jnp.float32)
        .astype(jnp.bfloat16)
        .astype(jnp.float32)
    )
    grad_weight_out = jnp.einsum("te,td->ed", normout, cot_all, preferred_element_type=jnp.float32)
    weighted = grad_normout * norm_gain
    grad_norm_gain = jnp.sum(grad_normout * gated * scale[:, None], axis=0)
    cross = lax.psum(jnp.sum(weighted * gated, axis=1), "tensor")
    cubed = scale * scale * scale
    grad_gated = scale[:, None] * weighted - gated * (cubed * cross / DI)[:, None]
    grad_mixed = (grad_gated * gate).reshape(tokens, heads, head_dim)
    grad_gate_raw = (grad_gated * mixed * silu_slope(gate_raw)).astype(jnp.bfloat16)
    grad_skip_weight = jnp.sum(grad_mixed * inner, axis=(0, 2))
    toward = jnp.einsum("th,thp,tn->hpn", reach, grad_mixed, cvals, precision=HIGH)
    outgoing = entering(
        (through, toward), "dp", chain_join, (jnp.ones_like(through), jnp.zeros_like(toward)), True
    )[1]

    def local_ssd(inner_v, bvals_v, cvals_v, steps_v, logdec_v):
        return ssd_block(inner_v, bvals_v, cvals_v, steps_v, logdec_v, starts, incoming)

    _, pull = jax.vjp(local_ssd, inner, bvals, cvals, steps, logdec)
    grad_inner, grad_bvals, grad_cvals, grad_steps, grad_logdec = pull((grad_mixed, outgoing))
    grad_inner = grad_inner + skip_weight[None, :, None] * grad_mixed
    grad_steps = grad_steps + grad_logdec * rates
    grad_decay_log = jnp.sum(grad_logdec * logdec, axis=0)
    grad_step_in = grad_steps * jax.nn.sigmoid(step_in)
    grad_step_bias = jnp.sum(grad_step_in, axis=0)
    grad_step_raw = grad_step_in.astype(jnp.bfloat16)
    grad_act = jnp.concatenate(
        [grad_inner.reshape(tokens, local_width), grad_bvals, grad_cvals], axis=1
    )
    grad_pre = grad_act * silu_slope(pre_act)
    returned = shifted(grad_pre[: KERNEL - 1], "dp", -1)
    extended = jnp.concatenate([grad_pre, returned], axis=0)
    masks_ext = tap_masks(first_pos, tokens + KERNEL - 1, scene_offsets)
    grad_conv_cat = jnp.zeros_like(grad_pre)
    for delay in range(KERNEL):
        moved = extended[delay : delay + tokens] * masks_ext[delay][delay : delay + tokens][:, None]
        grad_conv_cat = grad_conv_cat + kernel[KERNEL - 1 - delay][None, :] * moved
    kernel_rows = []
    for column in range(KERNEL):
        delay = KERNEL - 1 - column
        source = padded[column : column + tokens]
        kernel_rows.append(jnp.sum(grad_pre * source * masks[delay][:, None], axis=0))
    grad_kernel = jnp.stack(kernel_rows)
    grad_bias = jnp.sum(grad_pre, axis=0)
    grad_inner_raw = grad_conv_cat[:, :local_width].astype(jnp.bfloat16)
    grad_bc = lax.psum_scatter(
        grad_conv_cat[:, local_width:], "tensor", scatter_dimension=0, tiled=True
    ).astype(jnp.bfloat16)
    grad_proj = jnp.concatenate([grad_gate_raw, grad_inner_raw], axis=1)
    weight_main = jnp.concatenate([weight_zx[0], weight_zx[1]], axis=1)
    total = jnp.einsum("te,de->td", grad_proj, weight_main, preferred_element_type=jnp.float32)
    grad_normed = lax.psum_scatter(
        total
        + jnp.einsum("th,dh->td", grad_step_raw, weight_step, preferred_element_type=jnp.float32),
        "tensor",
        scatter_dimension=0,
        tiled=True,
    )
    weight_bc_cat = jnp.concatenate([weight_bc[0], weight_bc[1]], axis=1)
    grad_normed = grad_normed + jnp.einsum(
        "ts,ds->td", grad_bc, weight_bc_cat, preferred_element_type=jnp.float32
    )
    grad_main = jnp.einsum("td,te->de", normed_all, grad_proj, preferred_element_type=jnp.float32)
    grad_weight_zx = jnp.stack([grad_main[:, :local_width], grad_main[:, local_width:]])
    grad_weight_step = jnp.einsum(
        "td,th->dh", normed_all, grad_step_raw, preferred_element_type=jnp.float32
    )
    grad_bc_both = jnp.einsum("td,ts->ds", normed, grad_bc, preferred_element_type=jnp.float32)
    grad_weight_bc = jnp.stack([grad_bc_both[:, :states_n], grad_bc_both[:, states_n:]])
    grad_input_gain = jnp.sum(grad_normed * unit, axis=0)
    grad_unit = grad_normed * input_gain
    grad_tokens = grad_out.astype(jnp.float32) + rstd * (
        grad_unit - unit * jnp.mean(grad_unit * unit, axis=1, keepdims=True)
    )
    grad_conv_bc = jnp.stack(
        [
            grad_kernel[:, local_width : local_width + states_n],
            grad_kernel[:, local_width + states_n :],
        ]
    )
    grad_conv_bc_bias = jnp.stack(
        [grad_bias[local_width : local_width + states_n], grad_bias[local_width + states_n :]]
    )
    summed = lax.psum(
        (
            grad_weight_zx,
            grad_weight_step,
            grad_weight_out,
            grad_kernel[:, :local_width],
            grad_bias[:local_width],
            grad_step_bias,
            grad_decay_log,
            grad_skip_weight,
            grad_norm_gain,
        ),
        "dp",
    )
    shared = lax.psum(
        (grad_input_gain, grad_weight_bc, grad_conv_bc, grad_conv_bc_bias), ("dp", "tensor")
    )
    return (
        layer_out,
        grad_tokens,
        shared[0],
        summed[0],
        shared[1],
        summed[1],
        summed[3],
        summed[4],
        shared[2],
        shared[3],
        summed[5],
        summed[6],
        summed[7],
        summed[8],
        summed[2],
    )


def solution(mesh):
    in_specs = (
        P(("dp", "tensor"), None),
        P(("dp", "tensor"), None),
        P(),
        P(),
        P(None, None, "tensor"),
        P(),
        P(None, "tensor"),
        P(None, "tensor"),
        P("tensor"),
        P(),
        P(),
        P("tensor"),
        P("tensor"),
        P("tensor"),
        P("tensor"),
        P("tensor", None),
    )
    out_specs = (
        P(("dp", "tensor"), None),
        P(("dp", "tensor"), None),
        P(),
        P(None, None, "tensor"),
        P(),
        P(None, "tensor"),
        P(None, "tensor"),
        P("tensor"),
        P(),
        P(),
        P("tensor"),
        P("tensor"),
        P("tensor"),
        P("tensor"),
        P("tensor", None),
    )
    return jax.shard_map(
        on_device, mesh=mesh, in_specs=in_specs, out_specs=out_specs, check_vma=False
    )
```

profile of v0, /device:TPU:0, one launch (start us, length us, event | category | flops | bytes accessed | tf_op | source)
XLA Modules:
  0.0 802.5 jit_solution(13176269541920386181)
XLA Ops:
  18.8 17.9 %all-gather.8.cloned.1.call-done = bf16[1024,1024]{1,0:T(8,128)(2,1)} async-done(((bf16[256,1024]{1,0:T(8,128)(2,1)}), bf16[1024,1024]{1,0:T(8,128)(2,1)}) %all-gather.8.cloned.1.call-update) | async-done | bytes 2097168 | tf_op jit(solution)/shard_map/all_gather | solution.py:153
  44.4 4.6 convolution_convert_fusion
  49.0 3.7 collective-permute-start
  56.3 4.1 fusion.18
  69.5 2.8 fusion.86
  77.4 20.5 %all-gather.2 = f32[8,1,8]{2,1,0:T(1,128)} all-gather(f32[1,1,8]{2,1,0:T(1,128)S(1)} %bitcast.287), channel_id=1, replica_groups=mesh['dp'=8,'tensor'=4] {'dp'}, dimensions={0}, use_global_device_ids=true | all-gather | bytes 288 | tf_op jit(solution)/shard_map/all_gather | solution.py:25
  102.3 10.7 %fusion.5 = f32[8,8,64,128]{3,2,1,0:T(8,128)} fusion(f32[8,128,8]{1,2,0:T(8,128)S(1)} %copy-done.58, f32[8,128,8]{1,2,0:T(8,128)S(1)} %copy.263, f32[8,128,128]{2,1,0:T(8,128)S(1)} %fusion.231, pred[128,128]{1,0:T(8,128)(4,1)S(1)} %iota_compare_fusion, f32[8,128,8,64]{1,0,3,2:T(8,128)} %bitcast.249), kind=kOutput, calls=%fused_computation.16 | convolution fusion | flops 809500672 | bytes 4800512 | tf_op jit(solution)/shard_map/clsh,cshp->clhp/dot_general | solution.py:79
  113.0 8.7 %all-gather.12.cloned.1.call-done = f32[64,64,128]{2,1,0:T(8,128)} async-done(((f32[8,64,128]{2,1,0:T(8,128)}), f32[64,64,128]{2,1,0:T(8,128)}) %all-gather.12.cloned.1.call-update) | async-done | bytes 2097168 | tf_op jit(solution)/shard_map/all_gather | solution.py:25
  121.8 5.4 bitcast_add_fusion.4
  129.4 4.6 fusion.41
  134.1 2.9 copy.279
  137.0 3.9 multiply_reduce_fusion.8
  140.8 6.2 psum.105
  147.7 5.3 fusion.33
  153.0 7.6 psum.106
  161.3 6.0 multiply_reduce_fusion.6
  167.3 2.9 copy.282
  170.2 4.2 fusion.50
  184.2 13.5 %fusion.29 = (f32[8,128,8]{1,2,0:T(8,128)}, f32[8,128,8]{1,2,0:T(8,128)}, f32[8,128,8]{1,2,0:T(8,128)S(1)}, f32[8,128,128]{2,1,0:T(8,128)}) fusion(f32[8,128,8]{1,2,0:T(8,128)} %copy-done.57, f32[8,128,8]{1,2,0:T(8,128)} %copy-done.85, f32[8,128,128]{2,1,0:T(8,128)} %copy-done.55, pred[128,128]{1,0:T(8,128)(4,1)} %copy-done.94, ...), kind=kOutput, calls=%fused_computation.53 | convolution fusion | flops 818782208 | bytes 5423104 | tf_op jit(solution)/shard_map/transpose(jvp(clsh,cshp->clhp))/dot_general | solution.py:79
  202.2 3.8 fusion.82
  209.4 8.9 %fusion.223 = (f32[8,8]{0,1:T(8,128)}, f32[8,8]{0,1:T(8,128)S(1)}) fusion(f32[8,8]{0,1:T(8,128)S(1)} %reduce_window_sum.64, f32[8,8]{0,1:T(8,128)S(1)} %copy-done.63, f32[8,8,64,128]{3,2,1,0:T(8,128)S(1)} %fusion.80, f32[8,64,128,8]{2,1,0,3:T(8,128)} %bitcast.258, pred[8,8]{1,0:T(8,128)(4,1)S(1)} %copy-done.100), kind=kOutput, calls=%fused_computation.340 | convolution fusion | flops 50334592 | bytes 4195392 | tf_op jit(solution)/shard_map/transpose(jvp(cdh,dhpn->chpn))/dot_general | solution.py:94
  219.0 6.4 fusion.112
  226.9 7.1 all-gather.14.cloned.1.call-done
  234.7 17.8 %while.27 = (s32[]{:T(128)}, f32[8,64,128]{2,1,0:T(8,128)}, s32[]{:T(128)}, f32[8,8]{1,0:T(8,128)}, f32[8,8,64,128]{3,2,1,0:T(8,128)}, /*index=5*/s32[]{:T(128)}, s32[]{:T(128)}, s32[]{:T(128)}, s32[]{:T(128)}) while((s32[]{:T(128)}, f32[8,64,128]{2,1,0:T(8,128)}, s32[]{:T(128)}, f32[8,8]{1,0:T(8,128)}, f32[8,8,64,128]{3,2,1,0:T(8,128)}, ...), condition=%wide.region_14.15_spmd, body=%wide.region_13.14_spmd.sunk | while | flops 131078 | bytes 786683 | solution.py:34
  253.7 5.1 add_bitcast_fusion
  258.8 4.7 fusion.107
  263.5 3.3 fusion.73
  268.3 6.1 fusion.84
  276.3 6.4 bitcast_add_fusion.3
  282.7 2.8 copy.333
  285.4 5.0 reshape.460
  293.3 5.5 multiply_reduce_fusion.4
  302.5 3.6 collective-permute-done.1
  306.1 8.8 %fusion.11 = f32[1024,768]{1,0:T(8,128)S(1)} fusion(f32[3,768]{1,0:T(4,128)S(1)} %collective-permute-done.1, f32[1024,768]{1,0:T(8,128)} %copy-done.28, f32[1024]{0:T(1024)S(1)} %copy-done.97, f32[1024]{0:T(1024)S(1)} %copy-done.98, f32[1024]{0:T(1024)S(1)} %copy-done.99, f32[1024]{0:T(1024)S(1)} %copy-done.96, f32[768]{0:T(1024)S(1)} %copy-done.80, ...), kind=kLoop, calls=%fused_computation.22 | loop fusion | flops 11010048 | bytes 6329344 | tf_op jit(solution)/shard_map/add | solution.py:246
  318.6 2.8 multiply_reduce_fusion.5
  322.6 2.5 fusion.227
  334.4 2.8 convolution_add_fusion
  338.8 3.3 fusion.222
  342.3 4.4 fusion.221
  346.8 4.5 fusion.106
  353.8 2.7 slice_bitcast_fusion.1
  356.6 2.4 pad_maximum_fusion
  361.0 34.2 %all-reduce.4 = (f32[1024,8]{0,1:T(8,128)}, f32[4,512]{1,0:T(4,128)}, f32[512]{0:T(512)}, f32[8]{0:T(128)}, f32[8]{0:T(128)}, /*index=5*/f32[8]{0:T(128)}, f32[512]{0:T(512)}) all-reduce(f32[1024,8]{0,1:T(8,128)S(1)} %fusion.181, f32[4,512]{1,0:T(4,128)S(1)} %slice.245, ...), channel_id=1, replica_groups=mesh['dp'=8,'tensor'=4] {'dp'}, use_global_device_ids=true, to_apply=%region_36.37 | all-reduce | flops 11288 | bytes 90304 | tf_op jit(solution)/shard_map/psum | solution.py:293
  397.5 37.7 %all-reduce.3 = (f32[1024]{0:T(1024)}, f32[2,4,128]{2,1,0:T(4,128)}, f32[2,128]{1,0:T(2,128)}) all-reduce(f32[1024]{0:T(1024)S(1)} %get-tuple-element.156, f32[2,4,128]{2,1,0:T(4,128)S(1)} %pad_maximum_fusion.9, f32[2,128]{1,0:T(2,128)S(1)} %pad_maximum_fusion.10), channel_id=1, replica_groups=mesh['dp'=8,'tensor'=4] {'dp','tensor'}, use_global_device_ids=true, to_apply=%region_33.34 | all-reduce | flops 2304 | bytes 18432 | tf_op jit(solution)/shard_map/psum | solution.py:307
  435.4 2.7 fusion.139
  438.1 133.8 %all-reduce.9.cloned.1.call-done = f32[2,1024,128]{2,1,0:T(8,128)} async-done(((f32[2,1024,128]{2,1,0:T(8,128)}), f32[2,1024,128]{2,1,0:T(8,128)}) %all-reduce.9.cloned.1.call-update) | async-done | bytes 1048592 | tf_op jit(solution)/shard_map/psum | solution.py:307
  571.9 215.9 %all-reduce.11.cloned.1.call-done = (f32[2,1024,512]{2,1,0:T(8,128)}, f32[512,1024]{1,0:T(8,128)}) async-done(((f32[2,1024,512]{2,1,0:T(8,128)}, f32[512,1024]{1,0:T(8,128)}), (f32[2,1024,512]{2,1,0:T(8,128)}, f32[512,1024]{1,0:T(8,128)})) %all-reduce.11.cloned.1.call-update) | async-done | bytes 6291472 | tf_op jit(solution)/shard_map/psum | solution.py:293
  787.8 4.7 copy.441
  (406 shorter events, 119.7 us)
Async XLA Ops:
  7.2 140.6 %copy-start = (bf16[512,1024]{1,0:T(8,128)(2,1)S(1)}, bf16[512,1024]{1,0:T(8,128)(2,1)}, u32[]{:S(2)}) copy-start(bf16[512,1024]{1,0:T(8,128)(2,1)} %param.35) | copy-start | bytes 3145732
  7.3 10.1 %copy-start.39 = (bf16[2,1024,512]{2,1,0:T(8,128)(2,1)S(1)}, bf16[2,1024,512]{2,1,0:T(8,128)(2,1)}, u32[]{:S(2)}) copy-start(bf16[2,1024,512]{2,1,0:T(8,128)(2,1)} %param.24) | copy-start | bytes 6291460
  7.3 29.5 %all-gather.8.cloned.1.call-start = ((), (), s32[]{:S(2)}) async-start(), calls=%async_computation.3 | async-start | bytes 2621440 | tf_op jit(solution)/shard_map/all_gather | solution.py:153
  11.3 110.4 %all-gather.12.cloned.1.call-start = ((), (), s32[]{:S(2)}) async-start(), calls=%async_computation.9 | async-start | bytes 2359296 | tf_op jit(solution)/shard_map/all_gather | solution.py:25
  12.9 39.8 %copy-start.102 = (f32[8]{0:T(128)}, f32[8]{0:T(128)S(1)}, u32[]{:S(2)}) copy-start(f32[8]{0:T(128)S(1)} %get-tuple-element.249) | copy-start | bytes 100
  12.9 39.8 %copy-start.110 = (f32[8]{0:T(128)}, f32[8]{0:T(128)S(1)}, u32[]{:S(2)}) copy-start(f32[8]{0:T(128)S(1)} %get-tuple-element.248) | copy-start | bytes 100
  15.0 24.2 %copy-start.116 = (f32[8]{0:T(128)}, f32[8]{0:T(128)S(1)}, u32[]{:S(2)}) copy-start(f32[8]{0:T(128)S(1)} %exponential_negate_fusion) | copy-start | bytes 100
  15.6 40.3 %copy-start.69 = (f32[1024]{0:T(1024)}, f32[1024]{0:T(1024)S(1)}, u32[]{:S(2)}) copy-start(f32[1024]{0:T(1024)S(1)} %get-tuple-element.244) | copy-start | bytes 12292
  17.4 27.0 %copy-start.52 = (bf16[1024,128]{1,0:T(8,128)(2,1)}, bf16[1024,128]{1,0:T(8,128)(2,1)S(1)}, u32[]{:S(2)}) copy-start(bf16[1024,128]{1,0:T(8,128)(2,1)S(1)} %get-tuple-element.226) | copy-start | bytes 786436
  17.4 19.4 %copy-start.60 = (bf16[1024,8]{0,1:T(8,128)(2,1)S(1)}, bf16[1024,8]{0,1:T(8,128)(2,1)}, u32[]{:S(2)}) copy-start(bf16[1024,8]{0,1:T(8,128)(2,1)} %param.26) | copy-start | bytes 49156
  17.4 19.4 %copy-start.123 = (f32[8]{0:T(128)S(1)}, f32[8]{0:T(128)}, u32[]{:S(2)}) copy-start(f32[8]{0:T(128)} %param.31) | copy-start | bytes 100
  39.2 9.7 %copy-start.57 = (f32[8,128,8]{1,2,0:T(8,128)}, f32[8,128,8]{1,2,0:T(8,128)S(1)}, u32[]{:S(2)}) copy-start(f32[8,128,8]{1,2,0:T(8,128)S(1)} %get-tuple-element.230) | copy-start | bytes 98308
  42.6 11.9 %copy-start.108 = (f32[8]{0:T(128)}, f32[8]{0:T(128)S(1)}, u32[]{:S(2)}) copy-start(f32[8]{0:T(128)S(1)} %slice_reduce_fusion.1) | copy-start | bytes 100
  44.4 8.9 %copy-start.23 = (f32[8,128,8]{2,0,1:T(8,128)S(1)}, f32[8,128,8]{2,0,1:T(8,128)}, u32[]{:S(2)}) copy-start(f32[8,128,8]{2,0,1:T(8,128)} %copy-done.22) | copy-start | bytes 98308
  44.4 8.9 %copy-start.33 = (f32[8,128,8]{2,0,1:T(8,128)S(1)}, f32[8,128,8]{2,0,1:T(8,128)}, u32[]{:S(2)}) copy-start(f32[8,128,8]{2,0,1:T(8,128)} %copy.267) | copy-start | bytes 98308
  49.0 6.6 collective-permute-start
  53.3 16.2 %copy-start.67 = (f32[8,8]{0,1:T(8,128)}, f32[8,8]{0,1:T(8,128)S(1)}, u32[]{:S(2)}) copy-start(f32[8,8]{0,1:T(8,128)S(1)} %get-tuple-element.239) | copy-start | bytes 772
  73.1 29.2 %copy-start.58 = (f32[8,128,8]{1,2,0:T(8,128)S(1)}, f32[8,128,8]{1,2,0:T(8,128)}, u32[]{:S(2)}) copy-start(f32[8,128,8]{1,2,0:T(8,128)} %copy-done.57) | copy-start | bytes 98308
  73.2 74.6 %all-gather.10.cloned.1.call-start = ((), (), s32[]{:S(2)}) async-start(), calls=%async_computation.5 | async-start | bytes 2621440 | tf_op jit(solution)/shard_map/all_gather | solution.py:205
  73.9 160.1 %all-gather.14.cloned.1.call-start = ((), (), s32[]{:S(2)}) async-start(), calls=%async_computation.10 | async-start | bytes 2359296 | tf_op jit(solution)/shard_map/all_gather | solution.py:25
  74.0 39.0 %copy-start.94 = (pred[128,128]{1,0:T(8,128)(4,1)}, pred[128,128]{1,0:T(8,128)(4,1)S(1)}, u32[]{:S(2)}) copy-start(pred[128,128]{1,0:T(8,128)(4,1)S(1)} %iota_compare_fusion) | copy-start | bytes 49156
  74.7 47.0 %copy-start.62 = (f32[8,8]{0,1:T(8,128)}, f32[8,8]{0,1:T(8,128)S(1)}, u32[]{:S(2)}) copy-start(f32[8,8]{0,1:T(8,128)S(1)} %copy.272) | copy-start | bytes 772
  75.9 37.1 %copy-start.85 = (f32[8,128,8]{1,2,0:T(8,128)}, f32[8,128,8]{1,2,0:T(8,128)S(1)}, u32[]{:S(2)}) copy-start(f32[8,128,8]{1,2,0:T(8,128)S(1)} %copy.263) | copy-start | bytes 98308
  174.5 176.8 %reduce-scatter.8.cloned.1.call-start = ((), (), s32[]{:S(2)}) async-start(), calls=%async_computation.7 | async-start | bytes 1310720 | tf_op jit(solution)/shard_map/reduce_scatter | solution.py:255
  234.7 18.9 %copy-start.68 = (f32[8,8]{0,1:T(8,128)S(1)}, f32[8,8]{0,1:T(8,128)}, u32[]{:S(2)}) copy-start(f32[8,8]{0,1:T(8,128)} %copy-done.67) | copy-start | bytes 772
  268.3 8.0 copy-start.7
  268.3 8.0 copy-start.56
  268.3 8.0 copy-start.59
  293.2 8.9 %copy-start.109 = (f32[8]{0:T(128)S(1)}, f32[8]{0:T(128)}, u32[]{:S(2)}) copy-start(f32[8]{0:T(128)} %copy-done.108) | copy-start | bytes 100
  293.3 8.9 %copy-start.111 = (f32[8]{0:T(128)S(1)}, f32[8]{0:T(128)}, u32[]{:S(2)}) copy-start(f32[8]{0:T(128)} %copy-done.110) | copy-start | bytes 100
  293.3 12.8 %copy-start.78 = (f32[768]{0:T(1024)S(1)}, f32[768]{0:T(1024)}, u32[]{:S(2)}) copy-start(f32[768]{0:T(1024)} %get-tuple-element.160) | copy-start | bytes 9220
  293.3 12.8 %copy-start.80 = (f32[768]{0:T(1024)S(1)}, f32[768]{0:T(1024)}, u32[]{:S(2)}) copy-start(f32[768]{0:T(1024)} %get-tuple-element.161) | copy-start | bytes 9220
  293.3 12.8 %copy-start.82 = (f32[768]{0:T(1024)S(1)}, f32[768]{0:T(1024)}, u32[]{:S(2)}) copy-start(f32[768]{0:T(1024)} %get-tuple-element.162) | copy-start | bytes 9220
  293.3 12.8 %copy-start.84 = (f32[768]{0:T(1024)S(1)}, f32[768]{0:T(1024)}, u32[]{:S(2)}) copy-start(f32[768]{0:T(1024)} %get-tuple-element.163) | copy-start | bytes 9220
  293.3 12.8 %copy-start.96 = (f32[1024]{0:T(1024)S(1)}, f32[1024]{0:T(1024)}, u32[]{:S(2)}) copy-start(f32[1024]{0:T(1024)} %get-tuple-element.233) | copy-start | bytes 12292
  293.3 12.8 %copy-start.97 = (f32[1024]{0:T(1024)S(1)}, f32[1024]{0:T(1024)}, u32[]{:S(2)}) copy-start(f32[1024]{0:T(1024)} %get-tuple-element.234) | copy-start | bytes 12292
  293.3 12.8 %copy-start.98 = (f32[1024]{0:T(1024)S(1)}, f32[1024]{0:T(1024)}, u32[]{:S(2)}) copy-start(f32[1024]{0:T(1024)} %get-tuple-element.235) | copy-start | bytes 12292
  293.3 12.8 %copy-start.99 = (f32[1024]{0:T(1024)S(1)}, f32[1024]{0:T(1024)}, u32[]{:S(2)}) copy-start(f32[1024]{0:T(1024)} %get-tuple-element.236) | copy-start | bytes 12292
  300.5 5.6 collective-permute-start.1
  317.7 77.6 %reduce-scatter.6.cloned.1.call-start = ((), (), s32[]{:S(2)}) async-start(), calls=%async_computation.6 | async-start | bytes 5242880 | tf_op jit(solution)/shard_map/reduce_scatter | solution.py:261
  337.2 98.1 %reduce-scatter.4.cloned.1.call-start = ((), (), s32[]{:S(2)}) async-start(), calls=%async_computation.4 | async-start | bytes 5242880 | tf_op jit(solution)/shard_map/reduce_scatter | solution.py:198
  342.1 229.8 %all-reduce.9.cloned.1.call-start = ((), (), s32[]{:S(2)}) async-start(), calls=%async_computation.8 | async-start | bytes 2097152 | tf_op jit(solution)/shard_map/psum | solution.py:307
  353.8 434.0 %all-reduce.11.cloned.1.call-start = ((), (), s32[]{:S(2)}) async-start(), calls=%async_computation.11 | async-start | bytes 12582912 | tf_op jit(solution)/shard_map/psum | solution.py:293
  359.1 36.2 %copy-start.50 = (f32[256,256]{1,0:T(8,128)S(1)}, f32[256,256]{1,0:T(8,128)}, u32[]{:S(2)}) copy-start(f32[256,256]{1,0:T(8,128)} %reduce-scatter.8.cloned.1.call-done) | copy-start | bytes 786436
  359.1 36.2 %copy-start.64 = (f32[1024]{0:T(1024)S(1)}, f32[1024]{0:T(1024)}, u32[]{:S(2)}) copy-start(f32[1024]{0:T(1024)} %param.23) | copy-start | bytes 12292
  359.1 36.2 %copy-start.89 = (f32[256]{0:T(256)S(1)}, f32[256]{0:T(256)}, u32[]{:S(2)}) copy-start(f32[256]{0:T(256)} %copy-done.88) | copy-start | bytes 3076
  361.0 74.4 %copy-start.30 = (bf16[256,1024]{1,0:T(8,128)(2,1)S(1)}, bf16[256,1024]{1,0:T(8,128)(2,1)}, u32[]{:S(2)}) copy-start(bf16[256,1024]{1,0:T(8,128)(2,1)} %param.20) | copy-start | bytes 1572868
  361.0 74.4 %copy-start.38 = (bf16[256,1024]{1,0:T(8,128)(2,1)S(1)}, bf16[256,1024]{1,0:T(8,128)(2,1)}, u32[]{:S(2)}) copy-start(bf16[256,1024]{1,0:T(8,128)(2,1)} %param.21) | copy-start | bytes 1572868
  (88 other events, 299.6 us)
Sparse Core Ops, SparseCore 0:
  11.4 25.2 all-gather.7
  73.3 48.3 all-gather.11
  123.3 21.0 all-gather.9
  174.6 59.3 all-gather.13
  317.8 22.1 reduce-scatter.7
  343.1 44.5 reduce-scatter.5
  390.2 45.1 reduce-scatter.3
  442.0 129.8 all-reduce.8
  576.4 211.3 all-reduce.10
where the time goes:
time: 808 us; the launch traced here: 803 us
  waiting for transfers between devices  388 us (48%)
  matrix products  132 us (16%)
  blocking collectives  106 us (13%)
  local copies, waits for them, and re-layouts  78.8 us (10%)
  other arithmetic  76.4 us (9%)
  between operations  15.4 us (2%)
    psum x1, waiting for transfers between devices, on_device(): lax.psum((grad_weight_zx, grad_weight_step, grad_weight_out, grad_kernel[...  216 us
    psum x1, waiting for transfers between devices, on_device(): lax.psum((grad_input_gain, grad_weight_bc, grad_conv_bc, grad_conv_bc_bia...  134 us
    psum x1, blocking collectives, on_device(): lax.psum((grad_input_gain, grad_weight_bc, grad_conv_bc, grad_conv_bc_bia...  37.7 us
    psum x1, blocking collectives, on_device(): lax.psum((grad_weight_zx, grad_weight_step, grad_weight_out, grad_kernel[...  34.2 us
    dot_general x3, matrix products, ssd_block(): within = jnp.einsum('clsh,cshp->clhp', mixing, inner_c, precision=HIGH)  30.6 us
    unnamed x255, local copies, waits for them, and re-layouts  25.3 us
    all_gather x1, blocking collectives, entering(): gathered = jax.tree.map(lambda a: lax.all_gather(a, axis), part)  20.5 us
    dot_general x3, matrix products, ssd_block(): jnp.einsum('cdh,dhpn->chpn', carried, local, precision=HIGH)  19.3 us
  transfers between devices with their start and end apart: 11, of which 7 were waited for; matrix products, arithmetic and copies ran while one was open for 18% of the time, Pallas kernels for 0%

commit v1 on v0

v1 whole, which is shorter than its diff:
```python
import functools

import jax
import jax.numpy as jnp
from jax import lax
from jax.experimental import pallas as pl
from jax.experimental.pallas import tpu as pltpu
from jax.sharding import PartitionSpec as P

KERNEL = 4
L = 128
HD = 64
DI = 2048
EPS = 1e-05
F32 = jnp.float32
BF = jnp.bfloat16
MIB = 1 << 20


def dot(a, b, ca=1, cb=0):
    return lax.dot_general(a, b, (((ca,), (cb,)), ((), ())), preferred_element_type=F32)


def split(a):
    hi = a.astype(BF)
    return hi, (a - hi.astype(F32)).astype(BF)


def dot_l(a, b, ca=1, cb=0):
    hi, lo = split(a)
    return dot(hi, b, ca, cb) + dot(lo, b, ca, cb)


def dot_r(a, b, ca=1, cb=0):
    hi, lo = split(b)
    return dot(a, hi, ca, cb) + dot(a, lo, ca, cb)


def sigmoid(v):
    return 0.5 * jnp.tanh(0.5 * v) + 0.5


def softplus(v):
    u = jnp.exp(-jnp.abs(v))
    small = u * (1.0 - u * (0.5 - u * (1.0 / 3.0 - u * 0.25)))
    return jnp.maximum(v, 0.0) + jnp.where(u < 0.02, small, jnp.log(1.0 + u))


def per_head(row, heads):
    return jnp.concatenate(
        [jnp.broadcast_to(row[:, h : h + 1], (HD, L)) for h in range(heads)], axis=0
    )


def eights(v):
    return jnp.sum(v.reshape(v.shape[0] // 8, 8, v.shape[1]), axis=0)


def across_lanes(v, width):
    return jnp.concatenate([v] * (width // L), axis=1) if width > L else v


def proj_body(k, aliased, *refs):
    toks = refs[:k]
    gain, wzx, wbc, wst = refs[k : k + 4]
    normed_o, gate_o, cat_o, step_o = refs[k + 4 + (4 if aliased else 0) :]
    width = wzx.shape[2]

    def one(tok):
        x = tok[...].astype(F32)
        rstd = lax.rsqrt(jnp.mean(x * x, axis=1, keepdims=True) + EPS)
        normed = (x * rstd * gain[...]).astype(BF)
        normed_o[...] = normed
        gate_o[...] = dot(normed, wzx[0]).astype(BF)
        cat_o[:, :width] = dot(normed, wzx[1]).astype(BF)
        cat_o[:, width : width + L] = dot(normed, wbc[0]).astype(BF)
        cat_o[:, width + L :] = dot(normed, wbc[1]).astype(BF)
        step_o[...] = dot(normed, wst[...]).astype(BF)

    for j in range(k):
        pl.when(pl.program_id(0) == j)(functools.partial(one, toks[j]))


def project(toks, gain, wzx, wbc, wst, total, first, before):
    k = len(toks)
    share, d = toks[0].shape
    width = wzx.shape[2]

    def whole(a):
        return pl.BlockSpec(a.shape, lambda i: (0,) * a.ndim)

    cols = (d, width, width + 2 * L, L)
    ins = [*toks, gain, wzx, wbc, wst]
    specs = [whole(a) for a in ins]
    alias = {}
    if before is not None:
        alias = {len(ins) + j: j for j in range(4)}
        ins += before
        specs += [pl.BlockSpec(memory_space=pl.ANY)] * 4
    return pl.pallas_call(
        functools.partial(proj_body, k, before is not None),
        grid=(k,),
        in_specs=specs,
        out_specs=[pl.BlockSpec((share, c), lambda i: (i + first, 0)) for c in cols],
        out_shape=[jax.ShapeDtypeStruct((total, c), BF) for c in cols],
        input_output_aliases=alias,
        compiler_params=pltpu.CompilerParams(vmem_limit_bytes=40 * MIB),
        cost_estimate=pl.CostEstimate(
            flops=2 * k * share * d * sum(cols[1:]),
            bytes_accessed=2 * k * share * (d + sum(cols)),
            transcendentals=0,
        ),
        name="project",
    )(*ins)


def cot_body(k, *refs):
    cots = refs[:k]
    wout, all_o, gn_o = refs[k:]

    def one(cot):
        v = cot[...]
        all_o[...] = v
        gn_o[...] = dot(v, wout[...], 1, 1).astype(BF)

    for j in range(k):
        pl.when(pl.program_id(0) == j)(functools.partial(one, cots[j]))


def cotangent(cots, wout):
    k = len(cots)
    share, d = cots[0].shape
    width = wout.shape[0]

    def whole(a):
        return pl.BlockSpec(a.shape, lambda i: (0,) * a.ndim)

    return pl.pallas_call(
        functools.partial(cot_body, k),
        grid=(k,),
        in_specs=[whole(a) for a in (*cots, wout)],
        out_specs=[
            pl.BlockSpec((share, d), lambda i: (i, 0)),
            pl.BlockSpec((share, width), lambda i: (i, 0)),
        ],
        out_shape=[
            jax.ShapeDtypeStruct((k * share, d), BF),
            jax.ShapeDtypeStruct((k * share, width), BF),
        ],
        compiler_params=pltpu.CompilerParams(vmem_limit_bytes=32 * MIB),
        cost_estimate=pl.CostEstimate(
            flops=2 * k * share * d * width,
            bytes_accessed=2 * k * share * (2 * d + width),
            transcendentals=0,
        ),
        name="cotangent",
    )(*cots, wout)


def act_parts(pre, width):
    out = []
    for x0 in range(0, width + 2 * L, L):
        v = pre[:, x0 : x0 + L]
        out.append(v * sigmoid(v))
    return out


def states_body(
    meta, cat, step, rim, kern, bias, sbias, rates, spread, tri,
    pre_o, sin_o, send_o, cum_o, pfx_o, thr_o, buf, state, prod,
):
    c = pl.program_id(0)
    width = spread.shape[1]
    heads = width // HD
    keep = jnp.where(meta[1 + c] == 0, 1.0, 0.0)

    @pl.when(c == 0)
    def _():
        buf[0:8, :] = rim[...].astype(F32)[8:16, :] * keep
        state[...] = jnp.zeros_like(state)
        prod[...] = jnp.ones_like(prod)

    @pl.when(c > 0)
    def _():
        buf[0:8, :] = buf[L : L + 8, :] * keep

    buf[8 : 8 + L, :] = cat[...].astype(F32)
    acts = []
    for x0 in range(0, width + 2 * L, L):
        cols = slice(x0, x0 + L)
        v = bias[:, cols] + kern[3:4, cols] * buf[8 : 8 + L, cols]
        for j in range(1, KERNEL):
            v = v + kern[3 - j : 4 - j, cols] * buf[8 - j : 8 - j + L, cols]
        pre_o[:, cols] = v
        acts.append(v * sigmoid(v))
    steps = softplus(step[...].astype(F32) + sbias[...])
    cum = dot_r(tri[...], steps * rates[...])
    cum_o[...] = cum
    total = cum[L - 1 : L, :]
    weights = dot_l(jnp.exp(total - cum) * steps, spread[...])
    inner = jnp.concatenate(acts[: width // L], axis=1)
    local = dot((inner * weights).astype(BF), acts[-2].astype(BF), 0, 0)
    entering = state[...] * keep
    sin_o[0] = entering.astype(BF)
    dec = jnp.exp(total)
    leaving = per_head(dec, heads) * entering + local
    state[...] = leaving
    send_o[...] = leaving
    here = prod[...] * keep
    pfx_o[0] = here
    prod[...] = here * dec
    thr_o[...] = here * dec


def within_body(meta, pre, step, cum_r, sin, sbias, spread, y_o):
    width = spread.shape[1]
    heads = width // HD
    acts = act_parts(pre, width)
    bb, cb = acts[-2].astype(BF), acts[-1].astype(BF)
    scores = dot(cb, bb, 1, 1)
    steps = softplus(step[...].astype(F32) + sbias[...])
    cum = cum_r[...]
    cum_t, steps_t = cum.T, steps.T
    lower = lax.broadcasted_iota(jnp.int32, (L, L), 0) >= lax.broadcasted_iota(
        jnp.int32, (L, L), 1
    )
    first = lax.broadcasted_iota(jnp.int32, (L, L), 1) < HD
    grown = dot_l(jnp.exp(cum), spread[...])
    far = grown * dot(cb, sin[0], 1, 1)
    for pair in range(heads // 2):
        cols = slice(pair * L, pair * L + L)
        x = acts[pair].astype(BF)
        got = []
        for h in (2 * pair, 2 * pair + 1):
            gap = jnp.where(lower, cum[:, h : h + 1] - cum_t[h : h + 1, :], -1e30)
            mix = scores * jnp.exp(gap) * steps_t[h : h + 1, :]
            got.append(dot(mix.astype(BF), x))
        y_o[:, cols] = jnp.where(first, got[0], got[1]) + far[:, cols]


def gate_body(
    meta, pre, cum, pfx, y, gate, gn, incoming, ngain, skip, spread, ones,
    mixed_o, sums_o,
):
    width = spread.shape[1]
    reach = dot_l(jnp.exp(cum[...]) * pfx[0][0:1, :], spread[...])
    cv = pre[:, width + L :]
    cb = (cv * sigmoid(cv)).astype(BF)
    far = reach * dot(cb, incoming[...], 1, 1)
    squares, crosses = [], []
    for x0 in range(0, width, L):
        cols = slice(x0, x0 + L)
        v = pre[:, cols]
        mixed = y[:, cols] + far[:, cols] + skip[:, cols] * (v * sigmoid(v))
        mixed_o[:, cols] = mixed
        g = gate[:, cols].astype(F32)
        gated = mixed * (g * sigmoid(g))
        squares.append(gated * gated)
        crosses.append(gn[:, cols].astype(F32) * ngain[:, cols] * gated)
    square = dot_r(ones[...], jnp.concatenate(squares, axis=1), 1, 1)
    cross = dot_r(ones[...], jnp.concatenate(crosses, axis=1), 1, 1)
    row = lax.broadcasted_iota(jnp.int32, (8, L), 0)
    sums_o[0] = jnp.where(row == 0, square, cross)


def back_gate_body(
    count, meta, pre, cum_r, mixed_r, gate, gn, sums, ngain, skip, spread,
    normout_o, gm_o, ggr_o, gs_o, toward_o, sfx_o, acc_o, gstate, prod, acc,
):
    i = pl.program_id(0)
    c = count - 1 - i
    width = spread.shape[1]
    heads = width // HD
    keep = jnp.where(meta[1 + c] == 0, 1.0, 0.0)

    @pl.when(i == 0)
    def _():
        gstate[...] = jnp.zeros_like(gstate)
        prod[...] = jnp.ones_like(prod)
        acc[...] = jnp.zeros_like(acc)

    both = sums[0]
    square = jnp.broadcast_to(both[0:1, :], (L, L)).T
    cross = jnp.broadcast_to(both[1:2, :], (L, L)).T
    scale = lax.rsqrt(square * (1.0 / DI) + EPS)
    cubed = scale * scale * scale * cross * (1.0 / DI)
    cum = cum_r[...]
    total = cum[L - 1 : L, :]
    grown = dot_l(jnp.exp(cum), spread[...])
    cv = pre[:, width + L :]
    cb = (cv * sigmoid(cv)).astype(BF)
    moved = []
    for x0 in range(0, width, L):
        cols = slice(x0, x0 + L)
        v = pre[:, cols]
        inner = v * sigmoid(v)
        g = gate[:, cols].astype(F32)
        s = sigmoid(g)
        silu = g * s
        mixed = mixed_r[:, cols]
        gated = mixed * silu
        ng = ngain[:, cols]
        gnv = gn[:, cols].astype(F32)
        scaled = gated * scale
        normout_o[:, cols] = (scaled * ng).astype(BF)
        gg = scale * (gnv * ng) - gated * cubed
        gm = gg * silu
        gm_o[:, cols] = gm.astype(BF)
        ggr_o[:, cols] = (gg * mixed * (s + silu * (1.0 - s))).astype(BF)
        acc[0:8, cols] += eights(gnv * scaled)
        acc[8:16, cols] += eights(gm * inner)
        moved.append((gm * grown[:, cols]).astype(BF))
    leaving = gstate[...]
    gs_o[0] = leaving.astype(BF)
    here = prod[...]
    sfx_o[0] = here
    dec = jnp.exp(total)
    entering = per_head(dec, heads) * leaving + dot(jnp.concatenate(moved, axis=1), cb, 0, 0)
    entering = entering * keep
    gstate[...] = entering
    toward_o[...] = entering
    prod[...] = here * dec * keep

    @pl.when(i == count - 1)
    def _():
        row = lax.broadcasted_iota(jnp.int32, (8, width), 0)
        acc_o[...] = jnp.where(
            row == 0,
            jnp.sum(acc[0:8, :], axis=0, keepdims=True),
            jnp.sum(acc[8:16, :], axis=0, keepdims=True),
        )


def head_product(a, b, spread, ones):
    rows = dot(ones[:, :L], (a * b).astype(BF), 1, 1)
    return dot_l(rows, spread, 1, 1)[0:1, :]


def back_within_body(
    meta, pre, step, cum_r, sin, pfx, gs, gm_r, incoming, sbias, skip, spread, tri, ones,
    ginner_o, gbc_o, glog_o, gst_o,
):
    width = spread.shape[1]
    heads = width // HD
    acts = act_parts(pre, width)
    bb, cb = acts[-2].astype(BF), acts[-1].astype(BF)
    scores = dot(cb, bb, 1, 1)
    steps = softplus(step[...].astype(F32) + sbias[...])
    cum = cum_r[...]
    total = cum[L - 1 : L, :]
    cum_t, steps_t = cum.T, steps.T
    row = lax.broadcasted_iota(jnp.int32, (L, L), 0)
    col = lax.broadcasted_iota(jnp.int32, (L, L), 1)
    lower = row >= col
    first = col < HD
    e = jnp.exp(cum)
    wd = jnp.exp(total - cum)
    grown = dot_l(e, spread[...])
    weights = dot_l(wd * steps, spread[...])
    gsb = gs[0]
    entering = sin[0].astype(F32) + per_head(pfx[0][0:1, :], heads) * incoming[...].astype(F32)
    eb = entering.astype(BF)
    u = dot(bb, gsb, 1, 1)
    v = dot(cb, eb, 1, 1)
    inner = jnp.concatenate(acts[: width // L], axis=1)
    gm = gm_r[...].astype(F32)
    seen = dot((inner * u).astype(BF), spread[...], 1, 1)
    passed = dot((gm * v).astype(BF), spread[...], 1, 1) * e
    gb = dot((inner * weights).astype(BF), gsb)
    gc = dot((gm * grown).astype(BF), eb)
    through = head_product(gsb.astype(F32), entering, spread[...], ones) * jnp.exp(total)
    dscores = jnp.zeros((L, L), F32)
    rowsums = jnp.zeros((L, L), F32)
    colsums = jnp.zeros((L, L), F32)
    for pair in range(heads // 2):
        cols = slice(pair * L, pair * L + L)
        xb = acts[pair].astype(BF)
        gmb = gm_r[:, cols]
        got = []
        for h in (2 * pair, 2 * pair + 1):
            mine = first if h % 2 == 0 else jnp.logical_not(first)
            gmh = jnp.where(mine, gm[:, cols], 0.0).astype(BF)
            dm = dot(gmh, xb, 1, 1)
            gap = jnp.where(lower, cum[:, h : h + 1] - cum_t[h : h + 1, :], -1e30)
            decay = jnp.exp(gap)
            st = steps_t[h : h + 1, :]
            t1 = dm * decay
            dscores = dscores + t1 * st
            gp = t1 * scores
            rowsums = jnp.where(col == h, jnp.sum(gp * st, axis=1, keepdims=True), rowsums)
            colsums = jnp.where(row == h, jnp.sum(gp, axis=0, keepdims=True), colsums)
            mix = (scores * decay * st).astype(BF)
            got.append(dot(mix, gmb, 0, 0))
        ginner_o[:, cols] = (
            jnp.where(first, got[0], got[1])
            + weights[:, cols] * u[:, cols]
            + skip[:, cols] * gm[:, cols]
        )
    db = dscores.astype(BF)
    gbc_o[:, :L] = gb + dot(db, cb, 0, 0)
    gbc_o[:, L:] = gc + dot(db, bb)
    direct = colsums.T
    seen = seen * wd
    gst_o[...] = direct + seen
    later = rowsums - direct * steps + passed
    tr = tri[...]
    glog_o[...] = (
        dot_r(tr, later, 0, 0) + dot_r(tr, steps * seen) - steps * seen + through
    )


def back_conv_body(
    count, meta, cat, rim, pre, step, cum_r, sin, pfx, sfx, ginner_r, gbc_r, glog_r, gst_r,
    incoming, outgoing, kern, sbias, rates, spread, tri, ones,
    gcat_o, gsr_o, head_o, acc_o, hacc_o, buf, acc, hacc,
):
    i = pl.program_id(0)
    c = count - 1 - i
    width = spread.shape[1]
    heads = width // HD
    keep_next = jnp.where(meta[2 + c] == 0, 1.0, 0.0)
    keep = jnp.where(meta[1 + c] == 0, 1.0, 0.0)

    @pl.when(i == 0)
    def _():
        buf[L : L + 8, :] = jnp.zeros_like(buf[L : L + 8, :])
        acc[...] = jnp.zeros_like(acc)
        hacc[...] = jnp.zeros_like(hacc)

    @pl.when(i > 0)
    def _():
        buf[L : L + 8, :] = buf[0:8, :] * keep_next

    step_in = step[...].astype(F32) + sbias[...]
    steps = softplus(step_in)
    cum = cum_r[...]
    total = cum[L - 1 : L, :]
    wd = jnp.exp(total - cum)
    weights = dot_l(wd * steps, spread[...])
    far = outgoing[...].astype(F32) * per_head(sfx[0][0:1, :], heads)
    fb = far.astype(BF)
    entering = sin[0].astype(F32) + per_head(pfx[0][0:1, :], heads) * incoming[...].astype(F32)
    through = head_product(far, entering, spread[...], ones) * jnp.exp(total)
    acts, slopes = [], []
    for x0 in range(0, width + 2 * L, L):
        v = pre[:, x0 : x0 + L]
        s = sigmoid(v)
        a = v * s
        acts.append(a)
        slopes.append(s + a * (1.0 - s))
    bb = acts[-2].astype(BF)
    u = dot(bb, fb, 1, 1)
    inner = jnp.concatenate(acts[: width // L], axis=1)
    seen = dot((inner * u).astype(BF), spread[...], 1, 1) * wd
    gb = dot((inner * weights).astype(BF), fb)
    glog = glog_r[...] + dot_r(tri[...], steps * seen) - steps * seen + through
    gsi = (gst_r[...] + seen + glog * rates[...]) * sigmoid(step_in)
    gsr_o[...] = gsi.astype(BF)
    hacc[0:8, :] += eights(glog * steps * rates[...])
    hacc[8:16, :] += eights(gsi)
    for k, x0 in enumerate(range(0, width + 2 * L, L)):
        cols = slice(x0, x0 + L)
        if x0 < width:
            g = ginner_r[:, cols] + weights[:, cols] * u[:, cols]
        elif x0 == width:
            g = gbc_r[:, :L] + gb
        else:
            g = gbc_r[:, L:]
        g = g * slopes[k]
        buf[0:L, cols] = g
        acc[32:40, cols] += eights(g)
        here = cat[:, cols].astype(F32)
        out = kern[3:4, cols] * g
        acc[24:32, cols] += eights(g * here)
        for j in range(1, KERNEL):
            moved = buf[j : j + L, cols]
            out = out + kern[3 - j : 4 - j, cols] * moved
            acc[24 - 8 * j : 32 - 8 * j, cols] += eights(moved * here)
        gcat_o[:, cols] = out.astype(BF)
    head_o[...] = buf[0:8, :]

    @pl.when(i == count - 1)
    def _():
        past = rim[...].astype(F32)[8:16, :] * keep
        now = buf[0:8, :]
        row = lax.broadcasted_iota(jnp.int32, now.shape, 0)
        result = jnp.zeros_like(now)
        for k in range(5):
            part = jnp.sum(acc[8 * k : 8 * k + 8, :], axis=0, keepdims=True)
            j = 3 - k
            if 1 <= j <= 3:
                for t in range(j):
                    part = part + now[t : t + 1, :] * past[8 + t - j : 9 + t - j, :]
            result = jnp.where(row == k, part, result)
        acc_o[...] = result
        hrow = lax.broadcasted_iota(jnp.int32, (8, L), 0)
        hacc_o[...] = jnp.where(
            hrow == 0,
            jnp.sum(hacc[0:8, :], axis=0, keepdims=True),
            jnp.sum(hacc[8:16, :], axis=0, keepdims=True),
        )


def dgrad_body(k, ggr, gcat, gsr, wzx, wbc, wst, *outs):
    width = wzx.shape[2]

    def one(out):
        r = dot(ggr[...], wzx[0], 1, 1)
        r = r + dot(gcat[:, :width], wzx[1], 1, 1)
        r = r + dot(gcat[:, width : width + L], wbc[0], 1, 1)
        r = r + dot(gcat[:, width + L :], wbc[1], 1, 1)
        r = r + dot(gsr[...], wst[...], 1, 1)
        out[...] = r.astype(BF)

    for j in range(k):
        pl.when(pl.program_id(0) == j)(functools.partial(one, outs[j]))


def outproj_body(k, normout, wout, *outs):
    def one(out):
        out[...] = dot(normout[...], wout[...]).astype(BF)

    for j in range(k):
        pl.when(pl.program_id(0) == j)(functools.partial(one, outs[j]))


def rows_times(body, first, k, share, d, rows, consts, name):
    def whole(a):
        return pl.BlockSpec(a.shape, lambda i: (0,) * a.ndim)

    return pl.pallas_call(
        functools.partial(body, k),
        grid=(k,),
        in_specs=[
            pl.BlockSpec((share, r.shape[1]), lambda i: (first + k - 1 - i, 0)) for r in rows
        ]
        + [whole(a) for a in consts],
        out_specs=[pl.BlockSpec((share, d), lambda i: (0, 0))] * k,
        out_shape=[jax.ShapeDtypeStruct((share, d), BF)] * k,
        compiler_params=pltpu.CompilerParams(vmem_limit_bytes=40 * MIB),
        cost_estimate=pl.CostEstimate(
            flops=2 * k * share * d * sum(r.shape[1] for r in rows),
            bytes_accessed=2 * k * share * (d + sum(r.shape[1] for r in rows)),
            transcendentals=0,
        ),
        name=name,
    )(*rows, *consts)[::-1]


def swap(x, axis, mask):
    count = lax.axis_size(axis)
    return lax.ppermute(x, axis, [(i, i ^ mask) for i in range(count)])


def frames(x, count):
    got = {0: x}
    mask = count // 2
    while mask:
        for d in sorted(got):
            got[d ^ mask] = swap(got[d], "tensor", mask)
        mask //= 2
    return [got[d] for d in range(count)]


def add(a, b):
    return (a.astype(F32) + b.astype(F32)).astype(BF)


def scatter_frames(make, count):
    half = count // 2
    held = []
    for first in (half, 0):
        part = dict(enumerate(make(first, half)))
        mask = 1
        while mask < half:
            for d in list(part):
                if d & mask:
                    part[d ^ mask] = add(part[d ^ mask], swap(part.pop(d), "tensor", mask))
            mask *= 2
        held.append(part[0])
    return held[1].astype(F32) + swap(held[0], "tensor", half).astype(F32)


def bit_of(axis, mask):
    return (lax.axis_index(axis) // mask) % 2


def halves(x, axis, masks):
    for mask in masks:
        half = x.shape[0] // 2
        bit = bit_of(axis, mask)
        sent = lax.dynamic_slice_in_dim(x, (1 - bit) * half, half, 0)
        kept = lax.dynamic_slice_in_dim(x, bit * half, half, 0)
        x = add(kept, swap(sent, axis, mask))
    return x


def doubles(x, axis, masks):
    for mask in masks[::-1]:
        got = swap(x, axis, mask)
        x = jnp.where(
            bit_of(axis, mask) == 0,
            jnp.concatenate([x, got], axis=0),
            jnp.concatenate([got, x], axis=0),
        )
    return x


def masks_of(axis):
    masks, mask = [], 1
    while mask < lax.axis_size(axis):
        masks.append(mask)
        mask *= 2
    return masks


def everyone(x, axis):
    for mask in masks_of(axis):
        x = x + swap(x, axis, mask)
    return x


def chain(decay, state, levels, reverse):
    heads = state.shape[0] // HD

    def scaled(a, s):
        return (a[:heads, None, None] * s.reshape(heads, HD, L)).reshape(s.shape)

    known = levels is not None
    levels = list(levels) if known else []
    before, through = jnp.zeros_like(state), jnp.ones_like(decay)
    masks = masks_of("dp")
    for step, mask in enumerate(masks):
        if known:
            theirs = swap(state.astype(BF), "dp", mask).astype(F32)
            a = levels[step]
        else:
            hi, lo = split(decay)
            tail = jnp.concatenate([hi[None], lo[None], jnp.zeros((14, L), BF)], axis=0)
            got = swap(jnp.concatenate([state.astype(BF), tail], axis=0), "dp", mask).astype(F32)
            theirs, a = got[: state.shape[0]], got[state.shape[0]] + got[state.shape[0] + 1]
            levels.append(a)
        ahead = bit_of("dp", mask) == (0 if reverse else 1)
        before = before + jnp.where(ahead, scaled(through, theirs), 0.0)
        through = jnp.where(ahead, through * a, through)
        state = jnp.where(ahead, scaled(decay, theirs) + state, scaled(a, state) + theirs)
        decay = decay * a
    return before, levels


def on_device(
    tokens_in,
    grad_out,
    scene_offsets,
    input_gain,
    weight_zx,
    weight_bc,
    weight_step,
    conv_inner,
    conv_inner_bias,
    conv_bc,
    conv_bc_bias,
    step_bias,
    decay_log,
    skip_weight,
    norm_gain,
    weight_out,
):
    share, d = tokens_in.shape
    group = lax.axis_size("tensor")
    tokens = share * group
    heads = step_bias.shape[0]
    width = norm_gain.shape[0]
    wide = width + 2 * L
    count = tokens // L
    per = share // L
    half = group // 2
    me = lax.axis_index("tensor")
    place = lax.axis_index("dp")

    heads_pos = place * tokens + jnp.arange(count + 1, dtype=jnp.int32) * L
    starts = jnp.any(heads_pos[:, None] == scene_offsets[None, :], axis=1).astype(jnp.int32)
    meta = jnp.concatenate([me[None].astype(jnp.int32), starts])

    def pad_heads(v):
        return jnp.pad(v, (0, L - heads))[None]

    wst = jnp.pad(weight_step, ((0, 0), (0, L - heads)))
    sbias = pad_heads(step_bias)
    rates = pad_heads(-jnp.exp(decay_log))
    kernel = jnp.concatenate([conv_inner, conv_bc[0], conv_bc[1]], axis=1)
    bias = jnp.concatenate([conv_inner_bias, conv_bc_bias[0], conv_bc_bias[1]])[None]
    skip = jnp.repeat(skip_weight, HD)[None]
    ngain = norm_gain[None]
    gain = input_gain[None]
    spread = (
        jnp.arange(L, dtype=jnp.int32)[:, None] == jnp.arange(width, dtype=jnp.int32)[None] // HD
    ).astype(BF)
    tri = (
        jnp.arange(L, dtype=jnp.int32)[:, None] >= jnp.arange(L, dtype=jnp.int32)[None]
    ).astype(BF)
    ones = jnp.ones((8, width), BF)

    def place_of(c, meta):
        if per == 1:
            return lax.bitwise_xor(c, meta[0])
        return lax.bitwise_xor(lax.div(c, per), meta[0]) * per + lax.rem(c, per)

    def stretched(body, name, ins, outs, scratch, reverse, vmem, flops):
        def order(i):
            return count - 1 - i if reverse else i

        def spec(kind, shape):
            if kind == "rows":
                return pl.BlockSpec((L, shape[1]), lambda i, m: (place_of(order(i), m), 0))
            if kind == "each":
                return pl.BlockSpec((1, *shape[1:]), lambda i, m: (order(i), 0, 0))
            return pl.BlockSpec(shape, lambda i, m: (0,) * len(shape))

        return pl.pallas_call(
            body,
            grid_spec=pltpu.PrefetchScalarGridSpec(
                num_scalar_prefetch=1,
                grid=(count,),
                in_specs=[spec(k, a.shape) for k, a in ins],
                out_specs=[spec(k, s) for k, s, _ in outs],
                scratch_shapes=scratch,
            ),
            out_shape=[jax.ShapeDtypeStruct(s, t) for _, s, t in outs],
            compiler_params=pltpu.CompilerParams(vmem_limit_bytes=vmem * MIB),
            cost_estimate=pl.CostEstimate(
                flops=flops,
                bytes_accessed=sum(a.size * a.dtype.itemsize for _, a in ins),
                transcendentals=tokens * wide,
            ),
            name=name,
        )(meta, *[a for _, a in ins])

    toks = frames(tokens_in, group)
    before = project(toks[:half], gain, weight_zx, weight_bc, wst, tokens, 0, None)
    normed, gate_raw, cat, step_raw = project(
        toks[half:], gain, weight_zx, weight_bc, wst, tokens, half, before
    )
    held, grad_held = lax.optimization_barrier((toks[half], grad_out))
    del held
    cots = frames(grad_held, group)

    last = (lax.bitwise_xor(me, group - 1) + 1) * share - 16
    rim = lax.ppermute(
        lax.dynamic_slice_in_dim(cat, last, 16, 0),
        "dp",
        [(i, i + 1) for i in range(lax.axis_size("dp") - 1)],
    )
    tall = (tokens, L)
    state_shape = (width, L)
    pre, sin, own_end, cum, pfx, through = stretched(
        states_body,
        "states",
        [("rows", cat), ("rows", step_raw), ("one", rim), ("one", kernel), ("one", bias),
         ("one", sbias), ("one", rates), ("one", spread), ("one", tri)],
        [("rows", (tokens, wide), F32), ("each", (count, *state_shape), BF),
         ("one", state_shape, F32), ("rows", tall, F32), ("each", (count, 8, L), F32),
         ("one", (8, L), F32)],
        [pltpu.VMEM((L + 8, wide), F32), pltpu.VMEM(state_shape, F32), pltpu.VMEM((8, L), F32)],
        False, 32, 2 * tokens * width * L * 3,
    )
    incoming, levels = chain(through[0], own_end, None, False)
    incoming = incoming.astype(BF)

    (y,) = stretched(
        within_body,
        "within",
        [("rows", pre), ("rows", step_raw), ("rows", cum), ("each", sin), ("one", sbias),
         ("one", spread)],
        [("rows", (tokens, width), F32)],
        [], False, 32, 2 * tokens * width * L * 6,
    )
    cot_all, gn = cotangent(cots, weight_out)
    mixed, sums = stretched(
        gate_body,
        "gated",
        [("rows", pre), ("rows", cum), ("each", pfx), ("rows", y), ("rows", gate_raw),
         ("rows", gn), ("one", incoming), ("one", ngain), ("one", skip), ("one", spread),
         ("one", ones)],
        [("rows", (tokens, width), F32), ("each", (count, 8, L), F32)],
        [], False, 32, 2 * tokens * width * L * 4,
    )
    sums = everyone(sums, "tensor")
    normout, gm, ggr, gs, toward, sfx, gate_acc = stretched(
        functools.partial(back_gate_body, count),
        "back_gated",
        [("rows", pre), ("rows", cum), ("rows", mixed), ("rows", gate_raw), ("rows", gn),
         ("each", sums), ("one", ngain), ("one", skip), ("one", spread)],
        [("rows", (tokens, width), BF), ("rows", (tokens, width), BF),
         ("rows", (tokens, width), BF), ("each", (count, *state_shape), BF),
         ("one", state_shape, F32), ("each", (count, 8, L), F32), ("one", (8, width), F32)],
        [pltpu.VMEM(state_shape, F32), pltpu.VMEM((8, L), F32), pltpu.VMEM((16, width), F32)],
        True, 32, 2 * tokens * width * L * 3,
    )
    outgoing, _ = chain(through[0], toward, levels, True)
    outgoing = outgoing.astype(BF)

    branch = scatter_frames(
        lambda first, k: rows_times(
            outproj_body, first, k, share, d, [normout], [weight_out], "outproj"
        ),
        group,
    )
    layer_out = (tokens_in.astype(F32) + branch).astype(BF)

    def wgrad(a, b):
        return jnp.einsum("ta,tb->ab", a, b, preferred_element_type=F32).astype(BF)

    masks = masks_of("dp")

    def summed(x):
        return doubles(halves(x, "dp", masks), "dp", masks)

    grad_weight_out = summed(wgrad(normout, cot_all)).astype(F32)
    grad_gate_w = summed(wgrad(normed, ggr))

    ginner, gbc, glog, gst = stretched(
        back_within_body,
        "back_within",
        [("rows", pre), ("rows", step_raw), ("rows", cum), ("each", sin), ("each", pfx),
         ("each", gs), ("rows", gm), ("one", incoming), ("one", sbias), ("one", skip),
         ("one", spread), ("one", tri), ("one", ones)],
        [("rows", (tokens, width), F32), ("rows", (tokens, 2 * L), F32), ("rows", tall, F32),
         ("rows", tall, F32)],
        [], True, 32, 2 * tokens * width * L * 12,
    )
    gcat, gsr, head, conv_acc, head_acc = stretched(
        functools.partial(back_conv_body, count),
        "back_conv",
        [("rows", cat), ("one", rim), ("rows", pre), ("rows", step_raw), ("rows", cum),
         ("each", sin), ("each", pfx), ("each", sfx), ("rows", ginner), ("rows", gbc),
         ("rows", glog), ("rows", gst), ("one", incoming), ("one", outgoing), ("one", kernel),
         ("one", sbias), ("one", rates), ("one", spread), ("one", tri), ("one", ones)],
        [("rows", (tokens, wide), BF), ("rows", tall, BF), ("one", (8, wide), F32),
         ("one", (8, wide), F32), ("one", (8, L), F32)],
        [pltpu.VMEM((L + 8, wide), F32), pltpu.VMEM((40, wide), F32), pltpu.VMEM((16, L), F32)],
        True, 32, 2 * tokens * width * L * 6,
    )

    ahead = lax.ppermute(
        head, "dp", [(i + 1, i) for i in range(lax.axis_size("dp") - 1)]
    ) * (1 - starts[count]).astype(F32)
    extra = jnp.zeros((16, wide), F32)
    for j in range(1, KERNEL):
        extra = extra.at[16 - j :].add(kernel[3 - j] * ahead[:j])
    rim_rows = lax.dynamic_slice_in_dim(gcat, last, 16, 0)
    gcat = lax.dynamic_update_slice_in_dim(gcat, add(rim_rows, extra), last, 0)

    grad_normed = scatter_frames(
        lambda first, k: rows_times(
            dgrad_body, first, k, share, d, [ggr, gcat, gsr],
            [weight_zx, weight_bc, wst], "dgrad",
        ),
        group,
    )
    grad_main = wgrad(normed, gcat)
    grad_inner_w = summed(grad_main[:, :width])
    tmasks = masks_of("tensor")
    grad_bc_w = halves(grad_main[:, width:], "tensor", tmasks)
    grad_bc_w = doubles(summed(grad_bc_w), "tensor", tmasks).astype(F32)
    grad_step_w = jnp.einsum("th,td->hd", gsr, normed, preferred_element_type=F32)[:heads]

    rows_in = tokens_in.astype(F32)
    rstd = lax.rsqrt(jnp.mean(rows_in * rows_in, axis=1, keepdims=True) + EPS)
    unit = rows_in * rstd
    grad_unit = grad_normed * input_gain
    grad_tokens = grad_out.astype(F32) + rstd * (
        grad_unit - unit * jnp.mean(grad_unit * unit, axis=1, keepdims=True)
    )
    grad_input_gain = jnp.sum(grad_normed * unit, axis=0)

    shared = jnp.concatenate([grad_input_gain, conv_acc[:5, width:].reshape(-1)])
    own = jnp.concatenate(
        [
            grad_step_w.reshape(-1),
            conv_acc[:5, :width].reshape(-1),
            gate_acc[:2].reshape(-1),
            head_acc[:2].reshape(-1),
        ]
    )
    shared = everyone(shared, "tensor")
    small = everyone(jnp.concatenate([shared, own]).reshape(-1, L), "dp").reshape(-1)

    def take(n):
        nonlocal small
        got, small = small[:n], small[n:]
        return got

    grad_input_gain = take(d)
    bc_acc = take(5 * 2 * L).reshape(5, 2, L)
    grad_weight_step = take(heads * d).reshape(heads, d).T
    inner_acc = take(5 * width).reshape(5, width)
    gates = take(2 * width).reshape(2, width)
    per_heads = take(2 * L).reshape(2, L)[:, :heads]
    return (
        layer_out,
        grad_tokens,
        grad_input_gain,
        jnp.stack([grad_gate_w, grad_inner_w]).astype(F32),
        jnp.stack([grad_bc_w[:, :L], grad_bc_w[:, L:]]),
        grad_weight_step,
        inner_acc[:4],
        inner_acc[4],
        jnp.moveaxis(bc_acc[:4], 0, 1),
        bc_acc[4],
        per_heads[1],
        per_heads[0],
        jnp.sum(gates[1].reshape(heads, HD), axis=1),
        gates[0],
        grad_weight_out,
    )


def solution(mesh):
    rows = P(("dp", "tensor"), None)
    cols = P(None, "tensor")
    one = P("tensor")
    in_specs = (
        rows, rows, P(), P(), P(None, None, "tensor"), P(), cols, cols, one, P(), P(),
        one, one, one, one, P("tensor", None),
    )
    out_specs = (
        rows, rows, P(), P(None, None, "tensor"), P(), cols, cols, one, P(), P(),
        one, one, one, one, P("tensor", None),
    )
    return jax.shard_map(
        on_device, mesh=mesh, in_specs=in_specs, out_specs=out_specs, check_vma=False
    )
```

time: 808 us -> 362 us (0.45)
  waiting for transfers between devices: 388 us -> 127 us
  matrix products: 132 us -> 7.05 us
  blocking collectives: 106 us -> 0 us
  Pallas kernels: 0 us -> 62.3 us
  starting transfers between devices: 5.9 us -> 50.1 us
  other arithmetic: 76.4 us -> 40.6 us
  between operations: 15.4 us -> 2.94 us
  local copies, waits for them, and re-layouts: 78.8 us -> 70 us
    psum x2 -> x0, waiting for transfers between devices: 350 us -> none  [the longest x1 216 us: on_device(): lax.psum((grad_weight_zx, grad_weight_step, grad_weight_out, grad_kernel[...]
    dot_general x31 -> x4, matrix products: 132 us -> 7.05 us  [the longest x3 6.01 us: wgrad(): return jnp.einsum('ta,tb->ab', a, b, preferred_element_type=F32).astype(BF)]
    ppermute x2 -> x55, waiting for transfers between devices: 3.6 us -> 127 us  [the longest x53 124 us: swap(): return lax.ppermute(x, axis, [(i, i ^ mask) for i in range(count)])]
    psum x4 -> x0, blocking collectives: 85.6 us -> none  [the longest x1 37.7 us: on_device(): lax.psum((grad_input_gain, grad_weight_bc, grad_conv_bc, grad_conv_bc_bia...]
    pallas_call x0 -> x13, Pallas kernels: none -> 62.3 us  [the longest x6 45.3 us: stretched(): pl.pallas_call(body, grid_spec=pltpu.PrefetchScalarGridSpec(num_scalar_pr...]
    ppermute x2 -> x55, starting transfers between devices: 5.36 us -> 50.1 us  [the longest x53 45.2 us: swap(): return lax.ppermute(x, axis, [(i, i ^ mask) for i in range(count)])]
    all_gather x4 -> x0, waiting for transfers between devices: 33.7 us -> none  [the longest x1 17.9 us: on_device(): normed_all = lax.all_gather(normed, 'tensor', axis=0, tiled=True)]
    add x12 -> x9, other arithmetic: 27.6 us -> 4.51 us  [the longest x1 3.06 us: on_device(): grad_out.astype(F32)]
  transfers between devices with their start and end apart: 11 -> 55, of which waited for: 7 -> 28; matrix products, arithmetic and copies ran while one was open for 18% -> 21% of each run, Pallas kernels for 0% -> 13%
where the time goes in v1:
time: 362 us; the launch traced here: 360 us
  waiting for transfers between devices  127 us (35%)
  local copies, waits for them, and re-layouts  70 us (19%)
  Pallas kernels  62.3 us (17%)
  starting transfers between devices  50.1 us (14%)
  other arithmetic  40.6 us (11%)
  matrix products  7.05 us (2%)
    ppermute x53, waiting for transfers between devices, swap(): return lax.ppermute(x, axis, [(i, i ^ mask) for i in range(count)])  124 us
    pallas_call x6, Pallas kernels, stretched(): pl.pallas_call(body, grid_spec=pltpu.PrefetchScalarGridSpec(num_scalar_pr...  45.3 us
    ppermute x53, starting transfers between devices, swap(): return lax.ppermute(x, axis, [(i, i ^ mask) for i in range(count)])  45.2 us
    unnamed x202, local copies, waits for them, and re-layouts  38.2 us
    mul x17, local copies, waits for them, and re-layouts, scaled(): return (a[:heads, None, None] * s.reshape(heads, HD, L)).reshape(s.shape)  18 us
    pallas_call x4, Pallas kernels, rows_times(): pl.pallas_call(functools.partial(body, k), grid=(k,), in_specs=[pl.BlockS...  8.35 us
  transfers between devices with their start and end apart: 55, of which 28 were waited for; matrix products, arithmetic and copies ran while one was open for 21% of the time, Pallas kernels for 13%

profile of v1, /device:TPU:0, one launch (start us, length us, event | category | flops | bytes accessed | tf_op | source)
XLA Modules:
  0.0 359.9 jit_solution(1897649316487554728)
XLA Ops:
  1.2 2.6 collective-permute-start
  8.6 7.8 %collective-permute-done.refs_0_ = bf16[256,1024]{1,0:T(8,128)(2,1)S(1)} collective-permute-done((bf16[256,1024]{1,0:T(8,128)(2,1)}, bf16[256,1024]{1,0:T(8,128)(2,1)S(1)}, u32[]{:S(2)}, u32[]{:S(2)}) %collective-permute-start) | collective-permute-done | bytes 524320 | tf_op jit(solution)/shard_map/ppermute | solution.py:552
  25.5 2.5 project.2
  28.1 2.6 project.3
  34.2 3.4 collective-permute-start.3
  45.7 7.1 %states.1 = (f32[1024,768]{1,0:T(8,128)S(1)}, bf16[8,512,128]{2,1,0:T(8,128)(2,1)S(1)}, f32[512,128]{1,0:T(8,128)S(1)}, f32[1024,128]{1,0:T(8,128)S(1)}, f32[8,8,128]{2,1,0:T(8,128)S(1)}, /*index=5*/f32[8,128]{1,0:T(8,128)S(1)}) custom-call(s32[10]{0:T(128)S(1)} %copy-done.62, bf16[1024,768]{1,0:T(8,128)(2,1)S(1)} %copy-done.4, ...), custom_call_target="tpu_custom_call" | custom-call | flops 402653184 | bytes 2039808 | tf_op jit(solution)/shard_map/states/pallas_call | solution.py:720
  56.2 1.9 collective-permute-start.7
  63.6 4.5 %within.1.y = f32[1024,512]{1,0:T(8,128)S(1)} custom-call(s32[10]{0:T(128)S(1)} %copy-done.63, f32[1024,768]{1,0:T(8,128)S(1)} %get-tuple-element.100.pre, bf16[1024,128]{1,0:T(8,128)(2,1)S(1)} %get-tuple-element.99.step, f32[1024,128]{1,0:T(8,128)S(1)} %copy-done.7, bf16[8,512,128]{2,1,0:T(8,128)(2,1)S(1)} %copy-done.15, f32[1,128]{1,0:T(1,128)S(1)} %copy-done.71, ...), custom_call_target="tpu_custom_call" | custom-call | flops 805306368 | bytes 5112320 | tf_op jit(solution)/shard_map/within/pallas_call | solution.py:720
  94.5 2.6 collective-permute-start.9
  105.1 3.5 cotangent.1
  110.1 5.3 %gated.1 = (f32[1024,512]{1,0:T(8,128)S(1)}, f32[8,8,128]{2,1,0:T(8,128)S(1)}) custom-call(s32[10]{0:T(128)S(1)} %copy-done.64, f32[1024,768]{1,0:T(8,128)S(1)} %get-tuple-element.100.pre, f32[1024,128]{1,0:T(8,128)S(1)} %copy-done.8, f32[8,8,128]{2,1,0:T(8,128)S(1)} %copy-done.53, f32[1024,512]{1,0:T(8,128)S(1)} %copy-done.18, ...), custom_call_target="tpu_custom_call" | custom-call | flops 536870912 | bytes 8171520 | tf_op jit(solution)/shard_map/gated/pallas_call | solution.py:720
  134.2 5.6 %back_gated.1 = (bf16[1024,512]{1,0:T(8,128)(2,1)S(1)}, bf16[1024,512]{1,0:T(8,128)(2,1)S(1)}, bf16[1024,512]{1,0:T(8,128)(2,1)S(1)}, bf16[8,512,128]{2,1,0:T(8,...) custom-call(s32[10]{0:T(128)S(1)} %copy-done.65, ...), custom_call_target="tpu_custom_call" | custom-call | flops 402653184 | bytes 8032256 | tf_op jit(solution)/shard_map/back_gated/pallas_call | solution.py:720
  142.3 1.9 collective-permute-start.15
  146.7 13.3 %collective-permute-done.15 = bf16[512,128]{1,0:T(8,128)(2,1)S(1)} collective-permute-done((bf16[512,128]{1,0:T(8,128)(2,1)S(1)}, bf16[512,128]{1,0:T(8,128)(2,1)S(1)}, u32[]{:S(2)}, u32[]{:S(2)}) %collective-permute-start.15) | collective-permute-done | bytes 131104 | tf_op jit(solution)/shard_map/ppermute | solution.py:552
  167.0 3.0 collective-permute-start.17
  170.1 11.9 %back_within.1 = (f32[1024,512]{1,0:T(8,128)S(1)}, f32[1024,256]{1,0:T(8,128)S(1)}, f32[1024,128]{1,0:T(8,128)S(1)}, f32[1024,128]{1,0:T(8,128)S(1)}) custom-call(s32[10]{0:T(128)S(1)} %copy-done.66, f32[1024,768]{1,0:T(8,128)S(1)} %get-tuple-element.100.pre, bf16[1024,128]{1,0:T(8,128)(2,1)S(1)} %get-tuple-element.99.step, f32[1024,128]{1,0:T(8,128)S(1)} %copy-done.10, ...), custom_call_target="tpu_custom_call" | custom-call | flops 1610612736 | bytes 7416320 | tf_op jit(solution)/shard_map/back_within/pallas_call | solution.py:720
  182.3 10.9 %back_conv.1 = (bf16[1024,768]{1,0:T(8,128)(2,1)S(1)}, bf16[1024,128]{1,0:T(8,128)(2,1)S(1)}, f32[8,768]{1,0:T(8,128)}, f32[8,768]{1,0:T(8,128)S(1)}, f32[8,128]{1,0:T(8,128)S(1)}) custom-call(s32[10]{0:T(128)S(1)} %copy-done.66, bf16[1024,768]{1,0:T(8,128)(2,1)S(1)} %copy-done.5, bf16[16,768]{1,0:T(8,128)(2,1)S(1)} %copy-done.59, ...), custom_call_target="tpu_custom_call" | custom-call | flops 805306368 | bytes 11285504 | tf_op jit(solution)/shard_map/back_conv/pallas_call | solution.py:720
  196.4 3.0 collective-permute-done.18
  201.0 3.5 convolution_convert_fusion
  206.5 2.3 dgrad.2
  208.9 2.6 dgrad.3
  217.3 2.1 collective-permute-start.28
  219.5 5.7 %collective-permute-done.50 = bf16[128,1024]{1,0:T(8,128)(2,1)S(1)} collective-permute-done((bf16[128,1024]{1,0:T(8,128)(2,1)S(1)}, bf16[128,1024]{1,0:T(8,128)(2,1)S(1)}, u32[]{:S(2)}, u32[]{:S(2)}) %collective-permute-start.50) | collective-permute-done | bytes 262176 | tf_op jit(solution)/shard_map/ppermute | solution.py:552
  225.2 5.1 %collective-permute-done.28 = bf16[256,512]{1,0:T(8,128)(2,1)S(1)} collective-permute-done((bf16[256,512]{1,0:T(8,128)(2,1)S(1)}, bf16[256,512]{1,0:T(8,128)(2,1)S(1)}, u32[]{:S(2)}, u32[]{:S(2)}) %collective-permute-start.28) | collective-permute-done | bytes 262176 | tf_op jit(solution)/shard_map/ppermute | solution.py:552
  231.9 3.5 collective-permute-done.40
  236.0 3.9 %collective-permute-done.41 = bf16[128,256]{1,0:T(8,128)(2,1)S(1)} collective-permute-done((bf16[128,256]{1,0:T(8,128)(2,1)S(1)}, bf16[128,256]{1,0:T(8,128)(2,1)S(1)}, u32[]{:S(2)}, u32[]{:S(2)}) %collective-permute-start.41) | collective-permute-done | bytes 65568 | tf_op jit(solution)/shard_map/ppermute | solution.py:552
  240.4 3.4 collective-permute-done.42
  243.9 7.5 %collective-permute-done.51 = bf16[64,1024]{1,0:T(8,128)(2,1)S(1)} collective-permute-done((bf16[64,1024]{1,0:T(8,128)(2,1)S(1)}, bf16[64,1024]{1,0:T(8,128)(2,1)S(1)}, u32[]{:S(2)}, u32[]{:S(2)}) %collective-permute-start.51) | collective-permute-done | bytes 131104 | tf_op jit(solution)/shard_map/ppermute | solution.py:552
  251.5 4.6 %collective-permute-done.43 = bf16[32,256]{1,0:T(8,128)(2,1)S(1)} collective-permute-done((bf16[32,256]{1,0:T(8,128)(2,1)S(1)}, bf16[32,256]{1,0:T(8,128)(2,1)S(1)}, u32[]{:S(2)}, u32[]{:S(2)}) %collective-permute-start.43) | collective-permute-done | bytes 16416 | tf_op jit(solution)/shard_map/ppermute | solution.py:552
  256.2 6.1 %collective-permute-done.29 = bf16[128,512]{1,0:T(8,128)(2,1)S(1)} collective-permute-done((bf16[128,512]{1,0:T(8,128)(2,1)S(1)}, bf16[128,512]{1,0:T(8,128)(2,1)S(1)}, u32[]{:S(2)}, u32[]{:S(2)}) %collective-permute-start.29) | collective-permute-done | bytes 131104 | tf_op jit(solution)/shard_map/ppermute | solution.py:552
  262.3 6.2 %collective-permute-done.44 = bf16[32,256]{1,0:T(8,128)(2,1)S(1)} collective-permute-done((bf16[32,256]{1,0:T(8,128)(2,1)S(1)}, bf16[32,256]{1,0:T(8,128)(2,1)S(1)}, u32[]{:S(2)}, u32[]{:S(2)}) %collective-permute-start.44) | collective-permute-done | bytes 16416 | tf_op jit(solution)/shard_map/ppermute | solution.py:552
  268.6 3.0 collective-permute-start.30
  272.0 4.2 %collective-permute-done.45 = bf16[64,256]{1,0:T(8,128)(2,1)S(1)} collective-permute-done((bf16[64,256]{1,0:T(8,128)(2,1)S(1)}, bf16[64,256]{1,0:T(8,128)(2,1)S(1)}, u32[]{:S(2)}, u32[]{:S(2)}) %collective-permute-start.45) | collective-permute-done | bytes 32800 | tf_op jit(solution)/shard_map/ppermute | solution.py:552
  276.7 3.9 %collective-permute-done.46 = bf16[128,256]{1,0:T(8,128)(2,1)S(1)} collective-permute-done((bf16[128,256]{1,0:T(8,128)(2,1)S(1)}, bf16[128,256]{1,0:T(8,128)(2,1)S(1)}, u32[]{:S(2)}, u32[]{:S(2)}) %collective-permute-start.46) | collective-permute-done | bytes 65568 | tf_op jit(solution)/shard_map/ppermute | solution.py:552
  280.5 2.5 collective-permute-start.34
  285.4 2.7 collective-permute-done.47
  288.8 1.9 collective-permute-start.31
  290.8 3.7 %collective-permute-done.53 = bf16[128,1024]{1,0:T(8,128)(2,1)S(1)} collective-permute-done((bf16[128,1024]{1,0:T(8,128)(2,1)S(1)}, bf16[128,1024]{1,0:T(8,128)(2,1)S(1)}, u32[]{:S(2)}, u32[]{:S(2)}) %collective-permute-start.53) | collective-permute-done | bytes 262176 | tf_op jit(solution)/shard_map/ppermute | solution.py:552
  297.5 3.7 %collective-permute-done.35 = bf16[128,512]{1,0:T(8,128)(2,1)S(1)} collective-permute-done((bf16[128,512]{1,0:T(8,128)(2,1)S(1)}, bf16[128,512]{1,0:T(8,128)(2,1)S(1)}, u32[]{:S(2)}, u32[]{:S(2)}) %collective-permute-start.35) | collective-permute-done | bytes 131104 | tf_op jit(solution)/shard_map/ppermute | solution.py:552
  308.5 3.7 %collective-permute-done.23 = f32[2304]{0:T(1024)S(1)} collective-permute-done((f32[2304]{0:T(1024)S(1)}, f32[2304]{0:T(1024)S(1)}, u32[]{:S(2)}, u32[]{:S(2)}) %collective-permute-start.23) | collective-permute-done | bytes 9248 | tf_op jit(solution)/shard_map/ppermute | solution.py:552
  312.7 13.0 %collective-permute-done.24 = f32[112,128]{1,0:T(8,128)S(1)} collective-permute-done((f32[112,128]{1,0:T(8,128)S(1)}, f32[112,128]{1,0:T(8,128)S(1)}, u32[]{:S(2)}, u32[]{:S(2)}) %collective-permute-start.24) | collective-permute-done | bytes 57376 | tf_op jit(solution)/shard_map/ppermute | solution.py:552
  326.6 5.8 %collective-permute-done.36 = bf16[128,512]{1,0:T(8,128)(2,1)S(1)} collective-permute-done((bf16[128,512]{1,0:T(8,128)(2,1)S(1)}, bf16[128,512]{1,0:T(8,128)(2,1)S(1)}, u32[]{:S(2)}, u32[]{:S(2)}) %collective-permute-start.36) | collective-permute-done | bytes 131104 | tf_op jit(solution)/shard_map/ppermute | solution.py:552
  332.6 4.8 %collective-permute-done.25 = f32[112,128]{1,0:T(8,128)S(1)} collective-permute-done((f32[112,128]{1,0:T(8,128)S(1)}, f32[112,128]{1,0:T(8,128)S(1)}, u32[]{:S(2)}, u32[]{:S(2)}) %collective-permute-start.25) | collective-permute-done | bytes 57376 | tf_op jit(solution)/shard_map/ppermute | solution.py:552
  337.4 2.9 collective-permute-start.26
  340.3 3.1 fusion.6
  349.3 2.9 fusion.10
  352.2 4.9 %collective-permute-done.38 = bf16[512,512]{1,0:T(8,128)(2,1)S(1)} collective-permute-done((bf16[512,512]{1,0:T(8,128)(2,1)S(1)}, bf16[512,512]{1,0:T(8,128)(2,1)S(1)}, u32[]{:S(2)}, u32[]{:S(2)}) %collective-permute-start.38) | collective-permute-done | bytes 524320 | tf_op jit(solution)/shard_map/ppermute | solution.py:552
  357.6 2.3 maximum_convert_fusion
  (431 shorter events, 138.1 us)
Async XLA Ops:
  0.6 20.4 %collective-permute-start.2 = (bf16[256,1024]{1,0:T(8,128)(2,1)}, bf16[256,1024]{1,0:T(8,128)(2,1)S(1)}, u32[]{:S(2)}, u32[]{:S(2)}) collective-permute-start(bf16[256,1024]{1,0:T(8,128)(2,1)} %refs_0_.1), channel_id=1, source_target_pairs={{0,1},{1,0},{2,3},{3,2},{4,5},{5,4},{6,7},{7,6},{8,9},{9,8},{10,11... | collective-permute-start | bytes 1572872 | tf_op jit(solution)/shard_map/ppermute | solution.py:552
  1.2 15.3 %collective-permute-start = (bf16[256,1024]{1,0:T(8,128)(2,1)}, bf16[256,1024]{1,0:T(8,128)(2,1)S(1)}, u32[]{:S(2)}, u32[]{:S(2)}) collective-permute-start(bf16[256,1024]{1,0:T(8,128)(2,1)} %refs_0_.1), channel_id=1, source_target_pairs={{0,2},{1,3},{2,0},{3,1},{4,6},{5,7},{6,4},{7,5},{8,10},{9,11},{10,... | collective-permute-start | bytes 1572872 | tf_op jit(solution)/shard_map/ppermute | solution.py:552
  16.5 11.6 %collective-permute-start.1 = (bf16[256,1024]{1,0:T(8,128)(2,1)S(1)}, bf16[256,1024]{1,0:T(8,128)(2,1)S(1)}, u32[]{:S(2)}, u32[]{:S(2)}) collective-permute-start(bf16[256,1024]{1,0:T(8,128)(2,1)S(1)} %collective-permute-done.refs_0_), channel_id=1, source_target_pairs={{0,1},{1,0},{2,3},{3,2},{4,5},{5,4},{6,7},{7,6},{8,9},{9,8},{10,11... | collective-permute-start | bytes 1572872 | tf_op jit(solution)/shard_map/ppermute | solution.py:552
  17.7 21.4 %collective-permute-start.5 = (bf16[256,1024]{1,0:T(8,128)(2,1)}, bf16[256,1024]{1,0:T(8,128)(2,1)}, u32[]{:S(2)}, u32[]{:S(2)}) collective-permute-start(bf16[256,1024]{1,0:T(8,128)(2,1)} %refs_0_.2), channel_id=1, source_target_pairs={{0,2},{1,3},{2,0},{3,1},{4,6},{5,7},{6,4},{7,5},{8,10},{9,11},{10,... | collective-permute-start | bytes 1572872 | tf_op jit(solution)/shard_map/ppermute | solution.py:552
  34.2 5.4 %collective-permute-start.3 = (bf16[16,768]{1,0:T(8,128)(2,1)S(1)}, bf16[16,768]{1,0:T(8,128)(2,1)S(1)}, u32[]{:S(2)}, u32[]{:S(2)}) collective-permute-start(bf16[16,768]{1,0:T(8,128)(2,1)S(1)} %constant_dynamic-slice_fusion.14), channel_id=1, source_target_pairs={{0,4},{4,8},{8,12},{12,16},{16,20},{20,24},{24,28},{1,5},{5,9},{9,... | collective-permute-start | bytes 73736 | tf_op jit(solution)/shard_map/ppermute | solution.py:749
  39.0 64.7 %collective-permute-start.4 = (bf16[256,1024]{1,0:T(8,128)(2,1)}, bf16[256,1024]{1,0:T(8,128)(2,1)}, u32[]{:S(2)}, u32[]{:S(2)}) collective-permute-start(bf16[256,1024]{1,0:T(8,128)(2,1)} %refs_0_.2), channel_id=1, source_target_pairs={{0,1},{1,0},{2,3},{3,2},{4,5},{5,4},{6,7},{7,6},{8,9},{9,8},{10,11... | collective-permute-start | bytes 1572872 | tf_op jit(solution)/shard_map/ppermute | solution.py:552
  39.0 64.7 %collective-permute-start.6 = (bf16[256,1024]{1,0:T(8,128)(2,1)}, bf16[256,1024]{1,0:T(8,128)(2,1)}, u32[]{:S(2)}, u32[]{:S(2)}) collective-permute-start(bf16[256,1024]{1,0:T(8,128)(2,1)} %collective-permute-done.5.refs_2_), channel_id=1, source_target_pairs={{0,1},{1,0},{2,3},{3,2},{4,5},{5,4},{6,7},{7,6},{8,9},{9,8},{10,11... | collective-permute-start | bytes 1572872 | tf_op jit(solution)/shard_map/ppermute | solution.py:552
  56.2 13.3 %collective-permute-start.7 = (bf16[528,128]{1,0:T(8,128)(2,1)}, bf16[528,128]{1,0:T(8,128)(2,1)}, u32[]{:S(2)}, u32[]{:S(2)}) collective-permute-start(bf16[528,128]{1,0:T(8,128)(2,1)} %maximum_maximum_fusion), channel_id=1, source_target_pairs={{0,4},{4,0},{8,12},{12,8},{16,20},{20,16},{24,28},{28,24},{1,5},{5... | collective-permute-start | bytes 405512 | tf_op jit(solution)/shard_map/ppermute | solution.py:552
  78.3 5.3 %collective-permute-start.8 = (bf16[528,128]{1,0:T(8,128)(2,1)}, bf16[528,128]{1,0:T(8,128)(2,1)}, u32[]{:S(2)}, u32[]{:S(2)}) collective-permute-start(bf16[528,128]{1,0:T(8,128)(2,1)} %maximum_maximum_fusion.1), channel_id=1, source_target_pairs={{0,8},{4,12},{8,0},{12,4},{16,24},{20,28},{24,16},{28,20},{1,9},{5... | collective-permute-start | bytes 405512 | tf_op jit(solution)/shard_map/ppermute | solution.py:552
  94.5 7.9 %collective-permute-start.9 = (bf16[528,128]{1,0:T(8,128)(2,1)}, bf16[528,128]{1,0:T(8,128)(2,1)}, u32[]{:S(2)}, u32[]{:S(2)}) collective-permute-start(bf16[528,128]{1,0:T(8,128)(2,1)} %maximum_maximum_fusion.2), channel_id=1, source_target_pairs={{0,16},{4,20},{8,24},{12,28},{16,0},{20,4},{24,8},{28,12},{1,17},{... | collective-permute-start | bytes 405512 | tf_op jit(solution)/shard_map/ppermute | solution.py:552
  118.5 8.5 %collective-permute-start.11 = (f32[8,8,128]{2,1,0:T(8,128)}, f32[8,8,128]{2,1,0:T(8,128)}, u32[]{:S(2)}, u32[]{:S(2)}) collective-permute-start(f32[8,8,128]{2,1,0:T(8,128)} %add.345), channel_id=1, source_target_pairs={{0,2},{1,3},{2,0},{3,1},{4,6},{5,7},{6,4},{7,5},{8,10},{9,11},{10,... | collective-permute-start | bytes 98312 | tf_op jit(solution)/shard_map/ppermute | solution.py:552
  142.1 69.4 %collective-permute-start.49 = (bf16[256,1024]{1,0:T(8,128)(2,1)}, bf16[256,1024]{1,0:T(8,128)(2,1)}, u32[]{:S(2)}, u32[]{:S(2)}) collective-permute-start(bf16[256,1024]{1,0:T(8,128)(2,1)} %constant_dynamic-slice_fusion.2), channel_id=1, source_target_pairs={{0,4},{4,0},{8,12},{12,8},{16,20},{20,16},{24,28},{28,24},{1,5},{5... | collective-permute-start | bytes 1572872 | tf_op jit(solution)/shard_map/ppermute | solution.py:552
  142.3 17.7 %collective-permute-start.15 = (bf16[512,128]{1,0:T(8,128)(2,1)S(1)}, bf16[512,128]{1,0:T(8,128)(2,1)S(1)}, u32[]{:S(2)}, u32[]{:S(2)}) collective-permute-start(bf16[512,128]{1,0:T(8,128)(2,1)S(1)} %convert_element_type.350), channel_id=1, source_target_pairs={{0,4},{4,0},{8,12},{12,8},{16,20},{20,16},{24,28},{28,24},{1,5},{5... | collective-permute-start | bytes 393224 | tf_op jit(solution)/shard_map/ppermute | solution.py:552
  146.5 68.1 %collective-permute-start.27 = (bf16[512,512]{1,0:T(8,128)(2,1)}, bf16[512,512]{1,0:T(8,128)(2,1)}, u32[]{:S(2)}, u32[]{:S(2)}) collective-permute-start(bf16[512,512]{1,0:T(8,128)(2,1)} %constant_dynamic-slice_fusion.13), channel_id=1, source_target_pairs={{0,4},{4,0},{8,12},{12,8},{16,20},{20,16},{24,28},{28,24},{1,5},{5... | collective-permute-start | bytes 1572872 | tf_op jit(solution)/shard_map/ppermute | solution.py:552
  160.2 6.5 %collective-permute-start.16 = (bf16[512,128]{1,0:T(8,128)(2,1)S(1)}, bf16[512,128]{1,0:T(8,128)(2,1)S(1)}, u32[]{:S(2)}, u32[]{:S(2)}) collective-permute-start(bf16[512,128]{1,0:T(8,128)(2,1)S(1)} %fusion.32), channel_id=1, source_target_pairs={{0,8},{4,12},{8,0},{12,4},{16,24},{20,28},{24,16},{28,20},{1,9},{5... | collective-permute-start | bytes 393224 | tf_op jit(solution)/shard_map/ppermute | solution.py:552
  164.5 51.5 %collective-permute-start.13 = (bf16[256,1024]{1,0:T(8,128)(2,1)}, bf16[256,1024]{1,0:T(8,128)(2,1)}, u32[]{:S(2)}, u32[]{:S(2)}) collective-permute-start(bf16[256,1024]{1,0:T(8,128)(2,1)} %get-tuple-element.115), channel_id=1, source_target_pairs={{0,1},{1,0},{2,3},{3,2},{4,5},{5,4},{6,7},{7,6},{8,9},{9,8},{10,11... | collective-permute-start | bytes 1572872 | tf_op jit(solution)/shard_map/ppermute | solution.py:552
  166.2 171.2 %collective-permute-start.12 = (bf16[256,1024]{1,0:T(8,128)(2,1)}, bf16[256,1024]{1,0:T(8,128)(2,1)}, u32[]{:S(2)}, u32[]{:S(2)}) collective-permute-start(bf16[256,1024]{1,0:T(8,128)(2,1)} %get-tuple-element.113), channel_id=1, source_target_pairs={{0,1},{1,0},{2,3},{3,2},{4,5},{5,4},{6,7},{7,6},{8,9},{9,8},{10,11... | collective-permute-start | bytes 1572872 | tf_op jit(solution)/shard_map/ppermute | solution.py:552
  167.0 15.0 %collective-permute-start.17 = (bf16[512,128]{1,0:T(8,128)(2,1)S(1)}, bf16[512,128]{1,0:T(8,128)(2,1)S(1)}, u32[]{:S(2)}, u32[]{:S(2)}) collective-permute-start(bf16[512,128]{1,0:T(8,128)(2,1)S(1)} %fusion.21), channel_id=1, source_target_pairs={{0,16},{4,20},{8,24},{12,28},{16,0},{20,4},{24,8},{28,12},{1,17},{... | collective-permute-start | bytes 393224 | tf_op jit(solution)/shard_map/ppermute | solution.py:552
  193.2 6.2 %collective-permute-start.18 = (f32[8,768]{1,0:T(8,128)}, f32[8,768]{1,0:T(8,128)S(1)}, u32[]{:S(2)}, u32[]{:S(2)}) collective-permute-start(f32[8,768]{1,0:T(8,128)} %get-tuple-element.126), channel_id=1, source_target_pairs={{4,0},{8,4},{12,8},{16,12},{20,16},{24,20},{28,24},{5,1},{9,5},{13... | collective-permute-start | bytes 73736 | tf_op jit(solution)/shard_map/ppermute | solution.py:845
  204.7 12.6 %collective-permute-start.39 = (bf16[512,256]{1,0:T(8,128)(2,1)S(1)}, bf16[512,256]{1,0:T(8,128)(2,1)S(1)}, u32[]{:S(2)}, u32[]{:S(2)}) collective-permute-start(bf16[512,256]{1,0:T(8,128)(2,1)S(1)} %constant_dynamic-slice_fusion.7), channel_id=1, source_target_pairs={{0,1},{1,0},{2,3},{3,2},{4,5},{5,4},{6,7},{7,6},{8,9},{9,8},{10,11... | collective-permute-start | bytes 786440 | tf_op jit(solution)/shard_map/ppermute | solution.py:552
  211.5 60.2 %collective-permute-start.33 = (bf16[512,512]{1,0:T(8,128)(2,1)S(1)}, bf16[512,512]{1,0:T(8,128)(2,1)S(1)}, u32[]{:S(2)}, u32[]{:S(2)}) collective-permute-start(bf16[512,512]{1,0:T(8,128)(2,1)S(1)} %constant_dynamic-slice_fusion.10), channel_id=1, source_target_pairs={{0,4},{4,0},{8,12},{12,8},{16,20},{20,16},{24,28},{28,24},{1,5},{5... | collective-permute-start | bytes 1572872 | tf_op jit(solution)/shard_map/ppermute | solution.py:552
  214.6 88.7 %collective-permute-start.19 = (bf16[256,1024]{1,0:T(8,128)(2,1)S(1)}, bf16[256,1024]{1,0:T(8,128)(2,1)S(1)}, u32[]{:S(2)}, u32[]{:S(2)}) collective-permute-start(bf16[256,1024]{1,0:T(8,128)(2,1)S(1)} %get-tuple-element.129), channel_id=1, source_target_pairs={{0,1},{1,0},{2,3},{3,2},{4,5},{5,4},{6,7},{7,6},{8,9},{9,8},{10,11... | collective-permute-start | bytes 1572872 | tf_op jit(solution)/shard_map/ppermute | solution.py:552
  216.0 9.2 %collective-permute-start.50 = (bf16[128,1024]{1,0:T(8,128)(2,1)S(1)}, bf16[128,1024]{1,0:T(8,128)(2,1)S(1)}, u32[]{:S(2)}, u32[]{:S(2)}) collective-permute-start(bf16[128,1024]{1,0:T(8,128)(2,1)S(1)} %constant_dynamic-slice_fusion.1), channel_id=1, source_target_pairs={{0,8},{4,12},{8,0},{12,4},{16,24},{20,28},{24,16},{28,20},{1,9},{5... | collective-permute-start | bytes 786440 | tf_op jit(solution)/shard_map/ppermute | solution.py:552
  217.3 13.0 %collective-permute-start.28 = (bf16[256,512]{1,0:T(8,128)(2,1)S(1)}, bf16[256,512]{1,0:T(8,128)(2,1)S(1)}, u32[]{:S(2)}, u32[]{:S(2)}) collective-permute-start(bf16[256,512]{1,0:T(8,128)(2,1)S(1)} %constant_dynamic-slice_fusion.12), channel_id=1, source_target_pairs={{0,8},{4,12},{8,0},{12,4},{16,24},{20,28},{24,16},{28,20},{1,9},{5... | collective-permute-start | bytes 786440 | tf_op jit(solution)/shard_map/ppermute | solution.py:552
  225.1 43.4 %collective-permute-start.20 = (bf16[256,1024]{1,0:T(8,128)(2,1)S(1)}, bf16[256,1024]{1,0:T(8,128)(2,1)S(1)}, u32[]{:S(2)}, u32[]{:S(2)}) collective-permute-start(bf16[256,1024]{1,0:T(8,128)(2,1)S(1)} %get-tuple-element.131), channel_id=1, source_target_pairs={{0,1},{1,0},{2,3},{3,2},{4,5},{5,4},{6,7},{7,6},{8,9},{9,8},{10,11... | collective-permute-start | bytes 1572872 | tf_op jit(solution)/shard_map/ppermute | solution.py:552
  230.3 5.1 %collective-permute-start.40 = (bf16[256,256]{1,0:T(8,128)(2,1)S(1)}, bf16[256,256]{1,0:T(8,128)(2,1)S(1)}, u32[]{:S(2)}, u32[]{:S(2)}) collective-permute-start(bf16[256,256]{1,0:T(8,128)(2,1)S(1)} %constant_dynamic-slice_fusion.6), channel_id=1, source_target_pairs={{0,2},{1,3},{2,0},{3,1},{4,6},{5,7},{6,4},{7,5},{8,10},{9,11},{10,... | collective-permute-start | bytes 393224 | tf_op jit(solution)/shard_map/ppermute | solution.py:552
  243.9 7.6 %collective-permute-start.51 = (bf16[64,1024]{1,0:T(8,128)(2,1)S(1)}, bf16[64,1024]{1,0:T(8,128)(2,1)S(1)}, u32[]{:S(2)}, u32[]{:S(2)}) collective-permute-start(bf16[64,1024]{1,0:T(8,128)(2,1)S(1)} %constant_dynamic-slice_fusion), channel_id=1, source_target_pairs={{0,16},{4,20},{8,24},{12,28},{16,0},{20,4},{24,8},{28,12},{1,17},{... | collective-permute-start | bytes 393224 | tf_op jit(solution)/shard_map/ppermute | solution.py:552
  256.1 6.1 %collective-permute-start.29 = (bf16[128,512]{1,0:T(8,128)(2,1)S(1)}, bf16[128,512]{1,0:T(8,128)(2,1)S(1)}, u32[]{:S(2)}, u32[]{:S(2)}) collective-permute-start(bf16[128,512]{1,0:T(8,128)(2,1)S(1)} %constant_dynamic-slice_fusion.11), channel_id=1, source_target_pairs={{0,16},{4,20},{8,24},{12,28},{16,0},{20,4},{24,8},{28,12},{1,17},{... | collective-permute-start | bytes 393224 | tf_op jit(solution)/shard_map/ppermute | solution.py:552
  262.2 6.3 %collective-permute-start.44 = (bf16[32,256]{1,0:T(8,128)(2,1)S(1)}, bf16[32,256]{1,0:T(8,128)(2,1)S(1)}, u32[]{:S(2)}, u32[]{:S(2)}) collective-permute-start(bf16[32,256]{1,0:T(8,128)(2,1)S(1)} %add_convert_fusion.19), channel_id=1, source_target_pairs={{0,16},{4,20},{8,24},{12,28},{16,0},{20,4},{24,8},{28,12},{1,17},{... | collective-permute-start | bytes 49160 | tf_op jit(solution)/shard_map/ppermute | solution.py:552
  268.5 14.5 %collective-permute-start.52 = (bf16[64,1024]{1,0:T(8,128)(2,1)S(1)}, bf16[64,1024]{1,0:T(8,128)(2,1)S(1)}, u32[]{:S(2)}, u32[]{:S(2)}) collective-permute-start(bf16[64,1024]{1,0:T(8,128)(2,1)S(1)} %add_convert_fusion.11), channel_id=1, source_target_pairs={{0,16},{4,20},{8,24},{12,28},{16,0},{20,4},{24,8},{28,12},{1,17},{... | collective-permute-start | bytes 393224 | tf_op jit(solution)/shard_map/ppermute | solution.py:552
  268.6 16.1 %collective-permute-start.30 = (bf16[128,512]{1,0:T(8,128)(2,1)S(1)}, bf16[128,512]{1,0:T(8,128)(2,1)S(1)}, u32[]{:S(2)}, u32[]{:S(2)}) collective-permute-start(bf16[128,512]{1,0:T(8,128)(2,1)S(1)} %add_convert_fusion.14), channel_id=1, source_target_pairs={{0,16},{4,20},{8,24},{12,28},{16,0},{20,4},{24,8},{28,12},{1,17},{... | collective-permute-start | bytes 393224 | tf_op jit(solution)/shard_map/ppermute | solution.py:552
  280.5 8.2 %collective-permute-start.34 = (bf16[256,512]{1,0:T(8,128)(2,1)S(1)}, bf16[256,512]{1,0:T(8,128)(2,1)S(1)}, u32[]{:S(2)}, u32[]{:S(2)}) collective-permute-start(bf16[256,512]{1,0:T(8,128)(2,1)S(1)} %constant_dynamic-slice_fusion.9), channel_id=1, source_target_pairs={{0,8},{4,12},{8,0},{12,4},{16,24},{20,28},{24,16},{28,20},{1,9},{5... | collective-permute-start | bytes 786440 | tf_op jit(solution)/shard_map/ppermute | solution.py:552
  283.1 5.0 %collective-permute-start.47 = (bf16[256,256]{1,0:T(8,128)(2,1)S(1)}, bf16[256,256]{1,0:T(8,128)(2,1)S(1)}, u32[]{:S(2)}, u32[]{:S(2)}) collective-permute-start(bf16[256,256]{1,0:T(8,128)(2,1)S(1)} %maximum_select_fusion.11), channel_id=1, source_target_pairs={{0,2},{1,3},{2,0},{3,1},{4,6},{5,7},{6,4},{7,5},{8,10},{9,11},{10,... | collective-permute-start | bytes 393224 | tf_op jit(solution)/shard_map/ppermute | solution.py:552
  284.7 20.3 %collective-permute-start.21 = (bf16[256,1024]{1,0:T(8,128)(2,1)S(1)}, bf16[256,1024]{1,0:T(8,128)(2,1)S(1)}, u32[]{:S(2)}, u32[]{:S(2)}) collective-permute-start(bf16[256,1024]{1,0:T(8,128)(2,1)S(1)} %add_convert_fusion.3), channel_id=1, source_target_pairs={{0,2},{1,3},{2,0},{3,1},{4,6},{5,7},{6,4},{7,5},{8,10},{9,11},{10,... | collective-permute-start | bytes 1572872 | tf_op jit(solution)/shard_map/ppermute | solution.py:552
  288.1 6.4 %collective-permute-start.53 = (bf16[128,1024]{1,0:T(8,128)(2,1)S(1)}, bf16[128,1024]{1,0:T(8,128)(2,1)S(1)}, u32[]{:S(2)}, u32[]{:S(2)}) collective-permute-start(bf16[128,1024]{1,0:T(8,128)(2,1)S(1)} %maximum_select_fusion.10), channel_id=1, source_target_pairs={{0,8},{4,12},{8,0},{12,4},{16,24},{20,28},{24,16},{28,20},{1,9},{5... | collective-permute-start | bytes 786440 | tf_op jit(solution)/shard_map/ppermute | solution.py:552
  288.8 8.5 %collective-permute-start.31 = (bf16[256,512]{1,0:T(8,128)(2,1)S(1)}, bf16[256,512]{1,0:T(8,128)(2,1)S(1)}, u32[]{:S(2)}, u32[]{:S(2)}) collective-permute-start(bf16[256,512]{1,0:T(8,128)(2,1)S(1)} %maximum_select_fusion.7), channel_id=1, source_target_pairs={{0,8},{4,12},{8,0},{12,4},{16,24},{20,28},{24,16},{28,20},{1,9},{5... | collective-permute-start | bytes 786440 | tf_op jit(solution)/shard_map/ppermute | solution.py:552
  294.5 6.7 %collective-permute-start.35 = (bf16[128,512]{1,0:T(8,128)(2,1)S(1)}, bf16[128,512]{1,0:T(8,128)(2,1)S(1)}, u32[]{:S(2)}, u32[]{:S(2)}) collective-permute-start(bf16[128,512]{1,0:T(8,128)(2,1)S(1)} %constant_dynamic-slice_fusion.8), channel_id=1, source_target_pairs={{0,16},{4,20},{8,24},{12,28},{16,0},{20,4},{24,8},{28,12},{1,17},{... | collective-permute-start | bytes 393224 | tf_op jit(solution)/shard_map/ppermute | solution.py:552
  297.3 5.4 %collective-permute-start.48 = (bf16[512,256]{1,0:T(8,128)(2,1)S(1)}, bf16[512,256]{1,0:T(8,128)(2,1)S(1)}, u32[]{:S(2)}, u32[]{:S(2)}) collective-permute-start(bf16[512,256]{1,0:T(8,128)(2,1)S(1)} %maximum_select_fusion.9), channel_id=1, source_target_pairs={{0,1},{1,0},{2,3},{3,2},{4,5},{5,4},{6,7},{7,6},{8,9},{9,8},{10,11... | collective-permute-start | bytes 786440 | tf_op jit(solution)/shard_map/ppermute | solution.py:552
  301.2 39.1 %collective-permute-start.14 = (bf16[256,1024]{1,0:T(8,128)(2,1)S(1)}, bf16[256,1024]{1,0:T(8,128)(2,1)S(1)}, u32[]{:S(2)}, u32[]{:S(2)}) collective-permute-start(bf16[256,1024]{1,0:T(8,128)(2,1)S(1)} %add_convert_fusion.5), channel_id=1, source_target_pairs={{0,2},{1,3},{2,0},{3,1},{4,6},{5,7},{6,4},{7,5},{8,10},{9,11},{10,... | collective-permute-start | bytes 1572872 | tf_op jit(solution)/shard_map/ppermute | solution.py:552
  302.7 46.6 %collective-permute-start.54 = (bf16[256,1024]{1,0:T(8,128)(2,1)S(1)}, bf16[256,1024]{1,0:T(8,128)(2,1)}, u32[]{:S(2)}, u32[]{:S(2)}) collective-permute-start(bf16[256,1024]{1,0:T(8,128)(2,1)S(1)} %maximum_select_fusion.6), channel_id=1, source_target_pairs={{0,4},{4,0},{8,12},{12,8},{16,20},{20,16},{24,28},{28,24},{1,5},{5... | collective-permute-start | bytes 1572872 | tf_op jit(solution)/shard_map/ppermute | solution.py:552
  303.3 45.5 %collective-permute-start.32 = (bf16[512,512]{1,0:T(8,128)(2,1)S(1)}, bf16[512,512]{1,0:T(8,128)(2,1)S(1)}, u32[]{:S(2)}, u32[]{:S(2)}) collective-permute-start(bf16[512,512]{1,0:T(8,128)(2,1)S(1)} %maximum_select_fusion.3), channel_id=1, source_target_pairs={{0,4},{4,0},{8,12},{12,8},{16,20},{20,16},{24,28},{28,24},{1,5},{5... | collective-permute-start | bytes 1572872 | tf_op jit(solution)/shard_map/ppermute | solution.py:552
  306.9 5.3 %collective-permute-start.23 = (f32[2304]{0:T(1024)S(1)}, f32[2304]{0:T(1024)S(1)}, u32[]{:S(2)}, u32[]{:S(2)}) collective-permute-start(f32[2304]{0:T(1024)S(1)} %fusion.31), channel_id=1, source_target_pairs={{0,2},{1,3},{2,0},{3,1},{4,6},{5,7},{6,4},{7,5},{8,10},{9,11},{10,... | collective-permute-start | bytes 27656 | tf_op jit(solution)/shard_map/ppermute | solution.py:552
  312.3 13.4 %collective-permute-start.24 = (f32[112,128]{1,0:T(8,128)S(1)}, f32[112,128]{1,0:T(8,128)S(1)}, u32[]{:S(2)}, u32[]{:S(2)}) collective-permute-start(f32[112,128]{1,0:T(8,128)S(1)} %bitcast.88), channel_id=1, source_target_pairs={{0,4},{4,0},{8,12},{12,8},{16,20},{20,16},{24,28},{28,24},{1,5},{5... | collective-permute-start | bytes 172040 | tf_op jit(solution)/shard_map/ppermute | solution.py:552
  325.7 6.8 %collective-permute-start.36 = (bf16[128,512]{1,0:T(8,128)(2,1)S(1)}, bf16[128,512]{1,0:T(8,128)(2,1)S(1)}, u32[]{:S(2)}, u32[]{:S(2)}) collective-permute-start(bf16[128,512]{1,0:T(8,128)(2,1)S(1)} %add_convert_fusion.13), channel_id=1, source_target_pairs={{0,16},{4,20},{8,24},{12,28},{16,0},{20,4},{24,8},{28,12},{1,17},{... | collective-permute-start | bytes 393224 | tf_op jit(solution)/shard_map/ppermute | solution.py:552
  332.5 4.9 %collective-permute-start.25 = (f32[112,128]{1,0:T(8,128)S(1)}, f32[112,128]{1,0:T(8,128)S(1)}, u32[]{:S(2)}, u32[]{:S(2)}) collective-permute-start(f32[112,128]{1,0:T(8,128)S(1)} %bitcast_add_fusion), channel_id=1, source_target_pairs={{0,8},{4,12},{8,0},{12,4},{16,24},{20,28},{24,16},{28,20},{1,9},{5... | collective-permute-start | bytes 172040 | tf_op jit(solution)/shard_map/ppermute | solution.py:552
  337.3 10.3 %collective-permute-start.37 = (bf16[256,512]{1,0:T(8,128)(2,1)S(1)}, bf16[256,512]{1,0:T(8,128)(2,1)S(1)}, u32[]{:S(2)}, u32[]{:S(2)}) collective-permute-start(bf16[256,512]{1,0:T(8,128)(2,1)S(1)} %maximum_select_fusion.8), channel_id=1, source_target_pairs={{0,8},{4,12},{8,0},{12,4},{16,24},{20,28},{24,16},{28,20},{1,9},{5... | collective-permute-start | bytes 786440 | tf_op jit(solution)/shard_map/ppermute | solution.py:552
  337.4 6.0 %collective-permute-start.26 = (f32[112,128]{1,0:T(8,128)S(1)}, f32[112,128]{1,0:T(8,128)S(1)}, u32[]{:S(2)}, u32[]{:S(2)}) collective-permute-start(f32[112,128]{1,0:T(8,128)S(1)} %fusion.43), channel_id=1, source_target_pairs={{0,16},{4,20},{8,24},{12,28},{16,0},{20,4},{24,8},{28,12},{1,17},{... | collective-permute-start | bytes 172040 | tf_op jit(solution)/shard_map/ppermute | solution.py:552
  347.9 9.2 %collective-permute-start.38 = (bf16[512,512]{1,0:T(8,128)(2,1)S(1)}, bf16[512,512]{1,0:T(8,128)(2,1)S(1)}, u32[]{:S(2)}, u32[]{:S(2)}) collective-permute-start(bf16[512,512]{1,0:T(8,128)(2,1)S(1)} %maximum_select_fusion.4), channel_id=1, source_target_pairs={{0,4},{4,0},{8,12},{12,8},{16,20},{20,16},{24,28},{28,24},{1,5},{5... | collective-permute-start | bytes 1572872 | tf_op jit(solution)/shard_map/ppermute | solution.py:552
  (105 other events, 561.7 us)

commit v2 on v1

v2 whole, which is shorter than its diff:
```python
import functools

import jax
import jax.numpy as jnp
from jax import lax
from jax.experimental import pallas as pl
from jax.experimental.pallas import tpu as pltpu
from jax.sharding import PartitionSpec as P

KERNEL = 4
L = 128
HD = 64
DI = 2048
EPS = 1e-05
F32 = jnp.float32
BF = jnp.bfloat16
MIB = 1 << 20


def dot(a, b, ca=1, cb=0):
    return lax.dot_general(a, b, (((ca,), (cb,)), ((), ())), preferred_element_type=F32)


def split(a):
    hi = a.astype(BF)
    return hi, (a - hi.astype(F32)).astype(BF)


def dot_l(a, b, ca=1, cb=0):
    hi, lo = split(a)
    return dot(hi, b, ca, cb) + dot(lo, b, ca, cb)


def dot_r(a, b, ca=1, cb=0):
    hi, lo = split(b)
    return dot(a, hi, ca, cb) + dot(a, lo, ca, cb)


def sigmoid(v):
    return 0.5 * jnp.tanh(0.5 * v) + 0.5


def softplus(v):
    u = jnp.exp(-jnp.abs(v))
    small = u * (1.0 - u * (0.5 - u * (1.0 / 3.0 - u * 0.25)))
    return jnp.maximum(v, 0.0) + jnp.where(u < 0.02, small, jnp.log(1.0 + u))


def per_head(row, heads):
    return jnp.concatenate(
        [jnp.broadcast_to(row[:, h : h + 1], (HD, L)) for h in range(heads)], axis=0
    )


def eights(v):
    return jnp.sum(v.reshape(v.shape[0] // 8, 8, v.shape[1]), axis=0)


def across_lanes(v, width):
    return jnp.concatenate([v] * (width // L), axis=1) if width > L else v


def whole(a):
    return pl.BlockSpec(a.shape, lambda *_: (0,) * a.ndim)


def params(vmem):
    return pltpu.CompilerParams(vmem_limit_bytes=vmem * MIB)


def cost(flops, ins):
    return pl.CostEstimate(
        flops=flops, bytes_accessed=2 * sum(a.size * a.dtype.itemsize for a in ins), transcendentals=0
    )


def unit_rows(x, gain):
    x = x.astype(F32)
    rstd = lax.rsqrt(jnp.mean(x * x, axis=1, keepdims=True) + EPS)
    return (x * rstd * gain).astype(BF)


def proj_body(k, rims, deps, meta, *refs):
    toks, past = refs[:k], refs[k : k + rims]
    gain, wzx, wbc, wst = refs[k + rims : k + rims + 4]
    outs = refs[k + rims + 4 + (4 if rims else deps) :]
    normed_o, gate_o, cat_o, step_o = outs[:4]
    width = wzx.shape[2]

    def conv_inputs(normed, out):
        out[:, :width] = dot(normed, wzx[1]).astype(BF)
        out[:, width : width + L] = dot(normed, wbc[0]).astype(BF)
        out[:, width + L :] = dot(normed, wbc[1]).astype(BF)

    def one(j):
        normed = unit_rows(toks[j][...], gain[...])
        normed_o[...] = normed
        conv_inputs(normed, cat_o)
        gate_o[...] = dot(normed, wzx[0]).astype(BF)
        step_o[...] = dot(normed, wst[...]).astype(BF)
        if rims and j == 0:
            rim = past[0][...].astype(F32)
            for p in past[1:]:
                rim = rim + p[...].astype(F32)
            normed = unit_rows(rim, gain[...])
            outs[5][...] = normed
            conv_inputs(normed, outs[4])

    for j in range(k):
        pl.when(pl.program_id(0) == j)(functools.partial(one, j))


def project(meta, toks, past, gain, wzx, wbc, wst, total, first, before):
    k = len(toks)
    share, d = toks[0].shape
    width = wzx.shape[2]
    wide = width + 2 * L
    cols = (d, width, wide, L)
    ins = [*toks, *past, gain, wzx, wbc, wst]
    specs = [whole(a) for a in ins]
    alias = {}
    out_specs = [pl.BlockSpec((share, c), lambda i, m: (i + first, 0)) for c in cols]
    out_shape = [jax.ShapeDtypeStruct((total, c), BF) for c in cols]
    if past:
        alias = {1 + len(ins) + j: j for j in range(4)}
        for c in (wide, d):
            out_specs.append(pl.BlockSpec((16, c), lambda i, m: (0, 0)))
            out_shape.append(jax.ShapeDtypeStruct((16, c), BF))
    ins += before
    specs += [pl.BlockSpec(memory_space=pl.ANY)] * len(before)
    return pl.pallas_call(
        functools.partial(proj_body, k, len(past), len(before)),
        grid_spec=pltpu.PrefetchScalarGridSpec(
            num_scalar_prefetch=1, grid=(k,), in_specs=specs, out_specs=out_specs
        ),
        out_shape=out_shape,
        input_output_aliases=alias,
        compiler_params=params(16),
        cost_estimate=cost(2 * k * share * d * sum(cols[1:]), ins),
        name="project",
    )(meta, *ins)


def prep_body(taps, tbias, btaps, bbias, sbias, decay, skip, ngain, tok, vecs, hv, mats, rows):
    width = taps.shape[1]
    heads = width // HD
    rows[...] = tok[...]
    head = lax.broadcasted_iota(jnp.int32, (L, width), 0)
    lane = lax.broadcasted_iota(jnp.int32, (L, width), 1)
    spread = jnp.where(lax.div(lane, HD) == head, 1.0, 0.0).astype(BF)
    mats[:, :width] = spread
    r = lax.broadcasted_iota(jnp.int32, (L, L), 0)
    c = lax.broadcasted_iota(jnp.int32, (L, L), 1)
    mats[:, width:] = jnp.where(r >= c, 1.0, 0.0).astype(BF)
    hv[...] = jnp.zeros_like(hv)
    hv[0:1, :heads] = sbias[...]
    hv[1:2, :heads] = -jnp.exp(decay[...])
    hv[2:3, :heads] = skip[...]
    vecs[...] = jnp.zeros_like(vecs)
    vecs[0:4, :width] = taps[...]
    vecs[4:5, :width] = tbias[...]
    for k in range(2):
        cols = slice(width + k * L, width + k * L + L)
        vecs[0:4, cols] = btaps[k]
        vecs[4:5, cols] = bbias[k : k + 1, :]
    vecs[5:6, :width] = dot_l(hv[...], spread)[2:3, :]
    vecs[6:7, :width] = ngain[...]


def cot_body(k, *refs):
    cots = refs[:k]
    wout, all_o, gn_o = refs[k:]

    def one(cot):
        v = cot[...]
        all_o[...] = v
        gn_o[...] = dot(v, wout[...], 1, 1).astype(BF)

    for j in range(k):
        pl.when(pl.program_id(0) == j)(functools.partial(one, cots[j]))


def cotangent(cots, wout):
    k = len(cots)
    share, d = cots[0].shape
    width = wout.shape[0]
    return pl.pallas_call(
        functools.partial(cot_body, k),
        grid=(k,),
        in_specs=[whole(a) for a in (*cots, wout)],
        out_specs=[
            pl.BlockSpec((share, d), lambda i: (i, 0)),
            pl.BlockSpec((share, width), lambda i: (i, 0)),
        ],
        out_shape=[
            jax.ShapeDtypeStruct((k * share, d), BF),
            jax.ShapeDtypeStruct((k * share, width), BF),
        ],
        compiler_params=params(12),
        cost_estimate=cost(2 * k * share * d * width, [*cots, wout]),
        name="cotangent",
    )(*cots, wout)


def act_parts(pre, width):
    out = []
    for x0 in range(0, width + 2 * L, L):
        v = pre[:, x0 : x0 + L]
        out.append(v * sigmoid(v))
    return out


def pack(out, state, decay):
    rows = state.shape[0]
    hi, lo = split(jnp.broadcast_to(decay[0:1, :], (16, L)))
    row = lax.broadcasted_iota(jnp.int32, (16, L), 0)
    out[:rows, :] = state.astype(BF)
    tail = jnp.where(row == 0, hi.astype(F32), jnp.where(row == 1, lo.astype(F32), 0.0))
    out[rows:, :] = tail.astype(BF)


def unpack(load):
    v = load[...].astype(F32)
    rows = v.shape[0] - 16
    return v[:rows], v[rows : rows + 1] + v[rows + 1 : rows + 2]


def bit_at(meta, level):
    return jnp.bitwise_and(jnp.right_shift(meta[1], level), 1)


def is_ahead(meta, level, reverse):
    bit = bit_at(meta, level)
    return jnp.where(bit == (0 if reverse else 1), 1.0, 0.0)


def link_body(level, reverse, meta, state, decay, before, through, load,
              load_o, state_o, decay_o, before_o, through_o):
    theirs, a = unpack(load)
    heads = theirs.shape[0] // HD
    ahead = is_ahead(meta, level, reverse)
    mine = decay[0:1, :]
    t = through[0:1, :]
    before_o[...] = before[...] + per_head(t * ahead, heads) * theirs
    through_o[...] = jnp.broadcast_to(t * (ahead * a + (1.0 - ahead)), (8, L))
    joined = (
        per_head(mine * ahead + (1.0 - ahead), heads) * theirs
        + per_head(a * (1.0 - ahead) + ahead, heads) * state[...]
    )
    state_o[...] = joined
    decay_o[...] = jnp.broadcast_to(mine * a, (8, L))
    pack(load_o, joined, mine * a)


def final_link(meta, level, reverse, before, through, load):
    theirs, _ = unpack(load)
    t = through[0:1, :] * is_ahead(meta, level, reverse)
    return before[...] + per_head(t, theirs.shape[0] // HD) * theirs


def states_body(
    meta, cat, step, rim, vecs, hv, mats,
    pre_o, sin_o, end_o, load_o, cum_o, pfx_o, thr_o, buf, state, prod,
):
    c = pl.program_id(0)
    width = vecs.shape[1] - 2 * L
    heads = width // HD
    keep = jnp.where(meta[2 + c] == 0, 1.0, 0.0)

    @pl.when(c == 0)
    def _():
        buf[0:8, :] = rim[...].astype(F32)[8:16, :] * keep
        state[...] = jnp.zeros_like(state)
        prod[...] = jnp.ones_like(prod)

    @pl.when(c > 0)
    def _():
        buf[0:8, :] = buf[L : L + 8, :] * keep

    buf[8 : 8 + L, :] = cat[...].astype(F32)
    acts = []
    for x0 in range(0, width + 2 * L, L):
        cols = slice(x0, x0 + L)
        v = vecs[4:5, cols] + vecs[3:4, cols] * buf[8 : 8 + L, cols]
        for j in range(1, KERNEL):
            v = v + vecs[3 - j : 4 - j, cols] * buf[8 - j : 8 - j + L, cols]
        pre_o[:, cols] = v
        acts.append(v * sigmoid(v))
    steps = softplus(step[...].astype(F32) + hv[0:1, :])
    cum = dot_r(mats[:, width:], steps * hv[1:2, :])
    cum_o[...] = cum
    total = cum[L - 1 : L, :]
    weights = dot_l(jnp.exp(total - cum) * steps, mats[:, :width])
    inner = jnp.concatenate(acts[: width // L], axis=1)
    local = dot((inner * weights).astype(BF), acts[-2].astype(BF), 0, 0)
    entering = state[...] * keep
    sin_o[0] = entering.astype(BF)
    dec = jnp.exp(total)
    leaving = per_head(dec, heads) * entering + local
    state[...] = leaving
    here = prod[...] * keep
    pfx_o[0] = here
    prod[...] = here * dec

    @pl.when(c == pl.num_programs(0) - 1)
    def _():
        end_o[...] = leaving
        thr_o[...] = here * dec
        pack(load_o, leaving, here * dec)


def within_body(meta, pre, step, cum_r, sin, vecs, hv, mats, y_o):
    width = vecs.shape[1] - 2 * L
    heads = width // HD
    acts = act_parts(pre, width)
    bb, cb = acts[-2].astype(BF), acts[-1].astype(BF)
    scores = dot(cb, bb, 1, 1)
    steps = softplus(step[...].astype(F32) + hv[0:1, :])
    cum = cum_r[...]
    cum_t, steps_t = cum.T, steps.T
    lower = lax.broadcasted_iota(jnp.int32, (L, L), 0) >= lax.broadcasted_iota(
        jnp.int32, (L, L), 1
    )
    first = lax.broadcasted_iota(jnp.int32, (L, L), 1) < HD
    grown = dot_l(jnp.exp(cum), mats[:, :width])
    far = grown * dot(cb, sin[0], 1, 1)
    for pair in range(heads // 2):
        cols = slice(pair * L, pair * L + L)
        x = acts[pair].astype(BF)
        got = []
        for h in (2 * pair, 2 * pair + 1):
            gap = jnp.where(lower, cum[:, h : h + 1] - cum_t[h : h + 1, :], -1e30)
            mix = scores * jnp.exp(gap) * steps_t[h : h + 1, :]
            got.append(dot(mix.astype(BF), x))
        y_o[:, cols] = jnp.where(first, got[0], got[1]) + far[:, cols]


def gate_body(
    level, meta, pre, cum, pfx, y, gate, gn, before, through, load, vecs, mats,
    mixed_o, sums_o, incoming,
):
    width = vecs.shape[1] - 2 * L
    ones = jnp.ones((8, width), BF)

    @pl.when(pl.program_id(0) == 0)
    def _():
        incoming[...] = final_link(meta, level, False, before, through, load).astype(BF)

    reach = dot_l(jnp.exp(cum[...]) * pfx[0][0:1, :], mats[:, :width])
    cv = pre[:, width + L :]
    cb = (cv * sigmoid(cv)).astype(BF)
    far = reach * dot(cb, incoming[...], 1, 1)
    squares, crosses = [], []
    for x0 in range(0, width, L):
        cols = slice(x0, x0 + L)
        v = pre[:, cols]
        mixed = y[:, cols] + far[:, cols] + vecs[5:6, cols] * (v * sigmoid(v))
        mixed_o[:, cols] = mixed
        g = gate[:, cols].astype(F32)
        gated = mixed * (g * sigmoid(g))
        squares.append(gated * gated)
        crosses.append(gn[:, cols].astype(F32) * vecs[6:7, cols] * gated)
    square = dot_r(ones, jnp.concatenate(squares, axis=1), 1, 1)
    cross = dot_r(ones, jnp.concatenate(crosses, axis=1), 1, 1)
    row = lax.broadcasted_iota(jnp.int32, (8, L), 0)
    sums_o[0] = jnp.where(row == 0, square, cross)


def back_gate_body(
    count, meta, pre, cum_r, mixed_r, gate, gn, sums, sums2, thr, vecs, mats,
    normout_o, gm_o, ggr_o, gs_o, toward_o, load_o, sfx_o, acc_o, gstate, prod, acc,
):
    i = pl.program_id(0)
    c = count - 1 - i
    width = vecs.shape[1] - 2 * L
    heads = width // HD
    keep = jnp.where(meta[2 + c] == 0, 1.0, 0.0)

    @pl.when(i == 0)
    def _():
        gstate[...] = jnp.zeros_like(gstate)
        prod[...] = jnp.ones_like(prod)
        acc[...] = jnp.zeros_like(acc)

    both = sums[0] + sums2[0]
    square = jnp.broadcast_to(both[0:1, :], (L, L)).T
    cross = jnp.broadcast_to(both[1:2, :], (L, L)).T
    scale = lax.rsqrt(square * (1.0 / DI) + EPS)
    cubed = scale * scale * scale * cross * (1.0 / DI)
    cum = cum_r[...]
    total = cum[L - 1 : L, :]
    grown = dot_l(jnp.exp(cum), mats[:, :width])
    cv = pre[:, width + L :]
    cb = (cv * sigmoid(cv)).astype(BF)
    moved = []
    for x0 in range(0, width, L):
        cols = slice(x0, x0 + L)
        v = pre[:, cols]
        inner = v * sigmoid(v)
        g = gate[:, cols].astype(F32)
        s = sigmoid(g)
        silu = g * s
        mixed = mixed_r[:, cols]
        gated = mixed * silu
        ng = vecs[6:7, cols]
        gnv = gn[:, cols].astype(F32)
        scaled = gated * scale
        normout_o[:, cols] = (scaled * ng).astype(BF)
        gg = scale * (gnv * ng) - gated * cubed
        gm = gg * silu
        gm_o[:, cols] = gm.astype(BF)
        ggr_o[:, cols] = (gg * mixed * (s + silu * (1.0 - s))).astype(BF)
        acc[0:8, cols] += eights(gnv * scaled)
        acc[8:16, cols] += eights(gm * inner)
        moved.append((gm * grown[:, cols]).astype(BF))
    leaving = gstate[...]
    gs_o[0] = leaving.astype(BF)
    here = prod[...]
    sfx_o[0] = here
    dec = jnp.exp(total)
    entering = per_head(dec, heads) * leaving + dot(jnp.concatenate(moved, axis=1), cb, 0, 0)
    entering = entering * keep
    gstate[...] = entering
    prod[...] = here * dec * keep

    @pl.when(i == count - 1)
    def _():
        toward_o[...] = entering
        pack(load_o, entering, thr[...])
        row = lax.broadcasted_iota(jnp.int32, (8, width), 0)
        acc_o[...] = jnp.where(
            row == 0,
            jnp.sum(acc[0:8, :], axis=0, keepdims=True),
            jnp.sum(acc[8:16, :], axis=0, keepdims=True),
        )


def head_product(a, b, spread):
    rows = dot(jnp.ones((8, L), BF), (a * b).astype(BF), 1, 1)
    return dot_l(rows, spread, 1, 1)[0:1, :]


def back_within_body(
    meta, pre, step, cum_r, sin, pfx, gs, gm_r, incoming, vecs, hv, mats,
    ginner_o, gbc_o, glog_o, gst_o,
):
    width = vecs.shape[1] - 2 * L
    heads = width // HD
    acts = act_parts(pre, width)
    bb, cb = acts[-2].astype(BF), acts[-1].astype(BF)
    scores = dot(cb, bb, 1, 1)
    steps = softplus(step[...].astype(F32) + hv[0:1, :])
    cum = cum_r[...]
    total = cum[L - 1 : L, :]
    cum_t, steps_t = cum.T, steps.T
    row = lax.broadcasted_iota(jnp.int32, (L, L), 0)
    col = lax.broadcasted_iota(jnp.int32, (L, L), 1)
    lower = row >= col
    first = col < HD
    e = jnp.exp(cum)
    wd = jnp.exp(total - cum)
    grown = dot_l(e, mats[:, :width])
    weights = dot_l(wd * steps, mats[:, :width])
    gsb = gs[0]
    entering = sin[0].astype(F32) + per_head(pfx[0][0:1, :], heads) * incoming[...].astype(F32)
    eb = entering.astype(BF)
    u = dot(bb, gsb, 1, 1)
    v = dot(cb, eb, 1, 1)
    inner = jnp.concatenate(acts[: width // L], axis=1)
    gm = gm_r[...].astype(F32)
    seen = dot((inner * u).astype(BF), mats[:, :width], 1, 1)
    passed = dot((gm * v).astype(BF), mats[:, :width], 1, 1) * e
    gb = dot((inner * weights).astype(BF), gsb)
    gc = dot((gm * grown).astype(BF), eb)
    through = head_product(gsb.astype(F32), entering, mats[:, :width]) * jnp.exp(total)
    dscores = jnp.zeros((L, L), F32)
    rowsums = jnp.zeros((L, L), F32)
    colsums = jnp.zeros((L, L), F32)
    for pair in range(heads // 2):
        cols = slice(pair * L, pair * L + L)
        xb = acts[pair].astype(BF)
        gmb = gm_r[:, cols]
        got = []
        for h in (2 * pair, 2 * pair + 1):
            mine = first if h % 2 == 0 else jnp.logical_not(first)
            gmh = jnp.where(mine, gm[:, cols], 0.0).astype(BF)
            dm = dot(gmh, xb, 1, 1)
            gap = jnp.where(lower, cum[:, h : h + 1] - cum_t[h : h + 1, :], -1e30)
            decay = jnp.exp(gap)
            st = steps_t[h : h + 1, :]
            t1 = dm * decay
            dscores = dscores + t1 * st
            gp = t1 * scores
            rowsums = jnp.where(col == h, jnp.sum(gp * st, axis=1, keepdims=True), rowsums)
            colsums = jnp.where(row == h, jnp.sum(gp, axis=0, keepdims=True), colsums)
            mix = (scores * decay * st).astype(BF)
            got.append(dot(mix, gmb, 0, 0))
        ginner_o[:, cols] = (
            jnp.where(first, got[0], got[1])
            + weights[:, cols] * u[:, cols]
            + vecs[5:6, cols] * gm[:, cols]
        )
    db = dscores.astype(BF)
    gbc_o[:, :L] = gb + dot(db, cb, 0, 0)
    gbc_o[:, L:] = gc + dot(db, bb)
    direct = colsums.T
    seen = seen * wd
    gst_o[...] = direct + seen
    later = rowsums - direct * steps + passed
    tr = mats[:, width:]
    glog_o[...] = (
        dot_r(tr, later, 0, 0) + dot_r(tr, steps * seen) - steps * seen + through
    )


def crossing(vecs, later):
    row = lax.broadcasted_iota(jnp.int32, (16, later.shape[1]), 0)
    extra = jnp.zeros((16, later.shape[1]), F32)
    for j in range(1, KERNEL):
        for t in range(j):
            part = vecs[3 - j : 4 - j, :] * later[t : t + 1, :]
            extra = extra + jnp.where(row == 16 - j + t, part, 0.0)
    return extra


def back_conv_body(
    count, level, meta, cat, rim, pre, step, cum_r, sin, pfx, sfx, ginner_r, gbc_r, glog_r, gst_r,
    incoming, before, through, load, vecs, hv, mats,
    gcat_o, gsr_o, head_o, extra_o, acc_o, hacc_o, buf, acc, hacc, outgoing,
):
    i = pl.program_id(0)
    c = count - 1 - i
    width = vecs.shape[1] - 2 * L
    heads = width // HD
    keep_next = jnp.where(meta[3 + c] == 0, 1.0, 0.0)
    keep = jnp.where(meta[2 + c] == 0, 1.0, 0.0)

    @pl.when(i == 0)
    def _():
        buf[L : L + 8, :] = jnp.zeros_like(buf[L : L + 8, :])
        acc[...] = jnp.zeros_like(acc)
        hacc[...] = jnp.zeros_like(hacc)
        outgoing[...] = final_link(meta, level, True, before, through, load)

    @pl.when(i > 0)
    def _():
        buf[L : L + 8, :] = buf[0:8, :] * keep_next

    step_in = step[...].astype(F32) + hv[0:1, :]
    steps = softplus(step_in)
    cum = cum_r[...]
    total = cum[L - 1 : L, :]
    wd = jnp.exp(total - cum)
    weights = dot_l(wd * steps, mats[:, :width])
    far = outgoing[...] * per_head(sfx[0][0:1, :], heads)
    fb = far.astype(BF)
    entering = sin[0].astype(F32) + per_head(pfx[0][0:1, :], heads) * incoming[...].astype(F32)
    through = head_product(far, entering, mats[:, :width]) * jnp.exp(total)
    acts, slopes = [], []
    for x0 in range(0, width + 2 * L, L):
        v = pre[:, x0 : x0 + L]
        s = sigmoid(v)
        a = v * s
        acts.append(a)
        slopes.append(s + a * (1.0 - s))
    bb = acts[-2].astype(BF)
    u = dot(bb, fb, 1, 1)
    inner = jnp.concatenate(acts[: width // L], axis=1)
    seen = dot((inner * u).astype(BF), mats[:, :width], 1, 1) * wd
    gb = dot((inner * weights).astype(BF), fb)
    glog = glog_r[...] + dot_r(mats[:, width:], steps * seen) - steps * seen + through
    gsi = (gst_r[...] + seen + glog * hv[1:2, :]) * sigmoid(step_in)
    gsr_o[...] = gsi.astype(BF)
    hacc[0:8, :] += eights(glog * steps * hv[1:2, :])
    hacc[8:16, :] += eights(gsi)
    for k, x0 in enumerate(range(0, width + 2 * L, L)):
        cols = slice(x0, x0 + L)
        if x0 < width:
            g = ginner_r[:, cols] + weights[:, cols] * u[:, cols]
        elif x0 == width:
            g = gbc_r[:, :L] + gb
        else:
            g = gbc_r[:, L:]
        g = g * slopes[k]
        buf[0:L, cols] = g
        acc[32:40, cols] += eights(g)
        here = cat[:, cols].astype(F32)
        out = vecs[3:4, cols] * g
        acc[24:32, cols] += eights(g * here)
        for j in range(1, KERNEL):
            moved = buf[j : j + L, cols]
            out = out + vecs[3 - j : 4 - j, cols] * moved
            acc[24 - 8 * j : 32 - 8 * j, cols] += eights(moved * here)
        gcat_o[:, cols] = out.astype(BF)
    @pl.when(i == count - 1)
    def _():
        head_o[...] = buf[0:8, :]
        past = rim[...].astype(F32)[8:16, :] * keep
        now = buf[0:8, :]
        extra_o[...] = crossing(vecs, now * keep).astype(BF)
        row = lax.broadcasted_iota(jnp.int32, now.shape, 0)
        result = jnp.zeros_like(now)
        for k in range(5):
            part = jnp.sum(acc[8 * k : 8 * k + 8, :], axis=0, keepdims=True)
            j = 3 - k
            if 1 <= j <= 3:
                for t in range(j):
                    part = part + now[t : t + 1, :] * past[8 + t - j : 9 + t - j, :]
            result = jnp.where(row == k, part, result)
        acc_o[...] = result
        hrow = lax.broadcasted_iota(jnp.int32, (8, L), 0)
        hacc_o[...] = jnp.where(
            hrow == 0,
            jnp.sum(hacc[0:8, :], axis=0, keepdims=True),
            jnp.sum(hacc[8:16, :], axis=0, keepdims=True),
        )


def dgrad_body(k, ggr, gcat, gsr, wzx, wbc, wst, *outs):
    width = wzx.shape[2]

    def one(out):
        r = dot(ggr[...], wzx[0], 1, 1)
        r = r + dot(gcat[:, :width], wzx[1], 1, 1)
        r = r + dot(gcat[:, width : width + L], wbc[0], 1, 1)
        r = r + dot(gcat[:, width + L :], wbc[1], 1, 1)
        r = r + dot(gsr[...], wst[...], 1, 1)
        out[...] = r.astype(BF)

    for j in range(k):
        pl.when(pl.program_id(0) == j)(functools.partial(one, outs[j]))


def outproj_body(k, normout, wout, *outs):
    def one(out):
        out[...] = dot(normout[...], wout[...]).astype(BF)

    for j in range(k):
        pl.when(pl.program_id(0) == j)(functools.partial(one, outs[j]))


def rows_times(body, frames_n, share, d, rows, consts, name):
    k = frames_n
    outs = pl.pallas_call(
        functools.partial(body, k),
        grid=(k,),
        in_specs=[pl.BlockSpec((share, r.shape[1]), lambda i: (k - 1 - i, 0)) for r in rows]
        + [whole(a) for a in consts],
        out_specs=[pl.BlockSpec((share, d), lambda i: (0, 0))] * k,
        out_shape=[jax.ShapeDtypeStruct((share, d), BF)] * k,
        compiler_params=params(20),
        cost_estimate=cost(2 * k * share * d * sum(r.shape[1] for r in rows), [*rows, *consts]),
        name=name,
    )(*rows, *consts)
    return list(outs)[::-1]


def after_body(*refs):
    pass


def after(x, *deps):
    return pl.pallas_call(
        after_body,
        in_specs=[pl.BlockSpec(memory_space=pl.ANY)] * (1 + len(deps)),
        out_specs=pl.BlockSpec(memory_space=pl.ANY),
        out_shape=jax.ShapeDtypeStruct(x.shape, x.dtype),
        input_output_aliases={0: 0},
        compiler_params=params(1),
        name="after",
    )(x, *deps)


def hold_body(x, *refs):
    refs[-1][...] = x[...]


def hold(x, *deps):
    return pl.pallas_call(
        hold_body,
        grid=(1,),
        in_specs=[whole(x)] + [pl.BlockSpec(memory_space=pl.ANY)] * len(deps),
        out_specs=whole(x),
        out_shape=jax.ShapeDtypeStruct(x.shape, x.dtype),
        compiler_params=params(4),
        name="hold",
    )(x, *deps)


def add_body(a, b, o):
    o[...] = (a[...].astype(F32) + b[...].astype(F32)).astype(o.dtype)


def add(a, b):
    return pl.pallas_call(
        add_body,
        in_specs=[whole(a), whole(b)],
        out_specs=whole(a),
        out_shape=jax.ShapeDtypeStruct(a.shape, a.dtype),
        grid=(1,),
        compiler_params=params(8),
        cost_estimate=cost(a.size, [a, b]),
        name="add",
    )(a, b)


def swap(x, axis, mask):
    count = lax.axis_size(axis)
    return lax.ppermute(x, axis, [(i, i ^ mask) for i in range(count)])


def frames(x, count):
    got = {0: x}
    mask = count // 2
    while mask:
        for d in sorted(got):
            got[d ^ mask] = swap(got[d], "tensor", mask)
        mask //= 2
    return [got[d] for d in range(count)]


def scatter_frames(parts, count):
    half = count // 2
    held = []
    for first in (half, 0):
        part = dict(enumerate(parts[first : first + half]))
        mask = 1
        while mask < half:
            for d in list(part):
                if d & mask:
                    part[d ^ mask] = add(part[d ^ mask], swap(part.pop(d), "tensor", mask))
            mask *= 2
        held.append(part[0])
    return held[1], swap(held[0], "tensor", half)


def masks_of(axis):
    masks, mask = [], 1
    while mask < lax.axis_size(axis):
        masks.append(mask)
        mask *= 2
    return masks


def halve_body(slot, level, meta, kept, got, send_o, keep_o):
    bit = jnp.bitwise_and(jnp.right_shift(meta[slot], level), 1)
    half = send_o.shape[0]
    for o, b in ((send_o, 1 - bit), (keep_o, bit)):
        rows = pl.ds(pl.multiple_of(b * half, half), half)
        o[...] = (kept[rows, :].astype(F32) + got[rows, :].astype(F32)).astype(BF)


def metaed(body, meta, ins, outs, name, vmem=8):
    return pl.pallas_call(
        body,
        grid_spec=pltpu.PrefetchScalarGridSpec(
            num_scalar_prefetch=1,
            grid=(1,),
            in_specs=[whole(a) for a in ins],
            out_specs=[whole(o) for o in outs],
        ),
        out_shape=outs,
        compiler_params=params(vmem),
        cost_estimate=cost(0, ins),
        name=name,
    )(meta, *ins)


def halve(meta, slot, level, kept, got):
    shape = jax.ShapeDtypeStruct((kept.shape[0] // 2, kept.shape[1]), BF)
    return metaed(
        functools.partial(halve_body, slot, level), meta, [kept, got], [shape, shape], "halve"
    )


def join_body(slot, level, meta, own, got, o):
    bit = jnp.bitwise_and(jnp.right_shift(meta[slot], level), 1)
    half = own.shape[0]
    o[pl.ds(pl.multiple_of(bit * half, half), half), :] = own[...].astype(o.dtype)
    o[pl.ds(pl.multiple_of((1 - bit) * half, half), half), :] = got[...].astype(o.dtype)


def join(meta, slot, level, own, got, dtype=BF):
    shape = jax.ShapeDtypeStruct((own.shape[0] * 2, own.shape[1]), dtype)
    (out,) = metaed(functools.partial(join_body, slot, level), meta, [own, got], [shape], "join")
    return out


def reduced(meta, slot, axis, masks, send, keep, first=0):
    for level in range(first, len(masks)):
        got = swap(send, axis, masks[level])
        if level == len(masks) - 1:
            return add(keep, got)
        send, keep = halve(meta, slot, level + 1, keep, got)


def gathered(meta, slot, axis, masks, x, last):
    for level in range(len(masks) - 1, last, -1):
        x = join(meta, slot, level, x, swap(x, axis, masks[level]))
    return x, swap(x, axis, masks[last])


def wgrad_body(blocks, half, tails, meta, *refs):
    ins, (send_o, keep_o) = refs[:-2], refs[-2:]
    bit = bit_at(meta, 0)
    i = pl.program_id(0)
    g = jnp.where(i < half, (1 - bit) * half + i, bit * half + i - half)
    for p, tail in enumerate(tails):
        (a, b), ins = ins[:2], ins[2:]
        ta = tb = None
        if tail:
            (ta, tb), ins = ins[:2], ins[2:]
        inside = jnp.logical_and(g >= p * blocks, g < (p + 1) * blocks)

        def into(o, a=a, b=b, ta=ta, tb=tb):
            v = dot(a[...], b[...], 0, 0)
            if ta is not None:
                v = v + dot(ta[...], tb[...], 0, 0)
            o[...] = v.astype(BF)

        pl.when(jnp.logical_and(inside, i < half))(functools.partial(into, send_o))
        pl.when(jnp.logical_and(inside, i >= half))(functools.partial(into, keep_o))


def wgrads(meta, pairs, width, blocks, name):
    half = blocks * len(pairs) // 2
    tokens = pairs[0][0].shape[0]

    def cut(i, m):
        bit = jnp.bitwise_and(m[1], 1)
        g = jnp.where(i < half, (1 - bit) * half + i, bit * half + i - half)
        return (0, lax.rem(g, blocks))

    specs, ins = [], []
    for a, b, which, *more in pairs:
        for pair in [(a, b), tuple(more)]:
            for j, v in enumerate(pair):
                ins.append(v)
                specs.append(
                    pl.BlockSpec((v.shape[0], width), cut if j == which else lambda i, m: (0, 0))
                )
    shape = jax.ShapeDtypeStruct((half * width, width), BF)
    return pl.pallas_call(
        functools.partial(wgrad_body, blocks, half, [len(p) > 3 for p in pairs]),
        grid_spec=pltpu.PrefetchScalarGridSpec(
            num_scalar_prefetch=1,
            grid=(2 * half,),
            in_specs=specs,
            out_specs=[
                pl.BlockSpec((width, width), lambda i, m: (jnp.minimum(i, half - 1), 0)),
                pl.BlockSpec((width, width), lambda i, m: (jnp.maximum(i - half, 0), 0)),
            ],
        ),
        out_shape=[shape, shape],
        compiler_params=params(20),
        cost_estimate=cost(4 * half * tokens * width * width, ins),
        name=name,
    )(meta, *ins)


def bc_body(meta, normed, gcat, gsr, rim, extra, send_o, keep_o, step_o):
    bit = jnp.bitwise_and(meta[0], 1)
    half = send_o.shape[0]
    for o, b in ((send_o, 1 - bit), (keep_o, bit)):
        cols = pl.ds(pl.multiple_of(b * half, half), half)
        v = dot(normed[:, cols], gcat[...], 0, 0) + dot(rim[:, cols], extra[...], 0, 0)
        o[...] = v.astype(BF)
    step_o[...] = dot(gsr[...], normed[...], 0, 0)[:8]


def bc_wgrad(meta, normed, gcat, gsr, rim, extra, width):
    tokens, d = normed.shape
    shape = jax.ShapeDtypeStruct((d // 2, 2 * L), BF)
    step = jax.ShapeDtypeStruct((8, d), F32)
    return pl.pallas_call(
        bc_body,
        grid_spec=pltpu.PrefetchScalarGridSpec(
            num_scalar_prefetch=1,
            grid=(1,),
            in_specs=[
                whole(normed),
                pl.BlockSpec((tokens, 2 * L), lambda i, m: (0, width // (2 * L))),
                whole(gsr),
                whole(rim),
                pl.BlockSpec((16, 2 * L), lambda i, m: (0, width // (2 * L))),
            ],
            out_specs=[whole(shape), whole(shape), whole(step)],
        ),
        out_shape=[shape, shape, step],
        compiler_params=params(12),
        cost_estimate=cost(2 * tokens * d * 3 * L, [normed, gsr]),
        name="bc_wgrad",
    )(meta, normed, gcat, gsr, rim, extra)


def wg_out_body(level, blocks, meta, own, got, wout_o, zx_o):
    bit = jnp.bitwise_and(jnp.right_shift(meta[1], level), 1)
    width = wout_o.shape[0]
    for g, src in ((0, own), (1, got)):
        mine = bit if g == 0 else 1 - bit

        @pl.when(mine == 0)
        def _():
            for k in range(blocks):
                wout_o[:, k * width : (k + 1) * width] = src[
                    k * width : (k + 1) * width, :
                ].astype(F32)

        @pl.when(mine == 1)
        def _():
            zx_o[0] = src[...].astype(F32)


def wg_out(meta, own, got, d, width):
    return pl.pallas_call(
        functools.partial(wg_out_body, 0, d // width),
        grid_spec=pltpu.PrefetchScalarGridSpec(
            num_scalar_prefetch=1,
            grid=(1,),
            in_specs=[whole(own), whole(got)],
            out_specs=[
                pl.BlockSpec((width, d), lambda i, m: (0, 0)),
                pl.BlockSpec((1, d, width), lambda i, m: (0, 0, 0)),
            ],
        ),
        out_shape=[
            jax.ShapeDtypeStruct((width, d), F32),
            jax.ShapeDtypeStruct((2, d, width), F32),
        ],
        compiler_params=params(16),
        cost_estimate=cost(0, [own, got]),
        name="out_and_gate_weights",
    )(meta, own, got)


def inner_out_body(meta, own, got, old, zx_o):
    del old
    bit = bit_at(meta, 0)
    half = own.shape[0]
    zx_o[0, pl.ds(pl.multiple_of(bit * half, half), half), :] = own[...].astype(F32)
    zx_o[0, pl.ds(pl.multiple_of((1 - bit) * half, half), half), :] = got[...].astype(F32)


def inner_out(meta, own, got, old):
    _, d, width = old.shape
    return pl.pallas_call(
        inner_out_body,
        grid_spec=pltpu.PrefetchScalarGridSpec(
            num_scalar_prefetch=1,
            grid=(1,),
            in_specs=[whole(own), whole(got), pl.BlockSpec(memory_space=pl.ANY)],
            out_specs=pl.BlockSpec((1, d, width), lambda i, m: (1, 0, 0)),
        ),
        out_shape=jax.ShapeDtypeStruct(old.shape, F32),
        input_output_aliases={3: 0},
        compiler_params=params(12),
        cost_estimate=cost(0, [own, got]),
        name="inner_weights",
    )(meta, own, got, old)


def bc_out_body(meta, own, got, o):
    bit = jnp.bitwise_and(meta[0], 1)
    half = own.shape[0]
    for v, b in ((own, bit), (got, 1 - bit)):
        rows = pl.ds(pl.multiple_of(b * half, half), half)
        o[0, rows, :] = v[:, :L].astype(F32)
        o[1, rows, :] = v[:, L:].astype(F32)


def patch_body(meta, gcat, ahead, vecs, o):
    count = meta.shape[0] - 3
    keep = jnp.where(meta[2 + count] == 0, 1.0, 0.0)
    o[...] = (gcat[...].astype(F32) + crossing(vecs, ahead[...] * keep)).astype(BF)


def patched(meta, gcat, ahead, kernel, share, group):
    wide = gcat.shape[1]

    def spot(i, m):
        return ((jnp.bitwise_xor(m[0], group - 1) + 1) * (share // 16) - 1, 0)

    return pl.pallas_call(
        patch_body,
        grid_spec=pltpu.PrefetchScalarGridSpec(
            num_scalar_prefetch=1,
            grid=(1,),
            in_specs=[pl.BlockSpec((16, wide), spot), whole(ahead), whole(kernel)],
            out_specs=pl.BlockSpec((16, wide), spot),
        ),
        out_shape=jax.ShapeDtypeStruct(gcat.shape, BF),
        input_output_aliases={1: 0},
        compiler_params=params(4),
        cost_estimate=cost(0, [ahead]),
        name="patch",
    )(meta, gcat, ahead, kernel)


def layer_body(tok, a, b, o):
    o[...] = (tok[...].astype(F32) + (a[...].astype(F32) + b[...].astype(F32))).astype(BF)


def tokens_body(tok, cot, a, b, gain, conv, gt_o, acc_o):
    x = tok[...].astype(F32)
    rstd = lax.rsqrt(jnp.mean(x * x, axis=1, keepdims=True) + EPS)
    unit = x * rstd
    gnormed = a[...].astype(F32) + b[...].astype(F32)
    gunit = gnormed * gain[...]
    gt_o[...] = cot[...].astype(F32) + rstd * (
        gunit - unit * jnp.mean(gunit * unit, axis=1, keepdims=True)
    )
    d = x.shape[1]
    acc_o[:, d:] = conv[:, conv.shape[1] - 2 * L :]
    row = lax.broadcasted_iota(jnp.int32, (8, d), 0)
    acc_o[:, :d] = jnp.where(row == 0, jnp.sum(gnormed * unit, axis=0, keepdims=True), 0.0)


def plain(body, ins, outs, name, vmem=12):
    return pl.pallas_call(
        body,
        grid=(1,),
        in_specs=[whole(a) for a in ins],
        out_specs=[whole(o) for o in outs],
        out_shape=outs,
        compiler_params=params(vmem),
        cost_estimate=cost(0, ins),
        name=name,
    )(*ins)


def on_device(
    tokens_in,
    grad_out,
    scene_offsets,
    input_gain,
    weight_zx,
    weight_bc,
    weight_step,
    conv_inner,
    conv_inner_bias,
    conv_bc,
    conv_bc_bias,
    step_bias,
    decay_log,
    skip_weight,
    norm_gain,
    weight_out,
):
    share, d = tokens_in.shape
    group = lax.axis_size("tensor")
    tokens = share * group
    heads = step_bias.shape[0]
    width = norm_gain.shape[0]
    wide = width + 2 * L
    count = tokens // L
    per = share // L
    half = group // 2
    me = lax.axis_index("tensor")
    place = lax.axis_index("dp")

    heads_pos = place * tokens + jnp.arange(count + 1, dtype=jnp.int32) * L
    starts = jnp.any(heads_pos[:, None] == scene_offsets[None, :], axis=1).astype(jnp.int32)
    meta = jnp.concatenate([me[None].astype(jnp.int32), place[None].astype(jnp.int32), starts])
    masks, tmasks = masks_of("dp"), masks_of("tensor")
    levels = len(masks)

    wst = jnp.pad(weight_step, ((0, 0), (0, L - heads)))
    gain = input_gain[None]
    prep_ins = [conv_inner, conv_inner_bias[None], conv_bc, conv_bc_bias, step_bias[None],
                decay_log[None], skip_weight[None], norm_gain[None]]
    prep_outs = [
        jax.ShapeDtypeStruct((8, wide), F32),
        jax.ShapeDtypeStruct((8, L), F32),
        jax.ShapeDtypeStruct((L, width + L), BF),
        jax.ShapeDtypeStruct((16, d), BF),
    ]
    vecs, hv, mats, last_rows = pl.pallas_call(
        prep_body,
        grid=(1,),
        in_specs=[whole(a) for a in prep_ins]
        + [pl.BlockSpec((16, d), lambda i: (share // 16 - 1, 0))],
        out_specs=[whole(o) for o in prep_outs],
        out_shape=prep_outs,
        compiler_params=params(4),
        name="prep",
    )(*prep_ins, tokens_in)

    def place_of(c, meta):
        if per == 1:
            return lax.bitwise_xor(c, meta[0])
        return lax.bitwise_xor(lax.div(c, per), meta[0]) * per + lax.rem(c, per)

    def stretched(body, name, ins, outs, scratch, reverse, vmem, flops):
        def order(i):
            return count - 1 - i if reverse else i

        def spec(kind, shape):
            if kind == "rows":
                return pl.BlockSpec((L, shape[1]), lambda i, m: (place_of(order(i), m), 0))
            if kind == "each":
                return pl.BlockSpec((1, *shape[1:]), lambda i, m: (order(i), 0, 0))
            return pl.BlockSpec(shape, lambda i, m: (0,) * len(shape))

        return pl.pallas_call(
            body,
            grid_spec=pltpu.PrefetchScalarGridSpec(
                num_scalar_prefetch=1,
                grid=(count,),
                in_specs=[spec(k, a.shape) for k, a in ins],
                out_specs=[spec(k, s) for k, s, _ in outs],
                scratch_shapes=scratch,
            ),
            out_shape=[jax.ShapeDtypeStruct(s, t) for _, s, t in outs],
            compiler_params=params(vmem),
            cost_estimate=cost(flops, [a for _, a in ins]),
            name=name,
        )(meta, *[a for _, a in ins])

    held = {0: tokens_in}
    held[half] = swap(tokens_in, "tensor", half)
    mask = half // 2
    while mask:
        for f in [f for f in held if f < half]:
            held[f ^ mask] = swap(held[f], "tensor", mask)
        mask //= 2
    dps = lax.axis_size("dp")
    past = [
        lax.ppermute(
            last_rows,
            ("dp", "tensor"),
            [(i * group + group - 1, (i + 1) * group + t) for i in range(dps - 1)],
        )
        for t in range(group)
    ]
    before = project(
        meta, [held[f] for f in range(half)], [], gain, weight_zx, weight_bc, wst, tokens, 0,
        [vecs, hv, mats],
    )
    mask = half // 2
    while mask:
        for f in [f for f in held if f >= half]:
            held[f ^ mask] = swap(held[f], "tensor", mask)
        mask //= 2
    normed, gate_raw, cat, step_raw, rim, normed_rim = project(
        meta, [held[f] for f in range(half, group)], past, gain, weight_zx, weight_bc, wst,
        tokens, half, before,
    )

    tall = (tokens, L)
    state_shape = (width, L)
    load_shape = (width + 16, L)
    small = (8, L)
    pre, sin, state, load, cum, pfx, decay = stretched(
        states_body,
        "states",
        [("rows", cat), ("rows", step_raw), ("one", rim), ("one", vecs), ("one", hv),
         ("one", mats)],
        [("rows", (tokens, wide), F32), ("each", (count, *state_shape), BF),
         ("one", state_shape, F32), ("one", load_shape, BF), ("rows", tall, F32),
         ("each", (count, 8, L), F32), ("one", small, F32)],
        [pltpu.VMEM((L + 8, wide), F32), pltpu.VMEM(state_shape, F32), pltpu.VMEM(small, F32)],
        False, 10, 2 * tokens * width * L * 3,
    )

    cots = {0: grad_out}
    cots[half] = swap(hold(grad_out, step_raw), "tensor", half)
    late = hold(cots[half], load)
    mask = half // 2
    while mask:
        for f in sorted(cots):
            cots[f ^ mask] = swap(late if f == half else cots[f], "tensor", mask)
        mask //= 2
    cots = [cots[f] for f in range(group)]

    def link(level, reverse, held, load):
        got = swap(load, "dp", masks[level])
        if level == levels - 1:
            return held[2:], got
        shapes = [load_shape, state_shape, small, state_shape, small]
        out = metaed(
            functools.partial(link_body, level, reverse), meta, [*held, got],
            [jax.ShapeDtypeStruct(s, BF if j == 0 else F32) for j, s in enumerate(shapes)],
            "link",
        )
        return out[1:], out[0]

    thr = decay
    fresh = [jnp.zeros(state_shape, F32), jnp.ones(small, F32)]
    own = [state, decay, *fresh]
    for level in range(levels):
        if level == 1 or levels == 1:
            (y,) = stretched(
                within_body,
                "within",
                [("rows", pre), ("rows", step_raw), ("rows", cum), ("each", sin), ("one", vecs),
                 ("one", hv), ("one", mats)],
                [("rows", (tokens, width), F32)],
                [], False, 10, 2 * tokens * width * L * 6,
            )
            load = after(load, y)
        if level == 2:
            cot_all, gn = cotangent(cots, weight_out)
        own, load = link(level, False, own, load)
    if levels < 3:
        cot_all, gn = cotangent(cots, weight_out)
    befores, throughs = own
    mixed, sums, incoming = stretched(
        functools.partial(gate_body, levels - 1),
        "gated",
        [("rows", pre), ("rows", cum), ("each", pfx), ("rows", y), ("rows", gate_raw),
         ("rows", gn), ("one", befores), ("one", throughs), ("one", load), ("one", vecs),
         ("one", mats)],
        [("rows", (tokens, width), F32), ("each", (count, 8, L), F32), ("one", state_shape, BF)],
        [], False, 10, 2 * tokens * width * L * 4,
    )
    for mask in tmasks[::-1][:-1]:
        sums = add(sums, swap(sums, "tensor", mask))
    sums2 = swap(sums, "tensor", 1)
    normout, gm, ggr, gs, toward, load, sfx, gate_acc = stretched(
        functools.partial(back_gate_body, count),
        "back_gated",
        [("rows", pre), ("rows", cum), ("rows", mixed), ("rows", gate_raw), ("rows", gn),
         ("each", sums), ("each", sums2), ("one", thr), ("one", vecs), ("one", mats)],
        [("rows", (tokens, width), BF), ("rows", (tokens, width), BF),
         ("rows", (tokens, width), BF), ("each", (count, *state_shape), BF),
         ("one", state_shape, F32), ("one", load_shape, BF), ("each", (count, 8, L), F32),
         ("one", (8, width), F32)],
        [pltpu.VMEM(state_shape, F32), pltpu.VMEM(small, F32), pltpu.VMEM((16, width), F32)],
        True, 10, 2 * tokens * width * L * 3,
    )

    blocks = d // width
    own, load = link(0, True, [toward, thr, *fresh], load)
    wg_send, wg_keep = wgrads(
        meta, [(normout, cot_all, 1), (normed, ggr, 0)], width, blocks, "out_gate_wgrad"
    )
    load = after(load, wg_keep)
    if levels > 1:
        own, load = link(1, True, own, load)
    wg_got = swap(after(wg_send, load), "dp", 1)
    ginner, gbc, glog, gst = stretched(
        back_within_body,
        "back_within",
        [("rows", pre), ("rows", step_raw), ("rows", cum), ("each", sin), ("each", pfx),
         ("each", gs), ("rows", gm), ("one", incoming), ("one", vecs), ("one", hv),
         ("one", mats)],
        [("rows", (tokens, width), F32), ("rows", (tokens, 2 * L), F32), ("rows", tall, F32),
         ("rows", tall, F32)],
        [], True, 12, 2 * tokens * width * L * 12,
    )
    for level in range(2, levels):
        own, load = link(level, True, own, load)
    befores, throughs = own
    gcat, gsr, head, extra, conv_acc, head_acc = stretched(
        functools.partial(back_conv_body, count, levels - 1),
        "back_conv",
        [("rows", cat), ("one", rim), ("rows", pre), ("rows", step_raw), ("rows", cum),
         ("each", sin), ("each", pfx), ("each", sfx), ("rows", ginner), ("rows", gbc),
         ("rows", glog), ("rows", gst), ("one", incoming), ("one", befores), ("one", throughs),
         ("one", load), ("one", vecs), ("one", hv), ("one", mats)],
        [("rows", (tokens, wide), BF), ("rows", tall, BF), ("one", (8, wide), F32),
         ("one", (16, wide), BF), ("one", (8, wide), F32), ("one", small, F32)],
        [pltpu.VMEM((L + 8, wide), F32), pltpu.VMEM((40, wide), F32), pltpu.VMEM((16, L), F32),
         pltpu.VMEM(state_shape, F32)],
        True, 12, 2 * tokens * width * L * 6,
    )

    in_send, in_keep = wgrads(
        meta, [(normed, gcat, 0, normed_rim, extra)], width, blocks, "inner_wgrad"
    )
    ahead = lax.ppermute(after(head, in_keep), "dp", [(i + 1, i) for i in range(dps - 1)])
    wg_send, wg_keep = halve(meta, 1, 1, after(wg_keep, in_keep), wg_got)
    bc_send, bc_keep, step_acc = bc_wgrad(meta, normed, gcat, gsr, normed_rim, extra, width)
    branch = rows_times(
        outproj_body, group, share, d, [after(normout, wg_keep)], [weight_out], "outproj"
    )
    gcat = patched(meta, gcat, ahead, vecs, share, group)
    grads = rows_times(
        dgrad_body, group, share, d, [ggr, gcat, gsr], [weight_zx, weight_bc, wst], "dgrad"
    )

    inner_sum = reduced(meta, 1, "dp", masks, in_send, in_keep)
    grad_a, grad_b = scatter_frames(grads, group)
    wg_sum = reduced(meta, 1, "dp", masks, wg_send, wg_keep, 1)
    out_a, out_b = scatter_frames(branch, group)
    bc_sum = reduced(meta, 0, "tensor", tmasks, bc_send, bc_keep)
    for mask in masks:
        bc_sum = add(bc_sum, swap(bc_sum, "dp", mask))

    own_shape = jax.ShapeDtypeStruct((share, d), F32)
    grad_tokens, shared = plain(
        tokens_body,
        [tokens_in, grad_out, grad_a, grad_b, gain, conv_acc],
        [own_shape, jax.ShapeDtypeStruct((8, d + 2 * L), F32)],
        "tokens",
    )
    (layer_out,) = plain(
        layer_body, [tokens_in, out_a, out_b], [jax.ShapeDtypeStruct((share, d), BF)], "layer"
    )
    for mask in tmasks:
        shared = add(shared, swap(shared, "tensor", mask))
    sums_all = jnp.concatenate(
        [shared, step_acc, conv_acc[:, :width], gate_acc, head_acc], axis=1
    )
    for mask in masks:
        sums_all = add(sums_all, swap(sums_all, "dp", mask))

    grad_weight_out, grad_zx = wg_out(
        meta, *gathered(meta, 1, "dp", masks, wg_sum, 0), d, width
    )
    grad_zx = inner_out(meta, *gathered(meta, 1, "dp", masks, inner_sum, 0), grad_zx)
    (grad_bc,) = metaed(
        bc_out_body, meta, list(gathered(meta, 0, "tensor", tmasks, bc_sum, 0)),
        [jax.ShapeDtypeStruct((2, d, L), F32)], "bc_weights",
    )

    at = 0

    def take(n):
        nonlocal at
        at += n
        return sums_all[:, at - n : at]

    grad_input_gain = take(d)[0]
    bc_acc = take(2 * L).reshape(8, 2, L)
    grad_weight_step = take(d)[:heads].T
    inner_acc = take(width)
    gates = take(width)
    per_heads = take(L)[:, :heads]
    return (
        layer_out,
        grad_tokens,
        grad_input_gain,
        grad_zx,
        grad_bc,
        grad_weight_step,
        inner_acc[:4],
        inner_acc[4],
        jnp.moveaxis(bc_acc[:4], 0, 1),
        bc_acc[4],
        per_heads[1],
        per_heads[0],
        jnp.sum(gates[1].reshape(heads, HD), axis=1),
        gates[0],
        grad_weight_out,
    )


def solution(mesh):
    rows = P(("dp", "tensor"), None)
    cols = P(None, "tensor")
    one = P("tensor")
    in_specs = (
        rows, rows, P(), P(), P(None, None, "tensor"), P(), cols, cols, one, P(), P(),
        one, one, one, one, P("tensor", None),
    )
    out_specs = (
        rows, rows, P(), P(None, None, "tensor"), P(), cols, cols, one, P(), P(),
        one, one, one, one, P("tensor", None),
    )
    return jax.shard_map(
        on_device, mesh=mesh, in_specs=in_specs, out_specs=out_specs, check_vma=False
    )
```

time: 362 us -> 280 us (0.77)
  local copies, waits for them, and re-layouts: 70 us -> 15.9 us
  other arithmetic: 40.6 us -> 1.46 us
  Pallas kernels: 62.3 us -> 92.6 us
  waiting for transfers between devices: 127 us -> 117 us
  matrix products: 7.05 us -> 0 us
    pallas_call x2 -> x50, Pallas kernels: 5.12 us -> 39.4 us  [the longest x15 12.1 us: metaed(): pl.pallas_call(body, grid_spec=pltpu.PrefetchScalarGridSpec(num_scalar_pr...]
    unnamed x202 -> x43, local copies, waits for them, and re-layouts: 38.2 us -> 11.7 us
    convert_element_type x35 -> x0, other arithmetic: 20.3 us -> none  [the longest x16 4.5 us: add(): return (a.astype(F32) + b.astype(F32)).astype(BF)]
    mul x17 -> x0, local copies, waits for them, and re-layouts: 18 us -> none  [scaled(): return (a[:heads, None, None] * s.reshape(heads, HD, L)).reshape(s.shape)]
    ppermute x53 -> x44, waiting for transfers between devices: 124 us -> 114 us  [swap(): return lax.ppermute(x, axis, [(i, i ^ mask) for i in range(count)])]
    dot_general x4 -> x0, matrix products: 7.05 us -> none  [the longest x3 6.01 us: wgrad(): return jnp.einsum('ta,tb->ab', a, b, preferred_element_type=F32).astype(BF)]
    concatenate x7 -> x1, other arithmetic: 5.75 us -> 0.08 us  [on_device(): jnp.concatenate([me[None].astype(jnp.int32), place[None].astype(jnp.int32...]
    add x8 -> x0, other arithmetic: 4.51 us -> none  [the longest x1 3.06 us: on_device(): grad_out.astype(F32)]
  transfers between devices with their start and end apart: 55 -> 49, of which waited for: 28 -> 20; matrix products, arithmetic and copies ran while one was open for 21% -> 2% of each run, Pallas kernels for 13% -> 27%
where the time goes in v2:
time: 280 us; the launch traced here: 279 us
  waiting for transfers between devices  117 us (42%)
  Pallas kernels  92.6 us (33%)
  starting transfers between devices  51 us (18%)
  local copies, waits for them, and re-layouts  15.9 us (6%)
    ppermute x44, waiting for transfers between devices, swap(): return lax.ppermute(x, axis, [(i, i ^ mask) for i in range(count)])  114 us
    ppermute x44, starting transfers between devices, swap(): return lax.ppermute(x, axis, [(i, i ^ mask) for i in range(count)])  47 us
    pallas_call x6, Pallas kernels, stretched(): pl.pallas_call(body, grid_spec=pltpu.PrefetchScalarGridSpec(num_scalar_pr...  44.7 us
    pallas_call x15, Pallas kernels, metaed(): pl.pallas_call(body, grid_spec=pltpu.PrefetchScalarGridSpec(num_scalar_pr...  12.1 us
    unnamed x43, local copies, waits for them, and re-layouts  11.7 us
    pallas_call x2, Pallas kernels, wgrads(): pl.pallas_call(functools.partial(wgrad_body, blocks, half, [len(p) > 3 fo...  7.02 us
    pallas_call x2, Pallas kernels, rows_times(): pl.pallas_call(functools.partial(body, k), grid=(k,), in_specs=[pl.BlockS...  6.53 us
    pallas_call x2, Pallas kernels, project(): pl.pallas_call(functools.partial(proj_body, k, len(past), len(before)), g...  6.46 us
  transfers between devices with their start and end apart: 49, of which 20 were waited for; matrix products, arithmetic and copies ran while one was open for 2% of the time, Pallas kernels for 27%

profile of v2, /device:TPU:0, one launch (start us, length us, event | category | flops | bytes accessed | tf_op | source)
XLA Modules:
  0.0 279.1 jit_solution(17803666055966862221)
XLA Ops:
  0.6 3.0 %collective-permute-start = (bf16[256,1024]{1,0:T(8,128)(2,1)}, bf16[256,1024]{1,0:T(8,128)(2,1)S(1)}, u32[]{:S(2)}, u32[]{:S(2)}) collective-permute-start(bf16[256,1024]{1,0:T(8,128)(2,1)} %tok.5), channel_id=1, source_target_pairs={{0,2},{1,3},{2,0},{3,1},{4,6},{5,7},{6,4},{7,5},{8,10},{9,11},{10,... | collective-permute-start | bytes 1572872 | tf_op jit(solution)/shard_map/ppermute | solution.py:709
  3.7 12.1 %collective-permute-done.refs_0_ = bf16[256,1024]{1,0:T(8,128)(2,1)S(1)} collective-permute-done((bf16[256,1024]{1,0:T(8,128)(2,1)}, bf16[256,1024]{1,0:T(8,128)(2,1)S(1)}, u32[]{:S(2)}, u32[]{:S(2)}) %collective-permute-start) | collective-permute-done | bytes 524320 | tf_op jit(solution)/shard_map/ppermute | solution.py:709
  31.2 3.1 %project.2 = (bf16[1024,1024]{1,0:T(8,128)(2,1)S(1)}, bf16[1024,512]{1,0:T(8,128)(2,1)S(1)}, bf16[1024,768]{1,0:T(8,128)(2,1)S(1)}, bf16[1024,128]{1,0:T(8,128)(2,1)S(1)}) custom-call(s32[11]{0:T(128)S(1)} %pad_add_fusion.meta, bf16[256,1024]{1,0:T(8,128)(2,1)S(1)} %copy-done.1, bf16[256,1024]{1,0:T(8,128)(2,1)S(1)} %collective-permute-done.6.refs_1_, ...), custom_call_target="tpu_custom_call" | custom-call | flops 1476395008 | bytes 8257536 | tf_op jit(solution)/shard_map/project/pallas_call | solution.py:131
  34.4 3.3 %project.3 = (bf16[1024,1024]{1,0:T(8,128)(2,1)S(1)}, bf16[1024,512]{1,0:T(8,128)(2,1)S(1)}, bf16[1024,768]{1,0:T(8,128)(2,1)S(1)}, bf16[1024,128]{1,0:T(8,128)(...) custom-call(s32[11]{0:T(128)S(1)} %pad_add_fusion.meta, ...), custom_call_target="tpu_custom_call", output_to_operand_aliasing={{0}: (11, {}), {1}: (12, {}), {2}: (13, {}), {3}: (14, {})} | custom-call | flops 1476395008 | bytes 18096128 | tf_op jit(solution)/shard_map/project/pallas_call | solution.py:131
  37.8 1.8 collective-permute-start.8
  39.6 4.6 %collective-permute-start.7 = (bf16[256,1024]{1,0:T(8,128)(2,1)S(1)}, bf16[256,1024]{1,0:T(8,128)(2,1)S(1)}, u32[]{:S(2)}, u32[]{:S(2)}) collective-permute-start(bf16[256,1024]{1,0:T(8,128)(2,1)S(1)} %copy-done.3), channel_id=1, source_target_pairs={{0,1},{1,0},{2,3},{3,2},{4,5},{5,4},{6,7},{7,6},{8,9},{9,8},{10,11... | collective-permute-start | bytes 1572872 | tf_op jit(solution)/shard_map/ppermute | solution.py:709
  44.2 7.0 %states.1 = (f32[1024,768]{1,0:T(8,128)S(1)}, bf16[8,512,128]{2,1,0:T(8,128)(2,1)S(1)}, f32[512,128]{1,0:T(8,128)S(1)}, bf16[528,128]{1,0:T(8,128)(2,1)S(1)}, f3...) custom-call(s32[11]{0:T(128)S(1)} %pad_add_fusion.meta, ...), custom_call_target="tpu_custom_call" | custom-call | flops 402653184 | bytes 4104192 | tf_op jit(solution)/shard_map/states/pallas_call | solution.py:1104
  52.6 2.4 collective-permute-start.10
  55.0 4.5 %within.1.refs_1_.y = f32[1024,512]{1,0:T(8,128)S(1)} custom-call(s32[11]{0:T(128)S(1)} %pad_add_fusion.meta, f32[1024,768]{1,0:T(8,128)S(1)} %get-tuple-element.115.pre, bf16[1024,128]{1,0:T(8,128)(2,1)S(1)} %get-tuple-element.113.step.refs_0_, f32[1024,128]{1,0:T(8,128)S(1)} %get-tuple-element.116.cum_r.cum, ...), custom_call_target="tpu_custom_call" | custom-call | flops 805306368 | bytes 10346496 | tf_op jit(solution)/shard_map/within/pallas_call | solution.py:1104
  60.3 1.6 collective-permute-start.11
  62.0 3.7 %collective-permute-done.11.load = bf16[528,128]{1,0:T(8,128)(2,1)S(1)} collective-permute-done((bf16[528,128]{1,0:T(8,128)(2,1)S(1)}, bf16[528,128]{1,0:T(8,128)(2,1)S(1)}, u32[]{:S(2)}, u32[]{:S(2)}) %collective-permute-start.11) | collective-permute-done | bytes 135200 | tf_op jit(solution)/shard_map/ppermute | solution.py:709
  67.1 2.6 collective-permute-start.12
  69.7 2.0 cotangent.1
  71.7 3.7 %collective-permute-done.12.load = bf16[528,128]{1,0:T(8,128)(2,1)S(1)} collective-permute-done((bf16[528,128]{1,0:T(8,128)(2,1)S(1)}, bf16[528,128]{1,0:T(8,128)(2,1)S(1)}, u32[]{:S(2)}, u32[]{:S(2)}) %collective-permute-start.12) | collective-permute-done | bytes 135200 | tf_op jit(solution)/shard_map/ppermute | solution.py:709
  75.4 5.4 %gated.1 = (f32[1024,512]{1,0:T(8,128)S(1)}, f32[8,8,128]{2,1,0:T(8,128)S(1)}, bf16[512,128]{1,0:T(8,128)(2,1)S(1)}) custom-call(s32[11]{0:T(128)S(1)} %pad_add_fusion.meta, f32[1024,768]{1,0:T(8,128)S(1)} %get-tuple-element.115.pre, f32[1024,128]{1,0:T(8,128)S(1)} %get-tuple-element.116.cum_r.cum, f32[8,8,128]{2,1,0:T(8,128)S(1)} %get-tuple-element.117.pfx, ...), custom_call_target="tpu_custom_call" | custom-call | flops 536870912 | bytes 16973824 | tf_op jit(solution)/shard_map/gated/pallas_call | solution.py:1104
  82.3 2.4 collective-permute-done.13.b
  85.9 5.7 %back_gated.1 = (bf16[1024,512]{1,0:T(8,128)(2,1)S(1)}, bf16[1024,512]{1,0:T(8,128)(2,1)S(1)}, bf16[1024,512]{1,0:T(8,128)(2,1)S(1)}, bf16[8,512,128]{2,1,0:T(8,...) custom-call(s32[11]{0:T(128)S(1)} %pad_add_fusion.meta, ...), custom_call_target="tpu_custom_call" | custom-call | flops 402653184 | bytes 16244736 | tf_op jit(solution)/shard_map/back_gated/pallas_call | solution.py:1104
  92.2 4.4 %out_gate_wgrad.1 = (bf16[1024,512]{1,0:T(8,128)(2,1)S(1)}, bf16[1024,512]{1,0:T(8,128)(2,1)S(1)}) custom-call(s32[11]{0:T(128)S(1)} %pad_add_fusion.meta, bf16[1024,512]{1,0:T(8,128)(2,1)S(1)} %get-tuple-element.134.refs_0_, bf16[1024,1024]{1,0:T(8,128)(2,1)S(1)} %get-tuple-element.135.refs_1_, ...), custom_call_target="tpu_custom_call" | custom-call | flops 2147483648 | bytes 12582912 | tf_op jit(solution)/shard_map/out_gate_wgrad/pallas_call | solution.py:843
  98.7 4.4 %collective-permute-done.16.load = bf16[528,128]{1,0:T(8,128)(2,1)S(1)} collective-permute-done((bf16[528,128]{1,0:T(8,128)(2,1)S(1)}, bf16[528,128]{1,0:T(8,128)(2,1)S(1)}, u32[]{:S(2)}, u32[]{:S(2)}) %collective-permute-start.16) | collective-permute-done | bytes 135200 | tf_op jit(solution)/shard_map/ppermute | solution.py:709
  104.5 2.1 collective-permute-start.17
  107.9 12.1 %back_within.1 = (f32[1024,512]{1,0:T(8,128)S(1)}, f32[1024,256]{1,0:T(8,128)S(1)}, f32[1024,128]{1,0:T(8,128)S(1)}, f32[1024,128]{1,0:T(8,128)S(1)}) custom-call(s32[11]{0:T(128)S(1)} %pad_add_fusion.meta, f32[1024,768]{1,0:T(8,128)S(1)} %get-tuple-element.115.pre, bf16[1024,128]{1,0:T(8,128)(2,1)S(1)} %get-tuple-element.113.step.refs_0_, ...), custom_call_target="tpu_custom_call" | custom-call | flops 1610612736 | bytes 14868480 | tf_op jit(solution)/shard_map/back_within/pallas_call | solution.py:1104
  120.0 10.1 %back_conv.1 = (bf16[1024,768]{1,0:T(8,128)(2,1)S(1)}, bf16[1024,128]{1,0:T(8,128)(2,1)S(1)}, f32[8,768]{1,0:T(8,128)S(1)}, bf16[16,768]{1,0:T(8,128)(2,1)S(1)},...) custom-call(s32[11]{0:T(128)S(1)} %pad_add_fusion.meta, bf16[1024,768]{1,0:T(8,128)(2,1)S(1)} %get-tuple-element.112.cat, ...), custom_call_target="tpu_custom_call" | custom-call | flops 805306368 | bytes 23126016 | tf_op jit(solution)/shard_map/back_conv/pallas_call | solution.py:1104
  130.1 2.7 inner_wgrad.1
  134.1 1.7 bc_wgrad.1
  135.8 2.7 collective-permute-done.22.ahead
  139.1 4.7 %dgrad.1 = (bf16[256,1024]{1,0:T(8,128)(2,1)S(1)}, bf16[256,1024]{1,0:T(8,128)(2,1)S(1)}, bf16[256,1024]{1,0:T(8,128)(2,1)S(1)}, bf16[256,1024]{1,0:T(8,128)(2,1)S(1)}) custom-call(bf16[1024,512]{1,0:T(8,128)(2,1)S(1)} %get-tuple-element.137.refs_3_.ggr, bf16[1024,768]{1,0:T(8,128)(2,1)S(1)} %patch.1.gcat, bf16[1024,128]{1,0:T(8,128)(2,1)S(1)} %get-tuple-element.168.gsr, ...), custom_call_target="tpu_custom_call" | custom-call | flops 2952790016 | bytes 11534336 | tf_op jit(solution)/shard_map/dgrad/pallas_call | solution.py:644
  143.8 1.7 collective-permute-start.31
  146.5 2.0 collective-permute-start.37
  151.4 14.4 %collective-permute-done.43.b = bf16[256,256]{1,0:T(8,128)(2,1)S(1)} collective-permute-done((bf16[256,256]{1,0:T(8,128)(2,1)S(1)}, bf16[256,256]{1,0:T(8,128)(2,1)S(1)}, u32[]{:S(2)}, u32[]{:S(2)}) %collective-permute-start.43) | collective-permute-done | bytes 131104 | tf_op jit(solution)/shard_map/ppermute | solution.py:709
  167.2 3.8 %collective-permute-done.44.b = bf16[256,256]{1,0:T(8,128)(2,1)S(1)} collective-permute-done((bf16[256,256]{1,0:T(8,128)(2,1)S(1)}, bf16[256,256]{1,0:T(8,128)(2,1)S(1)}, u32[]{:S(2)}, u32[]{:S(2)}) %collective-permute-start.44) | collective-permute-done | bytes 131104 | tf_op jit(solution)/shard_map/ppermute | solution.py:709
  172.8 7.7 %collective-permute-done.45.b = bf16[256,256]{1,0:T(8,128)(2,1)S(1)} collective-permute-done((bf16[256,256]{1,0:T(8,128)(2,1)S(1)}, bf16[256,256]{1,0:T(8,128)(2,1)S(1)}, u32[]{:S(2)}, u32[]{:S(2)}) %collective-permute-start.45) | collective-permute-done | bytes 131104 | tf_op jit(solution)/shard_map/ppermute | solution.py:709
  181.2 1.6 tokens.1
  183.5 2.5 collective-permute-start.33
  186.0 9.2 %collective-permute-done.46.b = bf16[256,256]{1,0:T(8,128)(2,1)S(1)} collective-permute-done((bf16[256,256]{1,0:T(8,128)(2,1)S(1)}, bf16[256,256]{1,0:T(8,128)(2,1)S(1)}, u32[]{:S(2)}, u32[]{:S(2)}) %collective-permute-start.46) | collective-permute-done | bytes 131104 | tf_op jit(solution)/shard_map/ppermute | solution.py:709
  197.4 1.8 outproj.1
  201.0 3.0 %collective-permute-start.39 = (bf16[256,512]{1,0:T(8,128)(2,1)S(1)}, bf16[256,512]{1,0:T(8,128)(2,1)S(1)}, u32[]{:S(2)}, u32[]{:S(2)}) collective-permute-start(bf16[256,512]{1,0:T(8,128)(2,1)S(1)} %add.50.own), channel_id=1, source_target_pairs={{0,16},{4,20},{8,24},{12,28},{16,0},{20,4},{24,8},{28,12},{1,17},{... | collective-permute-start | bytes 786440 | tf_op jit(solution)/shard_map/ppermute | solution.py:709
  204.0 15.2 %collective-permute-done.39.got = bf16[256,512]{1,0:T(8,128)(2,1)S(1)} collective-permute-done((bf16[256,512]{1,0:T(8,128)(2,1)S(1)}, bf16[256,512]{1,0:T(8,128)(2,1)S(1)}, u32[]{:S(2)}, u32[]{:S(2)}) %collective-permute-start.39) | collective-permute-done | bytes 262176 | tf_op jit(solution)/shard_map/ppermute | solution.py:709
  221.2 3.7 %collective-permute-done.28.b = f32[8,3456]{1,0:T(8,128)S(1)} collective-permute-done((f32[8,3456]{1,0:T(8,128)S(1)}, f32[8,3456]{1,0:T(8,128)S(1)}, u32[]{:S(2)}, u32[]{:S(2)}) %collective-permute-start.28) | collective-permute-done | bytes 110624 | tf_op jit(solution)/shard_map/ppermute | solution.py:709
  225.0 1.8 collective-permute-start.35
  226.7 7.9 %collective-permute-done.40.got = bf16[512,512]{1,0:T(8,128)(2,1)S(1)} collective-permute-done((bf16[512,512]{1,0:T(8,128)(2,1)S(1)}, bf16[512,512]{1,0:T(8,128)(2,1)S(1)}, u32[]{:S(2)}, u32[]{:S(2)}) %collective-permute-start.40) | collective-permute-done | bytes 524320 | tf_op jit(solution)/shard_map/ppermute | solution.py:709
  235.3 6.4 %collective-permute-done.29.b = f32[8,3456]{1,0:T(8,128)S(1)} collective-permute-done((f32[8,3456]{1,0:T(8,128)S(1)}, f32[8,3456]{1,0:T(8,128)S(1)}, u32[]{:S(2)}, u32[]{:S(2)}) %collective-permute-start.29) | collective-permute-done | bytes 110624 | tf_op jit(solution)/shard_map/ppermute | solution.py:709
  245.2 2.1 collective-permute-start.36
  254.6 6.3 %collective-permute-done.21.b = bf16[256,1024]{1,0:T(8,128)(2,1)} collective-permute-done((bf16[256,1024]{1,0:T(8,128)(2,1)}, bf16[256,1024]{1,0:T(8,128)(2,1)}, u32[]{:S(2)}, u32[]{:S(2)}) %collective-permute-start.21) | collective-permute-done | bytes 524320 | tf_op jit(solution)/shard_map/ppermute | solution.py:709
  261.0 2.0 layer.1
  263.0 4.9 %collective-permute-done.41.got = bf16[1024,512]{1,0:T(8,128)(2,1)} collective-permute-done((bf16[1024,512]{1,0:T(8,128)(2,1)S(1)}, bf16[1024,512]{1,0:T(8,128)(2,1)}, u32[]{:S(2)}, u32[]{:S(2)}) %collective-permute-start.41) | collective-permute-done | bytes 1048608 | tf_op jit(solution)/shard_map/ppermute | solution.py:709
  267.9 4.1 %out_and_gate_weights.1 = (f32[512,1024]{1,0:T(8,128)}, f32[2,1024,512]{2,1,0:T(8,128)}) custom-call(s32[11]{0:T(128)S(1)} %pad_add_fusion.meta, bf16[1024,512]{1,0:T(8,128)(2,1)S(1)} %join.8.own, bf16[1024,512]{1,0:T(8,128)(2,1)} %collective-permute-done.41.got), custom_call_target="tpu_custom_call" | custom-call | bytes 4194304 | tf_op jit(solution)/shard_map/out_and_gate_weights/pallas_call | solution.py:915
  271.9 5.2 %collective-permute-done.36.got = bf16[512,512]{1,0:T(8,128)(2,1)S(1)} collective-permute-done((bf16[512,512]{1,0:T(8,128)(2,1)S(1)}, bf16[512,512]{1,0:T(8,128)(2,1)S(1)}, u32[]{:S(2)}, u32[]{:S(2)}) %collective-permute-start.36) | collective-permute-done | bytes 524320 | tf_op jit(solution)/shard_map/ppermute | solution.py:709
  277.1 2.0 inner_weights.1
  (169 shorter events, 54.7 us)
Async XLA Ops:
  0.6 15.1 %collective-permute-start = (bf16[256,1024]{1,0:T(8,128)(2,1)}, bf16[256,1024]{1,0:T(8,128)(2,1)S(1)}, u32[]{:S(2)}, u32[]{:S(2)}) collective-permute-start(bf16[256,1024]{1,0:T(8,128)(2,1)} %tok.5), channel_id=1, source_target_pairs={{0,2},{1,3},{2,0},{3,1},{4,6},{5,7},{6,4},{7,5},{8,10},{9,11},{10,... | collective-permute-start | bytes 1572872 | tf_op jit(solution)/shard_map/ppermute | solution.py:709
  3.7 22.5 %collective-permute-start.6 = (bf16[256,1024]{1,0:T(8,128)(2,1)}, bf16[256,1024]{1,0:T(8,128)(2,1)S(1)}, u32[]{:S(2)}, u32[]{:S(2)}) collective-permute-start(bf16[256,1024]{1,0:T(8,128)(2,1)} %tok.5), channel_id=1, source_target_pairs={{0,1},{1,0},{2,3},{3,2},{4,5},{5,4},{6,7},{7,6},{8,9},{9,8},{10,11... | collective-permute-start | bytes 1572872 | tf_op jit(solution)/shard_map/ppermute | solution.py:709
  15.8 18.6 %collective-permute-start.1 = (bf16[256,1024]{1,0:T(8,128)(2,1)S(1)}, bf16[256,1024]{1,0:T(8,128)(2,1)S(1)}, u32[]{:S(2)}, u32[]{:S(2)}) collective-permute-start(bf16[256,1024]{1,0:T(8,128)(2,1)S(1)} %collective-permute-done.refs_0_), channel_id=1, source_target_pairs={{0,1},{1,0},{2,3},{3,2},{4,5},{5,4},{6,7},{7,6},{8,9},{9,8},{10,11... | collective-permute-start | bytes 1572872 | tf_op jit(solution)/shard_map/ppermute | solution.py:709
  22.4 12.0 %collective-permute-start.5 = (bf16[16,1024]{1,0:T(8,128)(2,1)S(1)}, bf16[16,1024]{1,0:T(8,128)(2,1)S(1)}, u32[]{:S(2)}, u32[]{:S(2)}) collective-permute-start(bf16[16,1024]{1,0:T(8,128)(2,1)S(1)} %get-tuple-element.104), channel_id=1, source_target_pairs={{3,7},{7,11},{11,15},{15,19},{19,23},{23,27},{27,31}} | collective-permute-start | bytes 98312 | tf_op jit(solution)/shard_map/ppermute | solution.py:1128
  23.0 11.3 %collective-permute-start.4 = (bf16[16,1024]{1,0:T(8,128)(2,1)S(1)}, bf16[16,1024]{1,0:T(8,128)(2,1)S(1)}, u32[]{:S(2)}, u32[]{:S(2)}) collective-permute-start(bf16[16,1024]{1,0:T(8,128)(2,1)S(1)} %get-tuple-element.104), channel_id=1, source_target_pairs={{3,6},{7,10},{11,14},{15,18},{19,22},{23,26},{27,30}} | collective-permute-start | bytes 98312 | tf_op jit(solution)/shard_map/ppermute | solution.py:1128
  23.7 10.7 %collective-permute-start.3 = (bf16[16,1024]{1,0:T(8,128)(2,1)S(1)}, bf16[16,1024]{1,0:T(8,128)(2,1)S(1)}, u32[]{:S(2)}, u32[]{:S(2)}) collective-permute-start(bf16[16,1024]{1,0:T(8,128)(2,1)S(1)} %get-tuple-element.104), channel_id=1, source_target_pairs={{3,5},{7,9},{11,13},{15,17},{19,21},{23,25},{27,29}} | collective-permute-start | bytes 98312 | tf_op jit(solution)/shard_map/ppermute | solution.py:1128
  26.2 8.2 %collective-permute-start.2 = (bf16[16,1024]{1,0:T(8,128)(2,1)S(1)}, bf16[16,1024]{1,0:T(8,128)(2,1)S(1)}, u32[]{:S(2)}, u32[]{:S(2)}) collective-permute-start(bf16[16,1024]{1,0:T(8,128)(2,1)S(1)} %get-tuple-element.104), channel_id=1, source_target_pairs={{3,4},{7,8},{11,12},{15,16},{19,20},{23,24},{27,28}} | collective-permute-start | bytes 98312 | tf_op jit(solution)/shard_map/ppermute | solution.py:1128
  37.8 13.4 %collective-permute-start.8 = (bf16[256,1024]{1,0:T(8,128)(2,1)S(1)}, bf16[256,1024]{1,0:T(8,128)(2,1)S(1)}, u32[]{:S(2)}, u32[]{:S(2)}) collective-permute-start(bf16[256,1024]{1,0:T(8,128)(2,1)S(1)} %hold.2), channel_id=1, source_target_pairs={{0,2},{1,3},{2,0},{3,1},{4,6},{5,7},{6,4},{7,5},{8,10},{9,11},{10,... | collective-permute-start | bytes 1572872 | tf_op jit(solution)/shard_map/ppermute | solution.py:709
  39.6 30.1 %collective-permute-start.7 = (bf16[256,1024]{1,0:T(8,128)(2,1)S(1)}, bf16[256,1024]{1,0:T(8,128)(2,1)S(1)}, u32[]{:S(2)}, u32[]{:S(2)}) collective-permute-start(bf16[256,1024]{1,0:T(8,128)(2,1)S(1)} %copy-done.3), channel_id=1, source_target_pairs={{0,1},{1,0},{2,3},{3,2},{4,5},{5,4},{6,7},{7,6},{8,9},{9,8},{10,11... | collective-permute-start | bytes 1572872 | tf_op jit(solution)/shard_map/ppermute | solution.py:709
  51.3 18.4 %collective-permute-start.9 = (bf16[256,1024]{1,0:T(8,128)(2,1)S(1)}, bf16[256,1024]{1,0:T(8,128)(2,1)S(1)}, u32[]{:S(2)}, u32[]{:S(2)}) collective-permute-start(bf16[256,1024]{1,0:T(8,128)(2,1)S(1)} %hold.3), channel_id=1, source_target_pairs={{0,1},{1,0},{2,3},{3,2},{4,5},{5,4},{6,7},{7,6},{8,9},{9,8},{10,11... | collective-permute-start | bytes 1572872 | tf_op jit(solution)/shard_map/ppermute | solution.py:709
  52.6 6.9 %collective-permute-start.10 = (bf16[528,128]{1,0:T(8,128)(2,1)S(1)}, bf16[528,128]{1,0:T(8,128)(2,1)S(1)}, u32[]{:S(2)}, u32[]{:S(2)}) collective-permute-start(bf16[528,128]{1,0:T(8,128)(2,1)S(1)} %get-tuple-element.120.refs_0_), channel_id=1, source_target_pairs={{0,4},{4,0},{8,12},{12,8},{16,20},{20,16},{24,28},{28,24},{1,5},{5... | collective-permute-start | bytes 405512 | tf_op jit(solution)/shard_map/ppermute | solution.py:709
  60.3 5.3 %collective-permute-start.11 = (bf16[528,128]{1,0:T(8,128)(2,1)S(1)}, bf16[528,128]{1,0:T(8,128)(2,1)S(1)}, u32[]{:S(2)}, u32[]{:S(2)}) collective-permute-start(bf16[528,128]{1,0:T(8,128)(2,1)S(1)} %after.6), channel_id=1, source_target_pairs={{0,8},{4,12},{8,0},{12,4},{16,24},{20,28},{24,16},{28,20},{1,9},{5... | collective-permute-start | bytes 405512 | tf_op jit(solution)/shard_map/ppermute | solution.py:709
  67.1 8.3 %collective-permute-start.12 = (bf16[528,128]{1,0:T(8,128)(2,1)S(1)}, bf16[528,128]{1,0:T(8,128)(2,1)S(1)}, u32[]{:S(2)}, u32[]{:S(2)}) collective-permute-start(bf16[528,128]{1,0:T(8,128)(2,1)S(1)} %get-tuple-element.131), channel_id=1, source_target_pairs={{0,16},{4,20},{8,24},{12,28},{16,0},{20,4},{24,8},{28,12},{1,17},{... | collective-permute-start | bytes 405512 | tf_op jit(solution)/shard_map/ppermute | solution.py:709
  80.8 3.9 %collective-permute-start.13 = (f32[8,8,128]{2,1,0:T(8,128)S(1)}, f32[8,8,128]{2,1,0:T(8,128)S(1)}, u32[]{:S(2)}, u32[]{:S(2)}) collective-permute-start(f32[8,8,128]{2,1,0:T(8,128)S(1)} %get-tuple-element.133.a), channel_id=1, source_target_pairs={{0,2},{1,3},{2,0},{3,1},{4,6},{5,7},{6,4},{7,5},{8,10},{9,11},{10,... | collective-permute-start | bytes 98312 | tf_op jit(solution)/shard_map/ppermute | solution.py:709
  91.6 5.7 %collective-permute-start.15 = (bf16[528,128]{1,0:T(8,128)(2,1)S(1)}, bf16[528,128]{1,0:T(8,128)(2,1)S(1)}, u32[]{:S(2)}, u32[]{:S(2)}) collective-permute-start(bf16[528,128]{1,0:T(8,128)(2,1)S(1)} %get-tuple-element.148), channel_id=1, source_target_pairs={{0,4},{4,0},{8,12},{12,8},{16,20},{20,16},{24,28},{28,24},{1,5},{5... | collective-permute-start | bytes 405512 | tf_op jit(solution)/shard_map/ppermute | solution.py:709
  98.0 5.1 %collective-permute-start.16 = (bf16[528,128]{1,0:T(8,128)(2,1)S(1)}, bf16[528,128]{1,0:T(8,128)(2,1)S(1)}, u32[]{:S(2)}, u32[]{:S(2)}) collective-permute-start(bf16[528,128]{1,0:T(8,128)(2,1)S(1)} %after.7), channel_id=1, source_target_pairs={{0,8},{4,12},{8,0},{12,4},{16,24},{20,28},{24,16},{28,20},{1,9},{5... | collective-permute-start | bytes 405512 | tf_op jit(solution)/shard_map/ppermute | solution.py:709
  104.5 15.5 %collective-permute-start.17 = (bf16[528,128]{1,0:T(8,128)(2,1)S(1)}, bf16[528,128]{1,0:T(8,128)(2,1)S(1)}, u32[]{:S(2)}, u32[]{:S(2)}) collective-permute-start(bf16[528,128]{1,0:T(8,128)(2,1)S(1)} %get-tuple-element.156.refs_1_), channel_id=1, source_target_pairs={{0,16},{4,20},{8,24},{12,28},{16,0},{20,4},{24,8},{28,12},{1,17},{... | collective-permute-start | bytes 405512 | tf_op jit(solution)/shard_map/ppermute | solution.py:709
  106.6 39.1 %collective-permute-start.18 = (bf16[1024,512]{1,0:T(8,128)(2,1)S(1)}, bf16[1024,512]{1,0:T(8,128)(2,1)S(1)}, u32[]{:S(2)}, u32[]{:S(2)}) collective-permute-start(bf16[1024,512]{1,0:T(8,128)(2,1)S(1)} %after.9), channel_id=1, source_target_pairs={{0,4},{4,0},{8,12},{12,8},{16,20},{20,16},{24,28},{28,24},{1,5},{5... | collective-permute-start | bytes 3145736 | tf_op jit(solution)/shard_map/ppermute | solution.py:709
  132.8 5.7 %collective-permute-start.22 = (f32[8,768]{1,0:T(8,128)S(1)}, f32[8,768]{1,0:T(8,128)S(1)}, u32[]{:S(2)}, u32[]{:S(2)}) collective-permute-start(f32[8,768]{1,0:T(8,128)S(1)} %after.11), channel_id=1, source_target_pairs={{4,0},{8,4},{12,8},{16,12},{20,16},{24,20},{28,24},{5,1},{9,5},{13... | collective-permute-start | bytes 73736 | tf_op jit(solution)/shard_map/ppermute | solution.py:1271
  143.8 4.8 %collective-permute-start.24 = (bf16[256,1024]{1,0:T(8,128)(2,1)S(1)}, bf16[256,1024]{1,0:T(8,128)(2,1)S(1)}, u32[]{:S(2)}, u32[]{:S(2)}) collective-permute-start(bf16[256,1024]{1,0:T(8,128)(2,1)S(1)} %get-tuple-element.172), channel_id=1, source_target_pairs={{0,1},{1,0},{2,3},{3,2},{4,5},{5,4},{6,7},{7,6},{8,9},{9,8},{10,11... | collective-permute-start | bytes 1572872 | tf_op jit(solution)/shard_map/ppermute | solution.py:709
  143.8 22.4 %collective-permute-start.31 = (bf16[512,512]{1,0:T(8,128)(2,1)S(1)}, bf16[512,512]{1,0:T(8,128)(2,1)S(1)}, u32[]{:S(2)}, u32[]{:S(2)}) collective-permute-start(bf16[512,512]{1,0:T(8,128)(2,1)S(1)} %get-tuple-element.179), channel_id=1, source_target_pairs={{0,4},{4,0},{8,12},{12,8},{16,20},{20,16},{24,28},{28,24},{1,5},{5... | collective-permute-start | bytes 1572872 | tf_op jit(solution)/shard_map/ppermute | solution.py:709
  145.5 4.7 %collective-permute-start.42 = (bf16[512,256]{1,0:T(8,128)(2,1)S(1)}, bf16[512,256]{1,0:T(8,128)(2,1)S(1)}, u32[]{:S(2)}, u32[]{:S(2)}) collective-permute-start(bf16[512,256]{1,0:T(8,128)(2,1)S(1)} %get-tuple-element.189), channel_id=1, source_target_pairs={{0,1},{1,0},{2,3},{3,2},{4,5},{5,4},{6,7},{7,6},{8,9},{9,8},{10,11... | collective-permute-start | bytes 786440 | tf_op jit(solution)/shard_map/ppermute | solution.py:709
  146.5 24.6 %collective-permute-start.37 = (bf16[512,512]{1,0:T(8,128)(2,1)S(1)}, bf16[512,512]{1,0:T(8,128)(2,1)S(1)}, u32[]{:S(2)}, u32[]{:S(2)}) collective-permute-start(bf16[512,512]{1,0:T(8,128)(2,1)S(1)} %get-tuple-element.184), channel_id=1, source_target_pairs={{0,8},{4,12},{8,0},{12,4},{16,24},{20,28},{24,16},{28,20},{1,9},{5... | collective-permute-start | bytes 1572872 | tf_op jit(solution)/shard_map/ppermute | solution.py:709
  148.5 32.6 %collective-permute-start.23 = (bf16[256,1024]{1,0:T(8,128)(2,1)S(1)}, bf16[256,1024]{1,0:T(8,128)(2,1)S(1)}, u32[]{:S(2)}, u32[]{:S(2)}) collective-permute-start(bf16[256,1024]{1,0:T(8,128)(2,1)S(1)} %get-tuple-element.170), channel_id=1, source_target_pairs={{0,1},{1,0},{2,3},{3,2},{4,5},{5,4},{6,7},{7,6},{8,9},{9,8},{10,11... | collective-permute-start | bytes 1572872 | tf_op jit(solution)/shard_map/ppermute | solution.py:709
  148.7 32.5 %collective-permute-start.25 = (bf16[256,1024]{1,0:T(8,128)(2,1)S(1)}, bf16[256,1024]{1,0:T(8,128)(2,1)S(1)}, u32[]{:S(2)}, u32[]{:S(2)}) collective-permute-start(bf16[256,1024]{1,0:T(8,128)(2,1)S(1)} %add.43), channel_id=1, source_target_pairs={{0,2},{1,3},{2,0},{3,1},{4,6},{5,7},{6,4},{7,5},{8,10},{9,11},{10,... | collective-permute-start | bytes 1572872 | tf_op jit(solution)/shard_map/ppermute | solution.py:709
  150.8 15.0 %collective-permute-start.43 = (bf16[256,256]{1,0:T(8,128)(2,1)S(1)}, bf16[256,256]{1,0:T(8,128)(2,1)S(1)}, u32[]{:S(2)}, u32[]{:S(2)}) collective-permute-start(bf16[256,256]{1,0:T(8,128)(2,1)S(1)} %get-tuple-element.191), channel_id=1, source_target_pairs={{0,2},{1,3},{2,0},{3,1},{4,6},{5,7},{6,4},{7,5},{8,10},{9,11},{10,... | collective-permute-start | bytes 393224 | tf_op jit(solution)/shard_map/ppermute | solution.py:709
  165.9 5.1 %collective-permute-start.44 = (bf16[256,256]{1,0:T(8,128)(2,1)S(1)}, bf16[256,256]{1,0:T(8,128)(2,1)S(1)}, u32[]{:S(2)}, u32[]{:S(2)}) collective-permute-start(bf16[256,256]{1,0:T(8,128)(2,1)S(1)} %add.51.a), channel_id=1, source_target_pairs={{0,4},{4,0},{8,12},{12,8},{16,20},{20,16},{24,28},{28,24},{1,5},{5... | collective-permute-start | bytes 393224 | tf_op jit(solution)/shard_map/ppermute | solution.py:709
  166.9 16.0 %collective-permute-start.32 = (bf16[256,512]{1,0:T(8,128)(2,1)S(1)}, bf16[256,512]{1,0:T(8,128)(2,1)S(1)}, u32[]{:S(2)}, u32[]{:S(2)}) collective-permute-start(bf16[256,512]{1,0:T(8,128)(2,1)S(1)} %get-tuple-element.181), channel_id=1, source_target_pairs={{0,8},{4,12},{8,0},{12,4},{16,24},{20,28},{24,16},{28,20},{1,9},{5... | collective-permute-start | bytes 786440 | tf_op jit(solution)/shard_map/ppermute | solution.py:709
  171.0 9.5 %collective-permute-start.45 = (bf16[256,256]{1,0:T(8,128)(2,1)S(1)}, bf16[256,256]{1,0:T(8,128)(2,1)S(1)}, u32[]{:S(2)}, u32[]{:S(2)}) collective-permute-start(bf16[256,256]{1,0:T(8,128)(2,1)S(1)} %add.52.a), channel_id=1, source_target_pairs={{0,8},{4,12},{8,0},{12,4},{16,24},{20,28},{24,16},{28,20},{1,9},{5... | collective-permute-start | bytes 393224 | tf_op jit(solution)/shard_map/ppermute | solution.py:709
  171.8 29.1 %collective-permute-start.38 = (bf16[256,512]{1,0:T(8,128)(2,1)S(1)}, bf16[256,512]{1,0:T(8,128)(2,1)S(1)}, u32[]{:S(2)}, u32[]{:S(2)}) collective-permute-start(bf16[256,512]{1,0:T(8,128)(2,1)S(1)} %get-tuple-element.186), channel_id=1, source_target_pairs={{0,16},{4,20},{8,24},{12,28},{16,0},{20,4},{24,8},{28,12},{1,17},{... | collective-permute-start | bytes 786440 | tf_op jit(solution)/shard_map/ppermute | solution.py:709
  180.6 14.7 %collective-permute-start.46 = (bf16[256,256]{1,0:T(8,128)(2,1)S(1)}, bf16[256,256]{1,0:T(8,128)(2,1)S(1)}, u32[]{:S(2)}, u32[]{:S(2)}) collective-permute-start(bf16[256,256]{1,0:T(8,128)(2,1)S(1)} %add.53.a), channel_id=1, source_target_pairs={{0,16},{4,20},{8,24},{12,28},{16,0},{20,4},{24,8},{28,12},{1,17},{... | collective-permute-start | bytes 393224 | tf_op jit(solution)/shard_map/ppermute | solution.py:709
  182.9 13.9 %collective-permute-start.26 = (f32[8,1280]{1,0:T(8,128)S(1)}, f32[8,1280]{1,0:T(8,128)S(1)}, u32[]{:S(2)}, u32[]{:S(2)}) collective-permute-start(f32[8,1280]{1,0:T(8,128)S(1)} %get-tuple-element.175.a), channel_id=1, source_target_pairs={{0,1},{1,0},{2,3},{3,2},{4,5},{5,4},{6,7},{7,6},{8,9},{9,8},{10,11... | collective-permute-start | bytes 122888 | tf_op jit(solution)/shard_map/ppermute | solution.py:709
  183.5 15.9 %collective-permute-start.33 = (bf16[128,512]{1,0:T(8,128)(2,1)S(1)}, bf16[128,512]{1,0:T(8,128)(2,1)S(1)}, u32[]{:S(2)}, u32[]{:S(2)}) collective-permute-start(bf16[128,512]{1,0:T(8,128)(2,1)S(1)} %get-tuple-element.183), channel_id=1, source_target_pairs={{0,16},{4,20},{8,24},{12,28},{16,0},{20,4},{24,8},{28,12},{1,17},{... | collective-permute-start | bytes 393224 | tf_op jit(solution)/shard_map/ppermute | solution.py:709
  195.3 24.6 %collective-permute-start.47 = (bf16[256,256]{1,0:T(8,128)(2,1)S(1)}, bf16[256,256]{1,0:T(8,128)(2,1)S(1)}, u32[]{:S(2)}, u32[]{:S(2)}) collective-permute-start(bf16[256,256]{1,0:T(8,128)(2,1)S(1)} %add.54.own), channel_id=1, source_target_pairs={{0,2},{1,3},{2,0},{3,1},{4,6},{5,7},{6,4},{7,5},{8,10},{9,11},{10,... | collective-permute-start | bytes 393224 | tf_op jit(solution)/shard_map/ppermute | solution.py:709
  196.8 4.1 %collective-permute-start.27 = (f32[8,1280]{1,0:T(8,128)S(1)}, f32[8,1280]{1,0:T(8,128)S(1)}, u32[]{:S(2)}, u32[]{:S(2)}) collective-permute-start(f32[8,1280]{1,0:T(8,128)S(1)} %add.44.a), channel_id=1, source_target_pairs={{0,2},{1,3},{2,0},{3,1},{4,6},{5,7},{6,4},{7,5},{8,10},{9,11},{10,... | collective-permute-start | bytes 122888 | tf_op jit(solution)/shard_map/ppermute | solution.py:709
  199.3 50.4 %collective-permute-start.19 = (bf16[256,1024]{1,0:T(8,128)(2,1)S(1)}, bf16[256,1024]{1,0:T(8,128)(2,1)S(1)}, u32[]{:S(2)}, u32[]{:S(2)}) collective-permute-start(bf16[256,1024]{1,0:T(8,128)(2,1)S(1)} %get-tuple-element.164), channel_id=1, source_target_pairs={{0,1},{1,0},{2,3},{3,2},{4,5},{5,4},{6,7},{7,6},{8,9},{9,8},{10,11... | collective-permute-start | bytes 1572872 | tf_op jit(solution)/shard_map/ppermute | solution.py:709
  199.4 47.9 %collective-permute-start.20 = (bf16[256,1024]{1,0:T(8,128)(2,1)S(1)}, bf16[256,1024]{1,0:T(8,128)(2,1)S(1)}, u32[]{:S(2)}, u32[]{:S(2)}) collective-permute-start(bf16[256,1024]{1,0:T(8,128)(2,1)S(1)} %get-tuple-element.166), channel_id=1, source_target_pairs={{0,1},{1,0},{2,3},{3,2},{4,5},{5,4},{6,7},{7,6},{8,9},{9,8},{10,11... | collective-permute-start | bytes 1572872 | tf_op jit(solution)/shard_map/ppermute | solution.py:709
  200.9 19.7 %collective-permute-start.34 = (bf16[128,512]{1,0:T(8,128)(2,1)S(1)}, bf16[128,512]{1,0:T(8,128)(2,1)S(1)}, u32[]{:S(2)}, u32[]{:S(2)}) collective-permute-start(bf16[128,512]{1,0:T(8,128)(2,1)S(1)} %add.49.own), channel_id=1, source_target_pairs={{0,16},{4,20},{8,24},{12,28},{16,0},{20,4},{24,8},{28,12},{1,17},{... | collective-permute-start | bytes 393224 | tf_op jit(solution)/shard_map/ppermute | solution.py:709
  201.0 18.2 %collective-permute-start.39 = (bf16[256,512]{1,0:T(8,128)(2,1)S(1)}, bf16[256,512]{1,0:T(8,128)(2,1)S(1)}, u32[]{:S(2)}, u32[]{:S(2)}) collective-permute-start(bf16[256,512]{1,0:T(8,128)(2,1)S(1)} %add.50.own), channel_id=1, source_target_pairs={{0,16},{4,20},{8,24},{12,28},{16,0},{20,4},{24,8},{28,12},{1,17},{... | collective-permute-start | bytes 786440 | tf_op jit(solution)/shard_map/ppermute | solution.py:709
  219.8 14.9 %collective-permute-start.40 = (bf16[512,512]{1,0:T(8,128)(2,1)S(1)}, bf16[512,512]{1,0:T(8,128)(2,1)S(1)}, u32[]{:S(2)}, u32[]{:S(2)}) collective-permute-start(bf16[512,512]{1,0:T(8,128)(2,1)S(1)} %join.7.own), channel_id=1, source_target_pairs={{0,8},{4,12},{8,0},{12,4},{16,24},{20,28},{24,16},{28,20},{1,9},{5... | collective-permute-start | bytes 1572872 | tf_op jit(solution)/shard_map/ppermute | solution.py:709
  219.9 5.0 %collective-permute-start.28 = (f32[8,3456]{1,0:T(8,128)S(1)}, f32[8,3456]{1,0:T(8,128)S(1)}, u32[]{:S(2)}, u32[]{:S(2)}) collective-permute-start(f32[8,3456]{1,0:T(8,128)S(1)} %constant_dynamic-update-slice_fusion.a), channel_id=1, source_target_pairs={{0,4},{4,0},{8,12},{12,8},{16,20},{20,16},{24,28},{28,24},{1,5},{5... | collective-permute-start | bytes 331784 | tf_op jit(solution)/shard_map/ppermute | solution.py:709
  220.6 21.1 %collective-permute-start.48 = (bf16[512,256]{1,0:T(8,128)(2,1)S(1)}, bf16[512,256]{1,0:T(8,128)(2,1)S(1)}, u32[]{:S(2)}, u32[]{:S(2)}) collective-permute-start(bf16[512,256]{1,0:T(8,128)(2,1)S(1)} %join.9.own), channel_id=1, source_target_pairs={{0,1},{1,0},{2,3},{3,2},{4,5},{5,4},{6,7},{7,6},{8,9},{9,8},{10,11... | collective-permute-start | bytes 786440 | tf_op jit(solution)/shard_map/ppermute | solution.py:709
  225.0 19.6 %collective-permute-start.35 = (bf16[256,512]{1,0:T(8,128)(2,1)S(1)}, bf16[256,512]{1,0:T(8,128)(2,1)S(1)}, u32[]{:S(2)}, u32[]{:S(2)}) collective-permute-start(bf16[256,512]{1,0:T(8,128)(2,1)S(1)} %join.5.own), channel_id=1, source_target_pairs={{0,8},{4,12},{8,0},{12,4},{16,24},{20,28},{24,16},{28,20},{1,9},{5... | collective-permute-start | bytes 786440 | tf_op jit(solution)/shard_map/ppermute | solution.py:709
  234.7 7.0 %collective-permute-start.29 = (f32[8,3456]{1,0:T(8,128)S(1)}, f32[8,3456]{1,0:T(8,128)S(1)}, u32[]{:S(2)}, u32[]{:S(2)}) collective-permute-start(f32[8,3456]{1,0:T(8,128)S(1)} %add.46.a), channel_id=1, source_target_pairs={{0,8},{4,12},{8,0},{12,4},{16,24},{20,28},{24,16},{28,20},{1,9},{5... | collective-permute-start | bytes 331784 | tf_op jit(solution)/shard_map/ppermute | solution.py:709
  241.7 26.2 %collective-permute-start.41 = (bf16[1024,512]{1,0:T(8,128)(2,1)S(1)}, bf16[1024,512]{1,0:T(8,128)(2,1)}, u32[]{:S(2)}, u32[]{:S(2)}) collective-permute-start(bf16[1024,512]{1,0:T(8,128)(2,1)S(1)} %join.8.own), channel_id=1, source_target_pairs={{0,4},{4,0},{8,12},{12,8},{16,20},{20,16},{24,28},{28,24},{1,5},{5... | collective-permute-start | bytes 3145736 | tf_op jit(solution)/shard_map/ppermute | solution.py:709
  241.7 8.1 %collective-permute-start.30 = (f32[8,3456]{1,0:T(8,128)S(1)}, f32[8,3456]{1,0:T(8,128)S(1)}, u32[]{:S(2)}, u32[]{:S(2)}) collective-permute-start(f32[8,3456]{1,0:T(8,128)S(1)} %add.47.a), channel_id=1, source_target_pairs={{0,16},{4,20},{8,24},{12,28},{16,0},{20,4},{24,8},{28,12},{1,17},{... | collective-permute-start | bytes 331784 | tf_op jit(solution)/shard_map/ppermute | solution.py:709
  245.2 32.0 %collective-permute-start.36 = (bf16[512,512]{1,0:T(8,128)(2,1)S(1)}, bf16[512,512]{1,0:T(8,128)(2,1)S(1)}, u32[]{:S(2)}, u32[]{:S(2)}) collective-permute-start(bf16[512,512]{1,0:T(8,128)(2,1)S(1)} %join.6.own), channel_id=1, source_target_pairs={{0,4},{4,0},{8,12},{12,8},{16,20},{20,16},{24,28},{28,24},{1,5},{5... | collective-permute-start | bytes 1572872 | tf_op jit(solution)/shard_map/ppermute | solution.py:709
  248.2 12.8 %collective-permute-start.21 = (bf16[256,1024]{1,0:T(8,128)(2,1)}, bf16[256,1024]{1,0:T(8,128)(2,1)}, u32[]{:S(2)}, u32[]{:S(2)}) collective-permute-start(bf16[256,1024]{1,0:T(8,128)(2,1)} %add.41), channel_id=1, source_target_pairs={{0,2},{1,3},{2,0},{3,1},{4,6},{5,7},{6,4},{7,5},{8,10},{9,11},{10,... | collective-permute-start | bytes 1572872 | tf_op jit(solution)/shard_map/ppermute | solution.py:709
  (20 other events, 62.7 us)

commit v3 on v2

--- a/solution.py
+++ b/solution.py
@@ -64,13 +64,63 @@
     return pl.BlockSpec(a.shape, lambda *_: (0,) * a.ndim)
 
 
-def params(vmem):
-    return pltpu.CompilerParams(vmem_limit_bytes=vmem * MIB)
-
-
-def cost(flops, ins):
-    return pl.CostEstimate(
-        flops=flops, bytes_accessed=2 * sum(a.size * a.dtype.itemsize for a in ins), transcendentals=0
+LAST = []
+
+LONG, SHORT = 10**10, 0
+
+
+def launch(body, ins, in_specs, outs, out_specs, name, grid=(1,), meta=None, scratch=(),
+           aliases=None, vmem=8, flops=0, token=True):
+    ins, in_specs = list(ins), list(in_specs)
+    lead = 0 if meta is None else 1
+    at = lead + len(ins)
+    given = LAST[-1] if LAST and not any(LAST[-1] is a for a in ins) else None
+    if given is not None:
+        ins.append(given)
+        in_specs.append(pl.BlockSpec(memory_space=pl.ANY))
+
+    def run(*refs):
+        body(*(refs if given is None else refs[:at] + refs[at + 1 :]))
+
+    results = pl.pallas_call(
+        run,
+        grid_spec=pltpu.PrefetchScalarGridSpec(
+            num_scalar_prefetch=lead,
+            grid=grid,
+            in_specs=in_specs,
+            out_specs=list(out_specs),
+            scratch_shapes=list(scratch),
+        ),
+        out_shape=list(outs),
+        input_output_aliases={lead + k: v for k, v in (aliases or {}).items()},
+        compiler_params=pltpu.CompilerParams(vmem_limit_bytes=vmem * MIB),
+        cost_estimate=pl.CostEstimate(
+            flops=SHORT if name in ("prep", "last_rows", "project") else LONG,
+            bytes_accessed=0,
+            transcendentals=0,
+        ),
+        name=name,
+    )(*([] if meta is None else [meta]), *ins)
+    if token:
+        LAST[:] = [min(results, key=lambda a: a.size)]
+    return results
+
+
+def shaped(shape, dtype=F32):
+    return jax.ShapeDtypeStruct(shape, dtype)
+
+
+def simple(body, ins, outs, name, meta=None, vmem=8, deps=()):
+    n = len(ins)
+
+    def run(*refs):
+        lead = 0 if meta is None else 1
+        body(*refs[: lead + n], *refs[lead + n + len(deps) :])
+
+    return launch(
+        run, [*ins, *deps],
+        [whole(a) for a in ins] + [pl.BlockSpec(memory_space=pl.ANY)] * len(deps),
+        outs, [whole(o) for o in outs], name, meta=meta, vmem=vmem,
     )
 
 
@@ -83,7 +133,7 @@
 def proj_body(k, rims, deps, meta, *refs):
     toks, past = refs[:k], refs[k : k + rims]
     gain, wzx, wbc, wst = refs[k + rims : k + rims + 4]
-    outs = refs[k + rims + 4 + (4 if rims else deps) :]
+    outs = refs[k + rims + 4 + deps :]
     normed_o, gate_o, cat_o, step_o = outs[:4]
     width = wzx.shape[2]
 
@@ -97,7 +147,7 @@
         normed_o[...] = normed
         conv_inputs(normed, cat_o)
         gate_o[...] = dot(normed, wzx[0]).astype(BF)
-        step_o[...] = dot(normed, wst[...]).astype(BF)
+        step_o[...] = dot(normed, wst[...], 1, 1).astype(BF)
         if rims and j == 0:
             rim = past[0][...].astype(F32)
             for p in past[1:]:
@@ -118,33 +168,34 @@
     cols = (d, width, wide, L)
     ins = [*toks, *past, gain, wzx, wbc, wst]
     specs = [whole(a) for a in ins]
-    alias = {}
     out_specs = [pl.BlockSpec((share, c), lambda i, m: (i + first, 0)) for c in cols]
-    out_shape = [jax.ShapeDtypeStruct((total, c), BF) for c in cols]
+    out_shape = [shaped((total, c), BF) for c in cols]
     if past:
-        alias = {1 + len(ins) + j: j for j in range(4)}
         for c in (wide, d):
             out_specs.append(pl.BlockSpec((16, c), lambda i, m: (0, 0)))
-            out_shape.append(jax.ShapeDtypeStruct((16, c), BF))
-    ins += before
-    specs += [pl.BlockSpec(memory_space=pl.ANY)] * len(before)
-    return pl.pallas_call(
+            out_shape.append(shaped((16, c), BF))
+    aliases = {len(ins) + j: j for j in range(4)} if before else {}
+    return launch(
         functools.partial(proj_body, k, len(past), len(before)),
-        grid_spec=pltpu.PrefetchScalarGridSpec(
-            num_scalar_prefetch=1, grid=(k,), in_specs=specs, out_specs=out_specs
-        ),
-        out_shape=out_shape,
-        input_output_aliases=alias,
-        compiler_params=params(16),
-        cost_estimate=cost(2 * k * share * d * sum(cols[1:]), ins),
-        name="project",
-    )(meta, *ins)
-
-
-def prep_body(taps, tbias, btaps, bbias, sbias, decay, skip, ngain, tok, vecs, hv, mats, rows):
+        ins + before,
+        specs + [pl.BlockSpec(memory_space=pl.ANY)] * len(before),
+        out_shape,
+        out_specs,
+        "project",
+        grid=(k,),
+        meta=meta,
+        aliases=aliases,
+        vmem=16,
+        flops=2 * k * share * d * sum(cols[1:]),
+        token=False,
+    )
+
+
+def prep_body(taps, tbias, btaps, bbias, sbias, decay, skip, ngain, wst, vecs, hv, mats, wst_o):
     width = taps.shape[1]
     heads = width // HD
-    rows[...] = tok[...]
+    wst_o[...] = jnp.zeros_like(wst_o)
+    wst_o[0:heads, :] = wst[...]
     head = lax.broadcasted_iota(jnp.int32, (L, width), 0)
     lane = lax.broadcasted_iota(jnp.int32, (L, width), 1)
     spread = jnp.where(lax.div(lane, HD) == head, 1.0, 0.0).astype(BF)
@@ -184,22 +235,17 @@
     k = len(cots)
     share, d = cots[0].shape
     width = wout.shape[0]
-    return pl.pallas_call(
+    return launch(
         functools.partial(cot_body, k),
+        [*cots, wout],
+        [whole(a) for a in (*cots, wout)],
+        [shaped((k * share, d), BF), shaped((k * share, width), BF)],
+        [pl.BlockSpec((share, c), lambda i: (i, 0)) for c in (d, width)],
+        "cotangent",
         grid=(k,),
-        in_specs=[whole(a) for a in (*cots, wout)],
-        out_specs=[
-            pl.BlockSpec((share, d), lambda i: (i, 0)),
-            pl.BlockSpec((share, width), lambda i: (i, 0)),
-        ],
-        out_shape=[
-            jax.ShapeDtypeStruct((k * share, d), BF),
-            jax.ShapeDtypeStruct((k * share, width), BF),
-        ],
-        compiler_params=params(12),
-        cost_estimate=cost(2 * k * share * d * width, [*cots, wout]),
-        name="cotangent",
-    )(*cots, wout)
+        vmem=12,
+        flops=2 * k * share * d * width,
+    )
 
 
 def act_parts(pre, width):
@@ -624,7 +670,7 @@
         r = r + dot(gcat[:, :width], wzx[1], 1, 1)
         r = r + dot(gcat[:, width : width + L], wbc[0], 1, 1)
         r = r + dot(gcat[:, width + L :], wbc[1], 1, 1)
-        r = r + dot(gsr[...], wst[...], 1, 1)
+        r = r + dot(gsr[...], wst[...])
         out[...] = r.astype(BF)
 
     for j in range(k):
@@ -641,50 +687,27 @@
 
 def rows_times(body, frames_n, share, d, rows, consts, name):
     k = frames_n
-    outs = pl.pallas_call(
+    outs = launch(
         functools.partial(body, k),
+        [*rows, *consts],
+        [pl.BlockSpec((share, r.shape[1]), lambda i: (k - 1 - i, 0)) for r in rows]
+        + [whole(a) for a in consts],
+        [shaped((share, d), BF)] * k,
+        [pl.BlockSpec((share, d), lambda i: (0, 0))] * k,
+        name,
         grid=(k,),
-        in_specs=[pl.BlockSpec((share, r.shape[1]), lambda i: (k - 1 - i, 0)) for r in rows]
-        + [whole(a) for a in consts],
-        out_specs=[pl.BlockSpec((share, d), lambda i: (0, 0))] * k,
-        out_shape=[jax.ShapeDtypeStruct((share, d), BF)] * k,
-        compiler_params=params(20),
-        cost_estimate=cost(2 * k * share * d * sum(r.shape[1] for r in rows), [*rows, *consts]),
-        name=name,
-    )(*rows, *consts)
+        vmem=20,
+        flops=2 * k * share * d * sum(r.shape[1] for r in rows),
+    )
     return list(outs)[::-1]
 
 
-def after_body(*refs):
-    pass
-
-
-def after(x, *deps):
-    return pl.pallas_call(
-        after_body,
-        in_specs=[pl.BlockSpec(memory_space=pl.ANY)] * (1 + len(deps)),
-        out_specs=pl.BlockSpec(memory_space=pl.ANY),
-        out_shape=jax.ShapeDtypeStruct(x.shape, x.dtype),
-        input_output_aliases={0: 0},
-        compiler_params=params(1),
-        name="after",
-    )(x, *deps)
-
-
-def hold_body(x, *refs):
-    refs[-1][...] = x[...]
+def hold_body(x, o):
+    o[...] = x[...]
 
 
 def hold(x, *deps):
-    return pl.pallas_call(
-        hold_body,
-        grid=(1,),
-        in_specs=[whole(x)] + [pl.BlockSpec(memory_space=pl.ANY)] * len(deps),
-        out_specs=whole(x),
-        out_shape=jax.ShapeDtypeStruct(x.shape, x.dtype),
-        compiler_params=params(4),
-        name="hold",
-    )(x, *deps)
+    return simple(hold_body, [x], [shaped(x.shape, x.dtype)], "hold", deps=deps)[0]
 
 
 def add_body(a, b, o):
@@ -692,46 +715,12 @@
 
 
 def add(a, b):
-    return pl.pallas_call(
-        add_body,
-        in_specs=[whole(a), whole(b)],
-        out_specs=whole(a),
-        out_shape=jax.ShapeDtypeStruct(a.shape, a.dtype),
-        grid=(1,),
-        compiler_params=params(8),
-        cost_estimate=cost(a.size, [a, b]),
-        name="add",
-    )(a, b)
+    return simple(add_body, [a, b], [shaped(a.shape, a.dtype)], "add")[0]
 
 
 def swap(x, axis, mask):
     count = lax.axis_size(axis)
     return lax.ppermute(x, axis, [(i, i ^ mask) for i in range(count)])
-
-
-def frames(x, count):
-    got = {0: x}
-    mask = count // 2
-    while mask:
-        for d in sorted(got):
-            got[d ^ mask] = swap(got[d], "tensor", mask)
-        mask //= 2
-    return [got[d] for d in range(count)]
-
-
-def scatter_frames(parts, count):
-    half = count // 2
-    held = []
-    for first in (half, 0):
-        part = dict(enumerate(parts[first : first + half]))
-        mask = 1
-        while mask < half:
-            for d in list(part):
-                if d & mask:
-                    part[d ^ mask] = add(part[d ^ mask], swap(part.pop(d), "tensor", mask))
-            mask *= 2
-        held.append(part[0])
-    return held[1], swap(held[0], "tensor", half)
 
 
 def masks_of(axis):
@@ -750,54 +739,23 @@
         o[...] = (kept[rows, :].astype(F32) + got[rows, :].astype(F32)).astype(BF)
 
 
-def metaed(body, meta, ins, outs, name, vmem=8):
-    return pl.pallas_call(
-        body,
-        grid_spec=pltpu.PrefetchScalarGridSpec(
-            num_scalar_prefetch=1,
-            grid=(1,),
-            in_specs=[whole(a) for a in ins],
-            out_specs=[whole(o) for o in outs],
-        ),
-        out_shape=outs,
-        compiler_params=params(vmem),
-        cost_estimate=cost(0, ins),
-        name=name,
-    )(meta, *ins)
-
-
 def halve(meta, slot, level, kept, got):
-    shape = jax.ShapeDtypeStruct((kept.shape[0] // 2, kept.shape[1]), BF)
-    return metaed(
-        functools.partial(halve_body, slot, level), meta, [kept, got], [shape, shape], "halve"
+    shape = shaped((kept.shape[0] // 2, kept.shape[1]), BF)
+    return simple(
+        functools.partial(halve_body, slot, level), [kept, got], [shape, shape], "halve", meta
     )
 
 
 def join_body(slot, level, meta, own, got, o):
     bit = jnp.bitwise_and(jnp.right_shift(meta[slot], level), 1)
     half = own.shape[0]
-    o[pl.ds(pl.multiple_of(bit * half, half), half), :] = own[...].astype(o.dtype)
-    o[pl.ds(pl.multiple_of((1 - bit) * half, half), half), :] = got[...].astype(o.dtype)
-
-
-def join(meta, slot, level, own, got, dtype=BF):
-    shape = jax.ShapeDtypeStruct((own.shape[0] * 2, own.shape[1]), dtype)
-    (out,) = metaed(functools.partial(join_body, slot, level), meta, [own, got], [shape], "join")
-    return out
-
-
-def reduced(meta, slot, axis, masks, send, keep, first=0):
-    for level in range(first, len(masks)):
-        got = swap(send, axis, masks[level])
-        if level == len(masks) - 1:
-            return add(keep, got)
-        send, keep = halve(meta, slot, level + 1, keep, got)
-
-
-def gathered(meta, slot, axis, masks, x, last):
-    for level in range(len(masks) - 1, last, -1):
-        x = join(meta, slot, level, x, swap(x, axis, masks[level]))
-    return x, swap(x, axis, masks[last])
+    o[pl.ds(pl.multiple_of(bit * half, half), half), :] = own[...]
+    o[pl.ds(pl.multiple_of((1 - bit) * half, half), half), :] = got[...]
+
+
+def join(meta, slot, level, own, got):
+    shape = shaped((own.shape[0] * 2, own.shape[1]), BF)
+    return simple(functools.partial(join_body, slot, level), [own, got], [shape], "join", meta)[0]
 
 
 def wgrad_body(blocks, half, tails, meta, *refs):
@@ -839,23 +797,21 @@
                 specs.append(
                     pl.BlockSpec((v.shape[0], width), cut if j == which else lambda i, m: (0, 0))
                 )
-    shape = jax.ShapeDtypeStruct((half * width, width), BF)
-    return pl.pallas_call(
+    return launch(
         functools.partial(wgrad_body, blocks, half, [len(p) > 3 for p in pairs]),
-        grid_spec=pltpu.PrefetchScalarGridSpec(
-            num_scalar_prefetch=1,
-            grid=(2 * half,),
-            in_specs=specs,
-            out_specs=[
-                pl.BlockSpec((width, width), lambda i, m: (jnp.minimum(i, half - 1), 0)),
-                pl.BlockSpec((width, width), lambda i, m: (jnp.maximum(i - half, 0), 0)),
-            ],
-        ),
-        out_shape=[shape, shape],
-        compiler_params=params(20),
-        cost_estimate=cost(4 * half * tokens * width * width, ins),
-        name=name,
-    )(meta, *ins)
+        ins,
+        specs,
+        [shaped((half * width, width), BF)] * 2,
+        [
+            pl.BlockSpec((width, width), lambda i, m: (jnp.minimum(i, half - 1), 0)),
+            pl.BlockSpec((width, width), lambda i, m: (jnp.maximum(i - half, 0), 0)),
+        ],
+        name,
+        grid=(2 * half,),
+        meta=meta,
+        vmem=20,
+        flops=4 * half * tokens * width * width,
+    )
 
 
 def bc_body(meta, normed, gcat, gsr, rim, extra, send_o, keep_o, step_o):
@@ -870,93 +826,64 @@
 
 def bc_wgrad(meta, normed, gcat, gsr, rim, extra, width):
     tokens, d = normed.shape
-    shape = jax.ShapeDtypeStruct((d // 2, 2 * L), BF)
-    step = jax.ShapeDtypeStruct((8, d), F32)
-    return pl.pallas_call(
+
+    def tail(rows):
+        return pl.BlockSpec((rows, 2 * L), lambda i, m: (0, width // (2 * L)))
+
+    outs = [shaped((d // 2, 2 * L), BF)] * 2 + [shaped((8, d))]
+    return launch(
         bc_body,
-        grid_spec=pltpu.PrefetchScalarGridSpec(
-            num_scalar_prefetch=1,
-            grid=(1,),
-            in_specs=[
-                whole(normed),
-                pl.BlockSpec((tokens, 2 * L), lambda i, m: (0, width // (2 * L))),
-                whole(gsr),
-                whole(rim),
-                pl.BlockSpec((16, 2 * L), lambda i, m: (0, width // (2 * L))),
-            ],
-            out_specs=[whole(shape), whole(shape), whole(step)],
-        ),
-        out_shape=[shape, shape, step],
-        compiler_params=params(12),
-        cost_estimate=cost(2 * tokens * d * 3 * L, [normed, gsr]),
-        name="bc_wgrad",
-    )(meta, normed, gcat, gsr, rim, extra)
-
-
-def wg_out_body(level, blocks, meta, own, got, wout_o, zx_o):
-    bit = jnp.bitwise_and(jnp.right_shift(meta[1], level), 1)
-    width = wout_o.shape[0]
-    for g, src in ((0, own), (1, got)):
-        mine = bit if g == 0 else 1 - bit
-
-        @pl.when(mine == 0)
-        def _():
-            for k in range(blocks):
-                wout_o[:, k * width : (k + 1) * width] = src[
-                    k * width : (k + 1) * width, :
-                ].astype(F32)
-
-        @pl.when(mine == 1)
-        def _():
-            zx_o[0] = src[...].astype(F32)
-
-
-def wg_out(meta, own, got, d, width):
-    return pl.pallas_call(
-        functools.partial(wg_out_body, 0, d // width),
-        grid_spec=pltpu.PrefetchScalarGridSpec(
-            num_scalar_prefetch=1,
-            grid=(1,),
-            in_specs=[whole(own), whole(got)],
-            out_specs=[
-                pl.BlockSpec((width, d), lambda i, m: (0, 0)),
-                pl.BlockSpec((1, d, width), lambda i, m: (0, 0, 0)),
-            ],
-        ),
-        out_shape=[
-            jax.ShapeDtypeStruct((width, d), F32),
-            jax.ShapeDtypeStruct((2, d, width), F32),
-        ],
-        compiler_params=params(16),
-        cost_estimate=cost(0, [own, got]),
-        name="out_and_gate_weights",
-    )(meta, own, got)
-
-
-def inner_out_body(meta, own, got, old, zx_o):
-    del old
+        [normed, gcat, gsr, rim, extra],
+        [whole(normed), tail(tokens), whole(gsr), whole(rim), tail(16)],
+        outs,
+        [whole(o) for o in outs],
+        "bc_wgrad",
+        meta=meta,
+        vmem=12,
+        flops=2 * tokens * d * 3 * L,
+    )
+
+
+def columns_body(blocks, meta, own, got, o):
+    width = o.shape[0]
+    bit = bit_at(meta, 0)
+    half = blocks // 2
+    for src, b in ((own, bit), (got, 1 - bit)):
+        for side in range(2):
+
+            @pl.when(b == side)
+            def _(src=src, side=side):
+                for k in range(half):
+                    at = (side * half + k) * width
+                    o[:, at : at + width] = src[k * width : (k + 1) * width, :].astype(F32)
+
+
+def columns(meta, own, got, d, width):
+    return simple(
+        functools.partial(columns_body, d // width), [own, got], [shaped((width, d))],
+        "out_weights", meta, 16,
+    )[0]
+
+
+def rows_body(meta, own, got, *rest):
+    zx_o = rest[-1]
     bit = bit_at(meta, 0)
     half = own.shape[0]
     zx_o[0, pl.ds(pl.multiple_of(bit * half, half), half), :] = own[...].astype(F32)
     zx_o[0, pl.ds(pl.multiple_of((1 - bit) * half, half), half), :] = got[...].astype(F32)
 
 
-def inner_out(meta, own, got, old):
-    _, d, width = old.shape
-    return pl.pallas_call(
-        inner_out_body,
-        grid_spec=pltpu.PrefetchScalarGridSpec(
-            num_scalar_prefetch=1,
-            grid=(1,),
-            in_specs=[whole(own), whole(got), pl.BlockSpec(memory_space=pl.ANY)],
-            out_specs=pl.BlockSpec((1, d, width), lambda i, m: (1, 0, 0)),
-        ),
-        out_shape=jax.ShapeDtypeStruct(old.shape, F32),
-        input_output_aliases={3: 0},
-        compiler_params=params(12),
-        cost_estimate=cost(0, [own, got]),
-        name="inner_weights",
-    )(meta, own, got, old)
+def rows_of(meta, own, got, which, d, width, old):
+    ins, specs, aliases = [own, got], [whole(own), whole(got)], {}
+    if old is not None:
+        ins.append(old)
+        specs.append(pl.BlockSpec(memory_space=pl.ANY))
+        aliases = {2: 0}
+    return launch(
+        rows_body, ins, specs, [shaped((2, d, width))],
+        [pl.BlockSpec((1, d, width), lambda i, m: (which, 0, 0))],
+        "zx_weights", meta=meta, aliases=aliases, vmem=16, token=False,
+    )[0]
 
 
 def bc_out_body(meta, own, got, o):
@@ -974,26 +901,23 @@
     o[...] = (gcat[...].astype(F32) + crossing(vecs, ahead[...] * keep)).astype(BF)
 
 
-def patched(meta, gcat, ahead, kernel, share, group):
+def patched(meta, gcat, ahead, vecs, share, group):
     wide = gcat.shape[1]
 
     def spot(i, m):
         return ((jnp.bitwise_xor(m[0], group - 1) + 1) * (share // 16) - 1, 0)
 
-    return pl.pallas_call(
+    return launch(
         patch_body,
-        grid_spec=pltpu.PrefetchScalarGridSpec(
-            num_scalar_prefetch=1,
-            grid=(1,),
-            in_specs=[pl.BlockSpec((16, wide), spot), whole(ahead), whole(kernel)],
-            out_specs=pl.BlockSpec((16, wide), spot),
-        ),
-        out_shape=jax.ShapeDtypeStruct(gcat.shape, BF),
-        input_output_aliases={1: 0},
-        compiler_params=params(4),
-        cost_estimate=cost(0, [ahead]),
-        name="patch",
-    )(meta, gcat, ahead, kernel)
+        [gcat, ahead, vecs],
+        [pl.BlockSpec((16, wide), spot), whole(ahead), whole(vecs)],
+        [shaped(gcat.shape, BF)],
+        [pl.BlockSpec((16, wide), spot)],
+        "patch",
+        meta=meta,
+        aliases={0: 0},
+        token=False,
+    )[0]
 
 
 def layer_body(tok, a, b, o):
@@ -1015,17 +939,79 @@
     acc_o[:, :d] = jnp.where(row == 0, jnp.sum(gnormed * unit, axis=0, keepdims=True), 0.0)
 
 
-def plain(body, ins, outs, name, vmem=12):
-    return pl.pallas_call(
-        body,
-        grid=(1,),
-        in_specs=[whole(a) for a in ins],
-        out_specs=[whole(o) for o in outs],
-        out_shape=outs,
-        compiler_params=params(vmem),
-        cost_estimate=cost(0, ins),
-        name=name,
-    )(*ins)
+def finish_body(a, b, mats, gain_o, bc_o, bcb_o, step_o, taps_o, bias_o, sb_o, dl_o, sk_o, ng_o):
+    d, width, heads = gain_o.shape[1], taps_o.shape[1], sb_o.shape[1]
+    at = [0]
+
+    def take(n):
+        at[0] += n
+        cols = slice(at[0] - n, at[0])
+        return a[:, cols] + b[:, cols]
+
+    gain_o[...] = take(d)[0:1]
+    for k in range(2):
+        v = take(L)
+        bc_o[k] = v[0:4]
+        bcb_o[k : k + 1, :] = v[4:5]
+    step_o[...] = take(d)[:heads]
+    v = take(width)
+    taps_o[...] = v[0:4]
+    bias_o[...] = v[4:5]
+    v = take(width)
+    ng_o[...] = v[0:1]
+    sk_o[...] = dot_l(v, mats[:, :width], 1, 1)[1:2, :heads]
+    v = take(L)
+    dl_o[...] = v[0:1, :heads]
+    sb_o[...] = v[1:2, :heads]
+
+
+def pack_body(shared, step, conv, gate, head, o):
+    at = 0
+    for ref in (shared, step, conv, gate, head):
+        n = ref.shape[1] if ref is not conv else ref.shape[1] - 2 * L
+        o[:, at : at + n] = ref[:, :n]
+        at += n
+
+
+class Plan:
+    def __init__(self):
+        self.now, self.links, self.chains, self.done = 0.0, {}, [], set()
+
+    def add(self, name, priority, chain):
+        self.chains.append([name, priority, chain, None])
+        self.step(self.chains[-1])
+
+    def step(self, entry):
+        try:
+            link, us, latency, spend = next(entry[2])
+        except StopIteration:
+            self.chains.remove(entry)
+            self.done.add(entry[0])
+            return
+        if link is None:
+            entry[3] = (us, 0.0, spend)
+            return
+        start = max(self.now, self.links.get(link, 0.0))
+        self.links[link] = start + us
+        entry[3] = (None, start + us + latency, spend)
+        self.now += 1.0
+
+    def ready(self, entry):
+        name, at, _ = entry[3]
+        if name is not None:
+            return 0.0 if name in self.done else 1e9
+        return at
+
+    def run(self, until=None):
+        while self.chains and (until is None or until not in self.done):
+            able = [e for e in self.chains if self.ready(e) <= self.now]
+            if able:
+                entry = min(able, key=lambda e: e[1])
+            else:
+                entry = min(self.chains, key=self.ready)
+                self.now = self.ready(entry)
+            self.now += entry[3][2]
+            self.step(entry)
 
 
 def on_device(
@@ -1064,35 +1050,33 @@
     masks, tmasks = masks_of("dp"), masks_of("tensor")
     levels = len(masks)
 
-    wst = jnp.pad(weight_step, ((0, 0), (0, L - heads)))
+    LAST.clear()
     gain = input_gain[None]
     prep_ins = [conv_inner, conv_inner_bias[None], conv_bc, conv_bc_bias, step_bias[None],
-                decay_log[None], skip_weight[None], norm_gain[None]]
-    prep_outs = [
-        jax.ShapeDtypeStruct((8, wide), F32),
-        jax.ShapeDtypeStruct((8, L), F32),
-        jax.ShapeDtypeStruct((L, width + L), BF),
-        jax.ShapeDtypeStruct((16, d), BF),
-    ]
-    vecs, hv, mats, last_rows = pl.pallas_call(
+                decay_log[None], skip_weight[None], norm_gain[None], weight_step.T]
+    prep_outs = [shaped((8, wide)), shaped((8, L)), shaped((L, width + L), BF),
+                 shaped((L, d), BF)]
+    (last_rows,) = launch(
+        hold_body, [tokens_in], [pl.BlockSpec((16, d), lambda i: (share // 16 - 1, 0))],
+        [shaped((16, d), BF)], [pl.BlockSpec((16, d), lambda i: (0, 0))], "last_rows",
+    )
+    vecs, hv, mats, wst = launch(
         prep_body,
-        grid=(1,),
-        in_specs=[whole(a) for a in prep_ins]
-        + [pl.BlockSpec((16, d), lambda i: (share // 16 - 1, 0))],
-        out_specs=[whole(o) for o in prep_outs],
-        out_shape=prep_outs,
-        compiler_params=params(4),
-        name="prep",
-    )(*prep_ins, tokens_in)
+        [pltpu.with_memory_space_constraint(a, pltpu.HBM) for a in prep_ins],
+        [whole(a) for a in prep_ins],
+        prep_outs, [whole(o) for o in prep_outs], "prep", vmem=4,
+    )
 
     def place_of(c, meta):
         if per == 1:
             return lax.bitwise_xor(c, meta[0])
         return lax.bitwise_xor(lax.div(c, per), meta[0]) * per + lax.rem(c, per)
 
-    def stretched(body, name, ins, outs, scratch, reverse, vmem, flops):
+    def stretched(body, name, ins, outs, scratch, reverse, vmem, flops, span=None, old=()):
+        begin, length = span or (0, count)
+
         def order(i):
-            return count - 1 - i if reverse else i
+            return count - 1 - i - begin if reverse else i + begin
 
         def spec(kind, shape):
             if kind == "rows":
@@ -1101,28 +1085,37 @@
                 return pl.BlockSpec((1, *shape[1:]), lambda i, m: (order(i), 0, 0))
             return pl.BlockSpec(shape, lambda i, m: (0,) * len(shape))
 
-        return pl.pallas_call(
-            body,
-            grid_spec=pltpu.PrefetchScalarGridSpec(
-                num_scalar_prefetch=1,
-                grid=(count,),
-                in_specs=[spec(k, a.shape) for k, a in ins],
-                out_specs=[spec(k, s) for k, s, _ in outs],
-                scratch_shapes=scratch,
-            ),
-            out_shape=[jax.ShapeDtypeStruct(s, t) for _, s, t in outs],
-            compiler_params=params(vmem),
-            cost_estimate=cost(flops, [a for _, a in ins]),
-            name=name,
-        )(meta, *[a for _, a in ins])
-
+        n = len(ins)
+
+        def run(*refs):
+            body(*refs[: 1 + n], *refs[1 + n + len(old) :])
+
+        return launch(
+            run,
+            [a for _, a in ins] + list(old),
+            [spec(k, a.shape) for k, a in ins] + [pl.BlockSpec(memory_space=pl.ANY)] * len(old),
+            [shaped(s, t) for _, s, t in outs],
+            [spec(k, s) for k, s, _ in outs],
+            name,
+            grid=(length,),
+            meta=meta,
+            scratch=scratch,
+            aliases={n + j: j for j in range(len(old))},
+            vmem=vmem,
+            flops=flops,
+        )
+
+    def spread_out(held, keys):
+        mask = half // 2
+        while mask:
+            for f in [f for f in held if f in keys]:
+                held[f ^ mask] = swap(held[f], "tensor", mask)
+            mask //= 2
+
+    near, far = range(half), range(half, group)
     held = {0: tokens_in}
-    held[half] = swap(tokens_in, "tensor", half)
-    mask = half // 2
-    while mask:
-        for f in [f for f in held if f < half]:
-            held[f ^ mask] = swap(held[f], "tensor", mask)
-        mask //= 2
+    arrived = swap(tokens_in, "tensor", half)
+    spread_out(held, near)
     dps = lax.axis_size("dp")
     past = [
         lax.ppermute(
@@ -1132,18 +1125,15 @@
         )
         for t in range(group)
     ]
-    before = project(
-        meta, [held[f] for f in range(half)], [], gain, weight_zx, weight_bc, wst, tokens, 0,
-        [vecs, hv, mats],
-    )
-    mask = half // 2
-    while mask:
-        for f in [f for f in held if f >= half]:
-            held[f ^ mask] = swap(held[f], "tensor", mask)
-        mask //= 2
-    normed, gate_raw, cat, step_raw, rim, normed_rim = project(
-        meta, [held[f] for f in range(half, group)], past, gain, weight_zx, weight_bc, wst,
-        tokens, half, before,
+    weights = (gain, weight_zx, weight_bc, wst)
+    *before, rim, normed_rim = project(meta, [held[f] for f in near], past, *weights, tokens, 0, [])
+    held[half] = hold(arrived, before[3])
+    spread_out(held, far)
+    cots = {0: grad_out}
+    cots[half] = swap(hold(grad_out), "tensor", half)
+    before = project(meta, [held[half]], [], *weights, tokens, half, list(before))
+    normed, gate_raw, cat, step_raw = project(
+        meta, [held[f] for f in far[1:]], [], *weights, tokens, half + 1, list(before)
     )
 
     tall = (tokens, L)
@@ -1162,48 +1152,36 @@
         False, 10, 2 * tokens * width * L * 3,
     )
 
-    cots = {0: grad_out}
-    cots[half] = swap(hold(grad_out, step_raw), "tensor", half)
-    late = hold(cots[half], load)
-    mask = half // 2
-    while mask:
-        for f in sorted(cots):
-            cots[f ^ mask] = swap(late if f == half else cots[f], "tensor", mask)
-        mask //= 2
-    cots = [cots[f] for f in range(group)]
-
     def link(level, reverse, held, load):
-        got = swap(load, "dp", masks[level])
-        if level == levels - 1:
-            return held[2:], got
         shapes = [load_shape, state_shape, small, state_shape, small]
-        out = metaed(
-            functools.partial(link_body, level, reverse), meta, [*held, got],
-            [jax.ShapeDtypeStruct(s, BF if j == 0 else F32) for j, s in enumerate(shapes)],
-            "link",
+        out = simple(
+            functools.partial(link_body, level, reverse), [*held, load],
+            [shaped(s, BF if j == 0 else F32) for j, s in enumerate(shapes)], "link", meta,
         )
         return out[1:], out[0]
 
     thr = decay
     fresh = [jnp.zeros(state_shape, F32), jnp.ones(small, F32)]
     own = [state, decay, *fresh]
-    for level in range(levels):
-        if level == 1 or levels == 1:
-            (y,) = stretched(
-                within_body,
-                "within",
-                [("rows", pre), ("rows", step_raw), ("rows", cum), ("each", sin), ("one", vecs),
-                 ("one", hv), ("one", mats)],
-                [("rows", (tokens, width), F32)],
-                [], False, 10, 2 * tokens * width * L * 6,
-            )
-            load = after(load, y)
-        if level == 2:
-            cot_all, gn = cotangent(cots, weight_out)
+    load = swap(load, "dp", 1)
+    late = {half: hold(cots[half])}
+    spread_out(late, far)
+    spread_out(cots, near)
+    cots.update({f: late[f] for f in far[1:]})
+    (y,) = stretched(
+        within_body,
+        "within",
+        [("rows", pre), ("rows", step_raw), ("rows", cum), ("each", sin), ("one", vecs),
+         ("one", hv), ("one", mats)],
+        [("rows", (tokens, width), F32)],
+        [], False, 10, 2 * tokens * width * L * 6,
+    )
+    for level in range(levels - 1):
         own, load = link(level, False, own, load)
-    if levels < 3:
-        cot_all, gn = cotangent(cots, weight_out)
-    befores, throughs = own
+        load = swap(load, "dp", masks[level + 1])
+        if level == levels - 2:
+            cot_all, gn = cotangent([cots[f] for f in range(group)], weight_out)
+    befores, throughs = own[2:]
     mixed, sums, incoming = stretched(
         functools.partial(gate_body, levels - 1),
         "gated",
@@ -1229,28 +1207,175 @@
         True, 10, 2 * tokens * width * L * 3,
     )
 
+    plan = Plan()
+    kept = {}
     blocks = d // width
-    own, load = link(0, True, [toward, thr, *fresh], load)
-    wg_send, wg_keep = wgrads(
-        meta, [(normout, cot_all, 1), (normed, ggr, 0)], width, blocks, "out_gate_wgrad"
-    )
-    load = after(load, wg_keep)
-    if levels > 1:
-        own, load = link(1, True, own, load)
-    wg_got = swap(after(wg_send, load), "dp", 1)
-    ginner, gbc, glog, gst = stretched(
-        back_within_body,
-        "back_within",
-        [("rows", pre), ("rows", step_raw), ("rows", cum), ("each", sin), ("each", pfx),
-         ("each", gs), ("rows", gm), ("one", incoming), ("one", vecs), ("one", hv),
-         ("one", mats)],
-        [("rows", (tokens, width), F32), ("rows", (tokens, 2 * L), F32), ("rows", tall, F32),
-         ("rows", tall, F32)],
-        [], True, 12, 2 * tokens * width * L * 12,
-    )
-    for level in range(2, levels):
-        own, load = link(level, True, own, load)
-    befores, throughs = own
+    axes = {"dp": ["y", "z", "z"] + ["z"] * levels, "tensor": ["core", "x"] + ["x"] * levels}
+    spans = {"dp": [1, 1, 2] + [2] * levels, "tensor": [1, 1] + [2] * levels}
+    hops = {"core": 1.0, "x": 4.0, "y": 4.0, "z": 4.5}
+    rates = {"core": 600.0, "x": 90.0, "y": 90.0, "z": 90.0}
+
+    def moved(x, axis, level):
+        link_name = axes[axis][level]
+        size = 2 * x.size * x.dtype.itemsize * spans[axis][level] / 1e3
+        got = swap(x, axis, 1 << level)
+        return got, link_name, size / rates[link_name], hops[link_name]
+
+    def halving(key, axis, send, keep, first=0):
+        top = len(masks_of(axis))
+        slot = 1 if axis == "dp" else 0
+        for level in range(first, top):
+            got, *way = moved(send, axis, level)
+            yield (*way, 0.8)
+            if level == top - 1:
+                kept[key] = add(keep, got)
+            else:
+                send, keep = halve(meta, slot, level + 1, keep, got)
+
+    def doubling(key, axis, x, finish):
+        slot = 1 if axis == "dp" else 0
+        for level in range(len(masks_of(axis)) - 1, -1, -1):
+            got, *way = moved(x, axis, level)
+            yield (*way, 2.0 if level == 0 else 0.7)
+            if level == 0:
+                finish(x, got)
+            else:
+                x = join(meta, slot, level, x, got)
+
+    def weights_chain(key, pairs, name, spend, finish):
+        send, keep = wgrads(meta, pairs, width, blocks, name)
+        yield from halving(key, "dp", send, keep)
+        yield from doubling(key, "dp", kept[key], finish)
+
+    def zx(which):
+        def finish(own, got):
+            kept["zx"] = rows_of(meta, own, got, which, d, width, kept.get("zx"))
+
+        return finish
+
+    def out_weights(own, got):
+        kept["wout"] = columns(meta, own, got, d, width)
+
+    def first_links():
+        own = [toward, thr, *fresh]
+        load = first_load
+        for level in range(levels):
+            got, *way = moved(load, "dp", level)
+            if level == levels - 1:
+                kept["links"] = (*own[2:], got)
+                yield (*way, 0.0)
+            else:
+                yield (*way, 1.0)
+                own, load = link(level, True, own, got)
+
+    def within_part(begin, length):
+        kept["within"] = stretched(
+            back_within_body,
+            "back_within",
+            [("rows", pre), ("rows", step_raw), ("rows", cum), ("each", sin), ("each", pfx),
+             ("each", gs), ("rows", gm), ("one", incoming), ("one", vecs), ("one", hv),
+             ("one", mats)],
+            [("rows", (tokens, width), F32), ("rows", (tokens, 2 * L), F32), ("rows", tall, F32),
+             ("rows", tall, F32)],
+            [], True, 12, 2 * tokens * width * L * 12, (begin, length), kept.get("within", ()),
+        )
+
+    def within_chain():
+        part = count // 2
+        for begin in range(0, count, part):
+            yield (None, "begin", 0.0, 6.0)
+            within_part(begin, part)
+
+    def scattered(key, frames_in):
+        sums_in = []
+        for first in (half, 0):
+            part = dict(enumerate(frames_in[first : first + half]))
+            mask, level = 1, 0
+            while mask < half:
+                sent = [(f, moved(part.pop(f), "tensor", level)) for f in list(part) if f & mask]
+                for f, (got, *way) in sent:
+                    yield (*way, 0.7)
+                    part[f ^ mask] = add(part[f ^ mask], got)
+                mask, level = 2 * mask, level + 1
+            sums_in.append(part[0])
+            if first:
+                got, *way = moved(part[0], "tensor", level)
+                crossing_way = way
+                sums_in[0] = got
+        kept[key] = (sums_in[1], sums_in[0])
+        yield (*crossing_way, 1.6)
+
+    def branch_chain():
+        yield (None, "begin", 0.0, 2.0)
+        branch = rows_times(
+            outproj_body, group, share, d, [normout], [weight_out], "outproj"
+        )
+        yield from scattered("branch", branch)
+        (kept["layer"],) = simple(
+            layer_body, [tokens_in, *kept["branch"]], [shaped((share, d), BF)], "layer"
+        )
+
+    def tokens_chain():
+        ahead = lax.ppermute(kept["head"], "dp", [(i + 1, i) for i in range(dps - 1)])
+        yield ("z", 0.5, 5.0, 5.4)
+        gcat = patched(meta, kept["gcat"], ahead, vecs, share, group)
+        grads = rows_times(
+            dgrad_body, group, share, d, [ggr, gcat, kept["gsr"]], [weight_zx, weight_bc, wst],
+            "dgrad",
+        )
+        yield from scattered("grad", grads)
+        kept["tokens"], shared = simple(
+            tokens_body, [tokens_in, grad_out, *kept["grad"], gain, kept["conv_acc"]],
+            [shaped((share, d)), shaped((8, d + 2 * L))], "tokens", None, 12,
+        )
+        for level in range(len(tmasks)):
+            got, *way = moved(shared, "tensor", level)
+            yield (*way, 0.6)
+            shared = add(shared, got)
+        parts = [shared, kept["step_acc"], kept["conv_acc"], gate_acc, kept["head_acc"]]
+        size = sum(a.shape[1] for a in parts) - 2 * L
+        (total,) = simple(pack_body, parts, [shaped((8, size))], "pack")
+        for level in range(levels):
+            got, *way = moved(total, "dp", level)
+            yield (*way, 0.6)
+            if level < levels - 1:
+                total = add(total, got)
+        outs = [(1, d), (2, 4, L), (2, L), (heads, d), (4, width), (1, width), (1, heads),
+                (1, heads), (1, heads), (1, width)]
+        kept["small"] = simple(
+            finish_body, [total, got, mats], [shaped(s) for s in outs], "finish"
+        )
+
+    def bc_chain():
+        yield (None, "begin", 0.0, 1.7)
+        send, keep, kept["step_acc"] = bc_wgrad(
+            meta, normed, kept["gcat"], kept["gsr"], normed_rim, kept["extra"], width
+        )
+        yield from halving("bc", "tensor", send, keep)
+        total = kept["bc"]
+        for level in range(levels):
+            got, *way = moved(total, "dp", level)
+            yield (*way, 0.6)
+            total = add(total, got)
+
+        def finish(own, got):
+            (kept["bc_out"],) = simple(
+                bc_out_body, [own, got], [shaped((2, d, L))], "bc_weights", meta
+            )
+
+        yield from doubling("bc", "tensor", total, finish)
+
+    plan.done.add("begin")
+    first_load = load
+    plan.add("links", 0, first_links())
+    plan.add("W", 5, weights_chain("W", [(normout, cot_all, 1)], "out_wgrad", 2.0, out_weights))
+    plan.add("G", 6, weights_chain("G", [(normed, ggr, 0)], "gate_wgrad", 2.0, zx(0)))
+    plan.add("within", 8, within_chain())
+    plan.add("branch", 9, branch_chain())
+    plan.run("links")
+    plan.run("within")
+    befores, throughs, load = kept["links"]
+    ginner, gbc, glog, gst = kept["within"]
     gcat, gsr, head, extra, conv_acc, head_acc = stretched(
         functools.partial(back_conv_body, count, levels - 1),
         "back_conv",
@@ -1264,85 +1389,34 @@
          pltpu.VMEM(state_shape, F32)],
         True, 12, 2 * tokens * width * L * 6,
     )
-
-    in_send, in_keep = wgrads(
-        meta, [(normed, gcat, 0, normed_rim, extra)], width, blocks, "inner_wgrad"
-    )
-    ahead = lax.ppermute(after(head, in_keep), "dp", [(i + 1, i) for i in range(dps - 1)])
-    wg_send, wg_keep = halve(meta, 1, 1, after(wg_keep, in_keep), wg_got)
-    bc_send, bc_keep, step_acc = bc_wgrad(meta, normed, gcat, gsr, normed_rim, extra, width)
-    branch = rows_times(
-        outproj_body, group, share, d, [after(normout, wg_keep)], [weight_out], "outproj"
-    )
-    gcat = patched(meta, gcat, ahead, vecs, share, group)
-    grads = rows_times(
-        dgrad_body, group, share, d, [ggr, gcat, gsr], [weight_zx, weight_bc, wst], "dgrad"
-    )
-
-    inner_sum = reduced(meta, 1, "dp", masks, in_send, in_keep)
-    grad_a, grad_b = scatter_frames(grads, group)
-    wg_sum = reduced(meta, 1, "dp", masks, wg_send, wg_keep, 1)
-    out_a, out_b = scatter_frames(branch, group)
-    bc_sum = reduced(meta, 0, "tensor", tmasks, bc_send, bc_keep)
-    for mask in masks:
-        bc_sum = add(bc_sum, swap(bc_sum, "dp", mask))
-
-    own_shape = jax.ShapeDtypeStruct((share, d), F32)
-    grad_tokens, shared = plain(
-        tokens_body,
-        [tokens_in, grad_out, grad_a, grad_b, gain, conv_acc],
-        [own_shape, jax.ShapeDtypeStruct((8, d + 2 * L), F32)],
-        "tokens",
-    )
-    (layer_out,) = plain(
-        layer_body, [tokens_in, out_a, out_b], [jax.ShapeDtypeStruct((share, d), BF)], "layer"
-    )
-    for mask in tmasks:
-        shared = add(shared, swap(shared, "tensor", mask))
-    sums_all = jnp.concatenate(
-        [shared, step_acc, conv_acc[:, :width], gate_acc, head_acc], axis=1
-    )
-    for mask in masks:
-        sums_all = add(sums_all, swap(sums_all, "dp", mask))
-
-    grad_weight_out, grad_zx = wg_out(
-        meta, *gathered(meta, 1, "dp", masks, wg_sum, 0), d, width
-    )
-    grad_zx = inner_out(meta, *gathered(meta, 1, "dp", masks, inner_sum, 0), grad_zx)
-    (grad_bc,) = metaed(
-        bc_out_body, meta, list(gathered(meta, 0, "tensor", tmasks, bc_sum, 0)),
-        [jax.ShapeDtypeStruct((2, d, L), F32)], "bc_weights",
-    )
-
-    at = 0
-
-    def take(n):
-        nonlocal at
-        at += n
-        return sums_all[:, at - n : at]
-
-    grad_input_gain = take(d)[0]
-    bc_acc = take(2 * L).reshape(8, 2, L)
-    grad_weight_step = take(d)[:heads].T
-    inner_acc = take(width)
-    gates = take(width)
-    per_heads = take(L)[:, :heads]
+    plan.now += 10.0
+
+    kept.update(head=head, gcat=gcat, gsr=gsr, extra=extra, conv_acc=conv_acc, head_acc=head_acc)
+    plan.add(
+        "I", 1,
+        weights_chain("I", [(normed, gcat, 0, normed_rim, extra)], "inner_wgrad", 2.7, zx(1)),
+    )
+    plan.add("tokens", 2, tokens_chain())
+    plan.add("bc", 3, bc_chain())
+    plan.run()
+
+    gain_g, bc_g, bcb_g, step_g, taps_g, bias_g, sb_g, dl_g, sk_g, ng_g = kept["small"]
     return (
-        layer_out,
-        grad_tokens,
-        grad_input_gain,
-        grad_zx,
-        grad_bc,
-        grad_weight_step,
-        inner_acc[:4],
-        inner_acc[4],
-        jnp.moveaxis(bc_acc[:4], 0, 1),
-        bc_acc[4],
-        per_heads[1],
-        per_heads[0],
-        jnp.sum(gates[1].reshape(heads, HD), axis=1),
-        gates[0],
-        grad_weight_out,
+        kept["layer"],
+        kept["tokens"],
+        gain_g[0],
+        kept["zx"],
+        kept["bc_out"],
+        step_g.T,
+        taps_g,
+        bias_g[0],
+        bc_g,
+        bcb_g,
+        sb_g[0],
+        dl_g[0],
+        sk_g[0],
+        ng_g[0],
+        kept["wout"],
     )
 
 

time: 280 us -> 233 us (0.83)
  waiting for transfers between devices: 117 us -> 60.7 us
  starting transfers between devices: 51 us -> 59.7 us
  Pallas kernels: 92.6 us -> 97 us
  local copies, waits for them, and re-layouts: 15.9 us -> 12.2 us
    ppermute x44 -> x50, waiting for transfers between devices: 114 us -> 60.7 us  [swap(): return lax.ppermute(x, axis, [(i, i ^ mask) for i in range(count)])]
    ppermute x44 -> x50, starting transfers between devices: 47 us -> 55.8 us  [swap(): return lax.ppermute(x, axis, [(i, i ^ mask) for i in range(count)])]
    pallas_call x59 -> x65, Pallas kernels: 92.6 us -> 97 us  [launch(): pl.pallas_call(run, grid_spec=pltpu.PrefetchScalarGridSpec(num_scalar_pre...]
    unnamed x43 -> x52, local copies, waits for them, and re-layouts: 11.7 us -> 12.2 us
  transfers between devices with their start and end apart: 49 -> 55, of which waited for: 20 -> 21; matrix products, arithmetic and copies ran while one was open for 2% -> 0% of each run, Pallas kernels for 27% -> 35%
where the time goes in v3:
time: 233 us; the launch traced here: 232 us
  Pallas kernels  97 us (42%)
  waiting for transfers between devices  60.7 us (26%)
  starting transfers between devices  59.7 us (26%)
  local copies, waits for them, and re-layouts  12.2 us (5%)
    pallas_call x65, Pallas kernels, launch(): pl.pallas_call(run, grid_spec=pltpu.PrefetchScalarGridSpec(num_scalar_pre...  97 us
    ppermute x50, waiting for transfers between devices, swap(): return lax.ppermute(x, axis, [(i, i ^ mask) for i in range(count)])  60.7 us
    ppermute x50, starting transfers between devices, swap(): return lax.ppermute(x, axis, [(i, i ^ mask) for i in range(count)])  55.8 us
    unnamed x52, local copies, waits for them, and re-layouts  12.2 us
  transfers between devices with their start and end apart: 55, of which 21 were waited for; matrix products, arithmetic and copies ran while one was open for 0% of the time, Pallas kernels for 35%

profile of v3, /device:TPU:0, one launch (start us, length us, event | category | flops | bytes accessed | tf_op | source)
XLA Modules:
  0.0 231.9 jit_solution(18282831971749540508)
XLA Ops:
  1.2 2.6 %collective-permute-start = (bf16[256,1024]{1,0:T(8,128)(2,1)}, bf16[256,1024]{1,0:T(8,128)(2,1)S(1)}, u32[]{:S(2)}, u32[]{:S(2)}) collective-permute-start(bf16[256,1024]{1,0:T(8,128)(2,1)} %refs_0_.11), channel_id=1, source_target_pairs={{0,2},{1,3},{2,0},{3,1},{4,6},{5,7},{6,4},{7,5},{8,10},{9,11},{10,... | collective-permute-start | bytes 1572872 | tf_op jit(solution)/shard_map/ppermute | solution.py:723
  13.8 3.3 %project.3 = (bf16[1024,1024]{1,0:T(8,128)(2,1)S(1)}, bf16[1024,512]{1,0:T(8,128)(2,1)S(1)}, bf16[1024,768]{1,0:T(8,128)(2,1)S(1)}, bf16[1024,128]{1,0:T(8,128)(...) custom-call(s32[11]{0:T(128)S(1)} %pad_add_fusion.refs_0_, bf16[256,1024]{1,0:T(8,128)(2,1)S(1)} %copy-done.9, ...), custom_call_target="tpu_custom_call" | custom-call | tf_op jit(solution)/shard_map/project/pallas_call | solution.py:85
  18.3 6.6 %collective-permute-start.7 = (bf16[256,1024]{1,0:T(8,128)(2,1)S(1)}, bf16[256,1024]{1,0:T(8,128)(2,1)S(1)}, u32[]{:S(2)}, u32[]{:S(2)}) collective-permute-start(bf16[256,1024]{1,0:T(8,128)(2,1)S(1)} %hold.4.refs_10_.refs_7_), channel_id=1, source_target_pairs={{0,2},{1,3},{2,0},{3,1},{4,6},{5,7},{6,4},{7,5},{8,10},{9,11},{10,... | collective-permute-start | bytes 1572872 | tf_op jit(solution)/shard_map/ppermute | solution.py:723
  24.9 1.8 project.4
  26.7 1.8 project.5
  28.5 7.0 %states.1 = (f32[1024,768]{1,0:T(8,128)S(1)}, bf16[8,512,128]{2,1,0:T(8,128)(2,1)S(1)}, f32[512,128]{1,0:T(8,128)S(1)}, bf16[528,128]{1,0:T(8,128)(2,1)S(1)}, f3...) custom-call(s32[11]{0:T(128)S(1)} %pad_add_fusion.refs_0_, ...), custom_call_target="tpu_custom_call" | custom-call | flops 10000000000 | tf_op jit(solution)/shard_map/states/pallas_call | solution.py:85
  35.5 3.4 %collective-permute-start.10 = (bf16[528,128]{1,0:T(8,128)(2,1)S(1)}, bf16[528,128]{1,0:T(8,128)(2,1)S(1)}, u32[]{:S(2)}, u32[]{:S(2)}) collective-permute-start(bf16[528,128]{1,0:T(8,128)(2,1)S(1)} %get-tuple-element.150), channel_id=1, source_target_pairs={{0,4},{4,0},{8,12},{12,8},{16,20},{20,16},{24,28},{28,24},{1,5},{5... | collective-permute-start | bytes 405512 | tf_op jit(solution)/shard_map/ppermute | solution.py:723
  38.9 4.5 %within.1.refs_6_.refs_4_ = f32[1024,512]{1,0:T(8,128)S(1)} custom-call(s32[11]{0:T(128)S(1)} %pad_add_fusion.refs_0_, f32[1024,768]{1,0:T(8,128)S(1)} %get-tuple-element.143.refs_1_.refs_3_, bf16[1024,128]{1,0:T(8,128)(2,1)S(1)} %get-tuple-element.139.refs_2_.refs_4_, f32[1024,128]{1,0:T(8,128)S(1)} %get-tuple-element.144.refs_3_.refs_2_.refs_5_, ...), custom_call_target="tpu_custom_call" | custom-call | flops 10000000000 | tf_op jit(solution)/shard_map/within/pallas_call | solution.py:85
  44.2 1.9 collective-permute-start.11
  46.6 2.7 %collective-permute-done.11.refs_5_ = bf16[528,128]{1,0:T(8,128)(2,1)S(1)} collective-permute-done((bf16[528,128]{1,0:T(8,128)(2,1)S(1)}, bf16[528,128]{1,0:T(8,128)(2,1)S(1)}, u32[]{:S(2)}, u32[]{:S(2)}) %collective-permute-start.11) | collective-permute-done | bytes 135200 | tf_op jit(solution)/shard_map/ppermute | solution.py:723
  50.7 2.9 %collective-permute-start.12 = (bf16[528,128]{1,0:T(8,128)(2,1)S(1)}, bf16[528,128]{1,0:T(8,128)(2,1)S(1)}, u32[]{:S(2)}, u32[]{:S(2)}) collective-permute-start(bf16[528,128]{1,0:T(8,128)(2,1)S(1)} %get-tuple-element.160), channel_id=1, source_target_pairs={{0,16},{4,20},{8,24},{12,28},{16,0},{20,4},{24,8},{28,12},{1,17},{... | collective-permute-start | bytes 405512 | tf_op jit(solution)/shard_map/ppermute | solution.py:723
  53.6 2.0 cotangent.1
  55.6 2.6 %collective-permute-done.12.refs_9_ = bf16[528,128]{1,0:T(8,128)(2,1)S(1)} collective-permute-done((bf16[528,128]{1,0:T(8,128)(2,1)S(1)}, bf16[528,128]{1,0:T(8,128)(2,1)S(1)}, u32[]{:S(2)}, u32[]{:S(2)}) %collective-permute-start.12) | collective-permute-done | bytes 135200 | tf_op jit(solution)/shard_map/ppermute | solution.py:723
  58.2 5.4 %gated.1 = (f32[1024,512]{1,0:T(8,128)S(1)}, f32[8,8,128]{2,1,0:T(8,128)S(1)}, bf16[512,128]{1,0:T(8,128)(2,1)S(1)}) custom-call(s32[11]{0:T(128)S(1)} %pad_add_fusion.refs_0_, f32[1024,768]{1,0:T(8,128)S(1)} %get-tuple-element.143.refs_1_.refs_3_, f32[1024,128]{1,0:T(8,128)S(1)} %get-tuple-element.144.refs_3_.refs_2_.refs_5_, ...), custom_call_target="tpu_custom_call" | custom-call | flops 10000000000 | tf_op jit(solution)/shard_map/gated/pallas_call | solution.py:85
  65.1 2.3 %collective-permute-done.13.refs_1_ = f32[8,8,128]{2,1,0:T(8,128)S(1)} collective-permute-done((f32[8,8,128]{2,1,0:T(8,128)S(1)}, f32[8,8,128]{2,1,0:T(8,128)S(1)}, u32[]{:S(2)}, u32[]{:S(2)}) %collective-permute-start.13) | collective-permute-done | bytes 32800 | tf_op jit(solution)/shard_map/ppermute | solution.py:723
  68.7 5.6 %back_gated.1 = (bf16[1024,512]{1,0:T(8,128)(2,1)S(1)}, bf16[1024,512]{1,0:T(8,128)(2,1)S(1)}, bf16[1024,512]{1,0:T(8,128)(2,1)S(1)}, bf16[8,512,128]{2,1,0:T(8,...) custom-call(s32[11]{0:T(128)S(1)} %pad_add_fusion.refs_0_, ...), custom_call_target="tpu_custom_call" | custom-call | flops 10000000000 | tf_op jit(solution)/shard_map/back_gated/pallas_call | solution.py:85
  74.3 2.0 collective-permute-start.15
  76.4 2.3 out_wgrad.1
  78.8 2.3 gate_wgrad.1
  81.1 2.0 collective-permute-start.21
  83.1 6.3 %back_within.2 = (f32[1024,512]{1,0:T(8,128)S(1)}, f32[1024,256]{1,0:T(8,128)S(1)}, f32[1024,128]{1,0:T(8,128)S(1)}, f32[1024,128]{1,0:T(8,128)S(1)}) custom-call(s32[11]{0:T(128)S(1)} %pad_add_fusion.refs_0_, f32[1024,768]{1,0:T(8,128)S(1)} %get-tuple-element.143.refs_1_.refs_3_, bf16[1024,128]{1,0:T(8,128)(2,1)S(1)} %get-tuple-element.139.refs_2_.refs_4_, ...), custom_call_target="tpu_custom_call" | custom-call | flops 10000000000 | tf_op jit(solution)/shard_map/back_within/pallas_call | solution.py:85
  91.1 6.1 %back_within.3 = (f32[1024,512]{1,0:T(8,128)S(1)}, f32[1024,256]{1,0:T(8,128)S(1)}, f32[1024,128]{1,0:T(8,128)S(1)}, f32[1024,128]{1,0:T(8,128)S(1)}) custom-call(s32[11]{0:T(128)S(1)} %pad_add_fusion.refs_0_, f32[1024,768]{1,0:T(8,128)S(1)} %get-tuple-element.143.refs_1_.refs_3_, ...), custom_call_target="tpu_custom_call", output_to_operand_aliasing={{0}: (12, {}), {1}: (13, {}), {2}: (14, {}), {3}: (15, {})} | custom-call | flops 10000000000 | tf_op jit(solution)/shard_map/back_within/pallas_call | solution.py:85
  97.2 1.9 outproj.1
  101.1 3.4 %collective-permute-start.23 = (bf16[528,128]{1,0:T(8,128)(2,1)S(1)}, bf16[528,128]{1,0:T(8,128)(2,1)S(1)}, u32[]{:S(2)}, u32[]{:S(2)}) collective-permute-start(bf16[528,128]{1,0:T(8,128)(2,1)S(1)} %get-tuple-element.201), channel_id=1, source_target_pairs={{0,16},{4,20},{8,24},{12,28},{16,0},{20,4},{24,8},{28,12},{1,17},{... | collective-permute-start | bytes 405512 | tf_op jit(solution)/shard_map/ppermute | solution.py:723
  107.3 2.1 collective-permute-start.22
  109.3 1.7 collective-permute-done.23.refs_16_
  111.1 9.9 %back_conv.1 = (bf16[1024,768]{1,0:T(8,128)(2,1)S(1)}, bf16[1024,128]{1,0:T(8,128)(2,1)S(1)}, f32[8,768]{1,0:T(8,128)S(1)}, bf16[16,768]{1,0:T(8,128)(2,1)S(1)},...) custom-call(s32[11]{0:T(128)S(1)} %pad_add_fusion.refs_0_, bf16[1024,768]{1,0:T(8,128)(2,1)S(1)} %get-tuple-element.138.refs_1_, ...), custom_call_target="tpu_custom_call" | custom-call | flops 10000000000 | tf_op jit(solution)/shard_map/back_conv/pallas_call | solution.py:85
  122.3 2.7 %inner_wgrad.1 = (bf16[512,512]{1,0:T(8,128)(2,1)S(1)}, bf16[512,512]{1,0:T(8,128)(2,1)S(1)}) custom-call(s32[11]{0:T(128)S(1)} %pad_add_fusion.refs_0_, bf16[1024,1024]{1,0:T(8,128)(2,1)S(1)} %get-tuple-element.167.refs_1_, bf16[1024,768]{1,0:T(8,128)(2,1)S(1)} %get-tuple-element.202.refs_2_.refs_1_, ...), custom_call_target="tpu_custom_call" | custom-call | flops 10000000000 | tf_op jit(solution)/shard_map/inner_wgrad/pallas_call | solution.py:85
  124.9 2.7 %collective-permute-start.30 = (bf16[512,512]{1,0:T(8,128)(2,1)S(1)}, bf16[512,512]{1,0:T(8,128)(2,1)S(1)}, u32[]{:S(2)}, u32[]{:S(2)}) collective-permute-start(bf16[512,512]{1,0:T(8,128)(2,1)S(1)} %get-tuple-element.207.refs_6_), channel_id=1, source_target_pairs={{0,4},{4,0},{8,12},{12,8},{16,20},{20,16},{24,28},{28,24},{1,5},{5... | collective-permute-start | bytes 1572872 | tf_op jit(solution)/shard_map/ppermute | solution.py:723
  131.8 4.7 %dgrad.1 = (bf16[256,1024]{1,0:T(8,128)(2,1)S(1)}, bf16[256,1024]{1,0:T(8,128)(2,1)S(1)}, bf16[256,1024]{1,0:T(8,128)(2,1)S(1)}, bf16[256,1024]{1,0:T(8,128)(2,1)S(1)}) custom-call(bf16[1024,512]{1,0:T(8,128)(2,1)S(1)} %get-tuple-element.168.refs_2_.refs_0_, bf16[1024,768]{1,0:T(8,128)(2,1)S(1)} %patch.1.refs_1_, ...), custom_call_target="tpu_custom_call" | custom-call | flops 10000000000 | tf_op jit(solution)/shard_map/dgrad/pallas_call | solution.py:85
  143.8 2.0 collective-permute-done.27.refs_1_
  148.8 2.0 layer.1.refs_3_
  157.6 1.8 collective-permute-start.38
  160.5 1.8 collective-permute-start.41
  163.3 4.4 %collective-permute-done.38.refs_1_ = bf16[128,512]{1,0:T(8,128)(2,1)S(1)} collective-permute-done((bf16[128,512]{1,0:T(8,128)(2,1)S(1)}, bf16[128,512]{1,0:T(8,128)(2,1)S(1)}, u32[]{:S(2)}, u32[]{:S(2)}) %collective-permute-start.38) | collective-permute-done | bytes 131104 | tf_op jit(solution)/shard_map/ppermute | solution.py:723
  169.4 3.9 %collective-permute-done.41.refs_1_ = bf16[128,512]{1,0:T(8,128)(2,1)S(1)} collective-permute-done((bf16[128,512]{1,0:T(8,128)(2,1)S(1)}, bf16[128,512]{1,0:T(8,128)(2,1)S(1)}, u32[]{:S(2)}, u32[]{:S(2)}) %collective-permute-start.41) | collective-permute-done | bytes 131104 | tf_op jit(solution)/shard_map/ppermute | solution.py:723
  173.5 3.0 %collective-permute-start.43 = (bf16[256,256]{1,0:T(8,128)(2,1)S(1)}, bf16[256,256]{1,0:T(8,128)(2,1)S(1)}, u32[]{:S(2)}, u32[]{:S(2)}) collective-permute-start(bf16[256,256]{1,0:T(8,128)(2,1)S(1)} %add.46.refs_2_.refs_0_), channel_id=1, source_target_pairs={{0,16},{4,20},{8,24},{12,28},{16,0},{20,4},{24,8},{28,12},{1,17},{... | collective-permute-start | bytes 393224 | tf_op jit(solution)/shard_map/ppermute | solution.py:723
  176.6 2.8 %collective-permute-done.44.refs_2_ = bf16[256,512]{1,0:T(8,128)(2,1)S(1)} collective-permute-done((bf16[256,512]{1,0:T(8,128)(2,1)S(1)}, bf16[256,512]{1,0:T(8,128)(2,1)S(1)}, u32[]{:S(2)}, u32[]{:S(2)}) %collective-permute-start.44) | collective-permute-done | bytes 262176 | tf_op jit(solution)/shard_map/ppermute | solution.py:723
  181.4 7.0 %collective-permute-done.46.refs_2_ = bf16[128,512]{1,0:T(8,128)(2,1)S(1)} collective-permute-done((bf16[128,512]{1,0:T(8,128)(2,1)S(1)}, bf16[128,512]{1,0:T(8,128)(2,1)S(1)}, u32[]{:S(2)}, u32[]{:S(2)}) %collective-permute-start.46) | collective-permute-done | bytes 131104 | tf_op jit(solution)/shard_map/ppermute | solution.py:723
  189.0 4.8 %collective-permute-done.45.refs_2_ = bf16[512,512]{1,0:T(8,128)(2,1)S(1)} collective-permute-done((bf16[512,512]{1,0:T(8,128)(2,1)S(1)}, bf16[512,512]{1,0:T(8,128)(2,1)S(1)}, u32[]{:S(2)}, u32[]{:S(2)}) %collective-permute-start.45) | collective-permute-done | bytes 524320 | tf_op jit(solution)/shard_map/ppermute | solution.py:723
  193.8 2.0 out_weights.1.refs_2_
  198.9 3.6 %collective-permute-done.50.refs_2_ = bf16[256,256]{1,0:T(8,128)(2,1)S(1)} collective-permute-done((bf16[256,256]{1,0:T(8,128)(2,1)S(1)}, bf16[256,256]{1,0:T(8,128)(2,1)S(1)}, u32[]{:S(2)}, u32[]{:S(2)}) %collective-permute-start.50) | collective-permute-done | bytes 131104 | tf_op jit(solution)/shard_map/ppermute | solution.py:723
  203.2 1.8 collective-permute-start.48
  207.0 7.2 %collective-permute-done.49.refs_2_ = bf16[256,512]{1,0:T(8,128)(2,1)S(1)} collective-permute-done((bf16[256,512]{1,0:T(8,128)(2,1)S(1)}, bf16[256,512]{1,0:T(8,128)(2,1)S(1)}, u32[]{:S(2)}, u32[]{:S(2)}) %collective-permute-start.49) | collective-permute-done | bytes 262176 | tf_op jit(solution)/shard_map/ppermute | solution.py:723
  217.1 1.9 collective-permute-done.54.refs_2_
  219.6 2.0 zx_weights.2.refs_3_
  221.6 8.3 %collective-permute-done.53.refs_2_ = bf16[512,512]{1,0:T(8,128)(2,1)S(1)} collective-permute-done((bf16[512,512]{1,0:T(8,128)(2,1)S(1)}, bf16[512,512]{1,0:T(8,128)(2,1)S(1)}, u32[]{:S(2)}, u32[]{:S(2)}) %collective-permute-start.53) | collective-permute-done | bytes 524320 | tf_op jit(solution)/shard_map/ppermute | solution.py:723
  229.9 2.0 zx_weights.3
  (185 shorter events, 62.0 us)
Async XLA Ops:
  0.6 8.7 %collective-permute-start.1 = (bf16[256,1024]{1,0:T(8,128)(2,1)}, bf16[256,1024]{1,0:T(8,128)(2,1)S(1)}, u32[]{:S(2)}, u32[]{:S(2)}) collective-permute-start(bf16[256,1024]{1,0:T(8,128)(2,1)} %refs_0_.11), channel_id=1, source_target_pairs={{0,1},{1,0},{2,3},{3,2},{4,5},{5,4},{6,7},{7,6},{8,9},{9,8},{10,11... | collective-permute-start | bytes 1572872 | tf_op jit(solution)/shard_map/ppermute | solution.py:723
  1.2 16.0 %collective-permute-start = (bf16[256,1024]{1,0:T(8,128)(2,1)}, bf16[256,1024]{1,0:T(8,128)(2,1)S(1)}, u32[]{:S(2)}, u32[]{:S(2)}) collective-permute-start(bf16[256,1024]{1,0:T(8,128)(2,1)} %refs_0_.11), channel_id=1, source_target_pairs={{0,2},{1,3},{2,0},{3,1},{4,6},{5,7},{6,4},{7,5},{8,10},{9,11},{10,... | collective-permute-start | bytes 1572872 | tf_op jit(solution)/shard_map/ppermute | solution.py:723
  5.5 3.9 %collective-permute-start.4 = (bf16[16,1024]{1,0:T(8,128)(2,1)S(1)}, bf16[16,1024]{1,0:T(8,128)(2,1)S(1)}, u32[]{:S(2)}, u32[]{:S(2)}) collective-permute-start(bf16[16,1024]{1,0:T(8,128)(2,1)S(1)} %last_rows.1.refs_9_), channel_id=1, source_target_pairs={{3,6},{7,10},{11,14},{15,18},{19,22},{23,26},{27,30}} | collective-permute-start | bytes 98312 | tf_op jit(solution)/shard_map/ppermute | solution.py:1121
  17.3 9.4 %collective-permute-start.6 = (bf16[256,1024]{1,0:T(8,128)(2,1)S(1)}, bf16[256,1024]{1,0:T(8,128)(2,1)S(1)}, u32[]{:S(2)}, u32[]{:S(2)}) collective-permute-start(bf16[256,1024]{1,0:T(8,128)(2,1)S(1)} %hold.3.refs_1_), channel_id=1, source_target_pairs={{0,1},{1,0},{2,3},{3,2},{4,5},{5,4},{6,7},{7,6},{8,9},{9,8},{10,11... | collective-permute-start | bytes 1572872 | tf_op jit(solution)/shard_map/ppermute | solution.py:723
  18.3 20.6 %collective-permute-start.7 = (bf16[256,1024]{1,0:T(8,128)(2,1)S(1)}, bf16[256,1024]{1,0:T(8,128)(2,1)S(1)}, u32[]{:S(2)}, u32[]{:S(2)}) collective-permute-start(bf16[256,1024]{1,0:T(8,128)(2,1)S(1)} %hold.4.refs_10_.refs_7_), channel_id=1, source_target_pairs={{0,2},{1,3},{2,0},{3,1},{4,6},{5,7},{6,4},{7,5},{8,10},{9,11},{10,... | collective-permute-start | bytes 1572872 | tf_op jit(solution)/shard_map/ppermute | solution.py:723
  35.5 8.0 %collective-permute-start.10 = (bf16[528,128]{1,0:T(8,128)(2,1)S(1)}, bf16[528,128]{1,0:T(8,128)(2,1)S(1)}, u32[]{:S(2)}, u32[]{:S(2)}) collective-permute-start(bf16[528,128]{1,0:T(8,128)(2,1)S(1)} %get-tuple-element.150), channel_id=1, source_target_pairs={{0,4},{4,0},{8,12},{12,8},{16,20},{20,16},{24,28},{28,24},{1,5},{5... | collective-permute-start | bytes 405512 | tf_op jit(solution)/shard_map/ppermute | solution.py:723
  44.2 5.1 %collective-permute-start.11 = (bf16[528,128]{1,0:T(8,128)(2,1)S(1)}, bf16[528,128]{1,0:T(8,128)(2,1)S(1)}, u32[]{:S(2)}, u32[]{:S(2)}) collective-permute-start(bf16[528,128]{1,0:T(8,128)(2,1)S(1)} %get-tuple-element.155), channel_id=1, source_target_pairs={{0,8},{4,12},{8,0},{12,4},{16,24},{20,28},{24,16},{28,20},{1,9},{5... | collective-permute-start | bytes 405512 | tf_op jit(solution)/shard_map/ppermute | solution.py:723
  46.1 7.5 %collective-permute-start.8 = (bf16[256,1024]{1,0:T(8,128)(2,1)S(1)}, bf16[256,1024]{1,0:T(8,128)(2,1)S(1)}, u32[]{:S(2)}, u32[]{:S(2)}) collective-permute-start(bf16[256,1024]{1,0:T(8,128)(2,1)S(1)} %copy-done.14), channel_id=1, source_target_pairs={{0,1},{1,0},{2,3},{3,2},{4,5},{5,4},{6,7},{7,6},{8,9},{9,8},{10,11... | collective-permute-start | bytes 1572872 | tf_op jit(solution)/shard_map/ppermute | solution.py:723
  46.1 7.5 %collective-permute-start.9 = (bf16[256,1024]{1,0:T(8,128)(2,1)S(1)}, bf16[256,1024]{1,0:T(8,128)(2,1)S(1)}, u32[]{:S(2)}, u32[]{:S(2)}) collective-permute-start(bf16[256,1024]{1,0:T(8,128)(2,1)S(1)} %hold.5.refs_8_), channel_id=1, source_target_pairs={{0,1},{1,0},{2,3},{3,2},{4,5},{5,4},{6,7},{7,6},{8,9},{9,8},{10,11... | collective-permute-start | bytes 1572872 | tf_op jit(solution)/shard_map/ppermute | solution.py:723
  50.7 7.4 %collective-permute-start.12 = (bf16[528,128]{1,0:T(8,128)(2,1)S(1)}, bf16[528,128]{1,0:T(8,128)(2,1)S(1)}, u32[]{:S(2)}, u32[]{:S(2)}) collective-permute-start(bf16[528,128]{1,0:T(8,128)(2,1)S(1)} %get-tuple-element.160), channel_id=1, source_target_pairs={{0,16},{4,20},{8,24},{12,28},{16,0},{20,4},{24,8},{28,12},{1,17},{... | collective-permute-start | bytes 405512 | tf_op jit(solution)/shard_map/ppermute | solution.py:723
  63.5 3.9 %collective-permute-start.13 = (f32[8,8,128]{2,1,0:T(8,128)S(1)}, f32[8,8,128]{2,1,0:T(8,128)S(1)}, u32[]{:S(2)}, u32[]{:S(2)}) collective-permute-start(f32[8,8,128]{2,1,0:T(8,128)S(1)} %get-tuple-element.162.refs_0_), channel_id=1, source_target_pairs={{0,2},{1,3},{2,0},{3,1},{4,6},{5,7},{6,4},{7,5},{8,10},{9,11},{10,... | collective-permute-start | bytes 98312 | tf_op jit(solution)/shard_map/ppermute | solution.py:723
  74.3 15.0 %collective-permute-start.15 = (bf16[528,128]{1,0:T(8,128)(2,1)S(1)}, bf16[528,128]{1,0:T(8,128)(2,1)S(1)}, u32[]{:S(2)}, u32[]{:S(2)}) collective-permute-start(bf16[528,128]{1,0:T(8,128)(2,1)S(1)} %get-tuple-element.178), channel_id=1, source_target_pairs={{0,4},{4,0},{8,12},{12,8},{16,20},{20,16},{24,28},{28,24},{1,5},{5... | collective-permute-start | bytes 405512 | tf_op jit(solution)/shard_map/ppermute | solution.py:723
  78.6 25.8 %collective-permute-start.18 = (bf16[512,512]{1,0:T(8,128)(2,1)S(1)}, bf16[512,512]{1,0:T(8,128)(2,1)S(1)}, u32[]{:S(2)}, u32[]{:S(2)}) collective-permute-start(bf16[512,512]{1,0:T(8,128)(2,1)S(1)} %get-tuple-element.171.refs_3_), channel_id=1, source_target_pairs={{0,4},{4,0},{8,12},{12,8},{16,20},{20,16},{24,28},{28,24},{1,5},{5... | collective-permute-start | bytes 1572872 | tf_op jit(solution)/shard_map/ppermute | solution.py:723
  81.1 25.5 %collective-permute-start.21 = (bf16[512,512]{1,0:T(8,128)(2,1)S(1)}, bf16[512,512]{1,0:T(8,128)(2,1)S(1)}, u32[]{:S(2)}, u32[]{:S(2)}) collective-permute-start(bf16[512,512]{1,0:T(8,128)(2,1)S(1)} %get-tuple-element.172.refs_12_), channel_id=1, source_target_pairs={{0,4},{4,0},{8,12},{12,8},{16,20},{20,16},{24,28},{28,24},{1,5},{5... | collective-permute-start | bytes 1572872 | tf_op jit(solution)/shard_map/ppermute | solution.py:723
  90.1 9.6 %collective-permute-start.19 = (bf16[528,128]{1,0:T(8,128)(2,1)S(1)}, bf16[528,128]{1,0:T(8,128)(2,1)S(1)}, u32[]{:S(2)}, u32[]{:S(2)}) collective-permute-start(bf16[528,128]{1,0:T(8,128)(2,1)S(1)} %get-tuple-element.189), channel_id=1, source_target_pairs={{0,8},{4,12},{8,0},{12,4},{16,24},{20,28},{24,16},{28,20},{1,9},{5... | collective-permute-start | bytes 405512 | tf_op jit(solution)/shard_map/ppermute | solution.py:723
  99.1 7.3 %collective-permute-start.16 = (bf16[256,1024]{1,0:T(8,128)(2,1)S(1)}, bf16[256,1024]{1,0:T(8,128)(2,1)S(1)}, u32[]{:S(2)}, u32[]{:S(2)}) collective-permute-start(bf16[256,1024]{1,0:T(8,128)(2,1)S(1)} %get-tuple-element.182), channel_id=1, source_target_pairs={{0,1},{1,0},{2,3},{3,2},{4,5},{5,4},{6,7},{7,6},{8,9},{9,8},{10,11... | collective-permute-start | bytes 1572872 | tf_op jit(solution)/shard_map/ppermute | solution.py:723
  99.2 6.1 %collective-permute-start.17 = (bf16[256,1024]{1,0:T(8,128)(2,1)S(1)}, bf16[256,1024]{1,0:T(8,128)(2,1)S(1)}, u32[]{:S(2)}, u32[]{:S(2)}) collective-permute-start(bf16[256,1024]{1,0:T(8,128)(2,1)S(1)} %get-tuple-element.184.refs_6_), channel_id=1, source_target_pairs={{0,1},{1,0},{2,3},{3,2},{4,5},{5,4},{6,7},{7,6},{8,9},{9,8},{10,11... | collective-permute-start | bytes 1572872 | tf_op jit(solution)/shard_map/ppermute | solution.py:723
  101.1 10.0 %collective-permute-start.23 = (bf16[528,128]{1,0:T(8,128)(2,1)S(1)}, bf16[528,128]{1,0:T(8,128)(2,1)S(1)}, u32[]{:S(2)}, u32[]{:S(2)}) collective-permute-start(bf16[528,128]{1,0:T(8,128)(2,1)S(1)} %get-tuple-element.201), channel_id=1, source_target_pairs={{0,16},{4,20},{8,24},{12,28},{16,0},{20,4},{24,8},{28,12},{1,17},{... | collective-permute-start | bytes 405512 | tf_op jit(solution)/shard_map/ppermute | solution.py:723
  105.1 24.2 %collective-permute-start.26 = (bf16[256,512]{1,0:T(8,128)(2,1)S(1)}, bf16[256,512]{1,0:T(8,128)(2,1)S(1)}, u32[]{:S(2)}, u32[]{:S(2)}) collective-permute-start(bf16[256,512]{1,0:T(8,128)(2,1)S(1)} %get-tuple-element.191.refs_2_), channel_id=1, source_target_pairs={{0,8},{4,12},{8,0},{12,4},{16,24},{20,28},{24,16},{28,20},{1,9},{5... | collective-permute-start | bytes 786440 | tf_op jit(solution)/shard_map/ppermute | solution.py:723
  106.1 42.2 %collective-permute-start.20 = (bf16[256,1024]{1,0:T(8,128)(2,1)}, bf16[256,1024]{1,0:T(8,128)(2,1)}, u32[]{:S(2)}, u32[]{:S(2)}) collective-permute-start(bf16[256,1024]{1,0:T(8,128)(2,1)} %add.35.refs_2_), channel_id=1, source_target_pairs={{0,2},{1,3},{2,0},{3,1},{4,6},{5,7},{6,4},{7,5},{8,10},{9,11},{10,... | collective-permute-start | bytes 1572872 | tf_op jit(solution)/shard_map/ppermute | solution.py:723
  107.3 39.9 %collective-permute-start.22 = (bf16[256,512]{1,0:T(8,128)(2,1)S(1)}, bf16[256,512]{1,0:T(8,128)(2,1)S(1)}, u32[]{:S(2)}, u32[]{:S(2)}) collective-permute-start(bf16[256,512]{1,0:T(8,128)(2,1)S(1)} %get-tuple-element.194.refs_20_), channel_id=1, source_target_pairs={{0,8},{4,12},{8,0},{12,4},{16,24},{20,28},{24,16},{28,20},{1,9},{5... | collective-permute-start | bytes 786440 | tf_op jit(solution)/shard_map/ppermute | solution.py:723
  121.0 9.1 %collective-permute-start.25 = (f32[8,768]{1,0:T(8,128)S(1)}, f32[8,768]{1,0:T(8,128)S(1)}, u32[]{:S(2)}, u32[]{:S(2)}) collective-permute-start(f32[8,768]{1,0:T(8,128)S(1)} %get-tuple-element.210), channel_id=1, source_target_pairs={{4,0},{8,4},{12,8},{16,12},{20,16},{24,20},{28,24},{5,1},{9,5},{13... | collective-permute-start | bytes 73736 | tf_op jit(solution)/shard_map/ppermute | solution.py:1319
  124.9 14.5 %collective-permute-start.30 = (bf16[512,512]{1,0:T(8,128)(2,1)S(1)}, bf16[512,512]{1,0:T(8,128)(2,1)S(1)}, u32[]{:S(2)}, u32[]{:S(2)}) collective-permute-start(bf16[512,512]{1,0:T(8,128)(2,1)S(1)} %get-tuple-element.207.refs_6_), channel_id=1, source_target_pairs={{0,4},{4,0},{8,12},{12,8},{16,20},{20,16},{24,28},{28,24},{1,5},{5... | collective-permute-start | bytes 1572872 | tf_op jit(solution)/shard_map/ppermute | solution.py:723
  129.4 7.1 %collective-permute-start.24 = (bf16[512,256]{1,0:T(8,128)(2,1)S(1)}, bf16[512,256]{1,0:T(8,128)(2,1)S(1)}, u32[]{:S(2)}, u32[]{:S(2)}) collective-permute-start(bf16[512,256]{1,0:T(8,128)(2,1)S(1)} %get-tuple-element.209), channel_id=1, source_target_pairs={{0,1},{1,0},{2,3},{3,2},{4,5},{5,4},{6,7},{7,6},{8,9},{9,8},{10,11... | collective-permute-start | bytes 786440 | tf_op jit(solution)/shard_map/ppermute | solution.py:723
  130.1 12.2 %collective-permute-start.28 = (bf16[128,512]{1,0:T(8,128)(2,1)S(1)}, bf16[128,512]{1,0:T(8,128)(2,1)S(1)}, u32[]{:S(2)}, u32[]{:S(2)}) collective-permute-start(bf16[128,512]{1,0:T(8,128)(2,1)S(1)} %get-tuple-element.213.refs_4_.refs_6_), channel_id=1, source_target_pairs={{0,16},{4,20},{8,24},{12,28},{16,0},{20,4},{24,8},{28,12},{1,17},{... | collective-permute-start | bytes 393224 | tf_op jit(solution)/shard_map/ppermute | solution.py:723
  139.4 6.4 %collective-permute-start.27 = (bf16[256,256]{1,0:T(8,128)(2,1)S(1)}, bf16[256,256]{1,0:T(8,128)(2,1)S(1)}, u32[]{:S(2)}, u32[]{:S(2)}) collective-permute-start(bf16[256,256]{1,0:T(8,128)(2,1)S(1)} %get-tuple-element.216.refs_2_), channel_id=1, source_target_pairs={{0,2},{1,3},{2,0},{3,1},{4,6},{5,7},{6,4},{7,5},{8,10},{9,11},{10,... | collective-permute-start | bytes 393224 | tf_op jit(solution)/shard_map/ppermute | solution.py:723
  140.5 15.4 %collective-permute-start.32 = (bf16[256,1024]{1,0:T(8,128)(2,1)S(1)}, bf16[256,1024]{1,0:T(8,128)(2,1)S(1)}, u32[]{:S(2)}, u32[]{:S(2)}) collective-permute-start(bf16[256,1024]{1,0:T(8,128)(2,1)S(1)} %add.37.refs_3_), channel_id=1, source_target_pairs={{0,2},{1,3},{2,0},{3,1},{4,6},{5,7},{6,4},{7,5},{8,10},{9,11},{10,... | collective-permute-start | bytes 1572872 | tf_op jit(solution)/shard_map/ppermute | solution.py:723
  142.4 10.1 %collective-permute-start.35 = (bf16[256,512]{1,0:T(8,128)(2,1)S(1)}, bf16[256,512]{1,0:T(8,128)(2,1)S(1)}, u32[]{:S(2)}, u32[]{:S(2)}) collective-permute-start(bf16[256,512]{1,0:T(8,128)(2,1)S(1)} %get-tuple-element.222.refs_2_), channel_id=1, source_target_pairs={{0,8},{4,12},{8,0},{12,4},{16,24},{20,28},{24,16},{28,20},{1,9},{5... | collective-permute-start | bytes 786440 | tf_op jit(solution)/shard_map/ppermute | solution.py:723
  145.8 8.5 %collective-permute-start.33 = (bf16[128,512]{1,0:T(8,128)(2,1)S(1)}, bf16[128,512]{1,0:T(8,128)(2,1)S(1)}, u32[]{:S(2)}, u32[]{:S(2)}) collective-permute-start(bf16[128,512]{1,0:T(8,128)(2,1)S(1)} %add.39.refs_2_.refs_1_), channel_id=1, source_target_pairs={{0,16},{4,20},{8,24},{12,28},{16,0},{20,4},{24,8},{28,12},{1,17},{... | collective-permute-start | bytes 393224 | tf_op jit(solution)/shard_map/ppermute | solution.py:723
  147.2 6.9 %collective-permute-start.34 = (bf16[256,256]{1,0:T(8,128)(2,1)S(1)}, bf16[256,256]{1,0:T(8,128)(2,1)S(1)}, u32[]{:S(2)}, u32[]{:S(2)}) collective-permute-start(bf16[256,256]{1,0:T(8,128)(2,1)S(1)} %add.40.refs_3_.refs_0_), channel_id=1, source_target_pairs={{0,4},{4,0},{8,12},{12,8},{16,20},{20,16},{24,28},{28,24},{1,5},{5... | collective-permute-start | bytes 393224 | tf_op jit(solution)/shard_map/ppermute | solution.py:723
  157.6 5.0 %collective-permute-start.36 = (f32[8,1280]{1,0:T(8,128)S(1)}, f32[8,1280]{1,0:T(8,128)S(1)}, u32[]{:S(2)}, u32[]{:S(2)}) collective-permute-start(f32[8,1280]{1,0:T(8,128)S(1)} %get-tuple-element.228.refs_0_), channel_id=1, source_target_pairs={{0,1},{1,0},{2,3},{3,2},{4,5},{5,4},{6,7},{7,6},{8,9},{9,8},{10,11... | collective-permute-start | bytes 122888 | tf_op jit(solution)/shard_map/ppermute | solution.py:723
  157.6 10.1 %collective-permute-start.38 = (bf16[128,512]{1,0:T(8,128)(2,1)S(1)}, bf16[128,512]{1,0:T(8,128)(2,1)S(1)}, u32[]{:S(2)}, u32[]{:S(2)}) collective-permute-start(bf16[128,512]{1,0:T(8,128)(2,1)S(1)} %get-tuple-element.223.refs_3_), channel_id=1, source_target_pairs={{0,16},{4,20},{8,24},{12,28},{16,0},{20,4},{24,8},{28,12},{1,17},{... | collective-permute-start | bytes 393224 | tf_op jit(solution)/shard_map/ppermute | solution.py:723
  159.4 14.1 %collective-permute-start.40 = (bf16[256,256]{1,0:T(8,128)(2,1)S(1)}, bf16[256,256]{1,0:T(8,128)(2,1)S(1)}, u32[]{:S(2)}, u32[]{:S(2)}) collective-permute-start(bf16[256,256]{1,0:T(8,128)(2,1)S(1)} %add.41.refs_3_.refs_0_), channel_id=1, source_target_pairs={{0,8},{4,12},{8,0},{12,4},{16,24},{20,28},{24,16},{28,20},{1,9},{5... | collective-permute-start | bytes 393224 | tf_op jit(solution)/shard_map/ppermute | solution.py:723
  160.5 12.9 %collective-permute-start.41 = (bf16[128,512]{1,0:T(8,128)(2,1)S(1)}, bf16[128,512]{1,0:T(8,128)(2,1)S(1)}, u32[]{:S(2)}, u32[]{:S(2)}) collective-permute-start(bf16[128,512]{1,0:T(8,128)(2,1)S(1)} %get-tuple-element.226.refs_2_), channel_id=1, source_target_pairs={{0,16},{4,20},{8,24},{12,28},{16,0},{20,4},{24,8},{28,12},{1,17},{... | collective-permute-start | bytes 393224 | tf_op jit(solution)/shard_map/ppermute | solution.py:723
  162.3 17.1 %collective-permute-start.44 = (bf16[256,512]{1,0:T(8,128)(2,1)S(1)}, bf16[256,512]{1,0:T(8,128)(2,1)S(1)}, u32[]{:S(2)}, u32[]{:S(2)}) collective-permute-start(bf16[256,512]{1,0:T(8,128)(2,1)S(1)} %join.7.refs_6_.refs_1_), channel_id=1, source_target_pairs={{0,8},{4,12},{8,0},{12,4},{16,24},{20,28},{24,16},{28,20},{1,9},{5... | collective-permute-start | bytes 786440 | tf_op jit(solution)/shard_map/ppermute | solution.py:723
  162.5 5.3 %collective-permute-start.37 = (f32[8,1280]{1,0:T(8,128)S(1)}, f32[8,1280]{1,0:T(8,128)S(1)}, u32[]{:S(2)}, u32[]{:S(2)}) collective-permute-start(f32[8,1280]{1,0:T(8,128)S(1)} %add.42.refs_2_.refs_0_), channel_id=1, source_target_pairs={{0,2},{1,3},{2,0},{3,1},{4,6},{5,7},{6,4},{7,5},{8,10},{9,11},{10,... | collective-permute-start | bytes 122888 | tf_op jit(solution)/shard_map/ppermute | solution.py:723
  167.7 12.4 %collective-permute-start.47 = (bf16[128,512]{1,0:T(8,128)(2,1)S(1)}, bf16[128,512]{1,0:T(8,128)(2,1)S(1)}, u32[]{:S(2)}, u32[]{:S(2)}) collective-permute-start(bf16[128,512]{1,0:T(8,128)(2,1)S(1)} %add.43.refs_2_.refs_1_), channel_id=1, source_target_pairs={{0,16},{4,20},{8,24},{12,28},{16,0},{20,4},{24,8},{28,12},{1,17},{... | collective-permute-start | bytes 393224 | tf_op jit(solution)/shard_map/ppermute | solution.py:723
  168.5 8.0 %collective-permute-start.39 = (f32[8,3456]{1,0:T(8,128)S(1)}, f32[8,3456]{1,0:T(8,128)S(1)}, u32[]{:S(2)}, u32[]{:S(2)}) collective-permute-start(f32[8,3456]{1,0:T(8,128)S(1)} %pack.1.refs_2_.refs_0_), channel_id=1, source_target_pairs={{0,4},{4,0},{8,12},{12,8},{16,20},{20,16},{24,28},{28,24},{1,5},{5... | collective-permute-start | bytes 331784 | tf_op jit(solution)/shard_map/ppermute | solution.py:723
  173.4 15.0 %collective-permute-start.46 = (bf16[128,512]{1,0:T(8,128)(2,1)S(1)}, bf16[128,512]{1,0:T(8,128)(2,1)S(1)}, u32[]{:S(2)}, u32[]{:S(2)}) collective-permute-start(bf16[128,512]{1,0:T(8,128)(2,1)S(1)} %add.45.refs_2_.refs_1_), channel_id=1, source_target_pairs={{0,16},{4,20},{8,24},{12,28},{16,0},{20,4},{24,8},{28,12},{1,17},{... | collective-permute-start | bytes 393224 | tf_op jit(solution)/shard_map/ppermute | solution.py:723
  173.5 22.3 %collective-permute-start.43 = (bf16[256,256]{1,0:T(8,128)(2,1)S(1)}, bf16[256,256]{1,0:T(8,128)(2,1)S(1)}, u32[]{:S(2)}, u32[]{:S(2)}) collective-permute-start(bf16[256,256]{1,0:T(8,128)(2,1)S(1)} %add.46.refs_2_.refs_0_), channel_id=1, source_target_pairs={{0,16},{4,20},{8,24},{12,28},{16,0},{20,4},{24,8},{28,12},{1,17},{... | collective-permute-start | bytes 393224 | tf_op jit(solution)/shard_map/ppermute | solution.py:723
  176.5 21.8 %collective-permute-start.42 = (f32[8,3456]{1,0:T(8,128)S(1)}, f32[8,3456]{1,0:T(8,128)S(1)}, u32[]{:S(2)}, u32[]{:S(2)}) collective-permute-start(f32[8,3456]{1,0:T(8,128)S(1)} %add.47.refs_3_.refs_0_), channel_id=1, source_target_pairs={{0,8},{4,12},{8,0},{12,4},{16,24},{20,28},{24,16},{28,20},{1,9},{5... | collective-permute-start | bytes 331784 | tf_op jit(solution)/shard_map/ppermute | solution.py:723
  179.9 13.9 %collective-permute-start.45 = (bf16[512,512]{1,0:T(8,128)(2,1)S(1)}, bf16[512,512]{1,0:T(8,128)(2,1)S(1)}, u32[]{:S(2)}, u32[]{:S(2)}) collective-permute-start(bf16[512,512]{1,0:T(8,128)(2,1)S(1)} %join.8.refs_3_.refs_1_), channel_id=1, source_target_pairs={{0,4},{4,0},{8,12},{12,8},{16,20},{20,16},{24,28},{28,24},{1,5},{5... | collective-permute-start | bytes 1572872 | tf_op jit(solution)/shard_map/ppermute | solution.py:723
  180.7 17.5 %collective-permute-start.51 = (bf16[256,512]{1,0:T(8,128)(2,1)S(1)}, bf16[256,512]{1,0:T(8,128)(2,1)S(1)}, u32[]{:S(2)}, u32[]{:S(2)}) collective-permute-start(bf16[256,512]{1,0:T(8,128)(2,1)S(1)} %join.9.refs_3_.refs_1_), channel_id=1, source_target_pairs={{0,8},{4,12},{8,0},{12,4},{16,24},{20,28},{24,16},{28,20},{1,9},{5... | collective-permute-start | bytes 786440 | tf_op jit(solution)/shard_map/ppermute | solution.py:723
  197.4 5.0 %collective-permute-start.50 = (bf16[256,256]{1,0:T(8,128)(2,1)S(1)}, bf16[256,256]{1,0:T(8,128)(2,1)S(1)}, u32[]{:S(2)}, u32[]{:S(2)}) collective-permute-start(bf16[256,256]{1,0:T(8,128)(2,1)S(1)} %add.48.refs_2_.refs_1_), channel_id=1, source_target_pairs={{0,2},{1,3},{2,0},{3,1},{4,6},{5,7},{6,4},{7,5},{8,10},{9,11},{10,... | collective-permute-start | bytes 393224 | tf_op jit(solution)/shard_map/ppermute | solution.py:723
  203.1 11.1 %collective-permute-start.49 = (bf16[256,512]{1,0:T(8,128)(2,1)S(1)}, bf16[256,512]{1,0:T(8,128)(2,1)S(1)}, u32[]{:S(2)}, u32[]{:S(2)}) collective-permute-start(bf16[256,512]{1,0:T(8,128)(2,1)S(1)} %join.10.refs_3_.refs_1_), channel_id=1, source_target_pairs={{0,8},{4,12},{8,0},{12,4},{16,24},{20,28},{24,16},{28,20},{1,9},{5... | collective-permute-start | bytes 786440 | tf_op jit(solution)/shard_map/ppermute | solution.py:723
  203.2 13.2 %collective-permute-start.48 = (f32[8,3456]{1,0:T(8,128)S(1)}, f32[8,3456]{1,0:T(8,128)S(1)}, u32[]{:S(2)}, u32[]{:S(2)}) collective-permute-start(f32[8,3456]{1,0:T(8,128)S(1)} %add.49.refs_3_.refs_0_), channel_id=1, source_target_pairs={{0,16},{4,20},{8,24},{12,28},{16,0},{20,4},{24,8},{28,12},{1,17},{... | collective-permute-start | bytes 331784 | tf_op jit(solution)/shard_map/ppermute | solution.py:723
  205.0 14.0 %collective-permute-start.54 = (bf16[512,512]{1,0:T(8,128)(2,1)S(1)}, bf16[512,512]{1,0:T(8,128)(2,1)S(1)}, u32[]{:S(2)}, u32[]{:S(2)}) collective-permute-start(bf16[512,512]{1,0:T(8,128)(2,1)S(1)} %join.11.refs_3_.refs_1_), channel_id=1, source_target_pairs={{0,4},{4,0},{8,12},{12,8},{16,20},{20,16},{24,28},{28,24},{1,5},{5... | collective-permute-start | bytes 1572872 | tf_op jit(solution)/shard_map/ppermute | solution.py:723
  216.0 13.9 %collective-permute-start.53 = (bf16[512,512]{1,0:T(8,128)(2,1)S(1)}, bf16[512,512]{1,0:T(8,128)(2,1)S(1)}, u32[]{:S(2)}, u32[]{:S(2)}) collective-permute-start(bf16[512,512]{1,0:T(8,128)(2,1)S(1)} %join.13.refs_3_.refs_1_), channel_id=1, source_target_pairs={{0,4},{4,0},{8,12},{12,8},{16,20},{20,16},{24,28},{28,24},{1,5},{5... | collective-permute-start | bytes 1572872 | tf_op jit(solution)/shard_map/ppermute | solution.py:723
  (33 other events, 95.1 us)

commit v4 on v3

--- a/solution.py
+++ b/solution.py
@@ -15,6 +15,7 @@
 F32 = jnp.float32
 BF = jnp.bfloat16
 MIB = 1 << 20
+ROW = 256
 
 
 def dot(a, b, ca=1, cb=0):
@@ -65,9 +66,6 @@
 
 
 LAST = []
-
-LONG, SHORT = 10**10, 0
-
 
 def launch(body, ins, in_specs, outs, out_specs, name, grid=(1,), meta=None, scratch=(),
            aliases=None, vmem=8, flops=0, token=True):
@@ -95,7 +93,7 @@
         input_output_aliases={lead + k: v for k, v in (aliases or {}).items()},
         compiler_params=pltpu.CompilerParams(vmem_limit_bytes=vmem * MIB),
         cost_estimate=pl.CostEstimate(
-            flops=SHORT if name in ("prep", "last_rows", "project") else LONG,
+            flops=flops,
             bytes_accessed=0,
             transcendentals=0,
         ),
@@ -104,6 +102,15 @@
     if token:
         LAST[:] = [min(results, key=lambda a: a.size)]
     return results
+
+
+def space_body(o):
+    o[...] = jnp.zeros_like(o)
+
+
+def space():
+    o = shaped((8, L))
+    launch(space_body, [], [], [o], [whole(o)], "space", vmem=1, flops=10**10)
 
 
 def shaped(shape, dtype=F32):
@@ -186,7 +193,6 @@
         meta=meta,
         aliases=aliases,
         vmem=16,
-        flops=2 * k * share * d * sum(cols[1:]),
         token=False,
     )
 
@@ -244,7 +250,6 @@
         "cotangent",
         grid=(k,),
         vmem=12,
-        flops=2 * k * share * d * width,
     )
 
 
@@ -697,7 +702,6 @@
         name,
         grid=(k,),
         vmem=20,
-        flops=2 * k * share * d * sum(r.shape[1] for r in rows),
     )
     return list(outs)[::-1]
 
@@ -810,7 +814,6 @@
         grid=(2 * half,),
         meta=meta,
         vmem=20,
-        flops=4 * half * tokens * width * width,
     )
 
 
@@ -840,29 +843,33 @@
         "bc_wgrad",
         meta=meta,
         vmem=12,
-        flops=2 * tokens * d * 3 * L,
-    )
-
-
-def columns_body(blocks, meta, own, got, o):
-    width = o.shape[0]
+    )
+
+
+def wg_out_body(blocks, meta, own, got, wout_o, zx_o):
     bit = bit_at(meta, 0)
-    half = blocks // 2
-    for src, b in ((own, bit), (got, 1 - bit)):
-        for side in range(2):
-
-            @pl.when(b == side)
-            def _(src=src, side=side):
-                for k in range(half):
-                    at = (side * half + k) * width
-                    o[:, at : at + width] = src[k * width : (k + 1) * width, :].astype(F32)
-
-
-def columns(meta, own, got, d, width):
-    return simple(
-        functools.partial(columns_body, d // width), [own, got], [shaped((width, d))],
-        "out_weights", meta, 16,
-    )[0]
+    width = wout_o.shape[0]
+    for src, side in ((own, bit), (got, 1 - bit)):
+
+        @pl.when(side == 0)
+        def _(src=src):
+            for k in range(blocks):
+                rows = slice(k * width, (k + 1) * width)
+                wout_o[:, rows] = src[rows, :].astype(F32)
+
+        @pl.when(side == 1)
+        def _(src=src):
+            zx_o[0] = src[...].astype(F32)
+
+
+def wg_out(meta, own, got, d, width):
+    return launch(
+        functools.partial(wg_out_body, d // width), [own, got], [whole(own), whole(got)],
+        [shaped((width, d)), shaped((2, d, width))],
+        [pl.BlockSpec((width, d), lambda i, m: (0, 0)),
+         pl.BlockSpec((1, d, width), lambda i, m: (0, 0, 0))],
+        "out_weights", meta=meta, vmem=20, token=False,
+    )
 
 
 def rows_body(meta, own, got, *rest):
@@ -934,54 +941,118 @@
         gunit - unit * jnp.mean(gunit * unit, axis=1, keepdims=True)
     )
     d = x.shape[1]
-    acc_o[:, d:] = conv[:, conv.shape[1] - 2 * L :]
-    row = lax.broadcasted_iota(jnp.int32, (8, d), 0)
-    acc_o[:, :d] = jnp.where(row == 0, jnp.sum(gnormed * unit, axis=0, keepdims=True), 0.0)
-
-
-def finish_body(a, b, mats, gain_o, bc_o, bcb_o, step_o, taps_o, bias_o, sb_o, dl_o, sk_o, ng_o):
+    acc_o[...] = jnp.zeros_like(acc_o)
+    sums = jnp.sum(gnormed * unit, axis=0, keepdims=True)
+    for k in range(d // ROW):
+        acc_o[k : k + 1, :] = sums[:, k * ROW : (k + 1) * ROW]
+    acc_o[d // ROW : d // ROW + 5, :] = conv[0:5, conv.shape[1] - ROW :]
+
+
+def halves_of(v):
+    hi, lo = split(v)
+    return jnp.concatenate([hi, lo], axis=0)
+
+
+def whole_of(v):
+    n = v.shape[0] // 2
+    v = v.astype(F32)
+    return v[:n] + v[n:]
+
+
+def lead_body(bc, shared, o):
+    rows = bc.shape[0]
+    o[:rows, :] = bc[...]
+    o[rows:, :] = halves_of(shared[...])
+
+
+def misc_halve_body(level, meta, kept, shared, got, send_o, keep_o, shared_o):
+    bit = jnp.bitwise_and(jnp.right_shift(meta[0], level), 1)
+    half = keep_o.shape[0]
+    total = shared[...] + whole_of(got[2 * half :, :])
+    shared_o[...] = total
+    for o, b in ((send_o, 1 - bit), (keep_o, bit)):
+        rows = pl.ds(pl.multiple_of(b * half, half), half)
+        o[0:half, :] = (kept[rows, :].astype(F32) + got[rows, :].astype(F32)).astype(BF)
+    send_o[half:, :] = halves_of(total)
+
+
+def misc_pack_body(kept, shared, got, step, conv, gate, head, o):
+    rows = kept.shape[0]
+    o[0:rows, :] = (kept[...].astype(F32) + got[0:rows, :].astype(F32)).astype(BF)
+    d = step.shape[1]
+    at = rows
+    for k in range(d // ROW):
+        o[at : at + 8, :] = step[:, k * ROW : (k + 1) * ROW].astype(BF)
+        at += 8
+    total = shared[...] + whole_of(got[rows:, :])
+    width = gate.shape[1]
+    parts = [total]
+    for ref, first, n in ((conv, 0, 5), (gate, 0, 2)):
+        for k in range(width // ROW):
+            parts.append(ref[first : first + n, k * ROW : (k + 1) * ROW])
+    used = 7 * (width // ROW)
+    parts.append(jnp.concatenate([head[0:1, :], head[1:2, :]], axis=1))
+    parts.append(jnp.zeros((31 - used, ROW), F32))
+    o[at:, :] = halves_of(jnp.concatenate(parts, axis=0))
+
+
+def misc_sum(a, b, plain_rows):
+    first = a[0:plain_rows, :].astype(F32) + b[0:plain_rows, :].astype(F32)
+    return first, whole_of(a[plain_rows:, :]) + whole_of(b[plain_rows:, :])
+
+
+def misc_add_body(plain_rows, a, b, o):
+    first, rest = misc_sum(a, b, plain_rows)
+    o[0:plain_rows, :] = first.astype(BF)
+    o[plain_rows:, :] = halves_of(rest)
+
+
+def misc_finish_body(bc_rows, a, b, mats, bcw_o, gain_o, bc_o, bcb_o, step_o, taps_o, bias_o,
+                     sb_o, dl_o, sk_o, ng_o):
     d, width, heads = gain_o.shape[1], taps_o.shape[1], sb_o.shape[1]
-    at = [0]
-
-    def take(n):
-        at[0] += n
-        cols = slice(at[0] - n, at[0])
-        return a[:, cols] + b[:, cols]
-
-    gain_o[...] = take(d)[0:1]
+    n = d // ROW
+    first, rest = misc_sum(a, b, bc_rows + 8 * n)
+    bcw_o[...] = first[0:bc_rows].astype(BF)
+    for k in range(n):
+        cols = slice(k * ROW, (k + 1) * ROW)
+        at = bc_rows + 8 * k
+        step_o[:, cols] = first[at : at + heads]
+        gain_o[:, cols] = rest[k : k + 1]
     for k in range(2):
-        v = take(L)
+        v = rest[n : n + 5, k * L : (k + 1) * L]
         bc_o[k] = v[0:4]
         bcb_o[k : k + 1, :] = v[4:5]
-    step_o[...] = take(d)[:heads]
-    v = take(width)
-    taps_o[...] = v[0:4]
-    bias_o[...] = v[4:5]
-    v = take(width)
-    ng_o[...] = v[0:1]
-    sk_o[...] = dot_l(v, mats[:, :width], 1, 1)[1:2, :heads]
-    v = take(L)
-    dl_o[...] = v[0:1, :heads]
-    sb_o[...] = v[1:2, :heads]
-
-
-def pack_body(shared, step, conv, gate, head, o):
-    at = 0
-    for ref in (shared, step, conv, gate, head):
-        n = ref.shape[1] if ref is not conv else ref.shape[1] - 2 * L
-        o[:, at : at + n] = ref[:, :n]
-        at += n
+    at = 16
+    m = width // ROW
+    gates = []
+    for k in range(m):
+        cols = slice(k * ROW, (k + 1) * ROW)
+        taps_o[:, cols] = rest[at : at + 4]
+        bias_o[:, cols] = rest[at + 4 : at + 5]
+        at += 5
+    for k in range(m):
+        cols = slice(k * ROW, (k + 1) * ROW)
+        ng_o[:, cols] = rest[at : at + 1]
+        gates.append(jnp.broadcast_to(rest[at + 1 : at + 2], (8, ROW)))
+        at += 2
+    sk = dot_l(jnp.concatenate(gates, axis=1), mats[:, :width], 1, 1)
+    sk_o[...] = sk[0:1, :heads]
+    dl_o[...] = rest[at : at + 1, :heads]
+    sb_o[...] = rest[at : at + 1, L : L + heads]
 
 
 class Plan:
     def __init__(self):
         self.now, self.links, self.chains, self.done = 0.0, {}, [], set()
 
-    def add(self, name, priority, chain):
+    def add(self, name, priority, chain, spend=0.0):
         self.chains.append([name, priority, chain, None])
+        self.now += spend
         self.step(self.chains[-1])
 
     def step(self, entry):
+        if entry[3] and entry[3][0] is None:
+            space()
         try:
             link, us, latency, spend = next(entry[2])
         except StopIteration:
@@ -1056,17 +1127,12 @@
                 decay_log[None], skip_weight[None], norm_gain[None], weight_step.T]
     prep_outs = [shaped((8, wide)), shaped((8, L)), shaped((L, width + L), BF),
                  shaped((L, d), BF)]
-    (last_rows,) = launch(
-        hold_body, [tokens_in], [pl.BlockSpec((16, d), lambda i: (share // 16 - 1, 0))],
-        [shaped((16, d), BF)], [pl.BlockSpec((16, d), lambda i: (0, 0))], "last_rows",
-    )
     vecs, hv, mats, wst = launch(
         prep_body,
         [pltpu.with_memory_space_constraint(a, pltpu.HBM) for a in prep_ins],
         [whole(a) for a in prep_ins],
         prep_outs, [whole(o) for o in prep_outs], "prep", vmem=4,
     )
-
     def place_of(c, meta):
         if per == 1:
             return lax.bitwise_xor(c, meta[0])
@@ -1102,7 +1168,7 @@
             scratch=scratch,
             aliases={n + j: j for j in range(len(old))},
             vmem=vmem,
-            flops=flops,
+            flops=0,
         )
 
     def spread_out(held, keys):
@@ -1117,6 +1183,13 @@
     arrived = swap(tokens_in, "tensor", half)
     spread_out(held, near)
     dps = lax.axis_size("dp")
+    weights = (gain, weight_zx, weight_bc, wst)
+    before = project(meta, [held[f] for f in near], [], *weights, tokens, 0, [])
+    (last_rows,) = launch(
+        lambda tok, _, o: hold_body(tok, o), [tokens_in, before[3]],
+        [pl.BlockSpec((16, d), lambda i: (share // 16 - 1, 0)), pl.BlockSpec(memory_space=pl.ANY)],
+        [shaped((16, d), BF)], [pl.BlockSpec((16, d), lambda i: (0, 0))], "last_rows",
+    )
     past = [
         lax.ppermute(
             last_rows,
@@ -1125,16 +1198,16 @@
         )
         for t in range(group)
     ]
-    weights = (gain, weight_zx, weight_bc, wst)
-    *before, rim, normed_rim = project(meta, [held[f] for f in near], past, *weights, tokens, 0, [])
+    space()
     held[half] = hold(arrived, before[3])
     spread_out(held, far)
+    before = project(meta, [held[half]], [], *weights, tokens, half, list(before))
+    space()
+    normed, gate_raw, cat, step_raw, rim, normed_rim = project(
+        meta, [held[f] for f in far[1:]], past, *weights, tokens, half + 1, list(before)
+    )
     cots = {0: grad_out}
-    cots[half] = swap(hold(grad_out), "tensor", half)
-    before = project(meta, [held[half]], [], *weights, tokens, half, list(before))
-    normed, gate_raw, cat, step_raw = project(
-        meta, [held[f] for f in far[1:]], [], *weights, tokens, half + 1, list(before)
-    )
+    cots[half] = swap(hold(grad_out, rim), "tensor", half)
 
     tall = (tokens, L)
     state_shape = (width, L)
@@ -1164,10 +1237,6 @@
     fresh = [jnp.zeros(state_shape, F32), jnp.ones(small, F32)]
     own = [state, decay, *fresh]
     load = swap(load, "dp", 1)
-    late = {half: hold(cots[half])}
-    spread_out(late, far)
-    spread_out(cots, near)
-    cots.update({f: late[f] for f in far[1:]})
     (y,) = stretched(
         within_body,
         "within",
@@ -1177,11 +1246,20 @@
         [], False, 10, 2 * tokens * width * L * 6,
     )
     for level in range(levels - 1):
+        space()
         own, load = link(level, False, own, load)
         load = swap(load, "dp", masks[level + 1])
+        if level == 0:
+            space()
+            late = {half: hold(cots[half])}
+            spread_out(late, far)
+            spread_out(cots, near)
+            cots.update({f: late[f] for f in far[1:]})
         if level == levels - 2:
+            space()
             cot_all, gn = cotangent([cots[f] for f in range(group)], weight_out)
     befores, throughs = own[2:]
+    space()
     mixed, sums, incoming = stretched(
         functools.partial(gate_body, levels - 1),
         "gated",
@@ -1192,8 +1270,11 @@
         [], False, 10, 2 * tokens * width * L * 4,
     )
     for mask in tmasks[::-1][:-1]:
-        sums = add(sums, swap(sums, "tensor", mask))
+        got = swap(sums, "tensor", mask)
+        space()
+        sums = add(sums, got)
     sums2 = swap(sums, "tensor", 1)
+    space()
     normout, gm, ggr, gs, toward, load, sfx, gate_acc = stretched(
         functools.partial(back_gate_body, count),
         "back_gated",
@@ -1238,23 +1319,22 @@
             got, *way = moved(x, axis, level)
             yield (*way, 2.0 if level == 0 else 0.7)
             if level == 0:
+                if key == "I":
+                    yield (None, "WG", 0.0, 2.0)
                 finish(x, got)
             else:
                 x = join(meta, slot, level, x, got)
 
-    def weights_chain(key, pairs, name, spend, finish):
+    def weights_chain(key, pairs, name, finish):
         send, keep = wgrads(meta, pairs, width, blocks, name)
         yield from halving(key, "dp", send, keep)
         yield from doubling(key, "dp", kept[key], finish)
 
-    def zx(which):
-        def finish(own, got):
-            kept["zx"] = rows_of(meta, own, got, which, d, width, kept.get("zx"))
-
-        return finish
-
-    def out_weights(own, got):
-        kept["wout"] = columns(meta, own, got, d, width)
+    def inner_out(own, got):
+        kept["zx"] = rows_of(meta, own, got, 1, d, width, kept["zx"])
+
+    def out_gate(own, got):
+        kept["wout"], kept["zx"] = wg_out(meta, own, got, d, width)
 
     def first_links():
         own = [toward, thr, *fresh]
@@ -1326,54 +1406,70 @@
         yield from scattered("grad", grads)
         kept["tokens"], shared = simple(
             tokens_body, [tokens_in, grad_out, *kept["grad"], gain, kept["conv_acc"]],
-            [shaped((share, d)), shaped((8, d + 2 * L))], "tokens", None, 12,
+            [shaped((share, d)), shaped((16, ROW))], "tokens", None, 12,
         )
+        yield (None, "bc", 0.0, 0.5)
+        send, keep = kept["bc"]
+        (load,) = simple(lead_body, [send, shared], [shaped((send.shape[0] + 32, ROW), BF)], "lead")
         for level in range(len(tmasks)):
-            got, *way = moved(shared, "tensor", level)
+            got, *way = moved(load, "tensor", level)
             yield (*way, 0.6)
-            shared = add(shared, got)
-        parts = [shared, kept["step_acc"], kept["conv_acc"], gate_acc, kept["head_acc"]]
-        size = sum(a.shape[1] for a in parts) - 2 * L
-        (total,) = simple(pack_body, parts, [shaped((8, size))], "pack")
+            if level < len(tmasks) - 1:
+                rows = keep.shape[0] // 2
+                load, keep, shared = simple(
+                    functools.partial(misc_halve_body, level + 1), [keep, shared, got],
+                    [shaped((rows + 32, ROW), BF), shaped((rows, ROW), BF), shaped((16, ROW))],
+                    "misc_halve", meta,
+                )
+        rows = keep.shape[0]
+        flat = rows + 8 * (d // ROW)
+        (load,) = simple(
+            misc_pack_body,
+            [keep, shared, got, kept["step_acc"], kept["conv_acc"], gate_acc, kept["head_acc"]],
+            [shaped((flat + 96, ROW), BF)], "misc_pack",
+        )
         for level in range(levels):
-            got, *way = moved(total, "dp", level)
+            got, *way = moved(load, "dp", level)
             yield (*way, 0.6)
             if level < levels - 1:
-                total = add(total, got)
+                (load,) = simple(
+                    functools.partial(misc_add_body, flat), [load, got],
+                    [shaped(load.shape, BF)], "misc_add",
+                )
         outs = [(1, d), (2, 4, L), (2, L), (heads, d), (4, width), (1, width), (1, heads),
                 (1, heads), (1, heads), (1, width)]
-        kept["small"] = simple(
-            finish_body, [total, got, mats], [shaped(s) for s in outs], "finish"
+        total, *kept["small"] = simple(
+            functools.partial(misc_finish_body, rows), [load, got, mats],
+            [shaped((rows, ROW), BF)] + [shaped(s) for s in outs], "misc_finish",
         )
+
+        def finish(own, got):
+            (kept["bc_out"],) = simple(
+                bc_out_body, [own, got], [shaped((2, d, L))], "bc_weights", meta
+            )
+
+        yield from doubling("bc", "tensor", total, finish)
 
     def bc_chain():
         yield (None, "begin", 0.0, 1.7)
         send, keep, kept["step_acc"] = bc_wgrad(
             meta, normed, kept["gcat"], kept["gsr"], normed_rim, kept["extra"], width
         )
-        yield from halving("bc", "tensor", send, keep)
-        total = kept["bc"]
-        for level in range(levels):
-            got, *way = moved(total, "dp", level)
-            yield (*way, 0.6)
-            total = add(total, got)
-
-        def finish(own, got):
-            (kept["bc_out"],) = simple(
-                bc_out_body, [own, got], [shaped((2, d, L))], "bc_weights", meta
-            )
-
-        yield from doubling("bc", "tensor", total, finish)
+        kept["bc"] = (send, keep)
 
     plan.done.add("begin")
     first_load = load
     plan.add("links", 0, first_links())
-    plan.add("W", 5, weights_chain("W", [(normout, cot_all, 1)], "out_wgrad", 2.0, out_weights))
-    plan.add("G", 6, weights_chain("G", [(normed, ggr, 0)], "gate_wgrad", 2.0, zx(0)))
+    plan.add(
+        "WG", 5,
+        weights_chain("WG", [(normout, cot_all, 1), (normed, ggr, 0)], "out_wgrad", out_gate),
+        4.3,
+    )
     plan.add("within", 8, within_chain())
     plan.add("branch", 9, branch_chain())
     plan.run("links")
     plan.run("within")
+    space()
     befores, throughs, load = kept["links"]
     ginner, gbc, glog, gst = kept["within"]
     gcat, gsr, head, extra, conv_acc, head_acc = stretched(
@@ -1394,7 +1490,8 @@
     kept.update(head=head, gcat=gcat, gsr=gsr, extra=extra, conv_acc=conv_acc, head_acc=head_acc)
     plan.add(
         "I", 1,
-        weights_chain("I", [(normed, gcat, 0, normed_rim, extra)], "inner_wgrad", 2.7, zx(1)),
+        weights_chain("I", [(normed, gcat, 0, normed_rim, extra)], "inner_wgrad", inner_out),
+        2.7,
     )
     plan.add("tokens", 2, tokens_chain())
     plan.add("bc", 3, bc_chain())

time: 233 us -> 216 us (0.927)
  starting transfers between devices: 59.7 us -> 47 us
  Pallas kernels: 97 us -> 92.3 us
    ppermute x50 -> x39, starting transfers between devices: 55.8 us -> 43.1 us  [swap(): return lax.ppermute(x, axis, [(i, i ^ mask) for i in range(count)])]
    pallas_call x65 -> x92, Pallas kernels: 97 us -> 92.3 us  [launch(): pl.pallas_call(run, grid_spec=pltpu.PrefetchScalarGridSpec(num_scalar_pre...]
    ppermute x50 -> x39, waiting for transfers between devices: 60.7 us -> 62 us  [swap(): return lax.ppermute(x, axis, [(i, i ^ mask) for i in range(count)])]
    unnamed x52 -> x48, local copies, waits for them, and re-layouts: 12.2 us -> 11.9 us
  transfers between devices with their start and end apart: 55 -> 44, of which waited for: 21 -> 21; matrix products, arithmetic and copies ran while one was open for 0% -> 0% of each run, Pallas kernels for 35% -> 37%
where the time goes in v4:
time: 216 us
  Pallas kernels  92.3 us (43%)
  waiting for transfers between devices  62.1 us (29%)
  starting transfers between devices  47 us (22%)
  local copies, waits for them, and re-layouts  12 us (6%)
    pallas_call x92, Pallas kernels, launch(): pl.pallas_call(run, grid_spec=pltpu.PrefetchScalarGridSpec(num_scalar_pre...  92.3 us
    ppermute x39, waiting for transfers between devices, swap(): return lax.ppermute(x, axis, [(i, i ^ mask) for i in range(count)])  62 us
    ppermute x39, starting transfers between devices, swap(): return lax.ppermute(x, axis, [(i, i ^ mask) for i in range(count)])  43.1 us
    unnamed x48, local copies, waits for them, and re-layouts  11.9 us
  transfers between devices with their start and end apart: 44, of which 21 were waited for; matrix products, arithmetic and copies ran while one was open for 0% of the time, Pallas kernels for 37%

profile of v4, /device:TPU:0, one launch (start us, length us, event | category | flops | bytes accessed | tf_op | source)
XLA Modules:
  0.0 215.6 jit_solution(6418263211863095075)
XLA Ops:
  1.2 2.6 %collective-permute-start = (bf16[256,1024]{1,0:T(8,128)(2,1)}, bf16[256,1024]{1,0:T(8,128)(2,1)S(1)}, u32[]{:S(2)}, u32[]{:S(2)}) collective-permute-start(bf16[256,1024]{1,0:T(8,128)(2,1)} %refs_0_.11), channel_id=1, source_target_pairs={{0,2},{1,3},{2,0},{3,1},{4,6},{5,7},{6,4},{7,5},{8,10},{9,11},{10,... | collective-permute-start | bytes 1572872 | tf_op jit(solution)/shard_map/ppermute | solution.py:727
  5.6 1.6 copy-done
  10.0 3.2 %project.3 = (bf16[1024,1024]{1,0:T(8,128)(2,1)S(1)}, bf16[1024,512]{1,0:T(8,128)(2,1)S(1)}, bf16[1024,768]{1,0:T(8,128)(2,1)S(1)}, bf16[1024,128]{1,0:T(8,128)(2,1)S(1)}) custom-call(s32[11]{0:T(128)S(1)} %pad_add_fusion.refs_0_, bf16[256,1024]{1,0:T(8,128)(2,1)S(1)} %copy-done.5, bf16[256,1024]{1,0:T(8,128)(2,1)S(1)} %collective-permute-done.1.refs_2_, ...), custom_call_target="tpu_custom_call" | custom-call | tf_op jit(solution)/shard_map/project/pallas_call | solution.py:83
  18.2 1.8 project.4
  20.1 2.0 project.5
  22.2 4.5 %collective-permute-start.8 = (bf16[256,1024]{1,0:T(8,128)(2,1)S(1)}, bf16[256,1024]{1,0:T(8,128)(2,1)S(1)}, u32[]{:S(2)}, u32[]{:S(2)}) collective-permute-start(bf16[256,1024]{1,0:T(8,128)(2,1)S(1)} %hold.4.refs_7_), channel_id=1, source_target_pairs={{0,2},{1,3},{2,0},{3,1},{4,6},{5,7},{6,4},{7,5},{8,10},{9,11},{10,... | collective-permute-start | bytes 1572872 | tf_op jit(solution)/shard_map/ppermute | solution.py:727
  26.7 7.2 %states.1 = (f32[1024,768]{1,0:T(8,128)S(1)}, bf16[8,512,128]{2,1,0:T(8,128)(2,1)S(1)}, f32[512,128]{1,0:T(8,128)S(1)}, bf16[528,128]{1,0:T(8,128)(2,1)S(1)}, f3...) custom-call(s32[11]{0:T(128)S(1)} %pad_add_fusion.refs_0_, ...), custom_call_target="tpu_custom_call" | custom-call | tf_op jit(solution)/shard_map/states/pallas_call | solution.py:83
  33.8 1.6 collective-permute-start.9
  35.4 4.5 %within.1.refs_0_.refs_4_ = f32[1024,512]{1,0:T(8,128)S(1)} custom-call(s32[11]{0:T(128)S(1)} %pad_add_fusion.refs_0_, f32[1024,768]{1,0:T(8,128)S(1)} %get-tuple-element.141.refs_1_.refs_3_, bf16[1024,128]{1,0:T(8,128)(2,1)S(1)} %get-tuple-element.137.refs_2_.refs_4_, f32[1024,128]{1,0:T(8,128)S(1)} %get-tuple-element.142.refs_3_.refs_2_.refs_5_, ...), custom_call_target="tpu_custom_call" | custom-call | tf_op jit(solution)/shard_map/within/pallas_call | solution.py:83
  40.7 1.6 collective-permute-start.11
  42.5 3.3 %collective-permute-done.11.refs_5_ = bf16[528,128]{1,0:T(8,128)(2,1)S(1)} collective-permute-done((bf16[528,128]{1,0:T(8,128)(2,1)S(1)}, bf16[528,128]{1,0:T(8,128)(2,1)S(1)}, u32[]{:S(2)}, u32[]{:S(2)}) %collective-permute-start.11) | collective-permute-done | bytes 135200 | tf_op jit(solution)/shard_map/ppermute | solution.py:727
  47.2 2.6 %collective-permute-start.12 = (bf16[528,128]{1,0:T(8,128)(2,1)S(1)}, bf16[528,128]{1,0:T(8,128)(2,1)S(1)}, u32[]{:S(2)}, u32[]{:S(2)}) collective-permute-start(bf16[528,128]{1,0:T(8,128)(2,1)S(1)} %get-tuple-element.158), channel_id=1, source_target_pairs={{0,16},{4,20},{8,24},{12,28},{16,0},{20,4},{24,8},{28,12},{1,17},{... | collective-permute-start | bytes 405512 | tf_op jit(solution)/shard_map/ppermute | solution.py:727
  51.0 2.0 cotangent.1
  53.0 1.8 collective-permute-done.12.refs_9_
  54.8 5.3 %gated.1 = (f32[1024,512]{1,0:T(8,128)S(1)}, f32[8,8,128]{2,1,0:T(8,128)S(1)}, bf16[512,128]{1,0:T(8,128)(2,1)S(1)}) custom-call(s32[11]{0:T(128)S(1)} %pad_add_fusion.refs_0_, f32[1024,768]{1,0:T(8,128)S(1)} %get-tuple-element.141.refs_1_.refs_3_, f32[1024,128]{1,0:T(8,128)S(1)} %get-tuple-element.142.refs_3_.refs_2_.refs_5_, ...), custom_call_target="tpu_custom_call" | custom-call | tf_op jit(solution)/shard_map/gated/pallas_call | solution.py:83
  61.0 3.1 %collective-permute-done.13.refs_1_ = f32[8,8,128]{2,1,0:T(8,128)S(1)} collective-permute-done((f32[8,8,128]{2,1,0:T(8,128)S(1)}, f32[8,8,128]{2,1,0:T(8,128)S(1)}, u32[]{:S(2)}, u32[]{:S(2)}) %collective-permute-start.13) | collective-permute-done | bytes 32800 | tf_op jit(solution)/shard_map/ppermute | solution.py:727
  65.3 5.7 %back_gated.1 = (bf16[1024,512]{1,0:T(8,128)(2,1)S(1)}, bf16[1024,512]{1,0:T(8,128)(2,1)S(1)}, bf16[1024,512]{1,0:T(8,128)(2,1)S(1)}, bf16[8,512,128]{2,1,0:T(8,...) custom-call(s32[11]{0:T(128)S(1)} %pad_add_fusion.refs_0_, ...), custom_call_target="tpu_custom_call" | custom-call | tf_op jit(solution)/shard_map/back_gated/pallas_call | solution.py:83
  71.6 4.4 %out_wgrad.1 = (bf16[1024,512]{1,0:T(8,128)(2,1)S(1)}, bf16[1024,512]{1,0:T(8,128)(2,1)S(1)}) custom-call(s32[11]{0:T(128)S(1)} %pad_add_fusion.refs_0_, bf16[1024,512]{1,0:T(8,128)(2,1)S(1)} %get-tuple-element.161.refs_1_.refs_0_, bf16[1024,1024]{1,0:T(8,128)(2,1)S(1)} %get-tuple-element.165.refs_2_, ...), custom_call_target="tpu_custom_call" | custom-call | tf_op jit(solution)/shard_map/out_wgrad/pallas_call | solution.py:83
  76.0 1.6 collective-permute-start.20
  77.5 6.2 %back_within.2 = (f32[1024,512]{1,0:T(8,128)S(1)}, f32[1024,256]{1,0:T(8,128)S(1)}, f32[1024,128]{1,0:T(8,128)S(1)}, f32[1024,128]{1,0:T(8,128)S(1)}) custom-call(s32[11]{0:T(128)S(1)} %pad_add_fusion.refs_0_, f32[1024,768]{1,0:T(8,128)S(1)} %get-tuple-element.141.refs_1_.refs_3_, bf16[1024,128]{1,0:T(8,128)(2,1)S(1)} %get-tuple-element.137.refs_2_.refs_4_, ...), custom_call_target="tpu_custom_call" | custom-call | tf_op jit(solution)/shard_map/back_within/pallas_call | solution.py:83
  84.6 6.2 %back_within.3 = (f32[1024,512]{1,0:T(8,128)S(1)}, f32[1024,256]{1,0:T(8,128)S(1)}, f32[1024,128]{1,0:T(8,128)S(1)}, f32[1024,128]{1,0:T(8,128)S(1)}) custom-call(s32[11]{0:T(128)S(1)} %pad_add_fusion.refs_0_, f32[1024,768]{1,0:T(8,128)S(1)} %get-tuple-element.141.refs_1_.refs_3_, ...), custom_call_target="tpu_custom_call", output_to_operand_aliasing={{0}: (12, {}), {1}: (13, {}), {2}: (14, {}), {3}: (15, {})} | custom-call | tf_op jit(solution)/shard_map/back_within/pallas_call | solution.py:83
  90.8 1.9 outproj.1
  94.7 3.1 %collective-permute-start.22 = (bf16[528,128]{1,0:T(8,128)(2,1)S(1)}, bf16[528,128]{1,0:T(8,128)(2,1)S(1)}, u32[]{:S(2)}, u32[]{:S(2)}) collective-permute-start(bf16[528,128]{1,0:T(8,128)(2,1)S(1)} %get-tuple-element.196), channel_id=1, source_target_pairs={{0,16},{4,20},{8,24},{12,28},{16,0},{20,4},{24,8},{28,12},{1,17},{... | collective-permute-start | bytes 405512 | tf_op jit(solution)/shard_map/ppermute | solution.py:727
  98.5 2.5 %collective-permute-done.20.refs_2_ = bf16[1024,512]{1,0:T(8,128)(2,1)S(1)} collective-permute-done((bf16[1024,512]{1,0:T(8,128)(2,1)S(1)}, bf16[1024,512]{1,0:T(8,128)(2,1)S(1)}, u32[]{:S(2)}, u32[]{:S(2)}) %collective-permute-start.20) | collective-permute-done | bytes 1048608 | tf_op jit(solution)/shard_map/ppermute | solution.py:727
  102.5 2.1 collective-permute-done.22.refs_16_
  104.6 10.2 %back_conv.1 = (bf16[1024,768]{1,0:T(8,128)(2,1)S(1)}, bf16[1024,128]{1,0:T(8,128)(2,1)S(1)}, f32[8,768]{1,0:T(8,128)S(1)}, bf16[16,768]{1,0:T(8,128)(2,1)S(1)},...) custom-call(s32[11]{0:T(128)S(1)} %pad_add_fusion.refs_0_, bf16[1024,768]{1,0:T(8,128)(2,1)S(1)} %copy-done.4, ...), custom_call_target="tpu_custom_call" | custom-call | tf_op jit(solution)/shard_map/back_conv/pallas_call | solution.py:83
  116.1 2.7 %inner_wgrad.1 = (bf16[512,512]{1,0:T(8,128)(2,1)S(1)}, bf16[512,512]{1,0:T(8,128)(2,1)S(1)}) custom-call(s32[11]{0:T(128)S(1)} %pad_add_fusion.refs_0_, bf16[1024,1024]{1,0:T(8,128)(2,1)S(1)} %get-tuple-element.166.refs_3_.refs_1_, bf16[1024,768]{1,0:T(8,128)(2,1)S(1)} %get-tuple-element.197.refs_2_.refs_1_, ...), custom_call_target="tpu_custom_call" | custom-call | tf_op jit(solution)/shard_map/inner_wgrad/pallas_call | solution.py:83
  118.8 2.7 %collective-permute-start.25 = (bf16[512,512]{1,0:T(8,128)(2,1)S(1)}, bf16[512,512]{1,0:T(8,128)(2,1)S(1)}, u32[]{:S(2)}, u32[]{:S(2)}) collective-permute-start(bf16[512,512]{1,0:T(8,128)(2,1)S(1)} %get-tuple-element.202.refs_6_), channel_id=1, source_target_pairs={{0,4},{4,0},{8,12},{12,8},{16,20},{20,16},{24,28},{28,24},{1,5},{5... | collective-permute-start | bytes 1572872 | tf_op jit(solution)/shard_map/ppermute | solution.py:727
  121.5 1.7 bc_wgrad.1
  129.1 4.7 %dgrad.1 = (bf16[256,1024]{1,0:T(8,128)(2,1)S(1)}, bf16[256,1024]{1,0:T(8,128)(2,1)S(1)}, bf16[256,1024]{1,0:T(8,128)(2,1)S(1)}, bf16[256,1024]{1,0:T(8,128)(2,1)S(1)}) custom-call(bf16[1024,512]{1,0:T(8,128)(2,1)S(1)} %get-tuple-element.167.refs_4_.refs_0_, bf16[1024,768]{1,0:T(8,128)(2,1)S(1)} %patch.1.refs_1_, ...), custom_call_target="tpu_custom_call" | custom-call | tf_op jit(solution)/shard_map/dgrad/pallas_call | solution.py:83
  134.4 2.1 collective-permute-done.26.refs_1_
  140.5 9.8 %collective-permute-done.28.refs_2_ = bf16[256,512]{1,0:T(8,128)(2,1)S(1)} collective-permute-done((bf16[256,512]{1,0:T(8,128)(2,1)S(1)}, bf16[256,512]{1,0:T(8,128)(2,1)S(1)}, u32[]{:S(2)}, u32[]{:S(2)}) %collective-permute-start.28) | collective-permute-done | bytes 262176 | tf_op jit(solution)/shard_map/ppermute | solution.py:727
  152.0 1.6 tokens.1
  157.5 1.8 collective-permute-start.31
  160.4 1.6 collective-permute-start.37
  162.7 1.6 collective-permute-start.34
  164.3 4.2 %collective-permute-done.34.refs_1_ = bf16[384,256]{1,0:T(8,128)(2,1)S(1)} collective-permute-done((bf16[384,256]{1,0:T(8,128)(2,1)S(1)}, bf16[384,256]{1,0:T(8,128)(2,1)S(1)}, u32[]{:S(2)}, u32[]{:S(2)}) %collective-permute-start.34) | collective-permute-done | bytes 196640 | tf_op jit(solution)/shard_map/ppermute | solution.py:727
  168.5 2.5 %collective-permute-start.35 = (bf16[384,256]{1,0:T(8,128)(2,1)S(1)}, bf16[384,256]{1,0:T(8,128)(2,1)S(1)}, u32[]{:S(2)}, u32[]{:S(2)}) collective-permute-start(bf16[384,256]{1,0:T(8,128)(2,1)S(1)} %misc_add.2.refs_0_), channel_id=1, source_target_pairs={{0,8},{4,12},{8,0},{12,4},{16,24},{20,28},{24,16},{28,20},{1,9},{5... | collective-permute-start | bytes 589832 | tf_op jit(solution)/shard_map/ppermute | solution.py:727
  171.0 6.6 %collective-permute-done.37.refs_2_ = bf16[512,512]{1,0:T(8,128)(2,1)S(1)} collective-permute-done((bf16[512,512]{1,0:T(8,128)(2,1)S(1)}, bf16[512,512]{1,0:T(8,128)(2,1)S(1)}, u32[]{:S(2)}, u32[]{:S(2)}) %collective-permute-start.37) | collective-permute-done | bytes 524320 | tf_op jit(solution)/shard_map/ppermute | solution.py:727
  179.9 1.9 collective-permute-done.35.refs_1_
  181.9 1.9 collective-permute-start.38
  183.8 6.0 %collective-permute-done.39.refs_2_ = bf16[256,512]{1,0:T(8,128)(2,1)S(1)} collective-permute-done((bf16[256,512]{1,0:T(8,128)(2,1)S(1)}, bf16[256,512]{1,0:T(8,128)(2,1)S(1)}, u32[]{:S(2)}, u32[]{:S(2)}) %collective-permute-start.39) | collective-permute-done | bytes 262176 | tf_op jit(solution)/shard_map/ppermute | solution.py:727
  194.1 4.4 %collective-permute-done.42.refs_2_ = bf16[256,256]{1,0:T(8,128)(2,1)S(1)} collective-permute-done((bf16[256,256]{1,0:T(8,128)(2,1)S(1)}, bf16[256,256]{1,0:T(8,128)(2,1)S(1)}, u32[]{:S(2)}, u32[]{:S(2)}) %collective-permute-start.42) | collective-permute-done | bytes 131104 | tf_op jit(solution)/shard_map/ppermute | solution.py:727
  200.6 1.6 bc_weights.1.refs_0_
  203.5 1.9 collective-permute-done.41.refs_2_
  205.4 2.8 %out_weights.1 = (f32[512,1024]{1,0:T(8,128)}, f32[2,1024,512]{2,1,0:T(8,128)}) custom-call(s32[11]{0:T(128)S(1)} %pad_add_fusion.refs_0_, bf16[1024,512]{1,0:T(8,128)(2,1)S(1)} %join.6.refs_0_.refs_1_, bf16[1024,512]{1,0:T(8,128)(2,1)S(1)} %collective-permute-done.41.refs_2_, f32[8,128]{1,0:T(8,128)S(1)} %space.74.refs_3_.refs_0_), custom_call_target="tpu_custom_call" | custom-call | tf_op jit(solution)/shard_map/out_weights/pallas_call | solution.py:83
  208.2 5.4 %collective-permute-done.40.refs_2_ = bf16[512,512]{1,0:T(8,128)(2,1)S(1)} collective-permute-done((bf16[512,512]{1,0:T(8,128)(2,1)S(1)}, bf16[512,512]{1,0:T(8,128)(2,1)S(1)}, u32[]{:S(2)}, u32[]{:S(2)}) %collective-permute-start.40) | collective-permute-done | bytes 524320 | tf_op jit(solution)/shard_map/ppermute | solution.py:727
  213.6 2.0 zx_weights.1
  (186 shorter events, 50.2 us)
Async XLA Ops:
  0.6 4.9 %collective-permute-start.1 = (bf16[256,1024]{1,0:T(8,128)(2,1)}, bf16[256,1024]{1,0:T(8,128)(2,1)S(1)}, u32[]{:S(2)}, u32[]{:S(2)}) collective-permute-start(bf16[256,1024]{1,0:T(8,128)(2,1)} %refs_0_.11), channel_id=1, source_target_pairs={{0,1},{1,0},{2,3},{3,2},{4,5},{5,4},{6,7},{7,6},{8,9},{9,8},{10,11... | collective-permute-start | bytes 1572872 | tf_op jit(solution)/shard_map/ppermute | solution.py:727
  1.2 15.3 %collective-permute-start = (bf16[256,1024]{1,0:T(8,128)(2,1)}, bf16[256,1024]{1,0:T(8,128)(2,1)S(1)}, u32[]{:S(2)}, u32[]{:S(2)}) collective-permute-start(bf16[256,1024]{1,0:T(8,128)(2,1)} %refs_0_.11), channel_id=1, source_target_pairs={{0,2},{1,3},{2,0},{3,1},{4,6},{5,7},{6,4},{7,5},{8,10},{9,11},{10,... | collective-permute-start | bytes 1572872 | tf_op jit(solution)/shard_map/ppermute | solution.py:727
  5.5 14.6 %copy-start.12 = (bf16[128,1024]{1,0:T(8,128)(2,1)}, bf16[128,1024]{1,0:T(8,128)(2,1)S(1)}, u32[]{:S(2)}) copy-start(bf16[128,1024]{1,0:T(8,128)(2,1)S(1)} %get-tuple-element.126.refs_6_.refs_5_.refs_9_) | copy-start | bytes 786436
  13.2 6.8 %collective-permute-start.6 = (bf16[16,1024]{1,0:T(8,128)(2,1)S(1)}, bf16[16,1024]{1,0:T(8,128)(2,1)S(1)}, u32[]{:S(2)}, u32[]{:S(2)}) collective-permute-start(bf16[16,1024]{1,0:T(8,128)(2,1)S(1)} %last_rows.1.refs_0_), channel_id=1, source_target_pairs={{3,7},{7,11},{11,15},{15,19},{19,23},{23,27},{27,31}} | collective-permute-start | bytes 98312 | tf_op jit(solution)/shard_map/ppermute | solution.py:1194
  13.8 6.2 %collective-permute-start.5 = (bf16[16,1024]{1,0:T(8,128)(2,1)S(1)}, bf16[16,1024]{1,0:T(8,128)(2,1)S(1)}, u32[]{:S(2)}, u32[]{:S(2)}) collective-permute-start(bf16[16,1024]{1,0:T(8,128)(2,1)S(1)} %last_rows.1.refs_0_), channel_id=1, source_target_pairs={{3,6},{7,10},{11,14},{15,18},{19,22},{23,26},{27,30}} | collective-permute-start | bytes 98312 | tf_op jit(solution)/shard_map/ppermute | solution.py:1194
  14.5 5.6 %collective-permute-start.4 = (bf16[16,1024]{1,0:T(8,128)(2,1)S(1)}, bf16[16,1024]{1,0:T(8,128)(2,1)S(1)}, u32[]{:S(2)}, u32[]{:S(2)}) collective-permute-start(bf16[16,1024]{1,0:T(8,128)(2,1)S(1)} %last_rows.1.refs_0_), channel_id=1, source_target_pairs={{3,5},{7,9},{11,13},{15,17},{19,21},{23,25},{27,29}} | collective-permute-start | bytes 98312 | tf_op jit(solution)/shard_map/ppermute | solution.py:1194
  15.2 4.9 %collective-permute-start.3 = (bf16[16,1024]{1,0:T(8,128)(2,1)S(1)}, bf16[16,1024]{1,0:T(8,128)(2,1)S(1)}, u32[]{:S(2)}, u32[]{:S(2)}) collective-permute-start(bf16[16,1024]{1,0:T(8,128)(2,1)S(1)} %last_rows.1.refs_0_), channel_id=1, source_target_pairs={{3,4},{7,8},{11,12},{15,16},{19,20},{23,24},{27,28}} | collective-permute-start | bytes 98312 | tf_op jit(solution)/shard_map/ppermute | solution.py:1194
  16.5 3.6 %collective-permute-start.2 = (bf16[256,1024]{1,0:T(8,128)(2,1)S(1)}, bf16[256,1024]{1,0:T(8,128)(2,1)S(1)}, u32[]{:S(2)}, u32[]{:S(2)}) collective-permute-start(bf16[256,1024]{1,0:T(8,128)(2,1)S(1)} %hold.3.refs_1_.refs_0_), channel_id=1, source_target_pairs={{0,1},{1,0},{2,3},{3,2},{4,5},{5,4},{6,7},{7,6},{8,9},{9,8},{10,11... | collective-permute-start | bytes 1572872 | tf_op jit(solution)/shard_map/ppermute | solution.py:727
  20.0 29.9 %collective-permute-start.7 = (bf16[256,1024]{1,0:T(8,128)(2,1)S(1)}, bf16[256,1024]{1,0:T(8,128)(2,1)S(1)}, u32[]{:S(2)}, u32[]{:S(2)}) collective-permute-start(bf16[256,1024]{1,0:T(8,128)(2,1)S(1)} %copy-done.10), channel_id=1, source_target_pairs={{0,1},{1,0},{2,3},{3,2},{4,5},{5,4},{6,7},{7,6},{8,9},{9,8},{10,11... | collective-permute-start | bytes 1572872 | tf_op jit(solution)/shard_map/ppermute | solution.py:727
  22.1 17.8 %copy-start.3 = (bf16[1024,768]{1,0:T(8,128)(2,1)}, bf16[1024,768]{1,0:T(8,128)(2,1)S(1)}, u32[]{:S(2)}) copy-start(bf16[1024,768]{1,0:T(8,128)(2,1)S(1)} %get-tuple-element.136.refs_1_) | copy-start | bytes 4718596
  22.1 17.8 %copy-start.17 = (bf16[16,768]{1,0:T(8,128)(2,1)}, bf16[16,768]{1,0:T(8,128)(2,1)S(1)}, u32[]{:S(2)}) copy-start(bf16[16,768]{1,0:T(8,128)(2,1)S(1)} %get-tuple-element.138.refs_1_.refs_3_.refs_2_) | copy-start | bytes 73732
  22.2 20.2 %collective-permute-start.8 = (bf16[256,1024]{1,0:T(8,128)(2,1)S(1)}, bf16[256,1024]{1,0:T(8,128)(2,1)S(1)}, u32[]{:S(2)}, u32[]{:S(2)}) collective-permute-start(bf16[256,1024]{1,0:T(8,128)(2,1)S(1)} %hold.4.refs_7_), channel_id=1, source_target_pairs={{0,2},{1,3},{2,0},{3,1},{4,6},{5,7},{6,4},{7,5},{8,10},{9,11},{10,... | collective-permute-start | bytes 1572872 | tf_op jit(solution)/shard_map/ppermute | solution.py:727
  33.8 6.1 %collective-permute-start.9 = (bf16[528,128]{1,0:T(8,128)(2,1)S(1)}, bf16[528,128]{1,0:T(8,128)(2,1)S(1)}, u32[]{:S(2)}, u32[]{:S(2)}) collective-permute-start(bf16[528,128]{1,0:T(8,128)(2,1)S(1)} %get-tuple-element.148), channel_id=1, source_target_pairs={{0,4},{4,0},{8,12},{12,8},{16,20},{20,16},{24,28},{28,24},{1,5},{5... | collective-permute-start | bytes 405512 | tf_op jit(solution)/shard_map/ppermute | solution.py:727
  40.7 5.1 %collective-permute-start.11 = (bf16[528,128]{1,0:T(8,128)(2,1)S(1)}, bf16[528,128]{1,0:T(8,128)(2,1)S(1)}, u32[]{:S(2)}, u32[]{:S(2)}) collective-permute-start(bf16[528,128]{1,0:T(8,128)(2,1)S(1)} %get-tuple-element.153), channel_id=1, source_target_pairs={{0,8},{4,12},{8,0},{12,4},{16,24},{20,28},{24,16},{28,20},{1,9},{5... | collective-permute-start | bytes 405512 | tf_op jit(solution)/shard_map/ppermute | solution.py:727
  42.4 7.4 %collective-permute-start.10 = (bf16[256,1024]{1,0:T(8,128)(2,1)S(1)}, bf16[256,1024]{1,0:T(8,128)(2,1)S(1)}, u32[]{:S(2)}, u32[]{:S(2)}) collective-permute-start(bf16[256,1024]{1,0:T(8,128)(2,1)S(1)} %hold.5.refs_0_), channel_id=1, source_target_pairs={{0,1},{1,0},{2,3},{3,2},{4,5},{5,4},{6,7},{7,6},{8,9},{9,8},{10,11... | collective-permute-start | bytes 1572872 | tf_op jit(solution)/shard_map/ppermute | solution.py:727
  47.2 7.6 %collective-permute-start.12 = (bf16[528,128]{1,0:T(8,128)(2,1)S(1)}, bf16[528,128]{1,0:T(8,128)(2,1)S(1)}, u32[]{:S(2)}, u32[]{:S(2)}) collective-permute-start(bf16[528,128]{1,0:T(8,128)(2,1)S(1)} %get-tuple-element.158), channel_id=1, source_target_pairs={{0,16},{4,20},{8,24},{12,28},{16,0},{20,4},{24,8},{28,12},{1,17},{... | collective-permute-start | bytes 405512 | tf_op jit(solution)/shard_map/ppermute | solution.py:727
  60.2 3.9 %collective-permute-start.13 = (f32[8,8,128]{2,1,0:T(8,128)S(1)}, f32[8,8,128]{2,1,0:T(8,128)S(1)}, u32[]{:S(2)}, u32[]{:S(2)}) collective-permute-start(f32[8,8,128]{2,1,0:T(8,128)S(1)} %get-tuple-element.160.refs_0_), channel_id=1, source_target_pairs={{0,2},{1,3},{2,0},{3,1},{4,6},{5,7},{6,4},{7,5},{8,10},{9,11},{10,... | collective-permute-start | bytes 98312 | tf_op jit(solution)/shard_map/ppermute | solution.py:727
  64.1 1.2 collective-permute-start.14
  71.0 5.0 %copy-start.21 = (f32[8,512]{1,0:T(8,128)}, f32[8,512]{1,0:T(8,128)S(1)}, u32[]{:S(2)}) copy-start(f32[8,512]{1,0:T(8,128)S(1)} %get-tuple-element.168.refs_5_) | copy-start | bytes 49156
  71.0 12.8 %collective-permute-start.15 = (bf16[528,128]{1,0:T(8,128)(2,1)S(1)}, bf16[528,128]{1,0:T(8,128)(2,1)S(1)}, u32[]{:S(2)}, u32[]{:S(2)}) collective-permute-start(bf16[528,128]{1,0:T(8,128)(2,1)S(1)} %get-tuple-element.175), channel_id=1, source_target_pairs={{0,4},{4,0},{8,12},{12,8},{16,20},{20,16},{24,28},{28,24},{1,5},{5... | collective-permute-start | bytes 405512 | tf_op jit(solution)/shard_map/ppermute | solution.py:727
  76.0 25.0 %collective-permute-start.20 = (bf16[1024,512]{1,0:T(8,128)(2,1)S(1)}, bf16[1024,512]{1,0:T(8,128)(2,1)S(1)}, u32[]{:S(2)}, u32[]{:S(2)}) collective-permute-start(bf16[1024,512]{1,0:T(8,128)(2,1)S(1)} %get-tuple-element.169.refs_12_), channel_id=1, source_target_pairs={{0,4},{4,0},{8,12},{12,8},{16,20},{20,16},{24,28},{28,24},{1,5},{5... | collective-permute-start | bytes 3145736 | tf_op jit(solution)/shard_map/ppermute | solution.py:727
  84.5 8.8 %collective-permute-start.18 = (bf16[528,128]{1,0:T(8,128)(2,1)S(1)}, bf16[528,128]{1,0:T(8,128)(2,1)S(1)}, u32[]{:S(2)}, u32[]{:S(2)}) collective-permute-start(bf16[528,128]{1,0:T(8,128)(2,1)S(1)} %get-tuple-element.185), channel_id=1, source_target_pairs={{0,8},{4,12},{8,0},{12,4},{16,24},{20,28},{24,16},{28,20},{1,9},{5... | collective-permute-start | bytes 405512 | tf_op jit(solution)/shard_map/ppermute | solution.py:727
  92.7 5.1 %collective-permute-start.17 = (bf16[256,1024]{1,0:T(8,128)(2,1)S(1)}, bf16[256,1024]{1,0:T(8,128)(2,1)S(1)}, u32[]{:S(2)}, u32[]{:S(2)}) collective-permute-start(bf16[256,1024]{1,0:T(8,128)(2,1)S(1)} %get-tuple-element.181.refs_0_), channel_id=1, source_target_pairs={{0,1},{1,0},{2,3},{3,2},{4,5},{5,4},{6,7},{7,6},{8,9},{9,8},{10,11... | collective-permute-start | bytes 1572872 | tf_op jit(solution)/shard_map/ppermute | solution.py:727
  92.8 5.5 %collective-permute-start.16 = (bf16[256,1024]{1,0:T(8,128)(2,1)S(1)}, bf16[256,1024]{1,0:T(8,128)(2,1)S(1)}, u32[]{:S(2)}, u32[]{:S(2)}) collective-permute-start(bf16[256,1024]{1,0:T(8,128)(2,1)S(1)} %get-tuple-element.179), channel_id=1, source_target_pairs={{0,1},{1,0},{2,3},{3,2},{4,5},{5,4},{6,7},{7,6},{8,9},{9,8},{10,11... | collective-permute-start | bytes 1572872 | tf_op jit(solution)/shard_map/ppermute | solution.py:727
  94.7 9.9 %collective-permute-start.22 = (bf16[528,128]{1,0:T(8,128)(2,1)S(1)}, bf16[528,128]{1,0:T(8,128)(2,1)S(1)}, u32[]{:S(2)}, u32[]{:S(2)}) collective-permute-start(bf16[528,128]{1,0:T(8,128)(2,1)S(1)} %get-tuple-element.196), channel_id=1, source_target_pairs={{0,16},{4,20},{8,24},{12,28},{16,0},{20,4},{24,8},{28,12},{1,17},{... | collective-permute-start | bytes 405512 | tf_op jit(solution)/shard_map/ppermute | solution.py:727
  97.9 27.4 %collective-permute-start.19 = (bf16[256,1024]{1,0:T(8,128)(2,1)S(1)}, bf16[256,1024]{1,0:T(8,128)(2,1)S(1)}, u32[]{:S(2)}, u32[]{:S(2)}) collective-permute-start(bf16[256,1024]{1,0:T(8,128)(2,1)S(1)} %add.26.refs_0_), channel_id=1, source_target_pairs={{0,2},{1,3},{2,0},{3,1},{4,6},{5,7},{6,4},{7,5},{8,10},{9,11},{10,... | collective-permute-start | bytes 1572872 | tf_op jit(solution)/shard_map/ppermute | solution.py:727
  101.8 21.4 %collective-permute-start.21 = (bf16[512,512]{1,0:T(8,128)(2,1)S(1)}, bf16[512,512]{1,0:T(8,128)(2,1)S(1)}, u32[]{:S(2)}, u32[]{:S(2)}) collective-permute-start(bf16[512,512]{1,0:T(8,128)(2,1)S(1)} %get-tuple-element.189.refs_0_), channel_id=1, source_target_pairs={{0,8},{4,12},{8,0},{12,4},{16,24},{20,28},{24,16},{28,20},{1,9},{5... | collective-permute-start | bytes 1572872 | tf_op jit(solution)/shard_map/ppermute | solution.py:727
  114.8 12.6 %collective-permute-start.23 = (f32[8,768]{1,0:T(8,128)S(1)}, f32[8,768]{1,0:T(8,128)S(1)}, u32[]{:S(2)}, u32[]{:S(2)}) collective-permute-start(f32[8,768]{1,0:T(8,128)S(1)} %get-tuple-element.205), channel_id=1, source_target_pairs={{4,0},{8,4},{12,8},{16,12},{20,16},{24,20},{28,24},{5,1},{9,5},{13... | collective-permute-start | bytes 73736 | tf_op jit(solution)/shard_map/ppermute | solution.py:1399
  118.8 18.2 %collective-permute-start.25 = (bf16[512,512]{1,0:T(8,128)(2,1)S(1)}, bf16[512,512]{1,0:T(8,128)(2,1)S(1)}, u32[]{:S(2)}, u32[]{:S(2)}) collective-permute-start(bf16[512,512]{1,0:T(8,128)(2,1)S(1)} %get-tuple-element.202.refs_6_), channel_id=1, source_target_pairs={{0,4},{4,0},{8,12},{12,8},{16,20},{20,16},{24,28},{28,24},{1,5},{5... | collective-permute-start | bytes 1572872 | tf_op jit(solution)/shard_map/ppermute | solution.py:727
  123.9 15.3 %collective-permute-start.29 = (bf16[256,512]{1,0:T(8,128)(2,1)S(1)}, bf16[256,512]{1,0:T(8,128)(2,1)S(1)}, u32[]{:S(2)}, u32[]{:S(2)}) collective-permute-start(bf16[256,512]{1,0:T(8,128)(2,1)S(1)} %get-tuple-element.204.refs_0_), channel_id=1, source_target_pairs={{0,16},{4,20},{8,24},{12,28},{16,0},{20,4},{24,8},{28,12},{1,17},{... | collective-permute-start | bytes 786440 | tf_op jit(solution)/shard_map/ppermute | solution.py:727
  133.8 5.3 %collective-permute-start.24 = (bf16[256,1024]{1,0:T(8,128)(2,1)S(1)}, bf16[256,1024]{1,0:T(8,128)(2,1)S(1)}, u32[]{:S(2)}, u32[]{:S(2)}) collective-permute-start(bf16[256,1024]{1,0:T(8,128)(2,1)S(1)} %get-tuple-element.207), channel_id=1, source_target_pairs={{0,1},{1,0},{2,3},{3,2},{4,5},{5,4},{6,7},{7,6},{8,9},{9,8},{10,11... | collective-permute-start | bytes 1572872 | tf_op jit(solution)/shard_map/ppermute | solution.py:727
  133.9 2.6 %collective-permute-start.26 = (bf16[256,1024]{1,0:T(8,128)(2,1)S(1)}, bf16[256,1024]{1,0:T(8,128)(2,1)S(1)}, u32[]{:S(2)}, u32[]{:S(2)}) collective-permute-start(bf16[256,1024]{1,0:T(8,128)(2,1)S(1)} %get-tuple-element.210.refs_0_), channel_id=1, source_target_pairs={{0,1},{1,0},{2,3},{3,2},{4,5},{5,4},{6,7},{7,6},{8,9},{9,8},{10,11... | collective-permute-start | bytes 1572872 | tf_op jit(solution)/shard_map/ppermute | solution.py:727
  136.7 14.7 %collective-permute-start.27 = (bf16[256,1024]{1,0:T(8,128)(2,1)S(1)}, bf16[256,1024]{1,0:T(8,128)(2,1)S(1)}, u32[]{:S(2)}, u32[]{:S(2)}) collective-permute-start(bf16[256,1024]{1,0:T(8,128)(2,1)S(1)} %add.28.refs_0_), channel_id=1, source_target_pairs={{0,2},{1,3},{2,0},{3,1},{4,6},{5,7},{6,4},{7,5},{8,10},{9,11},{10,... | collective-permute-start | bytes 1572872 | tf_op jit(solution)/shard_map/ppermute | solution.py:727
  137.7 12.7 %collective-permute-start.28 = (bf16[256,512]{1,0:T(8,128)(2,1)S(1)}, bf16[256,512]{1,0:T(8,128)(2,1)S(1)}, u32[]{:S(2)}, u32[]{:S(2)}) collective-permute-start(bf16[256,512]{1,0:T(8,128)(2,1)S(1)} %get-tuple-element.211.refs_0_), channel_id=1, source_target_pairs={{0,8},{4,12},{8,0},{12,4},{16,24},{20,28},{24,16},{28,20},{1,9},{5... | collective-permute-start | bytes 786440 | tf_op jit(solution)/shard_map/ppermute | solution.py:727
  139.3 17.6 %collective-permute-start.33 = (bf16[256,512]{1,0:T(8,128)(2,1)S(1)}, bf16[256,512]{1,0:T(8,128)(2,1)S(1)}, u32[]{:S(2)}, u32[]{:S(2)}) collective-permute-start(bf16[256,512]{1,0:T(8,128)(2,1)S(1)} %add.30.refs_0_.refs_1_), channel_id=1, source_target_pairs={{0,16},{4,20},{8,24},{12,28},{16,0},{20,4},{24,8},{28,12},{1,17},{... | collective-permute-start | bytes 786440 | tf_op jit(solution)/shard_map/ppermute | solution.py:727
  151.0 8.3 %collective-permute-start.32 = (bf16[128,512]{1,0:T(8,128)(2,1)S(1)}, bf16[128,512]{1,0:T(8,128)(2,1)S(1)}, u32[]{:S(2)}, u32[]{:S(2)}) collective-permute-start(bf16[128,512]{1,0:T(8,128)(2,1)S(1)} %get-tuple-element.215.refs_0_), channel_id=1, source_target_pairs={{0,16},{4,20},{8,24},{12,28},{16,0},{20,4},{24,8},{28,12},{1,17},{... | collective-permute-start | bytes 393224 | tf_op jit(solution)/shard_map/ppermute | solution.py:727
  153.7 1.6 collective-permute-start.30
  157.5 5.2 %collective-permute-start.31 = (bf16[288,256]{1,0:T(8,128)(2,1)S(1)}, bf16[288,256]{1,0:T(8,128)(2,1)S(1)}, u32[]{:S(2)}, u32[]{:S(2)}) collective-permute-start(bf16[288,256]{1,0:T(8,128)(2,1)S(1)} %get-tuple-element.222), channel_id=1, source_target_pairs={{0,2},{1,3},{2,0},{3,1},{4,6},{5,7},{6,4},{7,5},{8,10},{9,11},{10,... | collective-permute-start | bytes 442376 | tf_op jit(solution)/shard_map/ppermute | solution.py:727
  159.4 18.8 %collective-permute-start.36 = (bf16[128,512]{1,0:T(8,128)(2,1)S(1)}, bf16[128,512]{1,0:T(8,128)(2,1)S(1)}, u32[]{:S(2)}, u32[]{:S(2)}) collective-permute-start(bf16[128,512]{1,0:T(8,128)(2,1)S(1)} %add.31.refs_0_.refs_1_), channel_id=1, source_target_pairs={{0,16},{4,20},{8,24},{12,28},{16,0},{20,4},{24,8},{28,12},{1,17},{... | collective-permute-start | bytes 393224 | tf_op jit(solution)/shard_map/ppermute | solution.py:727
  160.4 17.2 %collective-permute-start.37 = (bf16[512,512]{1,0:T(8,128)(2,1)S(1)}, bf16[512,512]{1,0:T(8,128)(2,1)S(1)}, u32[]{:S(2)}, u32[]{:S(2)}) collective-permute-start(bf16[512,512]{1,0:T(8,128)(2,1)S(1)} %join.5.refs_0_.refs_1_), channel_id=1, source_target_pairs={{0,8},{4,12},{8,0},{12,4},{16,24},{20,28},{24,16},{28,20},{1,9},{5... | collective-permute-start | bytes 1572872 | tf_op jit(solution)/shard_map/ppermute | solution.py:727
  162.7 5.7 %collective-permute-start.34 = (bf16[384,256]{1,0:T(8,128)(2,1)S(1)}, bf16[384,256]{1,0:T(8,128)(2,1)S(1)}, u32[]{:S(2)}, u32[]{:S(2)}) collective-permute-start(bf16[384,256]{1,0:T(8,128)(2,1)S(1)} %misc_pack.1.refs_0_), channel_id=1, source_target_pairs={{0,4},{4,0},{8,12},{12,8},{16,20},{20,16},{24,28},{28,24},{1,5},{5... | collective-permute-start | bytes 589832 | tf_op jit(solution)/shard_map/ppermute | solution.py:727
  168.5 13.3 %collective-permute-start.35 = (bf16[384,256]{1,0:T(8,128)(2,1)S(1)}, bf16[384,256]{1,0:T(8,128)(2,1)S(1)}, u32[]{:S(2)}, u32[]{:S(2)}) collective-permute-start(bf16[384,256]{1,0:T(8,128)(2,1)S(1)} %misc_add.2.refs_0_), channel_id=1, source_target_pairs={{0,8},{4,12},{8,0},{12,4},{16,24},{20,28},{24,16},{28,20},{1,9},{5... | collective-permute-start | bytes 589832 | tf_op jit(solution)/shard_map/ppermute | solution.py:727
  178.8 11.0 %collective-permute-start.39 = (bf16[256,512]{1,0:T(8,128)(2,1)S(1)}, bf16[256,512]{1,0:T(8,128)(2,1)S(1)}, u32[]{:S(2)}, u32[]{:S(2)}) collective-permute-start(bf16[256,512]{1,0:T(8,128)(2,1)S(1)} %join.7.refs_0_.refs_1_), channel_id=1, source_target_pairs={{0,8},{4,12},{8,0},{12,4},{16,24},{20,28},{24,16},{28,20},{1,9},{5... | collective-permute-start | bytes 786440 | tf_op jit(solution)/shard_map/ppermute | solution.py:727
  179.3 26.1 %collective-permute-start.41 = (bf16[1024,512]{1,0:T(8,128)(2,1)S(1)}, bf16[1024,512]{1,0:T(8,128)(2,1)S(1)}, u32[]{:S(2)}, u32[]{:S(2)}) collective-permute-start(bf16[1024,512]{1,0:T(8,128)(2,1)S(1)} %join.6.refs_0_.refs_1_), channel_id=1, source_target_pairs={{0,4},{4,0},{8,12},{12,8},{16,20},{20,16},{24,28},{28,24},{1,5},{5... | collective-permute-start | bytes 3145736 | tf_op jit(solution)/shard_map/ppermute | solution.py:727
  181.9 10.2 %collective-permute-start.38 = (bf16[384,256]{1,0:T(8,128)(2,1)S(1)}, bf16[384,256]{1,0:T(8,128)(2,1)S(1)}, u32[]{:S(2)}, u32[]{:S(2)}) collective-permute-start(bf16[384,256]{1,0:T(8,128)(2,1)S(1)} %misc_add.3.refs_0_), channel_id=1, source_target_pairs={{0,16},{4,20},{8,24},{12,28},{16,0},{20,4},{24,8},{28,12},{1,17},{... | collective-permute-start | bytes 589832 | tf_op jit(solution)/shard_map/ppermute | solution.py:727
  190.4 23.2 %collective-permute-start.40 = (bf16[512,512]{1,0:T(8,128)(2,1)S(1)}, bf16[512,512]{1,0:T(8,128)(2,1)S(1)}, u32[]{:S(2)}, u32[]{:S(2)}) collective-permute-start(bf16[512,512]{1,0:T(8,128)(2,1)S(1)} %join.8.refs_0_.refs_1_), channel_id=1, source_target_pairs={{0,4},{4,0},{8,12},{12,8},{16,20},{20,16},{24,28},{28,24},{1,5},{5... | collective-permute-start | bytes 1572872 | tf_op jit(solution)/shard_map/ppermute | solution.py:727
  193.5 5.0 %collective-permute-start.42 = (bf16[256,256]{1,0:T(8,128)(2,1)S(1)}, bf16[256,256]{1,0:T(8,128)(2,1)S(1)}, u32[]{:S(2)}, u32[]{:S(2)}) collective-permute-start(bf16[256,256]{1,0:T(8,128)(2,1)S(1)} %get-tuple-element.227.refs_1_), channel_id=1, source_target_pairs={{0,2},{1,3},{2,0},{3,1},{4,6},{5,7},{6,4},{7,5},{8,10},{9,11},{10,... | collective-permute-start | bytes 393224 | tf_op jit(solution)/shard_map/ppermute | solution.py:727
  199.0 1.6 collective-permute-start.43
  (20 other events, 31.1 us)

commit v5 on v4

--- a/solution.py
+++ b/solution.py
@@ -1,4 +1,5 @@
 import functools
+from typing import Any, NamedTuple
 
 import jax
 import jax.numpy as jnp
@@ -310,23 +311,28 @@
 
 
 def states_body(
-    meta, cat, step, rim, vecs, hv, mats,
+    at, meta, cat, step, rim, vecs, hv, mats,
     pre_o, sin_o, end_o, load_o, cum_o, pfx_o, thr_o, buf, state, prod,
 ):
-    c = pl.program_id(0)
     width = vecs.shape[1] - 2 * L
     heads = width // HD
-    keep = jnp.where(meta[2 + c] == 0, 1.0, 0.0)
-
-    @pl.when(c == 0)
-    def _():
-        buf[0:8, :] = rim[...].astype(F32)[8:16, :] * keep
-        state[...] = jnp.zeros_like(state)
-        prod[...] = jnp.ones_like(prod)
-
-    @pl.when(c > 0)
-    def _():
-        buf[0:8, :] = buf[L : L + 8, :] * keep
+    keep = jnp.where(meta[2 + at.c] == 0, 1.0, 0.0)
+    before, buf = buf.at[at.other], buf.at[at.sub]
+
+    def follow():
+        buf[0:8, :] = before[L : L + 8, :] * keep
+
+    if at.first is None:
+        follow()
+    else:
+
+        @pl.when(at.first)
+        def _():
+            buf[0:8, :] = rim[...].astype(F32)[8:16, :] * keep
+            state[...] = jnp.zeros_like(state)
+            prod[...] = jnp.ones_like(prod)
+
+        pl.when(jnp.logical_not(at.first))(follow)
 
     buf[8 : 8 + L, :] = cat[...].astype(F32)
     acts = []
@@ -353,14 +359,16 @@
     pfx_o[0] = here
     prod[...] = here * dec
 
-    @pl.when(c == pl.num_programs(0) - 1)
-    def _():
-        end_o[...] = leaving
-        thr_o[...] = here * dec
-        pack(load_o, leaving, here * dec)
-
-
-def within_body(meta, pre, step, cum_r, sin, vecs, hv, mats, y_o):
+    if at.last is not None:
+
+        @pl.when(at.last)
+        def _():
+            end_o[...] = leaving
+            thr_o[...] = here * dec
+            pack(load_o, leaving, here * dec)
+
+
+def within_body(at, meta, pre, step, cum_r, sin, vecs, hv, mats, y_o):
     width = vecs.shape[1] - 2 * L
     heads = width // HD
     acts = act_parts(pre, width)
@@ -387,15 +395,17 @@
 
 
 def gate_body(
-    level, meta, pre, cum, pfx, y, gate, gn, before, through, load, vecs, mats,
+    level, at, meta, pre, cum, pfx, y, gate, gn, before, through, load, vecs, mats,
     mixed_o, sums_o, incoming,
 ):
     width = vecs.shape[1] - 2 * L
     ones = jnp.ones((8, width), BF)
 
-    @pl.when(pl.program_id(0) == 0)
-    def _():
-        incoming[...] = final_link(meta, level, False, before, through, load).astype(BF)
+    if at.first is not None:
+
+        @pl.when(at.first)
+        def _():
+            incoming[...] = final_link(meta, level, False, before, through, load).astype(BF)
 
     reach = dot_l(jnp.exp(cum[...]) * pfx[0][0:1, :], mats[:, :width])
     cv = pre[:, width + L :]
@@ -418,20 +428,20 @@
 
 
 def back_gate_body(
-    count, meta, pre, cum_r, mixed_r, gate, gn, sums, sums2, thr, vecs, mats,
+    at, meta, pre, cum_r, mixed_r, gate, gn, sums, sums2, thr, vecs, mats,
     normout_o, gm_o, ggr_o, gs_o, toward_o, load_o, sfx_o, acc_o, gstate, prod, acc,
 ):
-    i = pl.program_id(0)
-    c = count - 1 - i
     width = vecs.shape[1] - 2 * L
     heads = width // HD
-    keep = jnp.where(meta[2 + c] == 0, 1.0, 0.0)
-
-    @pl.when(i == 0)
-    def _():
-        gstate[...] = jnp.zeros_like(gstate)
-        prod[...] = jnp.ones_like(prod)
-        acc[...] = jnp.zeros_like(acc)
+    keep = jnp.where(meta[2 + at.c] == 0, 1.0, 0.0)
+
+    if at.first is not None:
+
+        @pl.when(at.first)
+        def _():
+            gstate[...] = jnp.zeros_like(gstate)
+            prod[...] = jnp.ones_like(prod)
+            acc[...] = jnp.zeros_like(acc)
 
     both = sums[0] + sums2[0]
     square = jnp.broadcast_to(both[0:1, :], (L, L)).T
@@ -474,16 +484,18 @@
     gstate[...] = entering
     prod[...] = here * dec * keep
 
-    @pl.when(i == count - 1)
-    def _():
-        toward_o[...] = entering
-        pack(load_o, entering, thr[...])
-        row = lax.broadcasted_iota(jnp.int32, (8, width), 0)
-        acc_o[...] = jnp.where(
-            row == 0,
-            jnp.sum(acc[0:8, :], axis=0, keepdims=True),
-            jnp.sum(acc[8:16, :], axis=0, keepdims=True),
-        )
+    if at.last is not None:
+
+        @pl.when(at.last)
+        def _():
+            toward_o[...] = entering
+            pack(load_o, entering, thr[...])
+            row = lax.broadcasted_iota(jnp.int32, (8, width), 0)
+            acc_o[...] = jnp.where(
+                row == 0,
+                jnp.sum(acc[0:8, :], axis=0, keepdims=True),
+                jnp.sum(acc[8:16, :], axis=0, keepdims=True),
+            )
 
 
 def head_product(a, b, spread):
@@ -492,7 +504,7 @@
 
 
 def back_within_body(
-    meta, pre, step, cum_r, sin, pfx, gs, gm_r, incoming, vecs, hv, mats,
+    at, meta, pre, step, cum_r, sin, pfx, gs, gm_r, incoming, vecs, hv, mats,
     ginner_o, gbc_o, glog_o, gst_o,
 ):
     width = vecs.shape[1] - 2 * L
@@ -575,27 +587,31 @@
 
 
 def back_conv_body(
-    count, level, meta, cat, rim, pre, step, cum_r, sin, pfx, sfx, ginner_r, gbc_r, glog_r, gst_r,
+    level, at, meta, cat, rim, pre, step, cum_r, sin, pfx, sfx, ginner_r, gbc_r, glog_r, gst_r,
     incoming, before, through, load, vecs, hv, mats,
     gcat_o, gsr_o, head_o, extra_o, acc_o, hacc_o, buf, acc, hacc, outgoing,
 ):
-    i = pl.program_id(0)
-    c = count - 1 - i
     width = vecs.shape[1] - 2 * L
     heads = width // HD
-    keep_next = jnp.where(meta[3 + c] == 0, 1.0, 0.0)
-    keep = jnp.where(meta[2 + c] == 0, 1.0, 0.0)
-
-    @pl.when(i == 0)
-    def _():
-        buf[L : L + 8, :] = jnp.zeros_like(buf[L : L + 8, :])
-        acc[...] = jnp.zeros_like(acc)
-        hacc[...] = jnp.zeros_like(hacc)
-        outgoing[...] = final_link(meta, level, True, before, through, load)
-
-    @pl.when(i > 0)
-    def _():
-        buf[L : L + 8, :] = buf[0:8, :] * keep_next
+    keep_next = jnp.where(meta[3 + at.c] == 0, 1.0, 0.0)
+    keep = jnp.where(meta[2 + at.c] == 0, 1.0, 0.0)
+    later, buf = buf.at[at.other], buf.at[at.sub]
+
+    def follow():
+        buf[L : L + 8, :] = later[0:8, :] * keep_next
+
+    if at.first is None:
+        follow()
+    else:
+
+        @pl.when(at.first)
+        def _():
+            buf[L : L + 8, :] = jnp.zeros((8, width + 2 * L), F32)
+            acc[...] = jnp.zeros_like(acc)
+            hacc[...] = jnp.zeros_like(hacc)
+            outgoing[...] = final_link(meta, level, True, before, through, load)
+
+        pl.when(jnp.logical_not(at.first))(follow)
 
     step_in = step[...].astype(F32) + hv[0:1, :]
     steps = softplus(step_in)
@@ -643,28 +659,30 @@
             out = out + vecs[3 - j : 4 - j, cols] * moved
             acc[24 - 8 * j : 32 - 8 * j, cols] += eights(moved * here)
         gcat_o[:, cols] = out.astype(BF)
-    @pl.when(i == count - 1)
-    def _():
-        head_o[...] = buf[0:8, :]
-        past = rim[...].astype(F32)[8:16, :] * keep
-        now = buf[0:8, :]
-        extra_o[...] = crossing(vecs, now * keep).astype(BF)
-        row = lax.broadcasted_iota(jnp.int32, now.shape, 0)
-        result = jnp.zeros_like(now)
-        for k in range(5):
-            part = jnp.sum(acc[8 * k : 8 * k + 8, :], axis=0, keepdims=True)
-            j = 3 - k
-            if 1 <= j <= 3:
-                for t in range(j):
-                    part = part + now[t : t + 1, :] * past[8 + t - j : 9 + t - j, :]
-            result = jnp.where(row == k, part, result)
-        acc_o[...] = result
-        hrow = lax.broadcasted_iota(jnp.int32, (8, L), 0)
-        hacc_o[...] = jnp.where(
-            hrow == 0,
-            jnp.sum(hacc[0:8, :], axis=0, keepdims=True),
-            jnp.sum(hacc[8:16, :], axis=0, keepdims=True),
-        )
+    if at.last is not None:
+
+        @pl.when(at.last)
+        def _():
+            head_o[...] = buf[0:8, :]
+            past = rim[...].astype(F32)[8:16, :] * keep
+            now = buf[0:8, :]
+            extra_o[...] = crossing(vecs, now * keep).astype(BF)
+            row = lax.broadcasted_iota(jnp.int32, now.shape, 0)
+            result = jnp.zeros_like(now)
+            for k in range(5):
+                part = jnp.sum(acc[8 * k : 8 * k + 8, :], axis=0, keepdims=True)
+                j = 3 - k
+                if 1 <= j <= 3:
+                    for t in range(j):
+                        part = part + now[t : t + 1, :] * past[8 + t - j : 9 + t - j, :]
+                result = jnp.where(row == k, part, result)
+            acc_o[...] = result
+            hrow = lax.broadcasted_iota(jnp.int32, (8, L), 0)
+            hacc_o[...] = jnp.where(
+                hrow == 0,
+                jnp.sum(hacc[0:8, :], axis=0, keepdims=True),
+                jnp.sum(hacc[8:16, :], axis=0, keepdims=True),
+            )
 
 
 def dgrad_body(k, ggr, gcat, gsr, wzx, wbc, wst, *outs):
@@ -704,6 +722,13 @@
         vmem=20,
     )
     return list(outs)[::-1]
+
+
+def total_body(*refs):
+    total = refs[0][...].astype(F32)
+    for ref in refs[1:-1]:
+        total = total + ref[...].astype(F32)
+    refs[-1][...] = total.astype(BF)
 
 
 def hold_body(x, o):
@@ -1041,6 +1066,14 @@
     sb_o[...] = rest[at : at + 1, L : L + heads]
 
 
+class Spot(NamedTuple):
+    c: Any
+    sub: int
+    other: int
+    first: Any
+    last: Any
+
+
 class Plan:
     def __init__(self):
         self.now, self.links, self.chains, self.done = 0.0, {}, [], set()
@@ -1122,6 +1155,31 @@
     levels = len(masks)
 
     LAST.clear()
+    def spread_out(held, keys):
+        mask = half // 2
+        while mask:
+            for f in [f for f in held if f in keys]:
+                held[f ^ mask] = swap(held[f], "tensor", mask)
+            mask //= 2
+
+    near, far = range(half), range(half, group)
+    held = {0: tokens_in}
+    arrived = swap(tokens_in, "tensor", half)
+    spread_out(held, near)
+    dps = lax.axis_size("dp")
+    (last_rows,) = launch(
+        lambda tok, _, o: hold_body(tok, o), [tokens_in, held[1]],
+        [pl.BlockSpec((16, d), lambda i: (share // 16 - 1, 0)), pl.BlockSpec(memory_space=pl.ANY)],
+        [shaped((16, d), BF)], [pl.BlockSpec((16, d), lambda i: (0, 0))], "last_rows",
+    )
+    past = [
+        lax.ppermute(
+            last_rows,
+            ("dp", "tensor"),
+            [(i * group + group - 1, (i + 1) * group + t) for i in range(dps - 1)],
+        )
+        for t in range(1, group, 2)
+    ]
     gain = input_gain[None]
     prep_ins = [conv_inner, conv_inner_bias[None], conv_bc, conv_bc_bias, step_bias[None],
                 decay_log[None], skip_weight[None], norm_gain[None], weight_step.T]
@@ -1133,28 +1191,45 @@
         [whole(a) for a in prep_ins],
         prep_outs, [whole(o) for o in prep_outs], "prep", vmem=4,
     )
-    def place_of(c, meta):
-        if per == 1:
-            return lax.bitwise_xor(c, meta[0])
-        return lax.bitwise_xor(lax.div(c, per), meta[0]) * per + lax.rem(c, per)
-
     def stretched(body, name, ins, outs, scratch, reverse, vmem, flops, span=None, old=()):
-        begin, length = span or (0, count)
+        del flops
+        begin, length = span or (0, count // per)
 
         def order(i):
-            return count - 1 - i - begin if reverse else i + begin
+            return count // per - 1 - i - begin if reverse else i + begin
 
         def spec(kind, shape):
             if kind == "rows":
-                return pl.BlockSpec((L, shape[1]), lambda i, m: (place_of(order(i), m), 0))
+                return pl.BlockSpec(
+                    (share, shape[1]), lambda i, m: (lax.bitwise_xor(order(i), m[0]), 0)
+                )
             if kind == "each":
-                return pl.BlockSpec((1, *shape[1:]), lambda i, m: (order(i), 0, 0))
+                return pl.BlockSpec((per, *shape[1:]), lambda i, m: (order(i), 0, 0))
             return pl.BlockSpec(shape, lambda i, m: (0,) * len(shape))
 
+        kinds = [k for k, _ in ins] + [k for k, _, _ in outs]
         n = len(ins)
 
-        def run(*refs):
-            body(*refs[: 1 + n], *refs[1 + n + len(old) :])
+        def run(meta, *refs):
+            refs = refs[:n] + refs[n + len(old) :]
+            step = pl.program_id(0)
+            for sub in range(per):
+                pos = per - 1 - sub if reverse else sub
+
+                def view(kind, ref, pos=pos):
+                    if kind == "rows":
+                        return ref.at[pl.ds(pos * L, L)]
+                    return ref.at[pl.ds(pos, 1)] if kind == "each" else ref
+
+                views = [view(k, r) for k, r in zip(kinds, refs)]
+                at = Spot(
+                    order(step) * per + pos,
+                    sub,
+                    (sub - 1) % per,
+                    step == 0 if sub == 0 else None,
+                    step == length - 1 if sub == per - 1 else None,
+                )
+                body(at, meta, *views, *refs[len(kinds) :])
 
         return launch(
             run,
@@ -1168,38 +1243,14 @@
             scratch=scratch,
             aliases={n + j: j for j in range(len(old))},
             vmem=vmem,
-            flops=0,
         )
 
-    def spread_out(held, keys):
-        mask = half // 2
-        while mask:
-            for f in [f for f in held if f in keys]:
-                held[f ^ mask] = swap(held[f], "tensor", mask)
-            mask //= 2
-
-    near, far = range(half), range(half, group)
-    held = {0: tokens_in}
-    arrived = swap(tokens_in, "tensor", half)
-    spread_out(held, near)
-    dps = lax.axis_size("dp")
     weights = (gain, weight_zx, weight_bc, wst)
     before = project(meta, [held[f] for f in near], [], *weights, tokens, 0, [])
-    (last_rows,) = launch(
-        lambda tok, _, o: hold_body(tok, o), [tokens_in, before[3]],
-        [pl.BlockSpec((16, d), lambda i: (share // 16 - 1, 0)), pl.BlockSpec(memory_space=pl.ANY)],
-        [shaped((16, d), BF)], [pl.BlockSpec((16, d), lambda i: (0, 0))], "last_rows",
-    )
-    past = [
-        lax.ppermute(
-            last_rows,
-            ("dp", "tensor"),
-            [(i * group + group - 1, (i + 1) * group + t) for i in range(dps - 1)],
-        )
-        for t in range(group)
-    ]
     space()
     held[half] = hold(arrived, before[3])
+    (own_past,) = simple(total_body, past, [shaped((16, d), BF)], "past")
+    past = [own_past, swap(own_past, "tensor", 1)]
     spread_out(held, far)
     before = project(meta, [held[half]], [], *weights, tokens, half, list(before))
     space()
@@ -1221,8 +1272,9 @@
         [("rows", (tokens, wide), F32), ("each", (count, *state_shape), BF),
          ("one", state_shape, F32), ("one", load_shape, BF), ("rows", tall, F32),
          ("each", (count, 8, L), F32), ("one", small, F32)],
-        [pltpu.VMEM((L + 8, wide), F32), pltpu.VMEM(state_shape, F32), pltpu.VMEM(small, F32)],
-        False, 10, 2 * tokens * width * L * 3,
+        [pltpu.VMEM((per, L + 8, wide), F32), pltpu.VMEM(state_shape, F32),
+         pltpu.VMEM(small, F32)],
+        False, 14, 2 * tokens * width * L * 3,
     )
 
     def link(level, reverse, held, load):
@@ -1243,7 +1295,7 @@
         [("rows", pre), ("rows", step_raw), ("rows", cum), ("each", sin), ("one", vecs),
          ("one", hv), ("one", mats)],
         [("rows", (tokens, width), F32)],
-        [], False, 10, 2 * tokens * width * L * 6,
+        [], False, 14, 2 * tokens * width * L * 6,
     )
     for level in range(levels - 1):
         space()
@@ -1267,7 +1319,7 @@
          ("rows", gn), ("one", befores), ("one", throughs), ("one", load), ("one", vecs),
          ("one", mats)],
         [("rows", (tokens, width), F32), ("each", (count, 8, L), F32), ("one", state_shape, BF)],
-        [], False, 10, 2 * tokens * width * L * 4,
+        [], False, 14, 2 * tokens * width * L * 4,
     )
     for mask in tmasks[::-1][:-1]:
         got = swap(sums, "tensor", mask)
@@ -1276,7 +1328,7 @@
     sums2 = swap(sums, "tensor", 1)
     space()
     normout, gm, ggr, gs, toward, load, sfx, gate_acc = stretched(
-        functools.partial(back_gate_body, count),
+        back_gate_body,
         "back_gated",
         [("rows", pre), ("rows", cum), ("rows", mixed), ("rows", gate_raw), ("rows", gn),
          ("each", sums), ("each", sums2), ("one", thr), ("one", vecs), ("one", mats)],
@@ -1285,7 +1337,7 @@
          ("one", state_shape, F32), ("one", load_shape, BF), ("each", (count, 8, L), F32),
          ("one", (8, width), F32)],
         [pltpu.VMEM(state_shape, F32), pltpu.VMEM(small, F32), pltpu.VMEM((16, width), F32)],
-        True, 10, 2 * tokens * width * L * 3,
+        True, 14, 2 * tokens * width * L * 3,
     )
 
     plan = Plan()
@@ -1293,7 +1345,7 @@
     blocks = d // width
     axes = {"dp": ["y", "z", "z"] + ["z"] * levels, "tensor": ["core", "x"] + ["x"] * levels}
     spans = {"dp": [1, 1, 2] + [2] * levels, "tensor": [1, 1] + [2] * levels}
-    hops = {"core": 1.0, "x": 4.0, "y": 4.0, "z": 4.5}
+    hops = {"core": 2.5, "x": 5.0, "y": 5.0, "z": 6.0}
     rates = {"core": 600.0, "x": 90.0, "y": 90.0, "z": 90.0}
 
     def moved(x, axis, level):
@@ -1357,12 +1409,12 @@
              ("one", mats)],
             [("rows", (tokens, width), F32), ("rows", (tokens, 2 * L), F32), ("rows", tall, F32),
              ("rows", tall, F32)],
-            [], True, 12, 2 * tokens * width * L * 12, (begin, length), kept.get("within", ()),
+            [], True, 16, 2 * tokens * width * L * 12, (begin, length), kept.get("within", ()),
         )
 
     def within_chain():
-        part = count // 2
-        for begin in range(0, count, part):
+        part = group // 2
+        for begin in range(0, group, part):
             yield (None, "begin", 0.0, 6.0)
             within_part(begin, part)
 
@@ -1397,7 +1449,9 @@
 
     def tokens_chain():
         ahead = lax.ppermute(kept["head"], "dp", [(i + 1, i) for i in range(dps - 1)])
-        yield ("z", 0.5, 5.0, 5.4)
+        yield ("halo", 0.5, 9.0, 5.4)
+        space()
+        space()
         gcat = patched(meta, kept["gcat"], ahead, vecs, share, group)
         grads = rows_times(
             dgrad_body, group, share, d, [ggr, gcat, kept["gsr"]], [weight_zx, weight_bc, wst],
@@ -1473,7 +1527,7 @@
     befores, throughs, load = kept["links"]
     ginner, gbc, glog, gst = kept["within"]
     gcat, gsr, head, extra, conv_acc, head_acc = stretched(
-        functools.partial(back_conv_body, count, levels - 1),
+        functools.partial(back_conv_body, levels - 1),
         "back_conv",
         [("rows", cat), ("one", rim), ("rows", pre), ("rows", step_raw), ("rows", cum),
          ("each", sin), ("each", pfx), ("each", sfx), ("rows", ginner), ("rows", gbc),
@@ -1481,19 +1535,19 @@
          ("one", load), ("one", vecs), ("one", hv), ("one", mats)],
         [("rows", (tokens, wide), BF), ("rows", tall, BF), ("one", (8, wide), F32),
          ("one", (16, wide), BF), ("one", (8, wide), F32), ("one", small, F32)],
-        [pltpu.VMEM((L + 8, wide), F32), pltpu.VMEM((40, wide), F32), pltpu.VMEM((16, L), F32),
+        [pltpu.VMEM((per, L + 8, wide), F32), pltpu.VMEM((40, wide), F32), pltpu.VMEM((16, L), F32),
          pltpu.VMEM(state_shape, F32)],
-        True, 12, 2 * tokens * width * L * 6,
+        True, 16, 2 * tokens * width * L * 6,
     )
     plan.now += 10.0
 
     kept.update(head=head, gcat=gcat, gsr=gsr, extra=extra, conv_acc=conv_acc, head_acc=head_acc)
+    plan.add("tokens", 2, tokens_chain())
     plan.add(
         "I", 1,
         weights_chain("I", [(normed, gcat, 0, normed_rim, extra)], "inner_wgrad", inner_out),
         2.7,
     )
-    plan.add("tokens", 2, tokens_chain())
     plan.add("bc", 3, bc_chain())
     plan.run()
 

time: 216 us -> 204 us (0.944)
  Pallas kernels: 92.3 us -> 86.6 us
  local copies, waits for them, and re-layouts: 12 us -> 7.67 us
  starting transfers between devices: 47 us -> 44.5 us
    pallas_call x92 -> x95, Pallas kernels: 92.3 us -> 86.6 us  [launch(): pl.pallas_call(run, grid_spec=pltpu.PrefetchScalarGridSpec(num_scalar_pre...]
    unnamed x48 -> x52, local copies, waits for them, and re-layouts: 11.9 us -> 7.65 us
    ppermute x39 -> x40, starting transfers between devices: 43.1 us -> 41.9 us  [swap(): return lax.ppermute(x, axis, [(i, i ^ mask) for i in range(count)])]
    ppermute x39 -> x40, waiting for transfers between devices: 62 us -> 62.7 us  [swap(): return lax.ppermute(x, axis, [(i, i ^ mask) for i in range(count)])]
  transfers between devices with their start and end apart: 44 -> 43, of which waited for: 21 -> 18; matrix products, arithmetic and copies ran while one was open for 0% -> 0% of each run, Pallas kernels for 37% -> 37%
where the time goes in v5:
time: 204 us
  Pallas kernels  86.6 us (42%)
  waiting for transfers between devices  62.7 us (31%)
  starting transfers between devices  44.5 us (22%)
  local copies, waits for them, and re-layouts  7.67 us (4%)
    pallas_call x95, Pallas kernels, launch(): pl.pallas_call(run, grid_spec=pltpu.PrefetchScalarGridSpec(num_scalar_pre...  86.6 us
    ppermute x40, waiting for transfers between devices, swap(): return lax.ppermute(x, axis, [(i, i ^ mask) for i in range(count)])  62.7 us
    ppermute x40, starting transfers between devices, swap(): return lax.ppermute(x, axis, [(i, i ^ mask) for i in range(count)])  41.9 us
    unnamed x52, local copies, waits for them, and re-layouts  7.65 us
  transfers between devices with their start and end apart: 43, of which 18 were waited for; matrix products, arithmetic and copies ran while one was open for 0% of the time, Pallas kernels for 37%

profile of v5, /device:TPU:0, one launch (start us, length us, event | category | flops | bytes accessed | tf_op | source)
XLA Modules:
  0.0 203.8 jit_solution(17880708233466487972)
XLA Ops:
  1.2 2.6 %collective-permute-start = (bf16[256,1024]{1,0:T(8,128)(2,1)}, bf16[256,1024]{1,0:T(8,128)(2,1)S(1)}, u32[]{:S(2)}, u32[]{:S(2)}) collective-permute-start(bf16[256,1024]{1,0:T(8,128)(2,1)} %refs_0_.11), channel_id=1, source_target_pairs={{0,2},{1,3},{2,0},{3,1},{4,6},{5,7},{6,4},{7,5},{8,10},{9,11},{10,... | collective-permute-start | bytes 1572872 | tf_op jit(solution)/shard_map/ppermute | solution.py:752
  8.2 1.6 copy-done
  10.1 3.1 %project.3 = (bf16[1024,1024]{1,0:T(8,128)(2,1)S(1)}, bf16[1024,512]{1,0:T(8,128)(2,1)S(1)}, bf16[1024,768]{1,0:T(8,128)(2,1)S(1)}, bf16[1024,128]{1,0:T(8,128)(2,1)S(1)}) custom-call(s32[11]{0:T(128)S(1)} %pad_add_fusion.refs_0_, bf16[256,1024]{1,0:T(8,128)(2,1)S(1)} %copy-done.5, bf16[256,1024]{1,0:T(8,128)(2,1)S(1)} %collective-permute-done.1.refs_1_.refs_2_, ...), custom_call_target="tpu_custom_call" | custom-call | tf_op jit(solution)/shard_map/project/pallas_call | solution.py:84
  13.2 3.5 %collective-permute-done.refs_0_ = bf16[256,1024]{1,0:T(8,128)(2,1)S(1)} collective-permute-done((bf16[256,1024]{1,0:T(8,128)(2,1)}, bf16[256,1024]{1,0:T(8,128)(2,1)S(1)}, u32[]{:S(2)}, u32[]{:S(2)}) %collective-permute-start) | collective-permute-done | bytes 524320 | tf_op jit(solution)/shard_map/ppermute | solution.py:752
  17.4 1.8 project.4
  19.3 2.0 project.5
  21.4 1.6 collective-permute-start.7
  22.9 5.3 %states.1 = (f32[1024,768]{1,0:T(8,128)S(1)}, bf16[8,512,128]{2,1,0:T(8,128)(2,1)S(1)}, f32[512,128]{1,0:T(8,128)S(1)}, bf16[528,128]{1,0:T(8,128)(2,1)S(1)}, f3...) custom-call(s32[11]{0:T(128)S(1)} %pad_add_fusion.refs_0_, ...), custom_call_target="tpu_custom_call" | custom-call | tf_op jit(solution)/shard_map/states/pallas_call | solution.py:84
  28.3 1.6 collective-permute-start.8
  29.9 3.6 %within.1.refs_0_.refs_4_ = f32[1024,512]{1,0:T(8,128)S(1)} custom-call(s32[11]{0:T(128)S(1)} %pad_add_fusion.refs_0_, f32[1024,768]{1,0:T(8,128)S(1)} %get-tuple-element.141.refs_1_.refs_3_, bf16[1024,128]{1,0:T(8,128)(2,1)S(1)} %get-tuple-element.137.refs_2_.refs_4_, f32[1024,128]{1,0:T(8,128)S(1)} %get-tuple-element.142.refs_3_.refs_2_.refs_5_, ...), custom_call_target="tpu_custom_call" | custom-call | tf_op jit(solution)/shard_map/within/pallas_call | solution.py:84
  34.4 1.6 collective-permute-start.10
  36.1 3.3 %collective-permute-done.10.refs_5_ = bf16[528,128]{1,0:T(8,128)(2,1)S(1)} collective-permute-done((bf16[528,128]{1,0:T(8,128)(2,1)S(1)}, bf16[528,128]{1,0:T(8,128)(2,1)S(1)}, u32[]{:S(2)}, u32[]{:S(2)}) %collective-permute-start.10) | collective-permute-done | bytes 135200 | tf_op jit(solution)/shard_map/ppermute | solution.py:752
  40.9 2.6 %collective-permute-start.11 = (bf16[528,128]{1,0:T(8,128)(2,1)S(1)}, bf16[528,128]{1,0:T(8,128)(2,1)S(1)}, u32[]{:S(2)}, u32[]{:S(2)}) collective-permute-start(bf16[528,128]{1,0:T(8,128)(2,1)S(1)} %get-tuple-element.158), channel_id=1, source_target_pairs={{0,16},{4,20},{8,24},{12,28},{16,0},{20,4},{24,8},{28,12},{1,17},{... | collective-permute-start | bytes 405512 | tf_op jit(solution)/shard_map/ppermute | solution.py:752
  44.7 2.0 cotangent.1
  46.6 1.8 collective-permute-done.11.refs_9_
  48.4 4.9 %gated.1 = (f32[1024,512]{1,0:T(8,128)S(1)}, f32[8,8,128]{2,1,0:T(8,128)S(1)}, bf16[512,128]{1,0:T(8,128)(2,1)S(1)}) custom-call(s32[11]{0:T(128)S(1)} %pad_add_fusion.refs_0_, f32[1024,768]{1,0:T(8,128)S(1)} %get-tuple-element.141.refs_1_.refs_3_, f32[1024,128]{1,0:T(8,128)S(1)} %get-tuple-element.142.refs_3_.refs_2_.refs_5_, ...), custom_call_target="tpu_custom_call" | custom-call | tf_op jit(solution)/shard_map/gated/pallas_call | solution.py:84
  54.4 2.8 %collective-permute-done.12.refs_1_ = f32[8,8,128]{2,1,0:T(8,128)S(1)} collective-permute-done((f32[8,8,128]{2,1,0:T(8,128)S(1)}, f32[8,8,128]{2,1,0:T(8,128)S(1)}, u32[]{:S(2)}, u32[]{:S(2)}) %collective-permute-start.12) | collective-permute-done | bytes 32800 | tf_op jit(solution)/shard_map/ppermute | solution.py:752
  58.5 4.6 %back_gated.1 = (bf16[1024,512]{1,0:T(8,128)(2,1)S(1)}, bf16[1024,512]{1,0:T(8,128)(2,1)S(1)}, bf16[1024,512]{1,0:T(8,128)(2,1)S(1)}, bf16[8,512,128]{2,1,0:T(8,...) custom-call(s32[11]{0:T(128)S(1)} %pad_add_fusion.refs_0_, ...), custom_call_target="tpu_custom_call" | custom-call | tf_op jit(solution)/shard_map/back_gated/pallas_call | solution.py:84
  64.5 4.5 %out_wgrad.1 = (bf16[1024,512]{1,0:T(8,128)(2,1)S(1)}, bf16[1024,512]{1,0:T(8,128)(2,1)S(1)}) custom-call(s32[11]{0:T(128)S(1)} %pad_add_fusion.refs_0_, bf16[1024,512]{1,0:T(8,128)(2,1)S(1)} %get-tuple-element.161.refs_1_.refs_0_, bf16[1024,1024]{1,0:T(8,128)(2,1)S(1)} %get-tuple-element.165.refs_2_, ...), custom_call_target="tpu_custom_call" | custom-call | tf_op jit(solution)/shard_map/out_wgrad/pallas_call | solution.py:84
  69.8 5.7 %back_within.2 = (f32[1024,512]{1,0:T(8,128)S(1)}, f32[1024,256]{1,0:T(8,128)S(1)}, f32[1024,128]{1,0:T(8,128)S(1)}, f32[1024,128]{1,0:T(8,128)S(1)}) custom-call(s32[11]{0:T(128)S(1)} %pad_add_fusion.refs_0_, f32[1024,768]{1,0:T(8,128)S(1)} %get-tuple-element.141.refs_1_.refs_3_, bf16[1024,128]{1,0:T(8,128)(2,1)S(1)} %get-tuple-element.137.refs_2_.refs_4_, ...), custom_call_target="tpu_custom_call" | custom-call | tf_op jit(solution)/shard_map/back_within/pallas_call | solution.py:84
  77.0 5.7 %back_within.3 = (f32[1024,512]{1,0:T(8,128)S(1)}, f32[1024,256]{1,0:T(8,128)S(1)}, f32[1024,128]{1,0:T(8,128)S(1)}, f32[1024,128]{1,0:T(8,128)S(1)}) custom-call(s32[11]{0:T(128)S(1)} %pad_add_fusion.refs_0_, f32[1024,768]{1,0:T(8,128)S(1)} %get-tuple-element.141.refs_1_.refs_3_, ...), custom_call_target="tpu_custom_call", output_to_operand_aliasing={{0}: (12, {}), {1}: (13, {}), {2}: (14, {}), {3}: (15, {})} | custom-call | tf_op jit(solution)/shard_map/back_within/pallas_call | solution.py:84
  82.7 1.9 outproj.1
  86.5 3.4 %collective-permute-start.21 = (bf16[528,128]{1,0:T(8,128)(2,1)S(1)}, bf16[528,128]{1,0:T(8,128)(2,1)S(1)}, u32[]{:S(2)}, u32[]{:S(2)}) collective-permute-start(bf16[528,128]{1,0:T(8,128)(2,1)S(1)} %get-tuple-element.196), channel_id=1, source_target_pairs={{0,16},{4,20},{8,24},{12,28},{16,0},{20,4},{24,8},{28,12},{1,17},{... | collective-permute-start | bytes 405512 | tf_op jit(solution)/shard_map/ppermute | solution.py:752
  91.2 2.8 %collective-permute-done.19.refs_2_ = bf16[1024,512]{1,0:T(8,128)(2,1)S(1)} collective-permute-done((bf16[1024,512]{1,0:T(8,128)(2,1)S(1)}, bf16[1024,512]{1,0:T(8,128)(2,1)S(1)}, u32[]{:S(2)}, u32[]{:S(2)}) %collective-permute-start.19) | collective-permute-done | bytes 1048608 | tf_op jit(solution)/shard_map/ppermute | solution.py:752
  96.7 9.3 %back_conv.1 = (bf16[1024,768]{1,0:T(8,128)(2,1)S(1)}, bf16[1024,128]{1,0:T(8,128)(2,1)S(1)}, f32[8,768]{1,0:T(8,128)S(1)}, bf16[16,768]{1,0:T(8,128)(2,1)S(1)},...) custom-call(s32[11]{0:T(128)S(1)} %pad_add_fusion.refs_0_, bf16[1024,768]{1,0:T(8,128)(2,1)S(1)} %copy-done.3, ...), custom_call_target="tpu_custom_call" | custom-call | tf_op jit(solution)/shard_map/back_conv/pallas_call | solution.py:84
  107.3 2.9 %inner_wgrad.1 = (bf16[512,512]{1,0:T(8,128)(2,1)S(1)}, bf16[512,512]{1,0:T(8,128)(2,1)S(1)}) custom-call(s32[11]{0:T(128)S(1)} %pad_add_fusion.refs_0_, bf16[1024,1024]{1,0:T(8,128)(2,1)S(1)} %get-tuple-element.166.refs_3_.refs_1_, bf16[1024,768]{1,0:T(8,128)(2,1)S(1)} %get-tuple-element.197.refs_2_.refs_1_, ...), custom_call_target="tpu_custom_call" | custom-call | tf_op jit(solution)/shard_map/inner_wgrad/pallas_call | solution.py:84
  110.2 2.7 %collective-permute-start.24 = (bf16[512,512]{1,0:T(8,128)(2,1)S(1)}, bf16[512,512]{1,0:T(8,128)(2,1)S(1)}, u32[]{:S(2)}, u32[]{:S(2)}) collective-permute-start(bf16[512,512]{1,0:T(8,128)(2,1)S(1)} %get-tuple-element.202.refs_6_), channel_id=1, source_target_pairs={{0,4},{4,0},{8,12},{12,8},{16,20},{20,16},{24,28},{28,24},{1,5},{5... | collective-permute-start | bytes 1572872 | tf_op jit(solution)/shard_map/ppermute | solution.py:752
  112.9 1.7 bc_wgrad.1
  115.9 2.4 %collective-permute-start.28 = (bf16[256,512]{1,0:T(8,128)(2,1)S(1)}, bf16[256,512]{1,0:T(8,128)(2,1)S(1)}, u32[]{:S(2)}, u32[]{:S(2)}) collective-permute-start(bf16[256,512]{1,0:T(8,128)(2,1)S(1)} %get-tuple-element.204.refs_0_), channel_id=1, source_target_pairs={{0,16},{4,20},{8,24},{12,28},{16,0},{20,4},{24,8},{28,12},{1,17},{... | collective-permute-start | bytes 786440 | tf_op jit(solution)/shard_map/ppermute | solution.py:752
  122.1 4.7 %dgrad.1 = (bf16[256,1024]{1,0:T(8,128)(2,1)S(1)}, bf16[256,1024]{1,0:T(8,128)(2,1)S(1)}, bf16[256,1024]{1,0:T(8,128)(2,1)S(1)}, bf16[256,1024]{1,0:T(8,128)(2,1)S(1)}) custom-call(bf16[1024,512]{1,0:T(8,128)(2,1)S(1)} %get-tuple-element.167.refs_4_.refs_0_, bf16[1024,768]{1,0:T(8,128)(2,1)S(1)} %patch.1.refs_1_, ...), custom_call_target="tpu_custom_call" | custom-call | tf_op jit(solution)/shard_map/dgrad/pallas_call | solution.py:84
  127.3 2.1 %collective-permute-done.25.refs_1_ = bf16[256,1024]{1,0:T(8,128)(2,1)S(1)} collective-permute-done((bf16[256,1024]{1,0:T(8,128)(2,1)S(1)}, bf16[256,1024]{1,0:T(8,128)(2,1)S(1)}, u32[]{:S(2)}, u32[]{:S(2)}) %collective-permute-start.25) | collective-permute-done | bytes 524320 | tf_op jit(solution)/shard_map/ppermute | solution.py:752
  133.9 9.4 %collective-permute-done.27.refs_2_ = bf16[256,512]{1,0:T(8,128)(2,1)S(1)} collective-permute-done((bf16[256,512]{1,0:T(8,128)(2,1)S(1)}, bf16[256,512]{1,0:T(8,128)(2,1)S(1)}, u32[]{:S(2)}, u32[]{:S(2)}) %collective-permute-start.27) | collective-permute-done | bytes 262176 | tf_op jit(solution)/shard_map/ppermute | solution.py:752
  145.3 1.6 tokens.1
  147.0 3.8 %collective-permute-done.30.refs_2_ = bf16[256,512]{1,0:T(8,128)(2,1)S(1)} collective-permute-done((bf16[256,512]{1,0:T(8,128)(2,1)S(1)}, bf16[256,512]{1,0:T(8,128)(2,1)S(1)}, u32[]{:S(2)}, u32[]{:S(2)}) %collective-permute-start.30) | collective-permute-done | bytes 262176 | tf_op jit(solution)/shard_map/ppermute | solution.py:752
  153.5 3.8 %collective-permute-done.31.refs_2_ = bf16[288,256]{1,0:T(8,128)(2,1)S(1)} collective-permute-done((bf16[288,256]{1,0:T(8,128)(2,1)S(1)}, bf16[288,256]{1,0:T(8,128)(2,1)S(1)}, u32[]{:S(2)}, u32[]{:S(2)}) %collective-permute-start.31) | collective-permute-done | bytes 147488 | tf_op jit(solution)/shard_map/ppermute | solution.py:752
  157.4 1.6 collective-permute-start.33
  159.0 7.9 %collective-permute-done.34.refs_2_ = bf16[512,512]{1,0:T(8,128)(2,1)S(1)} collective-permute-done((bf16[512,512]{1,0:T(8,128)(2,1)S(1)}, bf16[512,512]{1,0:T(8,128)(2,1)S(1)}, u32[]{:S(2)}, u32[]{:S(2)}) %collective-permute-start.34) | collective-permute-done | bytes 524320 | tf_op jit(solution)/shard_map/ppermute | solution.py:752
  169.3 2.1 %collective-permute-start.38 = (bf16[256,512]{1,0:T(8,128)(2,1)S(1)}, bf16[256,512]{1,0:T(8,128)(2,1)S(1)}, u32[]{:S(2)}, u32[]{:S(2)}) collective-permute-start(bf16[256,512]{1,0:T(8,128)(2,1)S(1)} %join.7.refs_0_.refs_1_), channel_id=1, source_target_pairs={{0,8},{4,12},{8,0},{12,4},{16,24},{20,28},{24,16},{28,20},{1,9},{5... | collective-permute-start | bytes 786440 | tf_op jit(solution)/shard_map/ppermute | solution.py:752
  171.3 3.9 %collective-permute-done.35.refs_1_ = bf16[384,256]{1,0:T(8,128)(2,1)S(1)} collective-permute-done((bf16[384,256]{1,0:T(8,128)(2,1)S(1)}, bf16[384,256]{1,0:T(8,128)(2,1)S(1)}, u32[]{:S(2)}, u32[]{:S(2)}) %collective-permute-start.35) | collective-permute-done | bytes 196640 | tf_op jit(solution)/shard_map/ppermute | solution.py:752
  176.7 3.8 %collective-permute-done.38.refs_2_ = bf16[256,512]{1,0:T(8,128)(2,1)S(1)} collective-permute-done((bf16[256,512]{1,0:T(8,128)(2,1)S(1)}, bf16[256,512]{1,0:T(8,128)(2,1)S(1)}, u32[]{:S(2)}, u32[]{:S(2)}) %collective-permute-start.38) | collective-permute-done | bytes 262176 | tf_op jit(solution)/shard_map/ppermute | solution.py:752
  182.6 3.4 %collective-permute-done.37.refs_1_ = bf16[384,256]{1,0:T(8,128)(2,1)S(1)} collective-permute-done((bf16[384,256]{1,0:T(8,128)(2,1)S(1)}, bf16[384,256]{1,0:T(8,128)(2,1)S(1)}, u32[]{:S(2)}, u32[]{:S(2)}) %collective-permute-start.37) | collective-permute-done | bytes 196640 | tf_op jit(solution)/shard_map/ppermute | solution.py:752
  187.4 1.6 collective-permute-start.41
  188.9 3.4 %collective-permute-done.41.refs_2_ = bf16[256,256]{1,0:T(8,128)(2,1)S(1)} collective-permute-done((bf16[256,256]{1,0:T(8,128)(2,1)S(1)}, bf16[256,256]{1,0:T(8,128)(2,1)S(1)}, u32[]{:S(2)}, u32[]{:S(2)}) %collective-permute-start.41) | collective-permute-done | bytes 131104 | tf_op jit(solution)/shard_map/ppermute | solution.py:752
  193.0 1.5 collective-permute-done.42.refs_2_
  194.5 1.6 bc_weights.1
  196.1 2.8 %out_weights.1 = (f32[512,1024]{1,0:T(8,128)}, f32[2,1024,512]{2,1,0:T(8,128)}) custom-call(s32[11]{0:T(128)S(1)} %pad_add_fusion.refs_0_, bf16[1024,512]{1,0:T(8,128)(2,1)S(1)} %join.6.refs_0_.refs_1_, bf16[1024,512]{1,0:T(8,128)(2,1)S(1)} %collective-permute-done.40.refs_2_, f32[8,128]{1,0:T(8,128)S(1)} %space.78.refs_3_.refs_0_), custom_call_target="tpu_custom_call" | custom-call | tf_op jit(solution)/shard_map/out_weights/pallas_call | solution.py:84
  198.9 2.9 %collective-permute-done.39.refs_2_ = bf16[512,512]{1,0:T(8,128)(2,1)S(1)} collective-permute-done((bf16[512,512]{1,0:T(8,128)(2,1)S(1)}, bf16[512,512]{1,0:T(8,128)(2,1)S(1)}, u32[]{:S(2)}, u32[]{:S(2)}) %collective-permute-start.39) | collective-permute-done | bytes 524320 | tf_op jit(solution)/shard_map/ppermute | solution.py:752
  201.8 2.0 zx_weights.1
  (191 shorter events, 44.9 us)
Async XLA Ops:
  0.6 4.1 %collective-permute-start.1 = (bf16[256,1024]{1,0:T(8,128)(2,1)}, bf16[256,1024]{1,0:T(8,128)(2,1)S(1)}, u32[]{:S(2)}, u32[]{:S(2)}) collective-permute-start(bf16[256,1024]{1,0:T(8,128)(2,1)} %refs_0_.11), channel_id=1, source_target_pairs={{0,1},{1,0},{2,3},{3,2},{4,5},{5,4},{6,7},{7,6},{8,9},{9,8},{10,11... | collective-permute-start | bytes 1572872 | tf_op jit(solution)/shard_map/ppermute | solution.py:752
  1.2 15.6 %collective-permute-start = (bf16[256,1024]{1,0:T(8,128)(2,1)}, bf16[256,1024]{1,0:T(8,128)(2,1)S(1)}, u32[]{:S(2)}, u32[]{:S(2)}) collective-permute-start(bf16[256,1024]{1,0:T(8,128)(2,1)} %refs_0_.11), channel_id=1, source_target_pairs={{0,2},{1,3},{2,0},{3,1},{4,6},{5,7},{6,4},{7,5},{8,10},{9,11},{10,... | collective-permute-start | bytes 1572872 | tf_op jit(solution)/shard_map/ppermute | solution.py:752
  3.7 39.7 %collective-permute-start.6 = (bf16[256,1024]{1,0:T(8,128)(2,1)}, bf16[256,1024]{1,0:T(8,128)(2,1)S(1)}, u32[]{:S(2)}, u32[]{:S(2)}) collective-permute-start(bf16[256,1024]{1,0:T(8,128)(2,1)} %refs_1_.5), channel_id=1, source_target_pairs={{0,1},{1,0},{2,3},{3,2},{4,5},{5,4},{6,7},{7,6},{8,9},{9,8},{10,11... | collective-permute-start | bytes 1572872 | tf_op jit(solution)/shard_map/ppermute | solution.py:752
  5.8 11.1 %collective-permute-start.4 = (bf16[16,1024]{1,0:T(8,128)(2,1)S(1)}, bf16[16,1024]{1,0:T(8,128)(2,1)S(1)}, u32[]{:S(2)}, u32[]{:S(2)}) collective-permute-start(bf16[16,1024]{1,0:T(8,128)(2,1)S(1)} %last_rows.1.refs_9_), channel_id=1, source_target_pairs={{3,7},{7,11},{11,15},{15,19},{19,23},{23,27},{27,31}} | collective-permute-start | bytes 98312 | tf_op jit(solution)/shard_map/ppermute | solution.py:1176
  6.4 10.4 %collective-permute-start.3 = (bf16[16,1024]{1,0:T(8,128)(2,1)S(1)}, bf16[16,1024]{1,0:T(8,128)(2,1)S(1)}, u32[]{:S(2)}, u32[]{:S(2)}) collective-permute-start(bf16[16,1024]{1,0:T(8,128)(2,1)S(1)} %last_rows.1.refs_9_), channel_id=1, source_target_pairs={{3,5},{7,9},{11,13},{15,17},{19,21},{23,25},{27,29}} | collective-permute-start | bytes 98312 | tf_op jit(solution)/shard_map/ppermute | solution.py:1176
  8.1 11.1 %copy-start.11 = (bf16[128,1024]{1,0:T(8,128)(2,1)}, bf16[128,1024]{1,0:T(8,128)(2,1)S(1)}, u32[]{:S(2)}) copy-start(bf16[128,1024]{1,0:T(8,128)(2,1)S(1)} %get-tuple-element.126.refs_6_.refs_5_.refs_7_) | copy-start | bytes 786436
  16.8 2.5 %collective-permute-start.2 = (bf16[256,1024]{1,0:T(8,128)(2,1)S(1)}, bf16[256,1024]{1,0:T(8,128)(2,1)S(1)}, u32[]{:S(2)}, u32[]{:S(2)}) collective-permute-start(bf16[256,1024]{1,0:T(8,128)(2,1)S(1)} %hold.3.refs_2_.refs_1_), channel_id=1, source_target_pairs={{0,1},{1,0},{2,3},{3,2},{4,5},{5,4},{6,7},{7,6},{8,9},{9,8},{10,11... | collective-permute-start | bytes 1572872 | tf_op jit(solution)/shard_map/ppermute | solution.py:752
  16.9 2.4 %collective-permute-start.5 = (bf16[16,1024]{1,0:T(8,128)(2,1)S(1)}, bf16[16,1024]{1,0:T(8,128)(2,1)S(1)}, u32[]{:S(2)}, u32[]{:S(2)}) collective-permute-start(bf16[16,1024]{1,0:T(8,128)(2,1)S(1)} %past.1.refs_10_.refs_0_.refs_2_), channel_id=1, source_target_pairs={{0,1},{1,0},{2,3},{3,2},{4,5},{5,4},{6,7},{7,6},{8,9},{9,8},{10,11... | collective-permute-start | bytes 98312 | tf_op jit(solution)/shard_map/ppermute | solution.py:752
  21.3 12.2 %copy-start.2 = (bf16[1024,768]{1,0:T(8,128)(2,1)}, bf16[1024,768]{1,0:T(8,128)(2,1)S(1)}, u32[]{:S(2)}) copy-start(bf16[1024,768]{1,0:T(8,128)(2,1)S(1)} %get-tuple-element.136.refs_1_) | copy-start | bytes 4718596
  21.3 12.2 %copy-start.15 = (bf16[16,768]{1,0:T(8,128)(2,1)}, bf16[16,768]{1,0:T(8,128)(2,1)S(1)}, u32[]{:S(2)}) copy-start(bf16[16,768]{1,0:T(8,128)(2,1)S(1)} %get-tuple-element.138.refs_1_.refs_3_.refs_2_) | copy-start | bytes 73732
  21.4 14.6 %collective-permute-start.7 = (bf16[256,1024]{1,0:T(8,128)(2,1)S(1)}, bf16[256,1024]{1,0:T(8,128)(2,1)S(1)}, u32[]{:S(2)}, u32[]{:S(2)}) collective-permute-start(bf16[256,1024]{1,0:T(8,128)(2,1)S(1)} %hold.4.refs_7_), channel_id=1, source_target_pairs={{0,2},{1,3},{2,0},{3,1},{4,6},{5,7},{6,4},{7,5},{8,10},{9,11},{10,... | collective-permute-start | bytes 1572872 | tf_op jit(solution)/shard_map/ppermute | solution.py:752
  28.3 5.3 %collective-permute-start.8 = (bf16[528,128]{1,0:T(8,128)(2,1)S(1)}, bf16[528,128]{1,0:T(8,128)(2,1)S(1)}, u32[]{:S(2)}, u32[]{:S(2)}) collective-permute-start(bf16[528,128]{1,0:T(8,128)(2,1)S(1)} %get-tuple-element.148), channel_id=1, source_target_pairs={{0,4},{4,0},{8,12},{12,8},{16,20},{20,16},{24,28},{28,24},{1,5},{5... | collective-permute-start | bytes 405512 | tf_op jit(solution)/shard_map/ppermute | solution.py:752
  34.4 5.1 %collective-permute-start.10 = (bf16[528,128]{1,0:T(8,128)(2,1)S(1)}, bf16[528,128]{1,0:T(8,128)(2,1)S(1)}, u32[]{:S(2)}, u32[]{:S(2)}) collective-permute-start(bf16[528,128]{1,0:T(8,128)(2,1)S(1)} %get-tuple-element.153), channel_id=1, source_target_pairs={{0,8},{4,12},{8,0},{12,4},{16,24},{20,28},{24,16},{28,20},{1,9},{5... | collective-permute-start | bytes 405512 | tf_op jit(solution)/shard_map/ppermute | solution.py:752
  36.0 7.4 %collective-permute-start.9 = (bf16[256,1024]{1,0:T(8,128)(2,1)S(1)}, bf16[256,1024]{1,0:T(8,128)(2,1)S(1)}, u32[]{:S(2)}, u32[]{:S(2)}) collective-permute-start(bf16[256,1024]{1,0:T(8,128)(2,1)S(1)} %hold.5.refs_0_), channel_id=1, source_target_pairs={{0,1},{1,0},{2,3},{3,2},{4,5},{5,4},{6,7},{7,6},{8,9},{9,8},{10,11... | collective-permute-start | bytes 1572872 | tf_op jit(solution)/shard_map/ppermute | solution.py:752
  40.9 7.6 %collective-permute-start.11 = (bf16[528,128]{1,0:T(8,128)(2,1)S(1)}, bf16[528,128]{1,0:T(8,128)(2,1)S(1)}, u32[]{:S(2)}, u32[]{:S(2)}) collective-permute-start(bf16[528,128]{1,0:T(8,128)(2,1)S(1)} %get-tuple-element.158), channel_id=1, source_target_pairs={{0,16},{4,20},{8,24},{12,28},{16,0},{20,4},{24,8},{28,12},{1,17},{... | collective-permute-start | bytes 405512 | tf_op jit(solution)/shard_map/ppermute | solution.py:752
  53.3 3.9 %collective-permute-start.12 = (f32[8,8,128]{2,1,0:T(8,128)S(1)}, f32[8,8,128]{2,1,0:T(8,128)S(1)}, u32[]{:S(2)}, u32[]{:S(2)}) collective-permute-start(f32[8,8,128]{2,1,0:T(8,128)S(1)} %get-tuple-element.160.refs_0_), channel_id=1, source_target_pairs={{0,2},{1,3},{2,0},{3,1},{4,6},{5,7},{6,4},{7,5},{8,10},{9,11},{10,... | collective-permute-start | bytes 98312 | tf_op jit(solution)/shard_map/ppermute | solution.py:752
  57.3 1.2 collective-permute-start.13
  63.1 5.9 %copy-start.19 = (f32[8,512]{1,0:T(8,128)}, f32[8,512]{1,0:T(8,128)S(1)}, u32[]{:S(2)}) copy-start(f32[8,512]{1,0:T(8,128)S(1)} %get-tuple-element.168.refs_5_) | copy-start | bytes 49156
  63.1 12.4 %collective-permute-start.14 = (bf16[528,128]{1,0:T(8,128)(2,1)S(1)}, bf16[528,128]{1,0:T(8,128)(2,1)S(1)}, u32[]{:S(2)}, u32[]{:S(2)}) collective-permute-start(bf16[528,128]{1,0:T(8,128)(2,1)S(1)} %get-tuple-element.175), channel_id=1, source_target_pairs={{0,4},{4,0},{8,12},{12,8},{16,20},{20,16},{24,28},{28,24},{1,5},{5... | collective-permute-start | bytes 405512 | tf_op jit(solution)/shard_map/ppermute | solution.py:752
  69.0 25.0 %collective-permute-start.19 = (bf16[1024,512]{1,0:T(8,128)(2,1)S(1)}, bf16[1024,512]{1,0:T(8,128)(2,1)S(1)}, u32[]{:S(2)}, u32[]{:S(2)}) collective-permute-start(bf16[1024,512]{1,0:T(8,128)(2,1)S(1)} %get-tuple-element.169.refs_12_), channel_id=1, source_target_pairs={{0,4},{4,0},{8,12},{12,8},{16,20},{20,16},{24,28},{28,24},{1,5},{5... | collective-permute-start | bytes 3145736 | tf_op jit(solution)/shard_map/ppermute | solution.py:752
  76.3 8.9 %collective-permute-start.17 = (bf16[528,128]{1,0:T(8,128)(2,1)S(1)}, bf16[528,128]{1,0:T(8,128)(2,1)S(1)}, u32[]{:S(2)}, u32[]{:S(2)}) collective-permute-start(bf16[528,128]{1,0:T(8,128)(2,1)S(1)} %get-tuple-element.185), channel_id=1, source_target_pairs={{0,8},{4,12},{8,0},{12,4},{16,24},{20,28},{24,16},{28,20},{1,9},{5... | collective-permute-start | bytes 405512 | tf_op jit(solution)/shard_map/ppermute | solution.py:752
  84.5 5.4 %collective-permute-start.16 = (bf16[256,1024]{1,0:T(8,128)(2,1)S(1)}, bf16[256,1024]{1,0:T(8,128)(2,1)S(1)}, u32[]{:S(2)}, u32[]{:S(2)}) collective-permute-start(bf16[256,1024]{1,0:T(8,128)(2,1)S(1)} %get-tuple-element.181.refs_0_), channel_id=1, source_target_pairs={{0,1},{1,0},{2,3},{3,2},{4,5},{5,4},{6,7},{7,6},{8,9},{9,8},{10,11... | collective-permute-start | bytes 1572872 | tf_op jit(solution)/shard_map/ppermute | solution.py:752
  84.6 6.4 %collective-permute-start.15 = (bf16[256,1024]{1,0:T(8,128)(2,1)S(1)}, bf16[256,1024]{1,0:T(8,128)(2,1)S(1)}, u32[]{:S(2)}, u32[]{:S(2)}) collective-permute-start(bf16[256,1024]{1,0:T(8,128)(2,1)S(1)} %get-tuple-element.179), channel_id=1, source_target_pairs={{0,1},{1,0},{2,3},{3,2},{4,5},{5,4},{6,7},{7,6},{8,9},{9,8},{10,11... | collective-permute-start | bytes 1572872 | tf_op jit(solution)/shard_map/ppermute | solution.py:752
  86.5 10.1 %collective-permute-start.21 = (bf16[528,128]{1,0:T(8,128)(2,1)S(1)}, bf16[528,128]{1,0:T(8,128)(2,1)S(1)}, u32[]{:S(2)}, u32[]{:S(2)}) collective-permute-start(bf16[528,128]{1,0:T(8,128)(2,1)S(1)} %get-tuple-element.196), channel_id=1, source_target_pairs={{0,16},{4,20},{8,24},{12,28},{16,0},{20,4},{24,8},{28,12},{1,17},{... | collective-permute-start | bytes 405512 | tf_op jit(solution)/shard_map/ppermute | solution.py:752
  90.1 28.3 %collective-permute-start.18 = (bf16[256,1024]{1,0:T(8,128)(2,1)S(1)}, bf16[256,1024]{1,0:T(8,128)(2,1)S(1)}, u32[]{:S(2)}, u32[]{:S(2)}) collective-permute-start(bf16[256,1024]{1,0:T(8,128)(2,1)S(1)} %add.26.refs_0_), channel_id=1, source_target_pairs={{0,2},{1,3},{2,0},{3,1},{4,6},{5,7},{6,4},{7,5},{8,10},{9,11},{10,... | collective-permute-start | bytes 1572872 | tf_op jit(solution)/shard_map/ppermute | solution.py:752
  94.8 20.4 %collective-permute-start.20 = (bf16[512,512]{1,0:T(8,128)(2,1)S(1)}, bf16[512,512]{1,0:T(8,128)(2,1)S(1)}, u32[]{:S(2)}, u32[]{:S(2)}) collective-permute-start(bf16[512,512]{1,0:T(8,128)(2,1)S(1)} %get-tuple-element.189.refs_0_), channel_id=1, source_target_pairs={{0,8},{4,12},{8,0},{12,4},{16,24},{20,28},{24,16},{28,20},{1,9},{5... | collective-permute-start | bytes 1572872 | tf_op jit(solution)/shard_map/ppermute | solution.py:752
  106.0 8.6 %copy-start.23 = (f32[8,128]{1,0:T(8,128)}, f32[8,128]{1,0:T(8,128)S(1)}, u32[]{:S(2)}) copy-start(f32[8,128]{1,0:T(8,128)S(1)} %get-tuple-element.201.refs_5_.refs_6_) | copy-start | bytes 12292
  106.0 14.4 %collective-permute-start.22 = (f32[8,768]{1,0:T(8,128)S(1)}, f32[8,768]{1,0:T(8,128)S(1)}, u32[]{:S(2)}, u32[]{:S(2)}) collective-permute-start(f32[8,768]{1,0:T(8,128)S(1)} %get-tuple-element.205), channel_id=1, source_target_pairs={{4,0},{8,4},{12,8},{16,12},{20,16},{24,20},{28,24},{5,1},{9,5},{13... | collective-permute-start | bytes 73736 | tf_op jit(solution)/shard_map/ppermute | solution.py:1451
  110.2 20.4 %collective-permute-start.24 = (bf16[512,512]{1,0:T(8,128)(2,1)S(1)}, bf16[512,512]{1,0:T(8,128)(2,1)S(1)}, u32[]{:S(2)}, u32[]{:S(2)}) collective-permute-start(bf16[512,512]{1,0:T(8,128)(2,1)S(1)} %get-tuple-element.202.refs_6_), channel_id=1, source_target_pairs={{0,4},{4,0},{8,12},{12,8},{16,20},{20,16},{24,28},{28,24},{1,5},{5... | collective-permute-start | bytes 1572872 | tf_op jit(solution)/shard_map/ppermute | solution.py:752
  115.9 16.8 %collective-permute-start.28 = (bf16[256,512]{1,0:T(8,128)(2,1)S(1)}, bf16[256,512]{1,0:T(8,128)(2,1)S(1)}, u32[]{:S(2)}, u32[]{:S(2)}) collective-permute-start(bf16[256,512]{1,0:T(8,128)(2,1)S(1)} %get-tuple-element.204.refs_0_), channel_id=1, source_target_pairs={{0,16},{4,20},{8,24},{12,28},{16,0},{20,4},{24,8},{28,12},{1,17},{... | collective-permute-start | bytes 786440 | tf_op jit(solution)/shard_map/ppermute | solution.py:752
  126.8 5.8 %collective-permute-start.23 = (bf16[256,1024]{1,0:T(8,128)(2,1)S(1)}, bf16[256,1024]{1,0:T(8,128)(2,1)S(1)}, u32[]{:S(2)}, u32[]{:S(2)}) collective-permute-start(bf16[256,1024]{1,0:T(8,128)(2,1)S(1)} %get-tuple-element.207), channel_id=1, source_target_pairs={{0,1},{1,0},{2,3},{3,2},{4,5},{5,4},{6,7},{7,6},{8,9},{9,8},{10,11... | collective-permute-start | bytes 1572872 | tf_op jit(solution)/shard_map/ppermute | solution.py:752
  126.8 2.6 %collective-permute-start.25 = (bf16[256,1024]{1,0:T(8,128)(2,1)S(1)}, bf16[256,1024]{1,0:T(8,128)(2,1)S(1)}, u32[]{:S(2)}, u32[]{:S(2)}) collective-permute-start(bf16[256,1024]{1,0:T(8,128)(2,1)S(1)} %get-tuple-element.210.refs_0_), channel_id=1, source_target_pairs={{0,1},{1,0},{2,3},{3,2},{4,5},{5,4},{6,7},{7,6},{8,9},{9,8},{10,11... | collective-permute-start | bytes 1572872 | tf_op jit(solution)/shard_map/ppermute | solution.py:752
  129.6 15.6 %collective-permute-start.26 = (bf16[256,1024]{1,0:T(8,128)(2,1)S(1)}, bf16[256,1024]{1,0:T(8,128)(2,1)S(1)}, u32[]{:S(2)}, u32[]{:S(2)}) collective-permute-start(bf16[256,1024]{1,0:T(8,128)(2,1)S(1)} %add.28.refs_0_), channel_id=1, source_target_pairs={{0,2},{1,3},{2,0},{3,1},{4,6},{5,7},{6,4},{7,5},{8,10},{9,11},{10,... | collective-permute-start | bytes 1572872 | tf_op jit(solution)/shard_map/ppermute | solution.py:752
  131.3 12.0 %collective-permute-start.27 = (bf16[256,512]{1,0:T(8,128)(2,1)S(1)}, bf16[256,512]{1,0:T(8,128)(2,1)S(1)}, u32[]{:S(2)}, u32[]{:S(2)}) collective-permute-start(bf16[256,512]{1,0:T(8,128)(2,1)S(1)} %get-tuple-element.211.refs_0_), channel_id=1, source_target_pairs={{0,8},{4,12},{8,0},{12,4},{16,24},{20,28},{24,16},{28,20},{1,9},{5... | collective-permute-start | bytes 786440 | tf_op jit(solution)/shard_map/ppermute | solution.py:752
  132.9 18.0 %collective-permute-start.30 = (bf16[256,512]{1,0:T(8,128)(2,1)S(1)}, bf16[256,512]{1,0:T(8,128)(2,1)S(1)}, u32[]{:S(2)}, u32[]{:S(2)}) collective-permute-start(bf16[256,512]{1,0:T(8,128)(2,1)S(1)} %add.30.refs_0_.refs_1_), channel_id=1, source_target_pairs={{0,16},{4,20},{8,24},{12,28},{16,0},{20,4},{24,8},{28,12},{1,17},{... | collective-permute-start | bytes 786440 | tf_op jit(solution)/shard_map/ppermute | solution.py:752
  143.9 9.5 %collective-permute-start.32 = (bf16[128,512]{1,0:T(8,128)(2,1)S(1)}, bf16[128,512]{1,0:T(8,128)(2,1)S(1)}, u32[]{:S(2)}, u32[]{:S(2)}) collective-permute-start(bf16[128,512]{1,0:T(8,128)(2,1)S(1)} %get-tuple-element.215.refs_0_), channel_id=1, source_target_pairs={{0,16},{4,20},{8,24},{12,28},{16,0},{20,4},{24,8},{28,12},{1,17},{... | collective-permute-start | bytes 393224 | tf_op jit(solution)/shard_map/ppermute | solution.py:752
  146.9 4.6 %collective-permute-start.29 = (bf16[544,256]{1,0:T(8,128)(2,1)S(1)}, bf16[544,256]{1,0:T(8,128)(2,1)S(1)}, u32[]{:S(2)}, u32[]{:S(2)}) collective-permute-start(bf16[544,256]{1,0:T(8,128)(2,1)S(1)} %lead.1.refs_0_), channel_id=1, source_target_pairs={{0,1},{1,0},{2,3},{3,2},{4,5},{5,4},{6,7},{7,6},{8,9},{9,8},{10,11... | collective-permute-start | bytes 835592 | tf_op jit(solution)/shard_map/ppermute | solution.py:752
  151.4 15.5 %collective-permute-start.34 = (bf16[512,512]{1,0:T(8,128)(2,1)S(1)}, bf16[512,512]{1,0:T(8,128)(2,1)S(1)}, u32[]{:S(2)}, u32[]{:S(2)}) collective-permute-start(bf16[512,512]{1,0:T(8,128)(2,1)S(1)} %join.5.refs_0_.refs_1_), channel_id=1, source_target_pairs={{0,8},{4,12},{8,0},{12,4},{16,24},{20,28},{24,16},{28,20},{1,9},{5... | collective-permute-start | bytes 1572872 | tf_op jit(solution)/shard_map/ppermute | solution.py:752
  152.2 5.2 %collective-permute-start.31 = (bf16[288,256]{1,0:T(8,128)(2,1)S(1)}, bf16[288,256]{1,0:T(8,128)(2,1)S(1)}, u32[]{:S(2)}, u32[]{:S(2)}) collective-permute-start(bf16[288,256]{1,0:T(8,128)(2,1)S(1)} %get-tuple-element.222), channel_id=1, source_target_pairs={{0,2},{1,3},{2,0},{3,1},{4,6},{5,7},{6,4},{7,5},{8,10},{9,11},{10,... | collective-permute-start | bytes 442376 | tf_op jit(solution)/shard_map/ppermute | solution.py:752
  153.4 15.2 %collective-permute-start.36 = (bf16[128,512]{1,0:T(8,128)(2,1)S(1)}, bf16[128,512]{1,0:T(8,128)(2,1)S(1)}, u32[]{:S(2)}, u32[]{:S(2)}) collective-permute-start(bf16[128,512]{1,0:T(8,128)(2,1)S(1)} %add.31.refs_0_.refs_1_), channel_id=1, source_target_pairs={{0,16},{4,20},{8,24},{12,28},{16,0},{20,4},{24,8},{28,12},{1,17},{... | collective-permute-start | bytes 393224 | tf_op jit(solution)/shard_map/ppermute | solution.py:752
  157.4 11.1 %collective-permute-start.33 = (bf16[384,256]{1,0:T(8,128)(2,1)S(1)}, bf16[384,256]{1,0:T(8,128)(2,1)S(1)}, u32[]{:S(2)}, u32[]{:S(2)}) collective-permute-start(bf16[384,256]{1,0:T(8,128)(2,1)S(1)} %misc_pack.1.refs_0_), channel_id=1, source_target_pairs={{0,4},{4,0},{8,12},{12,8},{16,20},{20,16},{24,28},{28,24},{1,5},{5... | collective-permute-start | bytes 589832 | tf_op jit(solution)/shard_map/ppermute | solution.py:752
  167.6 28.5 %collective-permute-start.40 = (bf16[1024,512]{1,0:T(8,128)(2,1)S(1)}, bf16[1024,512]{1,0:T(8,128)(2,1)S(1)}, u32[]{:S(2)}, u32[]{:S(2)}) collective-permute-start(bf16[1024,512]{1,0:T(8,128)(2,1)S(1)} %join.6.refs_0_.refs_1_), channel_id=1, source_target_pairs={{0,4},{4,0},{8,12},{12,8},{16,20},{20,16},{24,28},{28,24},{1,5},{5... | collective-permute-start | bytes 3145736 | tf_op jit(solution)/shard_map/ppermute | solution.py:752
  168.6 6.7 %collective-permute-start.35 = (bf16[384,256]{1,0:T(8,128)(2,1)S(1)}, bf16[384,256]{1,0:T(8,128)(2,1)S(1)}, u32[]{:S(2)}, u32[]{:S(2)}) collective-permute-start(bf16[384,256]{1,0:T(8,128)(2,1)S(1)} %misc_add.2.refs_0_), channel_id=1, source_target_pairs={{0,8},{4,12},{8,0},{12,4},{16,24},{20,28},{24,16},{28,20},{1,9},{5... | collective-permute-start | bytes 589832 | tf_op jit(solution)/shard_map/ppermute | solution.py:752
  169.3 11.2 %collective-permute-start.38 = (bf16[256,512]{1,0:T(8,128)(2,1)S(1)}, bf16[256,512]{1,0:T(8,128)(2,1)S(1)}, u32[]{:S(2)}, u32[]{:S(2)}) collective-permute-start(bf16[256,512]{1,0:T(8,128)(2,1)S(1)} %join.7.refs_0_.refs_1_), channel_id=1, source_target_pairs={{0,8},{4,12},{8,0},{12,4},{16,24},{20,28},{24,16},{28,20},{1,9},{5... | collective-permute-start | bytes 786440 | tf_op jit(solution)/shard_map/ppermute | solution.py:752
  175.3 10.6 %collective-permute-start.37 = (bf16[384,256]{1,0:T(8,128)(2,1)S(1)}, bf16[384,256]{1,0:T(8,128)(2,1)S(1)}, u32[]{:S(2)}, u32[]{:S(2)}) collective-permute-start(bf16[384,256]{1,0:T(8,128)(2,1)S(1)} %misc_add.3.refs_0_), channel_id=1, source_target_pairs={{0,16},{4,20},{8,24},{12,28},{16,0},{20,4},{24,8},{28,12},{1,17},{... | collective-permute-start | bytes 589832 | tf_op jit(solution)/shard_map/ppermute | solution.py:752
  181.1 20.7 %collective-permute-start.39 = (bf16[512,512]{1,0:T(8,128)(2,1)S(1)}, bf16[512,512]{1,0:T(8,128)(2,1)S(1)}, u32[]{:S(2)}, u32[]{:S(2)}) collective-permute-start(bf16[512,512]{1,0:T(8,128)(2,1)S(1)} %join.8.refs_0_.refs_1_), channel_id=1, source_target_pairs={{0,4},{4,0},{8,12},{12,8},{16,20},{20,16},{24,28},{28,24},{1,5},{5... | collective-permute-start | bytes 1572872 | tf_op jit(solution)/shard_map/ppermute | solution.py:752
  187.4 5.0 %collective-permute-start.41 = (bf16[256,256]{1,0:T(8,128)(2,1)S(1)}, bf16[256,256]{1,0:T(8,128)(2,1)S(1)}, u32[]{:S(2)}, u32[]{:S(2)}) collective-permute-start(bf16[256,256]{1,0:T(8,128)(2,1)S(1)} %get-tuple-element.227.refs_1_), channel_id=1, source_target_pairs={{0,2},{1,3},{2,0},{3,1},{4,6},{5,7},{6,4},{7,5},{8,10},{9,11},{10,... | collective-permute-start | bytes 393224 | tf_op jit(solution)/shard_map/ppermute | solution.py:752
  192.9 1.6 collective-permute-start.42
  (21 other events, 39.6 us)

commit v6 on v5

--- a/solution.py
+++ b/solution.py
@@ -1,4 +1,5 @@
 import functools
+from types import SimpleNamespace
 from typing import Any, NamedTuple
 
 import jax
@@ -17,6 +18,8 @@
 BF = jnp.bfloat16
 MIB = 1 << 20
 ROW = 256
+DP, TP = "dp", "tensor"
+ROWS, EACH, ONE = range(3)
 
 
 def dot(a, b, ca=1, cb=0):
@@ -109,9 +112,9 @@
     o[...] = jnp.zeros_like(o)
 
 
-def space():
+def space(flops=10 * 10**9):
     o = shaped((8, L))
-    launch(space_body, [], [], [o], [whole(o)], "space", vmem=1, flops=10**10)
+    launch(space_body, [], [], [o], [whole(o)], "space", vmem=1, flops=flops)
 
 
 def shaped(shape, dtype=F32):
@@ -685,19 +688,36 @@
             )
 
 
-def dgrad_body(k, ggr, gcat, gsr, wzx, wbc, wst, *outs):
-    width = wzx.shape[2]
-
-    def one(out):
-        r = dot(ggr[...], wzx[0], 1, 1)
-        r = r + dot(gcat[:, :width], wzx[1], 1, 1)
-        r = r + dot(gcat[:, width : width + L], wbc[0], 1, 1)
-        r = r + dot(gcat[:, width + L :], wbc[1], 1, 1)
-        r = r + dot(gsr[...], wst[...])
-        out[...] = r.astype(BF)
+def dgrad_body(k, ggr, gcat, gsr, normed, wzx, wbc, wst, gain, conv, *refs):
+    outs, shared_o, acc = refs[:k], refs[k], refs[k + 1]
+    width, d = wzx.shape[2], gain.shape[1]
+    i = pl.program_id(0)
+
+    @pl.when(i == 0)
+    def _():
+        acc[...] = jnp.zeros_like(acc)
+
+    r = dot(ggr[...], wzx[0], 1, 1)
+    r = r + dot(gcat[:, :width], wzx[1], 1, 1)
+    r = r + dot(gcat[:, width : width + L], wbc[0], 1, 1)
+    r = r + dot(gcat[:, width + L :], wbc[1], 1, 1)
+    r = r + dot(gsr[...], wst[...])
+    acc[...] += eights(r * normed[...].astype(F32))
+    rounded = r.astype(BF)
+
+    def into(out):
+        out[...] = rounded
 
     for j in range(k):
-        pl.when(pl.program_id(0) == j)(functools.partial(one, outs[j]))
+        pl.when(i == j)(functools.partial(into, outs[j]))
+
+    @pl.when(i == k - 1)
+    def _():
+        shared_o[...] = jnp.zeros_like(shared_o)
+        sums = jnp.sum(acc[...], axis=0, keepdims=True) / gain[...]
+        for c in range(d // ROW):
+            shared_o[c : c + 1, :] = sums[:, c * ROW : (c + 1) * ROW]
+        shared_o[d // ROW : d // ROW + 5, :] = conv[0:5, conv.shape[1] - ROW :]
 
 
 def outproj_body(k, normout, wout, *outs):
@@ -708,20 +728,21 @@
         pl.when(pl.program_id(0) == j)(functools.partial(one, outs[j]))
 
 
-def rows_times(body, frames_n, share, d, rows, consts, name):
+def rows_times(body, frames_n, share, d, rows, consts, name, more=(), scratch=()):
     k = frames_n
     outs = launch(
         functools.partial(body, k),
         [*rows, *consts],
         [pl.BlockSpec((share, r.shape[1]), lambda i: (k - 1 - i, 0)) for r in rows]
         + [whole(a) for a in consts],
-        [shaped((share, d), BF)] * k,
-        [pl.BlockSpec((share, d), lambda i: (0, 0))] * k,
+        [shaped((share, d), BF)] * k + list(more),
+        [pl.BlockSpec((share, d), lambda i: (0, 0))] * k + [whole(o) for o in more],
         name,
         grid=(k,),
+        scratch=scratch,
         vmem=20,
     )
-    return list(outs)[::-1]
+    return [*outs[:k][::-1], *outs[k:]]
 
 
 def total_body(*refs):
@@ -809,7 +830,7 @@
         pl.when(jnp.logical_and(inside, i >= half))(functools.partial(into, keep_o))
 
 
-def wgrads(meta, pairs, width, blocks, name):
+def wgrads(meta, pairs, width, blocks):
     half = blocks * len(pairs) // 2
     tokens = pairs[0][0].shape[0]
 
@@ -835,7 +856,7 @@
             pl.BlockSpec((width, width), lambda i, m: (jnp.minimum(i, half - 1), 0)),
             pl.BlockSpec((width, width), lambda i, m: (jnp.maximum(i - half, 0), 0)),
         ],
-        name,
+        "wgrad",
         grid=(2 * half,),
         meta=meta,
         vmem=20,
@@ -871,30 +892,25 @@
     )
 
 
-def wg_out_body(blocks, meta, own, got, wout_o, zx_o):
+def columns_body(blocks, meta, own, got, o):
+    width = o.shape[0]
     bit = bit_at(meta, 0)
-    width = wout_o.shape[0]
-    for src, side in ((own, bit), (got, 1 - bit)):
-
-        @pl.when(side == 0)
-        def _(src=src):
-            for k in range(blocks):
-                rows = slice(k * width, (k + 1) * width)
-                wout_o[:, rows] = src[rows, :].astype(F32)
-
-        @pl.when(side == 1)
-        def _(src=src):
-            zx_o[0] = src[...].astype(F32)
-
-
-def wg_out(meta, own, got, d, width):
-    return launch(
-        functools.partial(wg_out_body, d // width), [own, got], [whole(own), whole(got)],
-        [shaped((width, d)), shaped((2, d, width))],
-        [pl.BlockSpec((width, d), lambda i, m: (0, 0)),
-         pl.BlockSpec((1, d, width), lambda i, m: (0, 0, 0))],
-        "out_weights", meta=meta, vmem=20, token=False,
-    )
+    half = blocks // 2
+    for src, b in ((own, bit), (got, 1 - bit)):
+        for side in range(2):
+
+            @pl.when(b == side)
+            def _(src=src, side=side):
+                for k in range(half):
+                    at = (side * half + k) * width
+                    o[:, at : at + width] = src[k * width : (k + 1) * width, :].astype(F32)
+
+
+def columns(meta, own, got, d, width):
+    return simple(
+        functools.partial(columns_body, d // width), [own, got], [shaped((width, d))],
+        "out_weights", meta, 16,
+    )[0]
 
 
 def rows_body(meta, own, got, *rest):
@@ -956,21 +972,14 @@
     o[...] = (tok[...].astype(F32) + (a[...].astype(F32) + b[...].astype(F32))).astype(BF)
 
 
-def tokens_body(tok, cot, a, b, gain, conv, gt_o, acc_o):
+def tokens_body(tok, cot, a, b, gain, gt_o):
     x = tok[...].astype(F32)
     rstd = lax.rsqrt(jnp.mean(x * x, axis=1, keepdims=True) + EPS)
     unit = x * rstd
-    gnormed = a[...].astype(F32) + b[...].astype(F32)
-    gunit = gnormed * gain[...]
+    gunit = (a[...].astype(F32) + b[...].astype(F32)) * gain[...]
     gt_o[...] = cot[...].astype(F32) + rstd * (
         gunit - unit * jnp.mean(gunit * unit, axis=1, keepdims=True)
     )
-    d = x.shape[1]
-    acc_o[...] = jnp.zeros_like(acc_o)
-    sums = jnp.sum(gnormed * unit, axis=0, keepdims=True)
-    for k in range(d // ROW):
-        acc_o[k : k + 1, :] = sums[:, k * ROW : (k + 1) * ROW]
-    acc_o[d // ROW : d // ROW + 5, :] = conv[0:5, conv.shape[1] - ROW :]
 
 
 def halves_of(v):
@@ -1074,48 +1083,31 @@
     last: Any
 
 
-class Plan:
-    def __init__(self):
-        self.now, self.links, self.chains, self.done = 0.0, {}, [], set()
-
-    def add(self, name, priority, chain, spend=0.0):
-        self.chains.append([name, priority, chain, None])
-        self.now += spend
-        self.step(self.chains[-1])
-
-    def step(self, entry):
-        if entry[3] and entry[3][0] is None:
+ORDER = "LWGLFLWFLTGIWGTWIMMTGMTWMIGMWITBGBMBIWIMGMBMI"
+
+
+def run_chains(chains, done, order):
+    needs = {name: next(chain) for name, chain in chains.items()}
+
+    def step(name):
+        need, waits = needs[name]
+        if need is not None and need not in done:
+            return False
+        if waits:
             space()
         try:
-            link, us, latency, spend = next(entry[2])
+            needs[name] = next(chains[name])
         except StopIteration:
-            self.chains.remove(entry)
-            self.done.add(entry[0])
-            return
-        if link is None:
-            entry[3] = (us, 0.0, spend)
-            return
-        start = max(self.now, self.links.get(link, 0.0))
-        self.links[link] = start + us
-        entry[3] = (None, start + us + latency, spend)
-        self.now += 1.0
-
-    def ready(self, entry):
-        name, at, _ = entry[3]
-        if name is not None:
-            return 0.0 if name in self.done else 1e9
-        return at
-
-    def run(self, until=None):
-        while self.chains and (until is None or until not in self.done):
-            able = [e for e in self.chains if self.ready(e) <= self.now]
-            if able:
-                entry = min(able, key=lambda e: e[1])
-            else:
-                entry = min(self.chains, key=self.ready)
-                self.now = self.ready(entry)
-            self.now += entry[3][2]
-            self.step(entry)
+            del needs[name]
+            done.add(name)
+        return True
+
+    for name in order:
+        if not step(name):
+            raise ValueError(name)
+    while needs:
+        for name in list(needs):
+            step(name)
 
 
 def on_device(
@@ -1137,7 +1129,7 @@
     weight_out,
 ):
     share, d = tokens_in.shape
-    group = lax.axis_size("tensor")
+    group = lax.axis_size(TP)
     tokens = share * group
     heads = step_bias.shape[0]
     width = norm_gain.shape[0]
@@ -1145,13 +1137,13 @@
     count = tokens // L
     per = share // L
     half = group // 2
-    me = lax.axis_index("tensor")
-    place = lax.axis_index("dp")
+    me = lax.axis_index(TP)
+    place = lax.axis_index(DP)
 
     heads_pos = place * tokens + jnp.arange(count + 1, dtype=jnp.int32) * L
     starts = jnp.any(heads_pos[:, None] == scene_offsets[None, :], axis=1).astype(jnp.int32)
     meta = jnp.concatenate([me[None].astype(jnp.int32), place[None].astype(jnp.int32), starts])
-    masks, tmasks = masks_of("dp"), masks_of("tensor")
+    masks, tmasks = masks_of(DP), masks_of(TP)
     levels = len(masks)
 
     LAST.clear()
@@ -1159,14 +1151,14 @@
         mask = half // 2
         while mask:
             for f in [f for f in held if f in keys]:
-                held[f ^ mask] = swap(held[f], "tensor", mask)
+                held[f ^ mask] = swap(held[f], TP, mask)
             mask //= 2
 
     near, far = range(half), range(half, group)
     held = {0: tokens_in}
-    arrived = swap(tokens_in, "tensor", half)
+    arrived = swap(tokens_in, TP, half)
     spread_out(held, near)
-    dps = lax.axis_size("dp")
+    dps = lax.axis_size(DP)
     (last_rows,) = launch(
         lambda tok, _, o: hold_body(tok, o), [tokens_in, held[1]],
         [pl.BlockSpec((16, d), lambda i: (share // 16 - 1, 0)), pl.BlockSpec(memory_space=pl.ANY)],
@@ -1175,7 +1167,7 @@
     past = [
         lax.ppermute(
             last_rows,
-            ("dp", "tensor"),
+            (DP, TP),
             [(i * group + group - 1, (i + 1) * group + t) for i in range(dps - 1)],
         )
         for t in range(1, group, 2)
@@ -1191,19 +1183,18 @@
         [whole(a) for a in prep_ins],
         prep_outs, [whole(o) for o in prep_outs], "prep", vmem=4,
     )
-    def stretched(body, name, ins, outs, scratch, reverse, vmem, flops, span=None, old=()):
-        del flops
+    def stretched(body, name, ins, outs, scratch, reverse, vmem, span=None, old=()):
         begin, length = span or (0, count // per)
 
         def order(i):
             return count // per - 1 - i - begin if reverse else i + begin
 
         def spec(kind, shape):
-            if kind == "rows":
+            if kind == ROWS:
                 return pl.BlockSpec(
                     (share, shape[1]), lambda i, m: (lax.bitwise_xor(order(i), m[0]), 0)
                 )
-            if kind == "each":
+            if kind == EACH:
                 return pl.BlockSpec((per, *shape[1:]), lambda i, m: (order(i), 0, 0))
             return pl.BlockSpec(shape, lambda i, m: (0,) * len(shape))
 
@@ -1217,9 +1208,9 @@
                 pos = per - 1 - sub if reverse else sub
 
                 def view(kind, ref, pos=pos):
-                    if kind == "rows":
+                    if kind == ROWS:
                         return ref.at[pl.ds(pos * L, L)]
-                    return ref.at[pl.ds(pos, 1)] if kind == "each" else ref
+                    return ref.at[pl.ds(pos, 1)] if kind == EACH else ref
 
                 views = [view(k, r) for k, r in zip(kinds, refs)]
                 at = Spot(
@@ -1250,7 +1241,7 @@
     space()
     held[half] = hold(arrived, before[3])
     (own_past,) = simple(total_body, past, [shaped((16, d), BF)], "past")
-    past = [own_past, swap(own_past, "tensor", 1)]
+    past = [own_past, swap(own_past, TP, 1)]
     spread_out(held, far)
     before = project(meta, [held[half]], [], *weights, tokens, half, list(before))
     space()
@@ -1258,7 +1249,7 @@
         meta, [held[f] for f in far[1:]], past, *weights, tokens, half + 1, list(before)
     )
     cots = {0: grad_out}
-    cots[half] = swap(hold(grad_out, rim), "tensor", half)
+    cots[half] = swap(hold(grad_out, rim), TP, half)
 
     tall = (tokens, L)
     state_shape = (width, L)
@@ -1267,14 +1258,14 @@
     pre, sin, state, load, cum, pfx, decay = stretched(
         states_body,
         "states",
-        [("rows", cat), ("rows", step_raw), ("one", rim), ("one", vecs), ("one", hv),
-         ("one", mats)],
-        [("rows", (tokens, wide), F32), ("each", (count, *state_shape), BF),
-         ("one", state_shape, F32), ("one", load_shape, BF), ("rows", tall, F32),
-         ("each", (count, 8, L), F32), ("one", small, F32)],
+        [(ROWS, cat), (ROWS, step_raw), (ONE, rim), (ONE, vecs), (ONE, hv),
+         (ONE, mats)],
+        [(ROWS, (tokens, wide), F32), (EACH, (count, *state_shape), BF),
+         (ONE, state_shape, F32), (ONE, load_shape, BF), (ROWS, tall, F32),
+         (EACH, (count, 8, L), F32), (ONE, small, F32)],
         [pltpu.VMEM((per, L + 8, wide), F32), pltpu.VMEM(state_shape, F32),
          pltpu.VMEM(small, F32)],
-        False, 14, 2 * tokens * width * L * 3,
+        False, 14,
     )
 
     def link(level, reverse, held, load):
@@ -1288,19 +1279,19 @@
     thr = decay
     fresh = [jnp.zeros(state_shape, F32), jnp.ones(small, F32)]
     own = [state, decay, *fresh]
-    load = swap(load, "dp", 1)
+    load = swap(load, DP, 1)
     (y,) = stretched(
         within_body,
         "within",
-        [("rows", pre), ("rows", step_raw), ("rows", cum), ("each", sin), ("one", vecs),
-         ("one", hv), ("one", mats)],
-        [("rows", (tokens, width), F32)],
-        [], False, 14, 2 * tokens * width * L * 6,
+        [(ROWS, pre), (ROWS, step_raw), (ROWS, cum), (EACH, sin), (ONE, vecs),
+         (ONE, hv), (ONE, mats)],
+        [(ROWS, (tokens, width), F32)],
+        [], False, 14,
     )
     for level in range(levels - 1):
         space()
         own, load = link(level, False, own, load)
-        load = swap(load, "dp", masks[level + 1])
+        load = swap(load, DP, masks[level + 1])
         if level == 0:
             space()
             late = {half: hold(cots[half])}
@@ -1315,159 +1306,148 @@
     mixed, sums, incoming = stretched(
         functools.partial(gate_body, levels - 1),
         "gated",
-        [("rows", pre), ("rows", cum), ("each", pfx), ("rows", y), ("rows", gate_raw),
-         ("rows", gn), ("one", befores), ("one", throughs), ("one", load), ("one", vecs),
-         ("one", mats)],
-        [("rows", (tokens, width), F32), ("each", (count, 8, L), F32), ("one", state_shape, BF)],
-        [], False, 14, 2 * tokens * width * L * 4,
+        [(ROWS, pre), (ROWS, cum), (EACH, pfx), (ROWS, y), (ROWS, gate_raw),
+         (ROWS, gn), (ONE, befores), (ONE, throughs), (ONE, load), (ONE, vecs),
+         (ONE, mats)],
+        [(ROWS, (tokens, width), F32), (EACH, (count, 8, L), F32), (ONE, state_shape, BF)],
+        [], False, 14,
     )
     for mask in tmasks[::-1][:-1]:
-        got = swap(sums, "tensor", mask)
+        got = swap(sums, TP, mask)
         space()
         sums = add(sums, got)
-    sums2 = swap(sums, "tensor", 1)
+    sums2 = swap(sums, TP, 1)
     space()
-    normout, gm, ggr, gs, toward, load, sfx, gate_acc = stretched(
+    normout, gm, ggr, gs, toward, first_load, sfx, gate_acc = stretched(
         back_gate_body,
         "back_gated",
-        [("rows", pre), ("rows", cum), ("rows", mixed), ("rows", gate_raw), ("rows", gn),
-         ("each", sums), ("each", sums2), ("one", thr), ("one", vecs), ("one", mats)],
-        [("rows", (tokens, width), BF), ("rows", (tokens, width), BF),
-         ("rows", (tokens, width), BF), ("each", (count, *state_shape), BF),
-         ("one", state_shape, F32), ("one", load_shape, BF), ("each", (count, 8, L), F32),
-         ("one", (8, width), F32)],
+        [(ROWS, pre), (ROWS, cum), (ROWS, mixed), (ROWS, gate_raw), (ROWS, gn),
+         (EACH, sums), (EACH, sums2), (ONE, thr), (ONE, vecs), (ONE, mats)],
+        [(ROWS, (tokens, width), BF), (ROWS, (tokens, width), BF),
+         (ROWS, (tokens, width), BF), (EACH, (count, *state_shape), BF),
+         (ONE, state_shape, F32), (ONE, load_shape, BF), (EACH, (count, 8, L), F32),
+         (ONE, (8, width), F32)],
         [pltpu.VMEM(state_shape, F32), pltpu.VMEM(small, F32), pltpu.VMEM((16, width), F32)],
-        True, 14, 2 * tokens * width * L * 3,
-    )
-
-    plan = Plan()
-    kept = {}
+        True, 14,
+    )
+
+    kept = SimpleNamespace(within=())
+    done = set()
     blocks = d // width
-    axes = {"dp": ["y", "z", "z"] + ["z"] * levels, "tensor": ["core", "x"] + ["x"] * levels}
-    spans = {"dp": [1, 1, 2] + [2] * levels, "tensor": [1, 1] + [2] * levels}
-    hops = {"core": 2.5, "x": 5.0, "y": 5.0, "z": 6.0}
-    rates = {"core": 600.0, "x": 90.0, "y": 90.0, "z": 90.0}
-
-    def moved(x, axis, level):
-        link_name = axes[axis][level]
-        size = 2 * x.size * x.dtype.itemsize * spans[axis][level] / 1e3
-        got = swap(x, axis, 1 << level)
-        return got, link_name, size / rates[link_name], hops[link_name]
-
-    def halving(key, axis, send, keep, first=0):
-        top = len(masks_of(axis))
-        slot = 1 if axis == "dp" else 0
-        for level in range(first, top):
-            got, *way = moved(send, axis, level)
-            yield (*way, 0.8)
-            if level == top - 1:
-                kept[key] = add(keep, got)
+
+    def weights_chain(pairs, finish, need=None, last=None):
+        yield need, False
+        send, keep = wgrads(meta, [pairs()], width, blocks)
+        for level in range(levels):
+            got = swap(send, DP, masks[level])
+            yield None, True
+            if level < levels - 1:
+                send, keep = halve(meta, 1, level + 1, keep, got)
             else:
-                send, keep = halve(meta, slot, level + 1, keep, got)
-
-    def doubling(key, axis, x, finish):
-        slot = 1 if axis == "dp" else 0
-        for level in range(len(masks_of(axis)) - 1, -1, -1):
-            got, *way = moved(x, axis, level)
-            yield (*way, 2.0 if level == 0 else 0.7)
-            if level == 0:
-                if key == "I":
-                    yield (None, "WG", 0.0, 2.0)
-                finish(x, got)
-            else:
-                x = join(meta, slot, level, x, got)
-
-    def weights_chain(key, pairs, name, finish):
-        send, keep = wgrads(meta, pairs, width, blocks, name)
-        yield from halving(key, "dp", send, keep)
-        yield from doubling(key, "dp", kept[key], finish)
-
-    def inner_out(own, got):
-        kept["zx"] = rows_of(meta, own, got, 1, d, width, kept["zx"])
-
-    def out_gate(own, got):
-        kept["wout"], kept["zx"] = wg_out(meta, own, got, d, width)
-
-    def first_links():
-        own = [toward, thr, *fresh]
-        load = first_load
+                total = add(keep, got)
+        for level in range(levels - 1, -1, -1):
+            got = swap(total, DP, masks[level])
+            yield None if level else last, True
+            if level:
+                total = join(meta, 1, level, total, got)
+        finish(total, got)
+
+    def out_weights(own, got):
+        kept.wout = columns(meta, own, got, d, width)
+
+    def gate_weights(own, got):
+        kept.zx = rows_of(meta, own, got, 0, d, width, None)
+
+    def inner_weights(own, got):
+        kept.zx = rows_of(meta, own, got, 1, d, width, kept.zx)
+
+    def links_chain():
+        yield None, False
+        own, load = [toward, thr, *fresh], first_load
         for level in range(levels):
-            got, *way = moved(load, "dp", level)
-            if level == levels - 1:
-                kept["links"] = (*own[2:], got)
-                yield (*way, 0.0)
-            else:
-                yield (*way, 1.0)
+            got = swap(load, DP, masks[level])
+            yield None if level < levels - 1 else "F", True
+            if level < levels - 1:
                 own, load = link(level, True, own, got)
-
-    def within_part(begin, length):
-        kept["within"] = stretched(
-            back_within_body,
-            "back_within",
-            [("rows", pre), ("rows", step_raw), ("rows", cum), ("each", sin), ("each", pfx),
-             ("each", gs), ("rows", gm), ("one", incoming), ("one", vecs), ("one", hv),
-             ("one", mats)],
-            [("rows", (tokens, width), F32), ("rows", (tokens, 2 * L), F32), ("rows", tall, F32),
-             ("rows", tall, F32)],
-            [], True, 16, 2 * tokens * width * L * 12, (begin, length), kept.get("within", ()),
+        befores, throughs = own[2:]
+        ginner, gbc, glog, gst = kept.within
+        kept.gcat, kept.gsr, kept.head, kept.extra, kept.conv_acc, kept.head_acc = stretched(
+            functools.partial(back_conv_body, levels - 1),
+            "back_conv",
+            [(ROWS, cat), (ONE, rim), (ROWS, pre), (ROWS, step_raw), (ROWS, cum),
+             (EACH, sin), (EACH, pfx), (EACH, sfx), (ROWS, ginner), (ROWS, gbc),
+             (ROWS, glog), (ROWS, gst), (ONE, incoming), (ONE, befores), (ONE, throughs),
+             (ONE, got), (ONE, vecs), (ONE, hv), (ONE, mats)],
+            [(ROWS, (tokens, wide), BF), (ROWS, tall, BF), (ONE, (8, wide), F32),
+             (ONE, (16, wide), BF), (ONE, (8, wide), F32), (ONE, small, F32)],
+            [pltpu.VMEM((per, L + 8, wide), F32), pltpu.VMEM((40, wide), F32),
+             pltpu.VMEM((16, L), F32), pltpu.VMEM(state_shape, F32)],
+            True, 16,
         )
 
     def within_chain():
-        part = group // 2
-        for begin in range(0, group, part):
-            yield (None, "begin", 0.0, 6.0)
-            within_part(begin, part)
-
-    def scattered(key, frames_in):
+        for begin in (0, half):
+            yield None, False
+            kept.within = stretched(
+                back_within_body,
+                "back_within",
+                [(ROWS, pre), (ROWS, step_raw), (ROWS, cum), (EACH, sin), (EACH, pfx),
+                 (EACH, gs), (ROWS, gm), (ONE, incoming), (ONE, vecs), (ONE, hv), (ONE, mats)],
+                [(ROWS, (tokens, width), F32), (ROWS, (tokens, 2 * L), F32), (ROWS, tall, F32),
+                 (ROWS, tall, F32)],
+                [], True, 16, (begin, half), kept.within,
+            )
+
+    def scattered(frames_in):
         sums_in = []
-        for first in (half, 0):
+        for first in (0, half):
             part = dict(enumerate(frames_in[first : first + half]))
-            mask, level = 1, 0
+            mask = 1
             while mask < half:
-                sent = [(f, moved(part.pop(f), "tensor", level)) for f in list(part) if f & mask]
-                for f, (got, *way) in sent:
-                    yield (*way, 0.7)
+                for f in [f for f in part if f & mask]:
+                    got = swap(part.pop(f), TP, mask)
+                    yield None, True
                     part[f ^ mask] = add(part[f ^ mask], got)
-                mask, level = 2 * mask, level + 1
+                mask *= 2
             sums_in.append(part[0])
-            if first:
-                got, *way = moved(part[0], "tensor", level)
-                crossing_way = way
-                sums_in[0] = got
-        kept[key] = (sums_in[1], sums_in[0])
-        yield (*crossing_way, 1.6)
+        got = swap(sums_in[1], TP, half)
+        yield None, True
+        return sums_in[0], got
 
     def branch_chain():
-        yield (None, "begin", 0.0, 2.0)
-        branch = rows_times(
-            outproj_body, group, share, d, [normout], [weight_out], "outproj"
+        yield None, False
+        branch = rows_times(outproj_body, group, share, d, [normout], [weight_out], "outproj")
+        parts = yield from scattered(branch)
+        (kept.layer,) = simple(layer_body, [tokens_in, *parts], [shaped((share, d), BF)], "layer")
+
+    def tokens_chain():
+        yield "L", False
+        ahead = lax.ppermute(kept.head, DP, [(i + 1, i) for i in range(dps - 1)])
+        yield None, True
+        gcat = patched(meta, kept.gcat, ahead, vecs, share, group)
+        *grads, kept.shared = rows_times(
+            dgrad_body, group, share, d, [ggr, gcat, kept.gsr, normed],
+            [weight_zx, weight_bc, wst, gain, kept.conv_acc],
+            "dgrad", [shaped((16, ROW))], [pltpu.VMEM((8, d), F32)],
         )
-        yield from scattered("branch", branch)
-        (kept["layer"],) = simple(
-            layer_body, [tokens_in, *kept["branch"]], [shaped((share, d), BF)], "layer"
+        done.add("dgrad")
+        parts = yield from scattered(grads)
+        (kept.tokens,) = simple(
+            tokens_body, [tokens_in, grad_out, *parts, gain], [shaped((share, d))], "tokens",
+            None, 12,
         )
 
-    def tokens_chain():
-        ahead = lax.ppermute(kept["head"], "dp", [(i + 1, i) for i in range(dps - 1)])
-        yield ("halo", 0.5, 9.0, 5.4)
-        space()
-        space()
-        gcat = patched(meta, kept["gcat"], ahead, vecs, share, group)
-        grads = rows_times(
-            dgrad_body, group, share, d, [ggr, gcat, kept["gsr"]], [weight_zx, weight_bc, wst],
-            "dgrad",
+    def misc_chain():
+        yield "L", False
+        send, keep, step_acc = bc_wgrad(
+            meta, normed, kept.gcat, kept.gsr, normed_rim, kept.extra, width
         )
-        yield from scattered("grad", grads)
-        kept["tokens"], shared = simple(
-            tokens_body, [tokens_in, grad_out, *kept["grad"], gain, kept["conv_acc"]],
-            [shaped((share, d)), shaped((16, ROW))], "tokens", None, 12,
-        )
-        yield (None, "bc", 0.0, 0.5)
-        send, keep = kept["bc"]
+        yield "dgrad", False
+        shared = kept.shared
         (load,) = simple(lead_body, [send, shared], [shaped((send.shape[0] + 32, ROW), BF)], "lead")
         for level in range(len(tmasks)):
-            got, *way = moved(load, "tensor", level)
-            yield (*way, 0.6)
+            got = swap(load, TP, tmasks[level])
+            yield None, True
             if level < len(tmasks) - 1:
                 rows = keep.shape[0] // 2
                 load, keep, shared = simple(
@@ -1479,12 +1459,12 @@
         flat = rows + 8 * (d // ROW)
         (load,) = simple(
             misc_pack_body,
-            [keep, shared, got, kept["step_acc"], kept["conv_acc"], gate_acc, kept["head_acc"]],
+            [keep, shared, got, step_acc, kept.conv_acc, gate_acc, kept.head_acc],
             [shaped((flat + 96, ROW), BF)], "misc_pack",
         )
         for level in range(levels):
-            got, *way = moved(load, "dp", level)
-            yield (*way, 0.6)
+            got = swap(load, DP, masks[level])
+            yield None, True
             if level < levels - 1:
                 (load,) = simple(
                     functools.partial(misc_add_body, flat), [load, got],
@@ -1492,72 +1472,41 @@
                 )
         outs = [(1, d), (2, 4, L), (2, L), (heads, d), (4, width), (1, width), (1, heads),
                 (1, heads), (1, heads), (1, width)]
-        total, *kept["small"] = simple(
+        total, *kept.small = simple(
             functools.partial(misc_finish_body, rows), [load, got, mats],
             [shaped((rows, ROW), BF)] + [shaped(s) for s in outs], "misc_finish",
         )
-
-        def finish(own, got):
-            (kept["bc_out"],) = simple(
-                bc_out_body, [own, got], [shaped((2, d, L))], "bc_weights", meta
-            )
-
-        yield from doubling("bc", "tensor", total, finish)
-
-    def bc_chain():
-        yield (None, "begin", 0.0, 1.7)
-        send, keep, kept["step_acc"] = bc_wgrad(
-            meta, normed, kept["gcat"], kept["gsr"], normed_rim, kept["extra"], width
-        )
-        kept["bc"] = (send, keep)
-
-    plan.done.add("begin")
-    first_load = load
-    plan.add("links", 0, first_links())
-    plan.add(
-        "WG", 5,
-        weights_chain("WG", [(normout, cot_all, 1), (normed, ggr, 0)], "out_wgrad", out_gate),
-        4.3,
-    )
-    plan.add("within", 8, within_chain())
-    plan.add("branch", 9, branch_chain())
-    plan.run("links")
-    plan.run("within")
-    space()
-    befores, throughs, load = kept["links"]
-    ginner, gbc, glog, gst = kept["within"]
-    gcat, gsr, head, extra, conv_acc, head_acc = stretched(
-        functools.partial(back_conv_body, levels - 1),
-        "back_conv",
-        [("rows", cat), ("one", rim), ("rows", pre), ("rows", step_raw), ("rows", cum),
-         ("each", sin), ("each", pfx), ("each", sfx), ("rows", ginner), ("rows", gbc),
-         ("rows", glog), ("rows", gst), ("one", incoming), ("one", befores), ("one", throughs),
-         ("one", load), ("one", vecs), ("one", hv), ("one", mats)],
-        [("rows", (tokens, wide), BF), ("rows", tall, BF), ("one", (8, wide), F32),
-         ("one", (16, wide), BF), ("one", (8, wide), F32), ("one", small, F32)],
-        [pltpu.VMEM((per, L + 8, wide), F32), pltpu.VMEM((40, wide), F32), pltpu.VMEM((16, L), F32),
-         pltpu.VMEM(state_shape, F32)],
-        True, 16, 2 * tokens * width * L * 6,
-    )
-    plan.now += 10.0
-
-    kept.update(head=head, gcat=gcat, gsr=gsr, extra=extra, conv_acc=conv_acc, head_acc=head_acc)
-    plan.add("tokens", 2, tokens_chain())
-    plan.add(
-        "I", 1,
-        weights_chain("I", [(normed, gcat, 0, normed_rim, extra)], "inner_wgrad", inner_out),
-        2.7,
-    )
-    plan.add("bc", 3, bc_chain())
-    plan.run()
-
-    gain_g, bc_g, bcb_g, step_g, taps_g, bias_g, sb_g, dl_g, sk_g, ng_g = kept["small"]
+        for level in range(len(tmasks) - 1, -1, -1):
+            got = swap(total, TP, tmasks[level])
+            yield None, True
+            if level:
+                total = join(meta, 0, level, total, got)
+        (kept.bc,) = simple(bc_out_body, [total, got], [shaped((2, d, L))], "bc_weights", meta)
+
+    run_chains(
+        {
+            "L": links_chain(),
+            "W": weights_chain(lambda: (normout, cot_all, 1), out_weights),
+            "G": weights_chain(lambda: (normed, ggr, 0), gate_weights),
+            "F": within_chain(),
+            "B": branch_chain(),
+            "T": tokens_chain(),
+            "I": weights_chain(
+                lambda: (normed, kept.gcat, 0, normed_rim, kept.extra), inner_weights, "L", "G"
+            ),
+            "M": misc_chain(),
+        },
+        done,
+        ORDER if (dps, group) == (8, 4) else "",
+    )
+
+    gain_g, bc_g, bcb_g, step_g, taps_g, bias_g, sb_g, dl_g, sk_g, ng_g = kept.small
     return (
-        kept["layer"],
-        kept["tokens"],
+        kept.layer,
+        kept.tokens,
         gain_g[0],
-        kept["zx"],
-        kept["bc_out"],
+        kept.zx,
+        kept.bc,
         step_g.T,
         taps_g,
         bias_g[0],
@@ -1567,21 +1516,21 @@
         dl_g[0],
         sk_g[0],
         ng_g[0],
-        kept["wout"],
+        kept.wout,
     )
 
 
 def solution(mesh):
-    rows = P(("dp", "tensor"), None)
-    cols = P(None, "tensor")
-    one = P("tensor")
+    rows = P((DP, TP), None)
+    cols = P(None, TP)
+    one = P(TP)
     in_specs = (
-        rows, rows, P(), P(), P(None, None, "tensor"), P(), cols, cols, one, P(), P(),
-        one, one, one, one, P("tensor", None),
+        rows, rows, P(), P(), P(None, None, TP), P(), cols, cols, one, P(), P(),
+        one, one, one, one, P(TP, None),
     )
     out_specs = (
-        rows, rows, P(), P(None, None, "tensor"), P(), cols, cols, one, P(), P(),
-        one, one, one, one, P("tensor", None),
+        rows, rows, P(), P(None, None, TP), P(), cols, cols, one, P(), P(),
+        one, one, one, one, P(TP, None),
     )
     return jax.shard_map(
         on_device, mesh=mesh, in_specs=in_specs, out_specs=out_specs, check_vma=False

time: 204 us -> 194 us (0.951)
  waiting for transfers between devices: 62.7 us -> 40.7 us
  Pallas kernels: 86.6 us -> 91 us
  starting transfers between devices: 44.5 us -> 48.5 us
  local copies, waits for them, and re-layouts: 7.67 us -> 10.9 us
    ppermute x40 -> x46, waiting for transfers between devices: 62.7 us -> 34.7 us  [swap(): return lax.ppermute(x, axis, [(i, i ^ mask) for i in range(count)])]
    ppermute x3, waiting for transfers between devices: 0.01 us -> 6.04 us  [the longest x1 6.03 us: tokens_chain(): ahead = lax.ppermute(kept.head, DP, [(i + 1, i) for i in range(dps - 1)])]
    pallas_call x95 -> x105, Pallas kernels: 86.6 us -> 91 us  [launch(): pl.pallas_call(run, grid_spec=pltpu.PrefetchScalarGridSpec(num_scalar_pre...]
    ppermute x40 -> x46, starting transfers between devices: 41.9 us -> 45.9 us  [swap(): return lax.ppermute(x, axis, [(i, i ^ mask) for i in range(count)])]
    unnamed x52 -> x53, local copies, waits for them, and re-layouts: 7.65 us -> 10.8 us
  transfers between devices with their start and end apart: 43 -> 49, of which waited for: 18 -> 14; matrix products, arithmetic and copies ran while one was open for 0% -> 0% of each run, Pallas kernels for 37% -> 41%
where the time goes in v6:
time: 194 us
  Pallas kernels  91 us (47%)
  starting transfers between devices  48.5 us (25%)
  waiting for transfers between devices  40.7 us (21%)
  local copies, waits for them, and re-layouts  10.9 us (6%)
    pallas_call x105, Pallas kernels, launch(): pl.pallas_call(run, grid_spec=pltpu.PrefetchScalarGridSpec(num_scalar_pre...  91 us
    ppermute x46, starting transfers between devices, swap(): return lax.ppermute(x, axis, [(i, i ^ mask) for i in range(count)])  45.9 us
    ppermute x46, waiting for transfers between devices, swap(): return lax.ppermute(x, axis, [(i, i ^ mask) for i in range(count)])  34.7 us
    unnamed x53, local copies, waits for them, and re-layouts  10.8 us
    ppermute x1, waiting for transfers between devices, tokens_chain(): ahead = lax.ppermute(kept.head, DP, [(i + 1, i) for i in range(dps - 1)])  6.03 us
  transfers between devices with their start and end apart: 49, of which 14 were waited for; matrix products, arithmetic and copies ran while one was open for 0% of the time, Pallas kernels for 41%

profile of v6, /device:TPU:0, one launch (start us, length us, event | category | flops | bytes accessed | tf_op | source)
XLA Modules:
  0.0 193.5 jit_solution(12407178987943542164)
XLA Ops:
  1.2 2.6 %collective-permute-start = (bf16[256,1024]{1,0:T(8,128)(2,1)}, bf16[256,1024]{1,0:T(8,128)(2,1)S(1)}, u32[]{:S(2)}, u32[]{:S(2)}) collective-permute-start(bf16[256,1024]{1,0:T(8,128)(2,1)} %refs_0_.11), channel_id=1, source_target_pairs={{0,2},{1,3},{2,0},{3,1},{4,6},{5,7},{6,4},{7,5},{8,10},{9,11},{10,... | collective-permute-start | bytes 1572872 | tf_op jit(solution)/shard_map/ppermute | solution.py:773
  8.2 1.7 copy-done
  10.1 3.1 %project.3 = (bf16[1024,1024]{1,0:T(8,128)(2,1)S(1)}, bf16[1024,512]{1,0:T(8,128)(2,1)S(1)}, bf16[1024,768]{1,0:T(8,128)(2,1)S(1)}, bf16[1024,128]{1,0:T(8,128)(2,1)S(1)}) custom-call(s32[11]{0:T(128)S(1)} %pad_add_fusion.refs_0_, bf16[256,1024]{1,0:T(8,128)(2,1)S(1)} %copy-done.5, bf16[256,1024]{1,0:T(8,128)(2,1)S(1)} %collective-permute-done.1.refs_1_.refs_2_, ...), custom_call_target="tpu_custom_call" | custom-call | tf_op jit(solution)/shard_map/project/pallas_call | solution.py:87
  13.3 3.4 %collective-permute-done.refs_0_ = bf16[256,1024]{1,0:T(8,128)(2,1)S(1)} collective-permute-done((bf16[256,1024]{1,0:T(8,128)(2,1)}, bf16[256,1024]{1,0:T(8,128)(2,1)S(1)}, u32[]{:S(2)}, u32[]{:S(2)}) %collective-permute-start) | collective-permute-done | bytes 524320 | tf_op jit(solution)/shard_map/ppermute | solution.py:773
  17.4 1.8 project.4
  19.3 2.0 %project.5 = (bf16[1024,1024]{1,0:T(8,128)(2,1)S(1)}, bf16[1024,512]{1,0:T(8,128)(2,1)S(1)}, bf16[1024,768]{1,0:T(8,128)(2,1)S(1)}, bf16[1024,128]{1,0:T(8,128)(...) custom-call(s32[11]{0:T(128)S(1)} %pad_add_fusion.refs_0_, ...), custom_call_target="tpu_custom_call", output_to_operand_aliasing={{0}: (8, {}), {1}: (9, {}), {2}: (10, {}), {3}: (11, {})} | custom-call | tf_op jit(solution)/shard_map/project/pallas_call | solution.py:87
  21.4 1.6 collective-permute-start.7
  22.9 5.3 %states.1 = (f32[1024,768]{1,0:T(8,128)S(1)}, bf16[8,512,128]{2,1,0:T(8,128)(2,1)S(1)}, f32[512,128]{1,0:T(8,128)S(1)}, bf16[528,128]{1,0:T(8,128)(2,1)S(1)}, f3...) custom-call(s32[11]{0:T(128)S(1)} %pad_add_fusion.refs_0_, ...), custom_call_target="tpu_custom_call" | custom-call | tf_op jit(solution)/shard_map/states/pallas_call | solution.py:87
  28.3 1.6 collective-permute-start.8
  29.8 3.7 %within.1.refs_0_.refs_4_ = f32[1024,512]{1,0:T(8,128)S(1)} custom-call(s32[11]{0:T(128)S(1)} %pad_add_fusion.refs_0_, f32[1024,768]{1,0:T(8,128)S(1)} %get-tuple-element.144.refs_1_.refs_3_, bf16[1024,128]{1,0:T(8,128)(2,1)S(1)} %get-tuple-element.140.refs_2_.refs_4_, f32[1024,128]{1,0:T(8,128)S(1)} %get-tuple-element.145.refs_3_.refs_2_.refs_5_, ...), custom_call_target="tpu_custom_call" | custom-call | tf_op jit(solution)/shard_map/within/pallas_call | solution.py:87
  34.4 1.6 collective-permute-start.10
  36.1 3.3 %collective-permute-done.10.refs_5_ = bf16[528,128]{1,0:T(8,128)(2,1)S(1)} collective-permute-done((bf16[528,128]{1,0:T(8,128)(2,1)S(1)}, bf16[528,128]{1,0:T(8,128)(2,1)S(1)}, u32[]{:S(2)}, u32[]{:S(2)}) %collective-permute-start.10) | collective-permute-done | bytes 135200 | tf_op jit(solution)/shard_map/ppermute | solution.py:773
  40.9 2.6 %collective-permute-start.11 = (bf16[528,128]{1,0:T(8,128)(2,1)S(1)}, bf16[528,128]{1,0:T(8,128)(2,1)S(1)}, u32[]{:S(2)}, u32[]{:S(2)}) collective-permute-start(bf16[528,128]{1,0:T(8,128)(2,1)S(1)} %get-tuple-element.161), channel_id=1, source_target_pairs={{0,16},{4,20},{8,24},{12,28},{16,0},{20,4},{24,8},{28,12},{1,17},{... | collective-permute-start | bytes 405512 | tf_op jit(solution)/shard_map/ppermute | solution.py:773
  44.7 2.0 %cotangent.1 = (bf16[1024,1024]{1,0:T(8,128)(2,1)S(1)}, bf16[1024,512]{1,0:T(8,128)(2,1)S(1)}) custom-call(bf16[256,1024]{1,0:T(8,128)(2,1)S(1)} %copy-done.9, bf16[256,1024]{1,0:T(8,128)(2,1)S(1)} %collective-permute-done.6.refs_1_, bf16[256,1024]{1,0:T(8,128)(2,1)S(1)} %collective-permute-done.7.refs_0_.refs_2_, ...), custom_call_target="tpu_custom_call" | custom-call | tf_op jit(solution)/shard_map/cotangent/pallas_call | solution.py:87
  46.7 1.8 collective-permute-done.11.refs_9_
  48.5 4.9 %gated.1 = (f32[1024,512]{1,0:T(8,128)S(1)}, f32[8,8,128]{2,1,0:T(8,128)S(1)}, bf16[512,128]{1,0:T(8,128)(2,1)S(1)}) custom-call(s32[11]{0:T(128)S(1)} %pad_add_fusion.refs_0_, f32[1024,768]{1,0:T(8,128)S(1)} %get-tuple-element.144.refs_1_.refs_3_, f32[1024,128]{1,0:T(8,128)S(1)} %get-tuple-element.145.refs_3_.refs_2_.refs_5_, ...), custom_call_target="tpu_custom_call" | custom-call | tf_op jit(solution)/shard_map/gated/pallas_call | solution.py:87
  54.6 2.8 %collective-permute-done.12.refs_1_ = f32[8,8,128]{2,1,0:T(8,128)S(1)} collective-permute-done((f32[8,8,128]{2,1,0:T(8,128)S(1)}, f32[8,8,128]{2,1,0:T(8,128)S(1)}, u32[]{:S(2)}, u32[]{:S(2)}) %collective-permute-start.12) | collective-permute-done | bytes 32800 | tf_op jit(solution)/shard_map/ppermute | solution.py:773
  58.5 4.7 %back_gated.1 = (bf16[1024,512]{1,0:T(8,128)(2,1)S(1)}, bf16[1024,512]{1,0:T(8,128)(2,1)S(1)}, bf16[1024,512]{1,0:T(8,128)(2,1)S(1)}, bf16[8,512,128]{2,1,0:T(8,...) custom-call(s32[11]{0:T(128)S(1)} %pad_add_fusion.refs_0_, ...), custom_call_target="tpu_custom_call" | custom-call | tf_op jit(solution)/shard_map/back_gated/pallas_call | solution.py:87
  64.6 2.3 %wgrad.3 = (bf16[512,512]{1,0:T(8,128)(2,1)S(1)}, bf16[512,512]{1,0:T(8,128)(2,1)S(1)}) custom-call(s32[11]{0:T(128)S(1)} %pad_add_fusion.refs_0_, bf16[1024,512]{1,0:T(8,128)(2,1)S(1)} %get-tuple-element.164.refs_1_.refs_0_, bf16[1024,1024]{1,0:T(8,128)(2,1)S(1)} %get-tuple-element.173.refs_2_, f32[8,512]{1,0:T(8,128)S(1)} %get-tuple-element.174.refs_3_.refs_5_), custom_call_target="tpu_custom_call" | custom-call | tf_op jit(solution)/shard_map/wgrad/pallas_call | solution.py:87
  67.7 2.4 %wgrad.4 = (bf16[512,512]{1,0:T(8,128)(2,1)S(1)}, bf16[512,512]{1,0:T(8,128)(2,1)S(1)}) custom-call(s32[11]{0:T(128)S(1)} %pad_add_fusion.refs_0_, bf16[1024,1024]{1,0:T(8,128)(2,1)S(1)} %get-tuple-element.172.refs_1_.refs_3_, bf16[1024,512]{1,0:T(8,128)(2,1)S(1)} %get-tuple-element.165.refs_2_.refs_0_, bf16[512,512]{1,0:T(8,128)(2,1)S(1)} %get-tuple-element.175.refs_3_), custom_call_target="tpu_custom_call" | custom-call | tf_op jit(solution)/shard_map/wgrad/pallas_call | solution.py:87
  73.0 5.8 %back_within.2 = (f32[1024,512]{1,0:T(8,128)S(1)}, f32[1024,256]{1,0:T(8,128)S(1)}, f32[1024,128]{1,0:T(8,128)S(1)}, f32[1024,128]{1,0:T(8,128)S(1)}) custom-call(s32[11]{0:T(128)S(1)} %pad_add_fusion.refs_0_, f32[1024,768]{1,0:T(8,128)S(1)} %get-tuple-element.144.refs_1_.refs_3_, bf16[1024,128]{1,0:T(8,128)(2,1)S(1)} %get-tuple-element.140.refs_2_.refs_4_, ...), custom_call_target="tpu_custom_call" | custom-call | tf_op jit(solution)/shard_map/back_within/pallas_call | solution.py:87
  80.2 3.4 %collective-permute-start.17 = (bf16[528,128]{1,0:T(8,128)(2,1)S(1)}, bf16[528,128]{1,0:T(8,128)(2,1)S(1)}, u32[]{:S(2)}, u32[]{:S(2)}) collective-permute-start(bf16[528,128]{1,0:T(8,128)(2,1)S(1)} %get-tuple-element.195), channel_id=1, source_target_pairs={{0,16},{4,20},{8,24},{12,28},{16,0},{20,4},{24,8},{28,12},{1,17},{... | collective-permute-start | bytes 405512 | tf_op jit(solution)/shard_map/ppermute | solution.py:773
  84.4 5.8 %back_within.3 = (f32[1024,512]{1,0:T(8,128)S(1)}, f32[1024,256]{1,0:T(8,128)S(1)}, f32[1024,128]{1,0:T(8,128)S(1)}, f32[1024,128]{1,0:T(8,128)S(1)}) custom-call(s32[11]{0:T(128)S(1)} %pad_add_fusion.refs_0_, f32[1024,768]{1,0:T(8,128)S(1)} %get-tuple-element.144.refs_1_.refs_3_, ...), custom_call_target="tpu_custom_call", output_to_operand_aliasing={{0}: (12, {}), {1}: (13, {}), {2}: (14, {}), {3}: (15, {})} | custom-call | tf_op jit(solution)/shard_map/back_within/pallas_call | solution.py:87
  90.3 9.5 %back_conv.1 = (bf16[1024,768]{1,0:T(8,128)(2,1)S(1)}, bf16[1024,128]{1,0:T(8,128)(2,1)S(1)}, f32[8,768]{1,0:T(8,128)S(1)}, bf16[16,768]{1,0:T(8,128)(2,1)S(1)},...) custom-call(s32[11]{0:T(128)S(1)} %pad_add_fusion.refs_0_, bf16[1024,768]{1,0:T(8,128)(2,1)S(1)} %get-tuple-element.139.refs_1_, ...), custom_call_target="tpu_custom_call" | custom-call | tf_op jit(solution)/shard_map/back_conv/pallas_call | solution.py:87
  100.4 2.1 %collective-permute-start.20 = (bf16[256,512]{1,0:T(8,128)(2,1)S(1)}, bf16[256,512]{1,0:T(8,128)(2,1)S(1)}, u32[]{:S(2)}, u32[]{:S(2)}) collective-permute-start(bf16[256,512]{1,0:T(8,128)(2,1)S(1)} %get-tuple-element.201.refs_5_), channel_id=1, source_target_pairs={{0,8},{4,12},{8,0},{12,4},{16,24},{20,28},{24,16},{28,20},{1,9},{5... | collective-permute-start | bytes 786440 | tf_op jit(solution)/shard_map/ppermute | solution.py:773
  102.5 2.7 %wgrad.5 = (bf16[512,512]{1,0:T(8,128)(2,1)S(1)}, bf16[512,512]{1,0:T(8,128)(2,1)S(1)}) custom-call(s32[11]{0:T(128)S(1)} %pad_add_fusion.refs_0_, bf16[1024,1024]{1,0:T(8,128)(2,1)S(1)} %get-tuple-element.172.refs_1_.refs_3_, bf16[1024,768]{1,0:T(8,128)(2,1)S(1)} %get-tuple-element.196.refs_2_, bf16[16,1024]{1,0:T(8,128)(2,1)S(1)} %get-tuple-element.203.refs_3_.refs_4_, ...), custom_call_target="tpu_custom_call" | custom-call | tf_op jit(solution)/shard_map/wgrad/pallas_call | solution.py:87
  108.8 2.8 %collective-permute-start.27 = (bf16[128,512]{1,0:T(8,128)(2,1)S(1)}, bf16[128,512]{1,0:T(8,128)(2,1)S(1)}, u32[]{:S(2)}, u32[]{:S(2)}) collective-permute-start(bf16[128,512]{1,0:T(8,128)(2,1)S(1)} %get-tuple-element.207.refs_0_), channel_id=1, source_target_pairs={{0,16},{4,20},{8,24},{12,28},{16,0},{20,4},{24,8},{28,12},{1,17},{... | collective-permute-start | bytes 393224 | tf_op jit(solution)/shard_map/ppermute | solution.py:773
  111.8 6.0 %collective-permute-done.18.refs_2_ = f32[8,768]{1,0:T(8,128)S(1)} collective-permute-done((f32[8,768]{1,0:T(8,128)S(1)}, f32[8,768]{1,0:T(8,128)S(1)}, u32[]{:S(2)}, u32[]{:S(2)}) %collective-permute-start.18) | collective-permute-done | bytes 24608 | tf_op jit(solution)/shard_map/ppermute | solution.py:1425
  118.4 5.1 %dgrad.1 = (bf16[256,1024]{1,0:T(8,128)(2,1)S(1)}, bf16[256,1024]{1,0:T(8,128)(2,1)S(1)}, bf16[256,1024]{1,0:T(8,128)(2,1)S(1)}, bf16[256,1024]{1,0:T(8,128)(2,1)S(1)}, f32[16,256]{1,0:T(8,128)S(1)}) custom-call(bf16[1024,512]{1,0:T(8,128)(2,1)S(1)} %get-tuple-element.165.refs_2_.refs_0_, bf16[1024,768]{1,0:T(8,128)(2,1)S(1)} %patch.1.refs_1_, ...), custom_call_target="tpu_custom_call" | custom-call | tf_op jit(solution)/shard_map/dgrad/pallas_call | solution.py:87
  125.2 1.7 bc_wgrad.1
  128.4 2.2 %collective-permute-start.35 = (bf16[128,512]{1,0:T(8,128)(2,1)S(1)}, bf16[128,512]{1,0:T(8,128)(2,1)S(1)}, u32[]{:S(2)}, u32[]{:S(2)}) collective-permute-start(bf16[128,512]{1,0:T(8,128)(2,1)S(1)} %add.29.refs_0_.refs_1_), channel_id=1, source_target_pairs={{0,16},{4,20},{8,24},{12,28},{16,0},{20,4},{24,8},{28,12},{1,17},{... | collective-permute-start | bytes 393224 | tf_op jit(solution)/shard_map/ppermute | solution.py:773
  135.6 1.9 collective-permute-done.30.refs_2_
  137.6 4.2 %collective-permute-done.29.refs_2_ = bf16[256,512]{1,0:T(8,128)(2,1)S(1)} collective-permute-done((bf16[256,512]{1,0:T(8,128)(2,1)S(1)}, bf16[256,512]{1,0:T(8,128)(2,1)S(1)}, u32[]{:S(2)}, u32[]{:S(2)}) %collective-permute-start.29) | collective-permute-done | bytes 262176 | tf_op jit(solution)/shard_map/ppermute | solution.py:773
  143.1 1.5 collective-permute-start.37
  144.6 3.6 %collective-permute-done.34.refs_1_ = bf16[384,256]{1,0:T(8,128)(2,1)S(1)} collective-permute-done((bf16[384,256]{1,0:T(8,128)(2,1)S(1)}, bf16[384,256]{1,0:T(8,128)(2,1)S(1)}, u32[]{:S(2)}, u32[]{:S(2)}) %collective-permute-start.34) | collective-permute-done | bytes 196640 | tf_op jit(solution)/shard_map/ppermute | solution.py:773
  148.2 2.3 %collective-permute-start.39 = (bf16[384,256]{1,0:T(8,128)(2,1)S(1)}, bf16[384,256]{1,0:T(8,128)(2,1)S(1)}, u32[]{:S(2)}, u32[]{:S(2)}) collective-permute-start(bf16[384,256]{1,0:T(8,128)(2,1)S(1)} %misc_add.2.refs_0_), channel_id=1, source_target_pairs={{0,8},{4,12},{8,0},{12,4},{16,24},{20,28},{24,16},{28,20},{1,9},{5... | collective-permute-start | bytes 589832 | tf_op jit(solution)/shard_map/ppermute | solution.py:773
  152.7 1.5 tokens.1.refs_2_
  155.5 1.8 outproj.1
  159.8 1.9 collective-permute-done.36.refs_1_
  162.0 2.0 %collective-permute-start.41 = (bf16[384,256]{1,0:T(8,128)(2,1)S(1)}, bf16[384,256]{1,0:T(8,128)(2,1)S(1)}, u32[]{:S(2)}, u32[]{:S(2)}) collective-permute-start(bf16[384,256]{1,0:T(8,128)(2,1)S(1)} %misc_add.3.refs_0_), channel_id=1, source_target_pairs={{0,16},{4,20},{8,24},{12,28},{16,0},{20,4},{24,8},{28,12},{1,17},{... | collective-permute-start | bytes 589832 | tf_op jit(solution)/shard_map/ppermute | solution.py:773
  166.9 2.0 %out_weights.1.refs_0_ = f32[512,1024]{1,0:T(8,128)} custom-call(s32[11]{0:T(128)S(1)} %pad_add_fusion.refs_0_, bf16[512,512]{1,0:T(8,128)(2,1)S(1)} %join.9.refs_0_.refs_1_, bf16[512,512]{1,0:T(8,128)(2,1)S(1)} %collective-permute-done.44.refs_2_, f32[8,128]{1,0:T(8,128)S(1)} %space.80.refs_3_), custom_call_target="tpu_custom_call" | custom-call | tf_op jit(solution)/shard_map/out_weights/pallas_call | solution.py:87
  168.9 1.6 copy-done.18
  170.5 6.1 %collective-permute-done.43.refs_2_ = bf16[256,512]{1,0:T(8,128)(2,1)S(1)} collective-permute-done((bf16[256,512]{1,0:T(8,128)(2,1)S(1)}, bf16[256,512]{1,0:T(8,128)(2,1)S(1)}, u32[]{:S(2)}, u32[]{:S(2)}) %collective-permute-start.43) | collective-permute-done | bytes 262176 | tf_op jit(solution)/shard_map/ppermute | solution.py:773
  177.2 2.5 %collective-permute-start.46 = (bf16[512,512]{1,0:T(8,128)(2,1)S(1)}, bf16[512,512]{1,0:T(8,128)(2,1)S(1)}, u32[]{:S(2)}, u32[]{:S(2)}) collective-permute-start(bf16[512,512]{1,0:T(8,128)(2,1)S(1)} %join.12.refs_0_.refs_1_), channel_id=1, source_target_pairs={{0,4},{4,0},{8,12},{12,8},{16,20},{20,16},{24,28},{28,24},{1,5},{5... | collective-permute-start | bytes 1572872 | tf_op jit(solution)/shard_map/ppermute | solution.py:773
  182.2 2.0 %zx_weights.2.refs_3_ = f32[2,1024,512]{2,1,0:T(8,128)} custom-call(s32[11]{0:T(128)S(1)} %pad_add_fusion.refs_0_, bf16[512,512]{1,0:T(8,128)(2,1)S(1)} %join.10.refs_0_.refs_1_, bf16[512,512]{1,0:T(8,128)(2,1)S(1)} %collective-permute-done.47.refs_2_, f32[8,128]{1,0:T(8,128)S(1)} %space.83.refs_0_.refs_3_), custom_call_target="tpu_custom_call" | custom-call | tf_op jit(solution)/shard_map/zx_weights/pallas_call | solution.py:87
  184.2 1.8 collective-permute-done.45.refs_2_
  188.7 1.6 bc_weights.1.refs_0_
  191.5 2.0 %zx_weights.3 = f32[2,1024,512]{2,1,0:T(8,128)} custom-call(s32[11]{0:T(128)S(1)} %pad_add_fusion.refs_0_, bf16[512,512]{1,0:T(8,128)(2,1)S(1)} %join.12.refs_0_.refs_1_, bf16[512,512]{1,0:T(8,128)(2,1)S(1)} %collective-permute-done.46.refs_2_, f32[2,1024,512]{2,1,0:T(8,128)} %zx_weights.2.refs_3_, ...), custom_call_target="tpu_custom_call", output_to_operand_aliasing={{}: (3, {})} | custom-call | tf_op jit(solution)/shard_map/zx_weights/pallas_call | solution.py:87
  (214 shorter events, 49.3 us)
Async XLA Ops:
  0.6 4.1 %collective-permute-start.1 = (bf16[256,1024]{1,0:T(8,128)(2,1)}, bf16[256,1024]{1,0:T(8,128)(2,1)S(1)}, u32[]{:S(2)}, u32[]{:S(2)}) collective-permute-start(bf16[256,1024]{1,0:T(8,128)(2,1)} %refs_0_.11), channel_id=1, source_target_pairs={{0,1},{1,0},{2,3},{3,2},{4,5},{5,4},{6,7},{7,6},{8,9},{9,8},{10,11... | collective-permute-start | bytes 1572872 | tf_op jit(solution)/shard_map/ppermute | solution.py:773
  1.2 15.6 %collective-permute-start = (bf16[256,1024]{1,0:T(8,128)(2,1)}, bf16[256,1024]{1,0:T(8,128)(2,1)S(1)}, u32[]{:S(2)}, u32[]{:S(2)}) collective-permute-start(bf16[256,1024]{1,0:T(8,128)(2,1)} %refs_0_.11), channel_id=1, source_target_pairs={{0,2},{1,3},{2,0},{3,1},{4,6},{5,7},{6,4},{7,5},{8,10},{9,11},{10,... | collective-permute-start | bytes 1572872 | tf_op jit(solution)/shard_map/ppermute | solution.py:773
  3.7 39.7 %collective-permute-start.6 = (bf16[256,1024]{1,0:T(8,128)(2,1)}, bf16[256,1024]{1,0:T(8,128)(2,1)S(1)}, u32[]{:S(2)}, u32[]{:S(2)}) collective-permute-start(bf16[256,1024]{1,0:T(8,128)(2,1)} %refs_1_.4), channel_id=1, source_target_pairs={{0,1},{1,0},{2,3},{3,2},{4,5},{5,4},{6,7},{7,6},{8,9},{9,8},{10,11... | collective-permute-start | bytes 1572872 | tf_op jit(solution)/shard_map/ppermute | solution.py:773
  5.8 11.1 %collective-permute-start.4 = (bf16[16,1024]{1,0:T(8,128)(2,1)S(1)}, bf16[16,1024]{1,0:T(8,128)(2,1)S(1)}, u32[]{:S(2)}, u32[]{:S(2)}) collective-permute-start(bf16[16,1024]{1,0:T(8,128)(2,1)S(1)} %last_rows.1.refs_9_), channel_id=1, source_target_pairs={{3,7},{7,11},{11,15},{15,19},{19,23},{23,27},{27,31}} | collective-permute-start | bytes 98312 | tf_op jit(solution)/shard_map/ppermute | solution.py:1168
  6.4 10.4 %collective-permute-start.3 = (bf16[16,1024]{1,0:T(8,128)(2,1)S(1)}, bf16[16,1024]{1,0:T(8,128)(2,1)S(1)}, u32[]{:S(2)}, u32[]{:S(2)}) collective-permute-start(bf16[16,1024]{1,0:T(8,128)(2,1)S(1)} %last_rows.1.refs_9_), channel_id=1, source_target_pairs={{3,5},{7,9},{11,13},{15,17},{19,21},{23,25},{27,29}} | collective-permute-start | bytes 98312 | tf_op jit(solution)/shard_map/ppermute | solution.py:1168
  16.8 2.5 %collective-permute-start.2 = (bf16[256,1024]{1,0:T(8,128)(2,1)S(1)}, bf16[256,1024]{1,0:T(8,128)(2,1)S(1)}, u32[]{:S(2)}, u32[]{:S(2)}) collective-permute-start(bf16[256,1024]{1,0:T(8,128)(2,1)S(1)} %hold.3.refs_2_.refs_1_), channel_id=1, source_target_pairs={{0,1},{1,0},{2,3},{3,2},{4,5},{5,4},{6,7},{7,6},{8,9},{9,8},{10,11... | collective-permute-start | bytes 1572872 | tf_op jit(solution)/shard_map/ppermute | solution.py:773
  16.9 2.4 %collective-permute-start.5 = (bf16[16,1024]{1,0:T(8,128)(2,1)S(1)}, bf16[16,1024]{1,0:T(8,128)(2,1)S(1)}, u32[]{:S(2)}, u32[]{:S(2)}) collective-permute-start(bf16[16,1024]{1,0:T(8,128)(2,1)S(1)} %past.1.refs_10_.refs_0_.refs_2_), channel_id=1, source_target_pairs={{0,1},{1,0},{2,3},{3,2},{4,5},{5,4},{6,7},{7,6},{8,9},{9,8},{10,11... | collective-permute-start | bytes 98312 | tf_op jit(solution)/shard_map/ppermute | solution.py:773
  21.4 14.7 %collective-permute-start.7 = (bf16[256,1024]{1,0:T(8,128)(2,1)S(1)}, bf16[256,1024]{1,0:T(8,128)(2,1)S(1)}, u32[]{:S(2)}, u32[]{:S(2)}) collective-permute-start(bf16[256,1024]{1,0:T(8,128)(2,1)S(1)} %hold.4.refs_7_), channel_id=1, source_target_pairs={{0,2},{1,3},{2,0},{3,1},{4,6},{5,7},{6,4},{7,5},{8,10},{9,11},{10,... | collective-permute-start | bytes 1572872 | tf_op jit(solution)/shard_map/ppermute | solution.py:773
  28.3 5.3 %collective-permute-start.8 = (bf16[528,128]{1,0:T(8,128)(2,1)S(1)}, bf16[528,128]{1,0:T(8,128)(2,1)S(1)}, u32[]{:S(2)}, u32[]{:S(2)}) collective-permute-start(bf16[528,128]{1,0:T(8,128)(2,1)S(1)} %get-tuple-element.151), channel_id=1, source_target_pairs={{0,4},{4,0},{8,12},{12,8},{16,20},{20,16},{24,28},{28,24},{1,5},{5... | collective-permute-start | bytes 405512 | tf_op jit(solution)/shard_map/ppermute | solution.py:773
  34.4 5.1 %collective-permute-start.10 = (bf16[528,128]{1,0:T(8,128)(2,1)S(1)}, bf16[528,128]{1,0:T(8,128)(2,1)S(1)}, u32[]{:S(2)}, u32[]{:S(2)}) collective-permute-start(bf16[528,128]{1,0:T(8,128)(2,1)S(1)} %get-tuple-element.156), channel_id=1, source_target_pairs={{0,8},{4,12},{8,0},{12,4},{16,24},{20,28},{24,16},{28,20},{1,9},{5... | collective-permute-start | bytes 405512 | tf_op jit(solution)/shard_map/ppermute | solution.py:773
  36.1 7.4 %collective-permute-start.9 = (bf16[256,1024]{1,0:T(8,128)(2,1)S(1)}, bf16[256,1024]{1,0:T(8,128)(2,1)S(1)}, u32[]{:S(2)}, u32[]{:S(2)}) collective-permute-start(bf16[256,1024]{1,0:T(8,128)(2,1)S(1)} %hold.5.refs_0_), channel_id=1, source_target_pairs={{0,1},{1,0},{2,3},{3,2},{4,5},{5,4},{6,7},{7,6},{8,9},{9,8},{10,11... | collective-permute-start | bytes 1572872 | tf_op jit(solution)/shard_map/ppermute | solution.py:773
  40.9 7.6 %collective-permute-start.11 = (bf16[528,128]{1,0:T(8,128)(2,1)S(1)}, bf16[528,128]{1,0:T(8,128)(2,1)S(1)}, u32[]{:S(2)}, u32[]{:S(2)}) collective-permute-start(bf16[528,128]{1,0:T(8,128)(2,1)S(1)} %get-tuple-element.161), channel_id=1, source_target_pairs={{0,16},{4,20},{8,24},{12,28},{16,0},{20,4},{24,8},{28,12},{1,17},{... | collective-permute-start | bytes 405512 | tf_op jit(solution)/shard_map/ppermute | solution.py:773
  53.4 3.9 %collective-permute-start.12 = (f32[8,8,128]{2,1,0:T(8,128)S(1)}, f32[8,8,128]{2,1,0:T(8,128)S(1)}, u32[]{:S(2)}, u32[]{:S(2)}) collective-permute-start(f32[8,8,128]{2,1,0:T(8,128)S(1)} %get-tuple-element.163.refs_0_), channel_id=1, source_target_pairs={{0,2},{1,3},{2,0},{3,1},{4,6},{5,7},{6,4},{7,5},{8,10},{9,11},{10,... | collective-permute-start | bytes 98312 | tf_op jit(solution)/shard_map/ppermute | solution.py:773
  63.3 8.2 %collective-permute-start.14 = (bf16[528,128]{1,0:T(8,128)(2,1)S(1)}, bf16[528,128]{1,0:T(8,128)(2,1)S(1)}, u32[]{:S(2)}, u32[]{:S(2)}) collective-permute-start(bf16[528,128]{1,0:T(8,128)(2,1)S(1)} %get-tuple-element.171), channel_id=1, source_target_pairs={{0,4},{4,0},{8,12},{12,8},{16,20},{20,16},{24,28},{28,24},{1,5},{5... | collective-permute-start | bytes 405512 | tf_op jit(solution)/shard_map/ppermute | solution.py:773
  66.9 16.8 %collective-permute-start.15 = (bf16[512,512]{1,0:T(8,128)(2,1)S(1)}, bf16[512,512]{1,0:T(8,128)(2,1)S(1)}, u32[]{:S(2)}, u32[]{:S(2)}) collective-permute-start(bf16[512,512]{1,0:T(8,128)(2,1)S(1)} %get-tuple-element.175.refs_3_), channel_id=1, source_target_pairs={{0,4},{4,0},{8,12},{12,8},{16,20},{20,16},{24,28},{28,24},{1,5},{5... | collective-permute-start | bytes 1572872 | tf_op jit(solution)/shard_map/ppermute | solution.py:773
  70.2 29.6 %collective-permute-start.19 = (bf16[512,512]{1,0:T(8,128)(2,1)S(1)}, bf16[512,512]{1,0:T(8,128)(2,1)S(1)}, u32[]{:S(2)}, u32[]{:S(2)}) collective-permute-start(bf16[512,512]{1,0:T(8,128)(2,1)S(1)} %get-tuple-element.176.refs_0_), channel_id=1, source_target_pairs={{0,4},{4,0},{8,12},{12,8},{16,20},{20,16},{24,28},{28,24},{1,5},{5... | collective-permute-start | bytes 1572872 | tf_op jit(solution)/shard_map/ppermute | solution.py:773
  72.2 6.6 %collective-permute-start.16 = (bf16[528,128]{1,0:T(8,128)(2,1)S(1)}, bf16[528,128]{1,0:T(8,128)(2,1)S(1)}, u32[]{:S(2)}, u32[]{:S(2)}) collective-permute-start(bf16[528,128]{1,0:T(8,128)(2,1)S(1)} %get-tuple-element.186), channel_id=1, source_target_pairs={{0,8},{4,12},{8,0},{12,4},{16,24},{20,28},{24,16},{28,20},{1,9},{5... | collective-permute-start | bytes 405512 | tf_op jit(solution)/shard_map/ppermute | solution.py:773
  80.2 10.0 %collective-permute-start.17 = (bf16[528,128]{1,0:T(8,128)(2,1)S(1)}, bf16[528,128]{1,0:T(8,128)(2,1)S(1)}, u32[]{:S(2)}, u32[]{:S(2)}) collective-permute-start(bf16[528,128]{1,0:T(8,128)(2,1)S(1)} %get-tuple-element.195), channel_id=1, source_target_pairs={{0,16},{4,20},{8,24},{12,28},{16,0},{20,4},{24,8},{28,12},{1,17},{... | collective-permute-start | bytes 405512 | tf_op jit(solution)/shard_map/ppermute | solution.py:773
  84.3 23.2 %collective-permute-start.21 = (bf16[256,512]{1,0:T(8,128)(2,1)S(1)}, bf16[256,512]{1,0:T(8,128)(2,1)S(1)}, u32[]{:S(2)}, u32[]{:S(2)}) collective-permute-start(bf16[256,512]{1,0:T(8,128)(2,1)S(1)} %get-tuple-element.188.refs_16_), channel_id=1, source_target_pairs={{0,8},{4,12},{8,0},{12,4},{16,24},{20,28},{24,16},{28,20},{1,9},{5... | collective-permute-start | bytes 786440 | tf_op jit(solution)/shard_map/ppermute | solution.py:773
  100.4 7.6 %collective-permute-start.20 = (bf16[256,512]{1,0:T(8,128)(2,1)S(1)}, bf16[256,512]{1,0:T(8,128)(2,1)S(1)}, u32[]{:S(2)}, u32[]{:S(2)}) collective-permute-start(bf16[256,512]{1,0:T(8,128)(2,1)S(1)} %get-tuple-element.201.refs_5_), channel_id=1, source_target_pairs={{0,8},{4,12},{8,0},{12,4},{16,24},{20,28},{24,16},{28,20},{1,9},{5... | collective-permute-start | bytes 786440 | tf_op jit(solution)/shard_map/ppermute | solution.py:773
  105.2 19.4 %collective-permute-start.23 = (bf16[512,512]{1,0:T(8,128)(2,1)S(1)}, bf16[512,512]{1,0:T(8,128)(2,1)S(1)}, u32[]{:S(2)}, u32[]{:S(2)}) collective-permute-start(bf16[512,512]{1,0:T(8,128)(2,1)S(1)} %get-tuple-element.205.refs_0_), channel_id=1, source_target_pairs={{0,4},{4,0},{8,12},{12,8},{16,20},{20,16},{24,28},{28,24},{1,5},{5... | collective-permute-start | bytes 1572872 | tf_op jit(solution)/shard_map/ppermute | solution.py:773
  106.2 11.6 %collective-permute-start.18 = (f32[8,768]{1,0:T(8,128)S(1)}, f32[8,768]{1,0:T(8,128)S(1)}, u32[]{:S(2)}, u32[]{:S(2)}) collective-permute-start(f32[8,768]{1,0:T(8,128)S(1)} %get-tuple-element.197), channel_id=1, source_target_pairs={{4,0},{8,4},{12,8},{16,12},{20,16},{24,20},{28,24},{5,1},{9,5},{13... | collective-permute-start | bytes 73736 | tf_op jit(solution)/shard_map/ppermute | solution.py:1425
  108.8 19.5 %collective-permute-start.27 = (bf16[128,512]{1,0:T(8,128)(2,1)S(1)}, bf16[128,512]{1,0:T(8,128)(2,1)S(1)}, u32[]{:S(2)}, u32[]{:S(2)}) collective-permute-start(bf16[128,512]{1,0:T(8,128)(2,1)S(1)} %get-tuple-element.207.refs_0_), channel_id=1, source_target_pairs={{0,16},{4,20},{8,24},{12,28},{16,0},{20,4},{24,8},{28,12},{1,17},{... | collective-permute-start | bytes 393224 | tf_op jit(solution)/shard_map/ppermute | solution.py:773
  111.6 12.5 %collective-permute-start.24 = (bf16[128,512]{1,0:T(8,128)(2,1)S(1)}, bf16[128,512]{1,0:T(8,128)(2,1)S(1)}, u32[]{:S(2)}, u32[]{:S(2)}) collective-permute-start(bf16[128,512]{1,0:T(8,128)(2,1)S(1)} %get-tuple-element.206.refs_0_), channel_id=1, source_target_pairs={{0,16},{4,20},{8,24},{12,28},{16,0},{20,4},{24,8},{28,12},{1,17},{... | collective-permute-start | bytes 393224 | tf_op jit(solution)/shard_map/ppermute | solution.py:773
  123.6 4.5 %collective-permute-start.22 = (bf16[256,1024]{1,0:T(8,128)(2,1)S(1)}, bf16[256,1024]{1,0:T(8,128)(2,1)S(1)}, u32[]{:S(2)}, u32[]{:S(2)}) collective-permute-start(bf16[256,1024]{1,0:T(8,128)(2,1)S(1)} %get-tuple-element.211), channel_id=1, source_target_pairs={{0,1},{1,0},{2,3},{3,2},{4,5},{5,4},{6,7},{7,6},{8,9},{9,8},{10,11... | collective-permute-start | bytes 1572872 | tf_op jit(solution)/shard_map/ppermute | solution.py:773
  123.7 8.3 %collective-permute-start.25 = (bf16[256,1024]{1,0:T(8,128)(2,1)S(1)}, bf16[256,1024]{1,0:T(8,128)(2,1)S(1)}, u32[]{:S(2)}, u32[]{:S(2)}) collective-permute-start(bf16[256,1024]{1,0:T(8,128)(2,1)S(1)} %get-tuple-element.219), channel_id=1, source_target_pairs={{0,1},{1,0},{2,3},{3,2},{4,5},{5,4},{6,7},{7,6},{8,9},{9,8},{10,11... | collective-permute-start | bytes 1572872 | tf_op jit(solution)/shard_map/ppermute | solution.py:773
  124.2 9.3 %collective-permute-start.31 = (bf16[128,512]{1,0:T(8,128)(2,1)S(1)}, bf16[128,512]{1,0:T(8,128)(2,1)S(1)}, u32[]{:S(2)}, u32[]{:S(2)}) collective-permute-start(bf16[128,512]{1,0:T(8,128)(2,1)S(1)} %add.27.refs_0_.refs_1_), channel_id=1, source_target_pairs={{0,16},{4,20},{8,24},{12,28},{16,0},{20,4},{24,8},{28,12},{1,17},{... | collective-permute-start | bytes 393224 | tf_op jit(solution)/shard_map/ppermute | solution.py:773
  127.0 14.8 %collective-permute-start.29 = (bf16[256,512]{1,0:T(8,128)(2,1)S(1)}, bf16[256,512]{1,0:T(8,128)(2,1)S(1)}, u32[]{:S(2)}, u32[]{:S(2)}) collective-permute-start(bf16[256,512]{1,0:T(8,128)(2,1)S(1)} %get-tuple-element.215.refs_6_), channel_id=1, source_target_pairs={{0,8},{4,12},{8,0},{12,4},{16,24},{20,28},{24,16},{28,20},{1,9},{5... | collective-permute-start | bytes 786440 | tf_op jit(solution)/shard_map/ppermute | solution.py:773
  128.1 2.5 %collective-permute-start.26 = (bf16[544,256]{1,0:T(8,128)(2,1)S(1)}, bf16[544,256]{1,0:T(8,128)(2,1)S(1)}, u32[]{:S(2)}, u32[]{:S(2)}) collective-permute-start(bf16[544,256]{1,0:T(8,128)(2,1)S(1)} %lead.1.refs_0_), channel_id=1, source_target_pairs={{0,1},{1,0},{2,3},{3,2},{4,5},{5,4},{6,7},{7,6},{8,9},{9,8},{10,11... | collective-permute-start | bytes 835592 | tf_op jit(solution)/shard_map/ppermute | solution.py:773
  128.4 14.2 %collective-permute-start.35 = (bf16[128,512]{1,0:T(8,128)(2,1)S(1)}, bf16[128,512]{1,0:T(8,128)(2,1)S(1)}, u32[]{:S(2)}, u32[]{:S(2)}) collective-permute-start(bf16[128,512]{1,0:T(8,128)(2,1)S(1)} %add.29.refs_0_.refs_1_), channel_id=1, source_target_pairs={{0,16},{4,20},{8,24},{12,28},{16,0},{20,4},{24,8},{28,12},{1,17},{... | collective-permute-start | bytes 393224 | tf_op jit(solution)/shard_map/ppermute | solution.py:773
  131.1 6.4 %collective-permute-start.30 = (bf16[288,256]{1,0:T(8,128)(2,1)S(1)}, bf16[288,256]{1,0:T(8,128)(2,1)S(1)}, u32[]{:S(2)}, u32[]{:S(2)}) collective-permute-start(bf16[288,256]{1,0:T(8,128)(2,1)S(1)} %get-tuple-element.225), channel_id=1, source_target_pairs={{0,2},{1,3},{2,0},{3,1},{4,6},{5,7},{6,4},{7,5},{8,10},{9,11},{10,... | collective-permute-start | bytes 442376 | tf_op jit(solution)/shard_map/ppermute | solution.py:773
  134.1 16.4 %collective-permute-start.33 = (bf16[256,512]{1,0:T(8,128)(2,1)S(1)}, bf16[256,512]{1,0:T(8,128)(2,1)S(1)}, u32[]{:S(2)}, u32[]{:S(2)}) collective-permute-start(bf16[256,512]{1,0:T(8,128)(2,1)S(1)} %join.7.refs_0_.refs_1_), channel_id=1, source_target_pairs={{0,8},{4,12},{8,0},{12,4},{16,24},{20,28},{24,16},{28,20},{1,9},{5... | collective-permute-start | bytes 786440 | tf_op jit(solution)/shard_map/ppermute | solution.py:773
  134.5 17.5 %collective-permute-start.28 = (bf16[256,1024]{1,0:T(8,128)(2,1)S(1)}, bf16[256,1024]{1,0:T(8,128)(2,1)S(1)}, u32[]{:S(2)}, u32[]{:S(2)}) collective-permute-start(bf16[256,1024]{1,0:T(8,128)(2,1)S(1)} %add.30.refs_0_), channel_id=1, source_target_pairs={{0,2},{1,3},{2,0},{3,1},{4,6},{5,7},{6,4},{7,5},{8,10},{9,11},{10,... | collective-permute-start | bytes 1572872 | tf_op jit(solution)/shard_map/ppermute | solution.py:773
  142.4 9.1 %collective-permute-start.32 = (bf16[128,512]{1,0:T(8,128)(2,1)S(1)}, bf16[128,512]{1,0:T(8,128)(2,1)S(1)}, u32[]{:S(2)}, u32[]{:S(2)}) collective-permute-start(bf16[128,512]{1,0:T(8,128)(2,1)S(1)} %get-tuple-element.227.refs_0_), channel_id=1, source_target_pairs={{0,16},{4,20},{8,24},{12,28},{16,0},{20,4},{24,8},{28,12},{1,17},{... | collective-permute-start | bytes 393224 | tf_op jit(solution)/shard_map/ppermute | solution.py:773
  142.4 5.7 %collective-permute-start.34 = (bf16[384,256]{1,0:T(8,128)(2,1)S(1)}, bf16[384,256]{1,0:T(8,128)(2,1)S(1)}, u32[]{:S(2)}, u32[]{:S(2)}) collective-permute-start(bf16[384,256]{1,0:T(8,128)(2,1)S(1)} %misc_pack.1.refs_0_), channel_id=1, source_target_pairs={{0,4},{4,0},{8,12},{12,8},{16,20},{20,16},{24,28},{28,24},{1,5},{5... | collective-permute-start | bytes 589832 | tf_op jit(solution)/shard_map/ppermute | solution.py:773
  143.1 15.5 %collective-permute-start.37 = (bf16[256,512]{1,0:T(8,128)(2,1)S(1)}, bf16[256,512]{1,0:T(8,128)(2,1)S(1)}, u32[]{:S(2)}, u32[]{:S(2)}) collective-permute-start(bf16[256,512]{1,0:T(8,128)(2,1)S(1)} %join.8.refs_0_.refs_1_), channel_id=1, source_target_pairs={{0,8},{4,12},{8,0},{12,4},{16,24},{20,28},{24,16},{28,20},{1,9},{5... | collective-permute-start | bytes 786440 | tf_op jit(solution)/shard_map/ppermute | solution.py:773
  148.2 13.7 %collective-permute-start.39 = (bf16[384,256]{1,0:T(8,128)(2,1)S(1)}, bf16[384,256]{1,0:T(8,128)(2,1)S(1)}, u32[]{:S(2)}, u32[]{:S(2)}) collective-permute-start(bf16[384,256]{1,0:T(8,128)(2,1)S(1)} %misc_add.2.refs_0_), channel_id=1, source_target_pairs={{0,8},{4,12},{8,0},{12,4},{16,24},{20,28},{24,16},{28,20},{1,9},{5... | collective-permute-start | bytes 589832 | tf_op jit(solution)/shard_map/ppermute | solution.py:773
  151.1 15.8 %collective-permute-start.44 = (bf16[512,512]{1,0:T(8,128)(2,1)S(1)}, bf16[512,512]{1,0:T(8,128)(2,1)S(1)}, u32[]{:S(2)}, u32[]{:S(2)}) collective-permute-start(bf16[512,512]{1,0:T(8,128)(2,1)S(1)} %join.9.refs_0_.refs_1_), channel_id=1, source_target_pairs={{0,4},{4,0},{8,12},{12,8},{16,20},{20,16},{24,28},{28,24},{1,5},{5... | collective-permute-start | bytes 1572872 | tf_op jit(solution)/shard_map/ppermute | solution.py:773
  151.5 13.4 %collective-permute-start.42 = (bf16[128,512]{1,0:T(8,128)(2,1)S(1)}, bf16[128,512]{1,0:T(8,128)(2,1)S(1)}, u32[]{:S(2)}, u32[]{:S(2)}) collective-permute-start(bf16[128,512]{1,0:T(8,128)(2,1)S(1)} %add.31.refs_0_.refs_1_), channel_id=1, source_target_pairs={{0,16},{4,20},{8,24},{12,28},{16,0},{20,4},{24,8},{28,12},{1,17},{... | collective-permute-start | bytes 393224 | tf_op jit(solution)/shard_map/ppermute | solution.py:773
  159.2 23.0 %collective-permute-start.47 = (bf16[512,512]{1,0:T(8,128)(2,1)S(1)}, bf16[512,512]{1,0:T(8,128)(2,1)S(1)}, u32[]{:S(2)}, u32[]{:S(2)}) collective-permute-start(bf16[512,512]{1,0:T(8,128)(2,1)S(1)} %join.10.refs_0_.refs_1_), channel_id=1, source_target_pairs={{0,4},{4,0},{8,12},{12,8},{16,20},{20,16},{24,28},{28,24},{1,5},{5... | collective-permute-start | bytes 1572872 | tf_op jit(solution)/shard_map/ppermute | solution.py:773
  159.7 1.9 collective-permute-start.36
  161.7 2.3 %collective-permute-start.38 = (bf16[256,1024]{1,0:T(8,128)(2,1)S(1)}, bf16[256,1024]{1,0:T(8,128)(2,1)S(1)}, u32[]{:S(2)}, u32[]{:S(2)}) collective-permute-start(bf16[256,1024]{1,0:T(8,128)(2,1)S(1)} %get-tuple-element.230.refs_0_), channel_id=1, source_target_pairs={{0,1},{1,0},{2,3},{3,2},{4,5},{5,4},{6,7},{7,6},{8,9},{9,8},{10,11... | collective-permute-start | bytes 1572872 | tf_op jit(solution)/shard_map/ppermute | solution.py:773
  162.0 17.7 %collective-permute-start.41 = (bf16[384,256]{1,0:T(8,128)(2,1)S(1)}, bf16[384,256]{1,0:T(8,128)(2,1)S(1)}, u32[]{:S(2)}, u32[]{:S(2)}) collective-permute-start(bf16[384,256]{1,0:T(8,128)(2,1)S(1)} %misc_add.3.refs_0_), channel_id=1, source_target_pairs={{0,16},{4,20},{8,24},{12,28},{16,0},{20,4},{24,8},{28,12},{1,17},{... | collective-permute-start | bytes 589832 | tf_op jit(solution)/shard_map/ppermute | solution.py:773
  164.1 22.6 %collective-permute-start.40 = (bf16[256,1024]{1,0:T(8,128)(2,1)S(1)}, bf16[256,1024]{1,0:T(8,128)(2,1)S(1)}, u32[]{:S(2)}, u32[]{:S(2)}) collective-permute-start(bf16[256,1024]{1,0:T(8,128)(2,1)S(1)} %add.33.refs_0_), channel_id=1, source_target_pairs={{0,2},{1,3},{2,0},{3,1},{4,6},{5,7},{6,4},{7,5},{8,10},{9,11},{10,... | collective-permute-start | bytes 1572872 | tf_op jit(solution)/shard_map/ppermute | solution.py:773
  165.5 11.1 %collective-permute-start.43 = (bf16[256,512]{1,0:T(8,128)(2,1)S(1)}, bf16[256,512]{1,0:T(8,128)(2,1)S(1)}, u32[]{:S(2)}, u32[]{:S(2)}) collective-permute-start(bf16[256,512]{1,0:T(8,128)(2,1)S(1)} %join.11.refs_0_.refs_1_), channel_id=1, source_target_pairs={{0,8},{4,12},{8,0},{12,4},{16,24},{20,28},{24,16},{28,20},{1,9},{5... | collective-permute-start | bytes 786440 | tf_op jit(solution)/shard_map/ppermute | solution.py:773
  177.2 14.3 %collective-permute-start.46 = (bf16[512,512]{1,0:T(8,128)(2,1)S(1)}, bf16[512,512]{1,0:T(8,128)(2,1)S(1)}, u32[]{:S(2)}, u32[]{:S(2)}) collective-permute-start(bf16[512,512]{1,0:T(8,128)(2,1)S(1)} %join.12.refs_0_.refs_1_), channel_id=1, source_target_pairs={{0,4},{4,0},{8,12},{12,8},{16,20},{20,16},{24,28},{28,24},{1,5},{5... | collective-permute-start | bytes 1572872 | tf_op jit(solution)/shard_map/ppermute | solution.py:773
  181.1 5.0 %collective-permute-start.45 = (bf16[256,256]{1,0:T(8,128)(2,1)S(1)}, bf16[256,256]{1,0:T(8,128)(2,1)S(1)}, u32[]{:S(2)}, u32[]{:S(2)}) collective-permute-start(bf16[256,256]{1,0:T(8,128)(2,1)S(1)} %get-tuple-element.232.refs_1_), channel_id=1, source_target_pairs={{0,2},{1,3},{2,0},{3,1},{4,6},{5,7},{6,4},{7,5},{8,10},{9,11},{10,... | collective-permute-start | bytes 393224 | tf_op jit(solution)/shard_map/ppermute | solution.py:773
  186.6 2.1 %collective-permute-start.48 = (bf16[512,256]{1,0:T(8,128)(2,1)S(1)}, bf16[512,256]{1,0:T(8,128)(2,1)S(1)}, u32[]{:S(2)}, u32[]{:S(2)}) collective-permute-start(bf16[512,256]{1,0:T(8,128)(2,1)S(1)} %join.13.refs_0_.refs_1_), channel_id=1, source_target_pairs={{0,1},{1,0},{2,3},{3,2},{4,5},{5,4},{6,7},{7,6},{8,9},{9,8},{10,11... | collective-permute-start | bytes 786440 | tf_op jit(solution)/shard_map/ppermute | solution.py:773
  (27 other events, 177.1 us)

commit v7 on v6

--- a/solution.py
+++ b/solution.py
@@ -289,8 +289,8 @@
     return jnp.where(bit == (0 if reverse else 1), 1.0, 0.0)
 
 
-def link_body(level, reverse, meta, state, decay, before, through, load,
-              load_o, state_o, decay_o, before_o, through_o):
+def link_body(level, reverse, final, meta, state, decay, before, through, load,
+              load_o, before_o, through_o, *more):
     theirs, a = unpack(load)
     heads = theirs.shape[0] // HD
     ahead = is_ahead(meta, level, reverse)
@@ -302,9 +302,11 @@
         per_head(mine * ahead + (1.0 - ahead), heads) * theirs
         + per_head(a * (1.0 - ahead) + ahead, heads) * state[...]
     )
-    state_o[...] = joined
-    decay_o[...] = jnp.broadcast_to(mine * a, (8, L))
     pack(load_o, joined, mine * a)
+    if not final:
+        state_o, decay_o = more
+        state_o[...] = joined
+        decay_o[...] = jnp.broadcast_to(mine * a, (8, L))
 
 
 def final_link(meta, level, reverse, before, through, load):
@@ -350,7 +352,7 @@
     cum = dot_r(mats[:, width:], steps * hv[1:2, :])
     cum_o[...] = cum
     total = cum[L - 1 : L, :]
-    weights = dot_l(jnp.exp(total - cum) * steps, mats[:, :width])
+    weights = dot((jnp.exp(total - cum) * steps).astype(BF), mats[:, :width])
     inner = jnp.concatenate(acts[: width // L], axis=1)
     local = dot((inner * weights).astype(BF), acts[-2].astype(BF), 0, 0)
     entering = state[...] * keep
@@ -384,7 +386,7 @@
         jnp.int32, (L, L), 1
     )
     first = lax.broadcasted_iota(jnp.int32, (L, L), 1) < HD
-    grown = dot_l(jnp.exp(cum), mats[:, :width])
+    grown = dot(jnp.exp(cum).astype(BF), mats[:, :width])
     far = grown * dot(cb, sin[0], 1, 1)
     for pair in range(heads // 2):
         cols = slice(pair * L, pair * L + L)
@@ -402,7 +404,7 @@
     mixed_o, sums_o, incoming,
 ):
     width = vecs.shape[1] - 2 * L
-    ones = jnp.ones((8, width), BF)
+    ones = jnp.ones((8, L), BF)
 
     if at.first is not None:
 
@@ -410,7 +412,7 @@
         def _():
             incoming[...] = final_link(meta, level, False, before, through, load).astype(BF)
 
-    reach = dot_l(jnp.exp(cum[...]) * pfx[0][0:1, :], mats[:, :width])
+    reach = dot((jnp.exp(cum[...]) * pfx[0][0:1, :]).astype(BF), mats[:, :width])
     cv = pre[:, width + L :]
     cb = (cv * sigmoid(cv)).astype(BF)
     far = reach * dot(cb, incoming[...], 1, 1)
@@ -424,10 +426,10 @@
         gated = mixed * (g * sigmoid(g))
         squares.append(gated * gated)
         crosses.append(gn[:, cols].astype(F32) * vecs[6:7, cols] * gated)
-    square = dot_r(ones, jnp.concatenate(squares, axis=1), 1, 1)
-    cross = dot_r(ones, jnp.concatenate(crosses, axis=1), 1, 1)
-    row = lax.broadcasted_iota(jnp.int32, (8, L), 0)
-    sums_o[0] = jnp.where(row == 0, square, cross)
+    square = dot_r(ones, functools.reduce(jnp.add, squares), 1, 1)
+    cross = dot_r(ones, functools.reduce(jnp.add, crosses), 1, 1)
+    sums_o[0, 0:1] = square[0:1]
+    sums_o[0, 1:2] = cross[0:1]
 
 
 def back_gate_body(
@@ -453,7 +455,7 @@
     cubed = scale * scale * scale * cross * (1.0 / DI)
     cum = cum_r[...]
     total = cum[L - 1 : L, :]
-    grown = dot_l(jnp.exp(cum), mats[:, :width])
+    grown = dot(jnp.exp(cum).astype(BF), mats[:, :width])
     cv = pre[:, width + L :]
     cb = (cv * sigmoid(cv)).astype(BF)
     moved = []
@@ -525,8 +527,8 @@
     first = col < HD
     e = jnp.exp(cum)
     wd = jnp.exp(total - cum)
-    grown = dot_l(e, mats[:, :width])
-    weights = dot_l(wd * steps, mats[:, :width])
+    grown = dot(e.astype(BF), mats[:, :width])
+    weights = dot((wd * steps).astype(BF), mats[:, :width])
     gsb = gs[0]
     entering = sin[0].astype(F32) + per_head(pfx[0][0:1, :], heads) * incoming[...].astype(F32)
     eb = entering.astype(BF)
@@ -621,7 +623,7 @@
     cum = cum_r[...]
     total = cum[L - 1 : L, :]
     wd = jnp.exp(total - cum)
-    weights = dot_l(wd * steps, mats[:, :width])
+    weights = dot((wd * steps).astype(BF), mats[:, :width])
     far = outgoing[...] * per_head(sfx[0][0:1, :], heads)
     fb = far.astype(BF)
     entering = sin[0].astype(F32) + per_head(pfx[0][0:1, :], heads) * incoming[...].astype(F32)
@@ -892,44 +894,41 @@
     )
 
 
-def columns_body(blocks, meta, own, got, o):
-    width = o.shape[0]
-    bit = bit_at(meta, 0)
-    half = blocks // 2
-    for src, b in ((own, bit), (got, 1 - bit)):
-        for side in range(2):
-
-            @pl.when(b == side)
-            def _(src=src, side=side):
-                for k in range(half):
-                    at = (side * half + k) * width
-                    o[:, at : at + width] = src[k * width : (k + 1) * width, :].astype(F32)
-
-
-def columns(meta, own, got, d, width):
-    return simple(
-        functools.partial(columns_body, d // width), [own, got], [shaped((width, d))],
-        "out_weights", meta, 16,
-    )[0]
-
-
-def rows_body(meta, own, got, *rest):
-    zx_o = rest[-1]
-    bit = bit_at(meta, 0)
-    half = own.shape[0]
-    zx_o[0, pl.ds(pl.multiple_of(bit * half, half), half), :] = own[...].astype(F32)
-    zx_o[0, pl.ds(pl.multiple_of((1 - bit) * half, half), half), :] = got[...].astype(F32)
-
-
-def rows_of(meta, own, got, which, d, width, old):
-    ins, specs, aliases = [own, got], [whole(own), whole(got)], {}
+def columns_body(blocks, width, src, *rest):
+    o = rest[-1]
+    for k in range(blocks):
+        o[:, k * width : (k + 1) * width] = src[k * width : (k + 1) * width, :].astype(F32)
+
+
+def columns(meta, src, mine, d, width, old):
+    half = src.shape[0]
+    ins, specs, aliases = [src], [whole(src)], {}
     if old is not None:
         ins.append(old)
         specs.append(pl.BlockSpec(memory_space=pl.ANY))
-        aliases = {2: 0}
+        aliases = {1: 0}
     return launch(
-        rows_body, ins, specs, [shaped((2, d, width))],
-        [pl.BlockSpec((1, d, width), lambda i, m: (which, 0, 0))],
+        lambda meta, *refs: columns_body(half // width, width, *refs), ins, specs,
+        [shaped((width, d))],
+        [pl.BlockSpec((width, half), lambda i, m: (0, bit_at(m, 0) ^ (1 - mine)))],
+        "out_weights", meta=meta, aliases=aliases, vmem=16, token=False,
+    )[0]
+
+
+def rows_body(src, *rest):
+    rest[-1][0] = src[...].astype(F32)
+
+
+def rows_of(meta, src, mine, which, d, width, old):
+    half = src.shape[0]
+    ins, specs, aliases = [src], [whole(src)], {}
+    if old is not None:
+        ins.append(old)
+        specs.append(pl.BlockSpec(memory_space=pl.ANY))
+        aliases = {1: 0}
+    return launch(
+        lambda meta, *refs: rows_body(*refs), ins, specs, [shaped((2, d, width))],
+        [pl.BlockSpec((1, half, width), lambda i, m: (which, bit_at(m, 0) ^ (1 - mine), 0))],
         "zx_weights", meta=meta, aliases=aliases, vmem=16, token=False,
     )[0]
 
@@ -1083,7 +1082,7 @@
     last: Any
 
 
-ORDER = "LWGLFLWFLTGIWGTWIMMTGMTWMIGMWITBGBMBIWIMGMBMI"
+ORDER = "LWLFLGFWLGTIWMGTWMIGTMTWMIGMWTIBBMBGIMIMWBGMI"
 
 
 def run_chains(chains, done, order):
@@ -1248,8 +1247,6 @@
     normed, gate_raw, cat, step_raw, rim, normed_rim = project(
         meta, [held[f] for f in far[1:]], past, *weights, tokens, half + 1, list(before)
     )
-    cots = {0: grad_out}
-    cots[half] = swap(hold(grad_out, rim), TP, half)
 
     tall = (tokens, L)
     state_shape = (width, L)
@@ -1269,17 +1266,20 @@
     )
 
     def link(level, reverse, held, load):
-        shapes = [load_shape, state_shape, small, state_shape, small]
-        out = simple(
-            functools.partial(link_body, level, reverse), [*held, load],
+        final = level == levels - 2
+        shapes = [load_shape, state_shape, small] + ([] if final else [state_shape, small])
+        load, before, through, *more = simple(
+            functools.partial(link_body, level, reverse, final), [*held, load],
             [shaped(s, BF if j == 0 else F32) for j, s in enumerate(shapes)], "link", meta,
         )
-        return out[1:], out[0]
+        return [*more, before, through], load
 
     thr = decay
     fresh = [jnp.zeros(state_shape, F32), jnp.ones(small, F32)]
     own = [state, decay, *fresh]
     load = swap(load, DP, 1)
+    cots = {0: grad_out}
+    cots[half] = swap(hold(grad_out), TP, half)
     (y,) = stretched(
         within_body,
         "within",
@@ -1292,16 +1292,15 @@
         space()
         own, load = link(level, False, own, load)
         load = swap(load, DP, masks[level + 1])
-        if level == 0:
+        if level == levels - 2:
             space()
             late = {half: hold(cots[half])}
             spread_out(late, far)
             spread_out(cots, near)
             cots.update({f: late[f] for f in far[1:]})
-        if level == levels - 2:
             space()
             cot_all, gn = cotangent([cots[f] for f in range(group)], weight_out)
-    befores, throughs = own[2:]
+    befores, throughs = own[-2:]
     space()
     mixed, sums, incoming = stretched(
         functools.partial(gate_body, levels - 1),
@@ -1309,7 +1308,7 @@
         [(ROWS, pre), (ROWS, cum), (EACH, pfx), (ROWS, y), (ROWS, gate_raw),
          (ROWS, gn), (ONE, befores), (ONE, throughs), (ONE, load), (ONE, vecs),
          (ONE, mats)],
-        [(ROWS, (tokens, width), F32), (EACH, (count, 8, L), F32), (ONE, state_shape, BF)],
+        [(ROWS, (tokens, width), F32), (EACH, (count, 2, L), F32), (ONE, state_shape, BF)],
         [], False, 14,
     )
     for mask in tmasks[::-1][:-1]:
@@ -1331,11 +1330,11 @@
         True, 14,
     )
 
-    kept = SimpleNamespace(within=())
+    kept = SimpleNamespace(within=(), zx=None, wout=None)
     done = set()
     blocks = d // width
 
-    def weights_chain(pairs, finish, need=None, last=None):
+    def weights_chain(pairs, finish, need=None):
         yield need, False
         send, keep = wgrads(meta, [pairs()], width, blocks)
         for level in range(levels):
@@ -1347,19 +1346,21 @@
                 total = add(keep, got)
         for level in range(levels - 1, -1, -1):
             got = swap(total, DP, masks[level])
-            yield None if level else last, True
+            if not level:
+                finish(total, 1)
+            yield None, True
             if level:
                 total = join(meta, 1, level, total, got)
-        finish(total, got)
-
-    def out_weights(own, got):
-        kept.wout = columns(meta, own, got, d, width)
-
-    def gate_weights(own, got):
-        kept.zx = rows_of(meta, own, got, 0, d, width, None)
-
-    def inner_weights(own, got):
-        kept.zx = rows_of(meta, own, got, 1, d, width, kept.zx)
+        finish(got, 0)
+
+    def out_weights(src, mine):
+        kept.wout = columns(meta, src, mine, d, width, kept.wout)
+
+    def gate_weights(src, mine):
+        kept.zx = rows_of(meta, src, mine, 0, d, width, kept.zx)
+
+    def inner_weights(src, mine):
+        kept.zx = rows_of(meta, src, mine, 1, d, width, kept.zx)
 
     def links_chain():
         yield None, False
@@ -1369,7 +1370,7 @@
             yield None if level < levels - 1 else "F", True
             if level < levels - 1:
                 own, load = link(level, True, own, got)
-        befores, throughs = own[2:]
+        befores, throughs = own[-2:]
         ginner, gbc, glog, gst = kept.within
         kept.gcat, kept.gsr, kept.head, kept.extra, kept.conv_acc, kept.head_acc = stretched(
             functools.partial(back_conv_body, levels - 1),
@@ -1492,7 +1493,7 @@
             "B": branch_chain(),
             "T": tokens_chain(),
             "I": weights_chain(
-                lambda: (normed, kept.gcat, 0, normed_rim, kept.extra), inner_weights, "L", "G"
+                lambda: (normed, kept.gcat, 0, normed_rim, kept.extra), inner_weights, "L"
             ),
             "M": misc_chain(),
         },

time: 194 us -> 187 us (0.964)
  waiting for transfers between devices: 40.7 us -> 35.8 us
    ppermute x1, waiting for transfers between devices: 6.03 us -> 0.01 us  [tokens_chain(): ahead = lax.ppermute(kept.head, DP, [(i + 1, i) for i in range(dps - 1)])]
    unnamed x53 -> x50, local copies, waits for them, and re-layouts: 10.8 us -> 9.45 us
    pallas_call x105 -> x108, Pallas kernels: 91 us -> 90.6 us  [launch(): pl.pallas_call(run, grid_spec=pltpu.PrefetchScalarGridSpec(num_scalar_pre...]
  transfers between devices with their start and end apart: 49 -> 49, of which waited for: 14 -> 16; matrix products, arithmetic and copies ran while one was open for 0% -> 0% of each run, Pallas kernels for 41% -> 43%
where the time goes in v7:
time: 187 us; the launch traced here: 186 us
  Pallas kernels  90.6 us (48%)
  starting transfers between devices  47.9 us (26%)
  waiting for transfers between devices  35.8 us (19%)
  local copies, waits for them, and re-layouts  9.47 us (5%)
    pallas_call x108, Pallas kernels, launch(): pl.pallas_call(run, grid_spec=pltpu.PrefetchScalarGridSpec(num_scalar_pre...  90.6 us
    ppermute x46, starting transfers between devices, swap(): return lax.ppermute(x, axis, [(i, i ^ mask) for i in range(count)])  45.3 us
    ppermute x46, waiting for transfers between devices, swap(): return lax.ppermute(x, axis, [(i, i ^ mask) for i in range(count)])  35.8 us
    unnamed x50, local copies, waits for them, and re-layouts  9.45 us
  transfers between devices with their start and end apart: 49, of which 16 were waited for; matrix products, arithmetic and copies ran while one was open for 0% of the time, Pallas kernels for 43%

profile of v7, /device:TPU:0, one launch (start us, length us, event | category | flops | bytes accessed | tf_op | source)
XLA Modules:
  0.0 186.2 jit_solution(17703157669161323730)
XLA Ops:
  1.2 2.6 %collective-permute-start = (bf16[256,1024]{1,0:T(8,128)(2,1)}, bf16[256,1024]{1,0:T(8,128)(2,1)S(1)}, u32[]{:S(2)}, u32[]{:S(2)}) collective-permute-start(bf16[256,1024]{1,0:T(8,128)(2,1)} %refs_0_.11), channel_id=1, source_target_pairs={{0,2},{1,3},{2,0},{3,1},{4,6},{5,7},{6,4},{7,5},{8,10},{9,11},{10,... | collective-permute-start | bytes 1572872 | tf_op jit(solution)/shard_map/ppermute | solution.py:775
  8.2 1.7 copy-done
  10.1 3.1 %project.3 = (bf16[1024,1024]{1,0:T(8,128)(2,1)S(1)}, bf16[1024,512]{1,0:T(8,128)(2,1)S(1)}, bf16[1024,768]{1,0:T(8,128)(2,1)S(1)}, bf16[1024,128]{1,0:T(8,128)(2,1)S(1)}) custom-call(s32[11]{0:T(128)S(1)} %pad_add_fusion.refs_0_, bf16[256,1024]{1,0:T(8,128)(2,1)S(1)} %copy-done.5, bf16[256,1024]{1,0:T(8,128)(2,1)S(1)} %collective-permute-done.1.refs_1_.refs_2_, ...), custom_call_target="tpu_custom_call" | custom-call | tf_op jit(solution)/shard_map/project/pallas_call | solution.py:87
  13.3 3.5 %collective-permute-done.refs_0_ = bf16[256,1024]{1,0:T(8,128)(2,1)S(1)} collective-permute-done((bf16[256,1024]{1,0:T(8,128)(2,1)}, bf16[256,1024]{1,0:T(8,128)(2,1)S(1)}, u32[]{:S(2)}, u32[]{:S(2)}) %collective-permute-start) | collective-permute-done | bytes 524320 | tf_op jit(solution)/shard_map/ppermute | solution.py:775
  17.4 1.8 project.4
  19.3 2.0 %project.5 = (bf16[1024,1024]{1,0:T(8,128)(2,1)S(1)}, bf16[1024,512]{1,0:T(8,128)(2,1)S(1)}, bf16[1024,768]{1,0:T(8,128)(2,1)S(1)}, bf16[1024,128]{1,0:T(8,128)(...) custom-call(s32[11]{0:T(128)S(1)} %pad_add_fusion.refs_0_, ...), custom_call_target="tpu_custom_call", output_to_operand_aliasing={{0}: (8, {}), {1}: (9, {}), {2}: (10, {}), {3}: (11, {})} | custom-call | tf_op jit(solution)/shard_map/project/pallas_call | solution.py:87
  21.3 5.1 %states.1 = (f32[1024,768]{1,0:T(8,128)S(1)}, bf16[8,512,128]{2,1,0:T(8,128)(2,1)S(1)}, f32[512,128]{1,0:T(8,128)S(1)}, bf16[528,128]{1,0:T(8,128)(2,1)S(1)}, f3...) custom-call(s32[11]{0:T(128)S(1)} %pad_add_fusion.refs_0_, ...), custom_call_target="tpu_custom_call" | custom-call | tf_op jit(solution)/shard_map/states/pallas_call | solution.py:87
  26.4 1.6 collective-permute-start.8
  28.0 1.5 collective-permute-start.7
  29.6 3.6 %within.1.refs_0_.refs_4_ = f32[1024,512]{1,0:T(8,128)S(1)} custom-call(s32[11]{0:T(128)S(1)} %pad_add_fusion.refs_0_, f32[1024,768]{1,0:T(8,128)S(1)} %get-tuple-element.142.refs_1_.refs_3_, bf16[1024,128]{1,0:T(8,128)(2,1)S(1)} %get-tuple-element.138.refs_2_.refs_4_, f32[1024,128]{1,0:T(8,128)S(1)} %get-tuple-element.143.refs_3_.refs_2_.refs_5_, ...), custom_call_target="tpu_custom_call" | custom-call | tf_op jit(solution)/shard_map/within/pallas_call | solution.py:87
  34.0 1.7 collective-permute-start.9
  35.6 3.4 %collective-permute-done.9.refs_5_ = bf16[528,128]{1,0:T(8,128)(2,1)S(1)} collective-permute-done((bf16[528,128]{1,0:T(8,128)(2,1)S(1)}, bf16[528,128]{1,0:T(8,128)(2,1)S(1)}, u32[]{:S(2)}, u32[]{:S(2)}) %collective-permute-start.9) | collective-permute-done | bytes 135200 | tf_op jit(solution)/shard_map/ppermute | solution.py:775
  39.8 2.7 %collective-permute-start.11 = (bf16[528,128]{1,0:T(8,128)(2,1)S(1)}, bf16[528,128]{1,0:T(8,128)(2,1)S(1)}, u32[]{:S(2)}, u32[]{:S(2)}) collective-permute-start(bf16[528,128]{1,0:T(8,128)(2,1)S(1)} %get-tuple-element.158), channel_id=1, source_target_pairs={{0,16},{4,20},{8,24},{12,28},{16,0},{20,4},{24,8},{28,12},{1,17},{... | collective-permute-start | bytes 405512 | tf_op jit(solution)/shard_map/ppermute | solution.py:775
  42.6 1.9 %collective-permute-done.10.refs_3_ = bf16[256,1024]{1,0:T(8,128)(2,1)S(1)} collective-permute-done((bf16[256,1024]{1,0:T(8,128)(2,1)S(1)}, bf16[256,1024]{1,0:T(8,128)(2,1)S(1)}, u32[]{:S(2)}, u32[]{:S(2)}) %collective-permute-start.10) | collective-permute-done | bytes 524320 | tf_op jit(solution)/shard_map/ppermute | solution.py:775
  44.5 2.0 %cotangent.1 = (bf16[1024,1024]{1,0:T(8,128)(2,1)S(1)}, bf16[1024,512]{1,0:T(8,128)(2,1)S(1)}) custom-call(bf16[256,1024]{1,0:T(8,128)(2,1)S(1)} %copy-done.9, bf16[256,1024]{1,0:T(8,128)(2,1)S(1)} %collective-permute-done.6.refs_1_, bf16[256,1024]{1,0:T(8,128)(2,1)S(1)} %collective-permute-done.7.refs_0_.refs_2_, ...), custom_call_target="tpu_custom_call" | custom-call | tf_op jit(solution)/shard_map/cotangent/pallas_call | solution.py:87
  47.8 4.0 %gated.1 = (f32[1024,512]{1,0:T(8,128)S(1)}, f32[8,2,128]{2,1,0:T(2,128)S(1)}, bf16[512,128]{1,0:T(8,128)(2,1)S(1)}) custom-call(s32[11]{0:T(128)S(1)} %pad_add_fusion.refs_0_, f32[1024,768]{1,0:T(8,128)S(1)} %get-tuple-element.142.refs_1_.refs_3_, f32[1024,128]{1,0:T(8,128)S(1)} %get-tuple-element.143.refs_3_.refs_2_.refs_5_, ...), custom_call_target="tpu_custom_call" | custom-call | tf_op jit(solution)/shard_map/gated/pallas_call | solution.py:87
  52.7 2.8 %collective-permute-done.12.refs_1_ = f32[8,2,128]{2,1,0:T(2,128)S(1)} collective-permute-done((f32[8,2,128]{2,1,0:T(2,128)S(1)}, f32[8,2,128]{2,1,0:T(2,128)S(1)}, u32[]{:S(2)}, u32[]{:S(2)}) %collective-permute-start.12) | collective-permute-done | bytes 8224 | tf_op jit(solution)/shard_map/ppermute | solution.py:775
  56.7 4.4 %back_gated.1 = (bf16[1024,512]{1,0:T(8,128)(2,1)S(1)}, bf16[1024,512]{1,0:T(8,128)(2,1)S(1)}, bf16[1024,512]{1,0:T(8,128)(2,1)S(1)}, bf16[8,512,128]{2,1,0:T(8,...) custom-call(s32[11]{0:T(128)S(1)} %pad_add_fusion.refs_0_, ...), custom_call_target="tpu_custom_call" | custom-call | tf_op jit(solution)/shard_map/back_gated/pallas_call | solution.py:87
  61.7 2.3 %wgrad.3 = (bf16[512,512]{1,0:T(8,128)(2,1)S(1)}, bf16[512,512]{1,0:T(8,128)(2,1)S(1)}) custom-call(s32[11]{0:T(128)S(1)} %pad_add_fusion.refs_0_, bf16[1024,512]{1,0:T(8,128)(2,1)S(1)} %get-tuple-element.161.refs_1_.refs_0_, bf16[1024,1024]{1,0:T(8,128)(2,1)S(1)} %get-tuple-element.169.refs_2_, f32[8,512]{1,0:T(8,128)S(1)} %get-tuple-element.170.refs_3_.refs_5_), custom_call_target="tpu_custom_call" | custom-call | tf_op jit(solution)/shard_map/wgrad/pallas_call | solution.py:87
  64.0 1.6 collective-permute-start.17
  68.5 5.7 %back_within.2 = (f32[1024,512]{1,0:T(8,128)S(1)}, f32[1024,256]{1,0:T(8,128)S(1)}, f32[1024,128]{1,0:T(8,128)S(1)}, f32[1024,128]{1,0:T(8,128)S(1)}) custom-call(s32[11]{0:T(128)S(1)} %pad_add_fusion.refs_0_, f32[1024,768]{1,0:T(8,128)S(1)} %get-tuple-element.142.refs_1_.refs_3_, bf16[1024,128]{1,0:T(8,128)(2,1)S(1)} %get-tuple-element.138.refs_2_.refs_4_, ...), custom_call_target="tpu_custom_call" | custom-call | tf_op jit(solution)/shard_map/back_within/pallas_call | solution.py:87
  75.0 3.4 %collective-permute-start.16 = (bf16[528,128]{1,0:T(8,128)(2,1)S(1)}, bf16[528,128]{1,0:T(8,128)(2,1)S(1)}, u32[]{:S(2)}, u32[]{:S(2)}) collective-permute-start(bf16[528,128]{1,0:T(8,128)(2,1)S(1)} %get-tuple-element.189), channel_id=1, source_target_pairs={{0,16},{4,20},{8,24},{12,28},{16,0},{20,4},{24,8},{28,12},{1,17},{... | collective-permute-start | bytes 405512 | tf_op jit(solution)/shard_map/ppermute | solution.py:775
  78.4 2.3 %wgrad.4 = (bf16[512,512]{1,0:T(8,128)(2,1)S(1)}, bf16[512,512]{1,0:T(8,128)(2,1)S(1)}) custom-call(s32[11]{0:T(128)S(1)} %pad_add_fusion.refs_0_, bf16[1024,1024]{1,0:T(8,128)(2,1)S(1)} %get-tuple-element.162.refs_1_.refs_3_, bf16[1024,512]{1,0:T(8,128)(2,1)S(1)} %get-tuple-element.177.refs_2_.refs_0_, f32[8,128]{1,0:T(8,128)S(1)} %get-tuple-element.182.refs_3_.refs_15_), custom_call_target="tpu_custom_call" | custom-call | tf_op jit(solution)/shard_map/wgrad/pallas_call | solution.py:87
  81.0 5.5 %back_within.3 = (f32[1024,512]{1,0:T(8,128)S(1)}, f32[1024,256]{1,0:T(8,128)S(1)}, f32[1024,128]{1,0:T(8,128)S(1)}, f32[1024,128]{1,0:T(8,128)S(1)}) custom-call(s32[11]{0:T(128)S(1)} %pad_add_fusion.refs_0_, f32[1024,768]{1,0:T(8,128)S(1)} %get-tuple-element.142.refs_1_.refs_3_, ...), custom_call_target="tpu_custom_call", output_to_operand_aliasing={{0}: (12, {}), {1}: (13, {}), {2}: (14, {}), {3}: (15, {})} | custom-call | tf_op jit(solution)/shard_map/back_within/pallas_call | solution.py:87
  87.4 9.2 %back_conv.1 = (bf16[1024,768]{1,0:T(8,128)(2,1)S(1)}, bf16[1024,128]{1,0:T(8,128)(2,1)S(1)}, f32[8,768]{1,0:T(8,128)S(1)}, bf16[16,768]{1,0:T(8,128)(2,1)S(1)},...) custom-call(s32[11]{0:T(128)S(1)} %pad_add_fusion.refs_0_, bf16[1024,768]{1,0:T(8,128)(2,1)S(1)} %get-tuple-element.137.refs_1_, ...), custom_call_target="tpu_custom_call" | custom-call | tf_op jit(solution)/shard_map/back_conv/pallas_call | solution.py:87
  98.6 3.9 %collective-permute-start.22 = (bf16[256,512]{1,0:T(8,128)(2,1)S(1)}, bf16[256,512]{1,0:T(8,128)(2,1)S(1)}, u32[]{:S(2)}, u32[]{:S(2)}) collective-permute-start(bf16[256,512]{1,0:T(8,128)(2,1)S(1)} %get-tuple-element.197.refs_5_), channel_id=1, source_target_pairs={{0,8},{4,12},{8,0},{12,4},{16,24},{20,28},{24,16},{28,20},{1,9},{5... | collective-permute-start | bytes 786440 | tf_op jit(solution)/shard_map/ppermute | solution.py:775
  102.5 2.9 %wgrad.5 = (bf16[512,512]{1,0:T(8,128)(2,1)S(1)}, bf16[512,512]{1,0:T(8,128)(2,1)S(1)}) custom-call(s32[11]{0:T(128)S(1)} %pad_add_fusion.refs_0_, bf16[1024,1024]{1,0:T(8,128)(2,1)S(1)} %get-tuple-element.162.refs_1_.refs_3_, bf16[1024,768]{1,0:T(8,128)(2,1)S(1)} %get-tuple-element.192.refs_2_.refs_1_, ...), custom_call_target="tpu_custom_call" | custom-call | tf_op jit(solution)/shard_map/wgrad/pallas_call | solution.py:87
  107.6 1.7 bc_wgrad.1
  110.0 2.4 %collective-permute-start.27 = (bf16[128,512]{1,0:T(8,128)(2,1)S(1)}, bf16[128,512]{1,0:T(8,128)(2,1)S(1)}, u32[]{:S(2)}, u32[]{:S(2)}) collective-permute-start(bf16[128,512]{1,0:T(8,128)(2,1)S(1)} %get-tuple-element.207.refs_0_), channel_id=1, source_target_pairs={{0,16},{4,20},{8,24},{12,28},{16,0},{20,4},{24,8},{28,12},{1,17},{... | collective-permute-start | bytes 393224 | tf_op jit(solution)/shard_map/ppermute | solution.py:775
  113.0 4.9 %dgrad.1 = (bf16[256,1024]{1,0:T(8,128)(2,1)S(1)}, bf16[256,1024]{1,0:T(8,128)(2,1)S(1)}, bf16[256,1024]{1,0:T(8,128)(2,1)S(1)}, bf16[256,1024]{1,0:T(8,128)(2,1)S(1)}, f32[16,256]{1,0:T(8,128)S(1)}) custom-call(bf16[1024,512]{1,0:T(8,128)(2,1)S(1)} %get-tuple-element.177.refs_2_.refs_0_, bf16[1024,768]{1,0:T(8,128)(2,1)S(1)} %patch.1.refs_1_, ...), custom_call_target="tpu_custom_call" | custom-call | tf_op jit(solution)/shard_map/dgrad/pallas_call | solution.py:87
  125.8 3.4 %collective-permute-done.29.refs_2_ = bf16[128,512]{1,0:T(8,128)(2,1)S(1)} collective-permute-done((bf16[128,512]{1,0:T(8,128)(2,1)S(1)}, bf16[128,512]{1,0:T(8,128)(2,1)S(1)}, u32[]{:S(2)}, u32[]{:S(2)}) %collective-permute-start.29) | collective-permute-done | bytes 131104 | tf_op jit(solution)/shard_map/ppermute | solution.py:775
  130.8 2.3 %collective-permute-start.34 = (bf16[384,256]{1,0:T(8,128)(2,1)S(1)}, bf16[384,256]{1,0:T(8,128)(2,1)S(1)}, u32[]{:S(2)}, u32[]{:S(2)}) collective-permute-start(bf16[384,256]{1,0:T(8,128)(2,1)S(1)} %misc_pack.1.refs_0_), channel_id=1, source_target_pairs={{0,4},{4,0},{8,12},{12,8},{16,20},{20,16},{24,28},{28,24},{1,5},{5... | collective-permute-start | bytes 589832 | tf_op jit(solution)/shard_map/ppermute | solution.py:775
  136.3 1.9 %collective-permute-start.42 = (bf16[256,512]{1,0:T(8,128)(2,1)S(1)}, bf16[256,512]{1,0:T(8,128)(2,1)S(1)}, u32[]{:S(2)}, u32[]{:S(2)}) collective-permute-start(bf16[256,512]{1,0:T(8,128)(2,1)S(1)} %join.8.refs_0_.refs_1_), channel_id=1, source_target_pairs={{0,8},{4,12},{8,0},{12,4},{16,24},{20,28},{24,16},{28,20},{1,9},{5... | collective-permute-start | bytes 786440 | tf_op jit(solution)/shard_map/ppermute | solution.py:775
  138.6 3.1 %collective-permute-done.33.refs_2_ = bf16[256,512]{1,0:T(8,128)(2,1)S(1)} collective-permute-done((bf16[256,512]{1,0:T(8,128)(2,1)S(1)}, bf16[256,512]{1,0:T(8,128)(2,1)S(1)}, u32[]{:S(2)}, u32[]{:S(2)}) %collective-permute-start.33) | collective-permute-done | bytes 262176 | tf_op jit(solution)/shard_map/ppermute | solution.py:775
  142.3 1.5 collective-permute-start.48
  143.8 1.6 out_weights.2.refs_2_
  146.6 1.5 tokens.1.refs_0_
  150.9 1.8 outproj.1
  152.8 1.9 %collective-permute-done.36.refs_1_ = bf16[256,1024]{1,0:T(8,128)(2,1)S(1)} collective-permute-done((bf16[256,1024]{1,0:T(8,128)(2,1)S(1)}, bf16[256,1024]{1,0:T(8,128)(2,1)S(1)}, u32[]{:S(2)}, u32[]{:S(2)}) %collective-permute-start.36) | collective-permute-done | bytes 524320 | tf_op jit(solution)/shard_map/ppermute | solution.py:775
  155.0 1.6 collective-permute-start.40
  160.5 1.6 zx_weights.4.refs_2_
  162.1 5.4 %collective-permute-done.40.refs_1_ = bf16[384,256]{1,0:T(8,128)(2,1)S(1)} collective-permute-done((bf16[384,256]{1,0:T(8,128)(2,1)S(1)}, bf16[384,256]{1,0:T(8,128)(2,1)S(1)}, u32[]{:S(2)}, u32[]{:S(2)}) %collective-permute-start.40) | collective-permute-done | bytes 196640 | tf_op jit(solution)/shard_map/ppermute | solution.py:775
  171.2 1.6 zx_weights.5.refs_2_
  172.8 3.2 %collective-permute-done.43.refs_2_ = bf16[256,256]{1,0:T(8,128)(2,1)S(1)} collective-permute-done((bf16[256,256]{1,0:T(8,128)(2,1)S(1)}, bf16[256,256]{1,0:T(8,128)(2,1)S(1)}, u32[]{:S(2)}, u32[]{:S(2)}) %collective-permute-start.43) | collective-permute-done | bytes 131104 | tf_op jit(solution)/shard_map/ppermute | solution.py:775
  176.6 1.6 out_weights.3
  180.3 1.6 zx_weights.6.refs_2_
  181.8 1.6 bc_weights.1.refs_0_
  184.7 1.6 zx_weights.7
  (214 shorter events, 50.9 us)
Async XLA Ops:
  0.6 4.1 %collective-permute-start.1 = (bf16[256,1024]{1,0:T(8,128)(2,1)}, bf16[256,1024]{1,0:T(8,128)(2,1)S(1)}, u32[]{:S(2)}, u32[]{:S(2)}) collective-permute-start(bf16[256,1024]{1,0:T(8,128)(2,1)} %refs_0_.11), channel_id=1, source_target_pairs={{0,1},{1,0},{2,3},{3,2},{4,5},{5,4},{6,7},{7,6},{8,9},{9,8},{10,11... | collective-permute-start | bytes 1572872 | tf_op jit(solution)/shard_map/ppermute | solution.py:775
  1.2 15.6 %collective-permute-start = (bf16[256,1024]{1,0:T(8,128)(2,1)}, bf16[256,1024]{1,0:T(8,128)(2,1)S(1)}, u32[]{:S(2)}, u32[]{:S(2)}) collective-permute-start(bf16[256,1024]{1,0:T(8,128)(2,1)} %refs_0_.11), channel_id=1, source_target_pairs={{0,2},{1,3},{2,0},{3,1},{4,6},{5,7},{6,4},{7,5},{8,10},{9,11},{10,... | collective-permute-start | bytes 1572872 | tf_op jit(solution)/shard_map/ppermute | solution.py:775
  3.7 38.9 %collective-permute-start.6 = (bf16[256,1024]{1,0:T(8,128)(2,1)}, bf16[256,1024]{1,0:T(8,128)(2,1)S(1)}, u32[]{:S(2)}, u32[]{:S(2)}) collective-permute-start(bf16[256,1024]{1,0:T(8,128)(2,1)} %refs_1_.4), channel_id=1, source_target_pairs={{0,1},{1,0},{2,3},{3,2},{4,5},{5,4},{6,7},{7,6},{8,9},{9,8},{10,11... | collective-permute-start | bytes 1572872 | tf_op jit(solution)/shard_map/ppermute | solution.py:775
  5.8 11.1 %collective-permute-start.4 = (bf16[16,1024]{1,0:T(8,128)(2,1)S(1)}, bf16[16,1024]{1,0:T(8,128)(2,1)S(1)}, u32[]{:S(2)}, u32[]{:S(2)}) collective-permute-start(bf16[16,1024]{1,0:T(8,128)(2,1)S(1)} %last_rows.1.refs_9_), channel_id=1, source_target_pairs={{3,7},{7,11},{11,15},{15,19},{19,23},{23,27},{27,31}} | collective-permute-start | bytes 98312 | tf_op jit(solution)/shard_map/ppermute | solution.py:1167
  6.4 10.4 %collective-permute-start.3 = (bf16[16,1024]{1,0:T(8,128)(2,1)S(1)}, bf16[16,1024]{1,0:T(8,128)(2,1)S(1)}, u32[]{:S(2)}, u32[]{:S(2)}) collective-permute-start(bf16[16,1024]{1,0:T(8,128)(2,1)S(1)} %last_rows.1.refs_9_), channel_id=1, source_target_pairs={{3,5},{7,9},{11,13},{15,17},{19,21},{23,25},{27,29}} | collective-permute-start | bytes 98312 | tf_op jit(solution)/shard_map/ppermute | solution.py:1167
  16.8 2.5 %collective-permute-start.2 = (bf16[256,1024]{1,0:T(8,128)(2,1)S(1)}, bf16[256,1024]{1,0:T(8,128)(2,1)S(1)}, u32[]{:S(2)}, u32[]{:S(2)}) collective-permute-start(bf16[256,1024]{1,0:T(8,128)(2,1)S(1)} %hold.3.refs_2_.refs_1_), channel_id=1, source_target_pairs={{0,1},{1,0},{2,3},{3,2},{4,5},{5,4},{6,7},{7,6},{8,9},{9,8},{10,11... | collective-permute-start | bytes 1572872 | tf_op jit(solution)/shard_map/ppermute | solution.py:775
  16.9 2.4 %collective-permute-start.5 = (bf16[16,1024]{1,0:T(8,128)(2,1)S(1)}, bf16[16,1024]{1,0:T(8,128)(2,1)S(1)}, u32[]{:S(2)}, u32[]{:S(2)}) collective-permute-start(bf16[16,1024]{1,0:T(8,128)(2,1)S(1)} %past.1.refs_10_.refs_0_.refs_2_), channel_id=1, source_target_pairs={{0,1},{1,0},{2,3},{3,2},{4,5},{5,4},{6,7},{7,6},{8,9},{9,8},{10,11... | collective-permute-start | bytes 98312 | tf_op jit(solution)/shard_map/ppermute | solution.py:775
  26.4 6.8 %collective-permute-start.8 = (bf16[528,128]{1,0:T(8,128)(2,1)S(1)}, bf16[528,128]{1,0:T(8,128)(2,1)S(1)}, u32[]{:S(2)}, u32[]{:S(2)}) collective-permute-start(bf16[528,128]{1,0:T(8,128)(2,1)S(1)} %get-tuple-element.149), channel_id=1, source_target_pairs={{0,4},{4,0},{8,12},{12,8},{16,20},{20,16},{24,28},{28,24},{1,5},{5... | collective-permute-start | bytes 405512 | tf_op jit(solution)/shard_map/ppermute | solution.py:775
  28.0 14.4 %collective-permute-start.7 = (bf16[256,1024]{1,0:T(8,128)(2,1)S(1)}, bf16[256,1024]{1,0:T(8,128)(2,1)S(1)}, u32[]{:S(2)}, u32[]{:S(2)}) collective-permute-start(bf16[256,1024]{1,0:T(8,128)(2,1)S(1)} %hold.4.refs_8_), channel_id=1, source_target_pairs={{0,2},{1,3},{2,0},{3,1},{4,6},{5,7},{6,4},{7,5},{8,10},{9,11},{10,... | collective-permute-start | bytes 1572872 | tf_op jit(solution)/shard_map/ppermute | solution.py:775
  34.0 5.1 %collective-permute-start.9 = (bf16[528,128]{1,0:T(8,128)(2,1)S(1)}, bf16[528,128]{1,0:T(8,128)(2,1)S(1)}, u32[]{:S(2)}, u32[]{:S(2)}) collective-permute-start(bf16[528,128]{1,0:T(8,128)(2,1)S(1)} %get-tuple-element.154), channel_id=1, source_target_pairs={{0,8},{4,12},{8,0},{12,4},{16,24},{20,28},{24,16},{28,20},{1,9},{5... | collective-permute-start | bytes 405512 | tf_op jit(solution)/shard_map/ppermute | solution.py:775
  39.8 8.0 %collective-permute-start.11 = (bf16[528,128]{1,0:T(8,128)(2,1)S(1)}, bf16[528,128]{1,0:T(8,128)(2,1)S(1)}, u32[]{:S(2)}, u32[]{:S(2)}) collective-permute-start(bf16[528,128]{1,0:T(8,128)(2,1)S(1)} %get-tuple-element.158), channel_id=1, source_target_pairs={{0,16},{4,20},{8,24},{12,28},{16,0},{20,4},{24,8},{28,12},{1,17},{... | collective-permute-start | bytes 405512 | tf_op jit(solution)/shard_map/ppermute | solution.py:775
  42.5 2.0 %collective-permute-start.10 = (bf16[256,1024]{1,0:T(8,128)(2,1)S(1)}, bf16[256,1024]{1,0:T(8,128)(2,1)S(1)}, u32[]{:S(2)}, u32[]{:S(2)}) collective-permute-start(bf16[256,1024]{1,0:T(8,128)(2,1)S(1)} %hold.5.refs_0_), channel_id=1, source_target_pairs={{0,1},{1,0},{2,3},{3,2},{4,5},{5,4},{6,7},{7,6},{8,9},{9,8},{10,11... | collective-permute-start | bytes 1572872 | tf_op jit(solution)/shard_map/ppermute | solution.py:775
  51.8 3.7 %collective-permute-start.12 = (f32[8,2,128]{2,1,0:T(2,128)S(1)}, f32[8,2,128]{2,1,0:T(2,128)S(1)}, u32[]{:S(2)}, u32[]{:S(2)}) collective-permute-start(f32[8,2,128]{2,1,0:T(2,128)S(1)} %get-tuple-element.160.refs_0_), channel_id=1, source_target_pairs={{0,2},{1,3},{2,0},{3,1},{4,6},{5,7},{6,4},{7,5},{8,10},{9,11},{10,... | collective-permute-start | bytes 24584 | tf_op jit(solution)/shard_map/ppermute | solution.py:775
  61.1 6.0 %collective-permute-start.14 = (bf16[528,128]{1,0:T(8,128)(2,1)S(1)}, bf16[528,128]{1,0:T(8,128)(2,1)S(1)}, u32[]{:S(2)}, u32[]{:S(2)}) collective-permute-start(bf16[528,128]{1,0:T(8,128)(2,1)S(1)} %get-tuple-element.168), channel_id=1, source_target_pairs={{0,4},{4,0},{8,12},{12,8},{16,20},{20,16},{24,28},{28,24},{1,5},{5... | collective-permute-start | bytes 405512 | tf_op jit(solution)/shard_map/ppermute | solution.py:775
  64.0 22.6 %collective-permute-start.17 = (bf16[512,512]{1,0:T(8,128)(2,1)S(1)}, bf16[512,512]{1,0:T(8,128)(2,1)S(1)}, u32[]{:S(2)}, u32[]{:S(2)}) collective-permute-start(bf16[512,512]{1,0:T(8,128)(2,1)S(1)} %get-tuple-element.171.refs_0_), channel_id=1, source_target_pairs={{0,4},{4,0},{8,12},{12,8},{16,20},{20,16},{24,28},{28,24},{1,5},{5... | collective-permute-start | bytes 1572872 | tf_op jit(solution)/shard_map/ppermute | solution.py:775
  67.8 6.4 %collective-permute-start.15 = (bf16[528,128]{1,0:T(8,128)(2,1)S(1)}, bf16[528,128]{1,0:T(8,128)(2,1)S(1)}, u32[]{:S(2)}, u32[]{:S(2)}) collective-permute-start(bf16[528,128]{1,0:T(8,128)(2,1)S(1)} %get-tuple-element.181), channel_id=1, source_target_pairs={{0,8},{4,12},{8,0},{12,4},{16,24},{20,28},{24,16},{28,20},{1,9},{5... | collective-permute-start | bytes 405512 | tf_op jit(solution)/shard_map/ppermute | solution.py:775
  75.0 12.4 %collective-permute-start.16 = (bf16[528,128]{1,0:T(8,128)(2,1)S(1)}, bf16[528,128]{1,0:T(8,128)(2,1)S(1)}, u32[]{:S(2)}, u32[]{:S(2)}) collective-permute-start(bf16[528,128]{1,0:T(8,128)(2,1)S(1)} %get-tuple-element.189), channel_id=1, source_target_pairs={{0,16},{4,20},{8,24},{12,28},{16,0},{20,4},{24,8},{28,12},{1,17},{... | collective-permute-start | bytes 405512 | tf_op jit(solution)/shard_map/ppermute | solution.py:775
  80.7 17.2 %collective-permute-start.18 = (bf16[512,512]{1,0:T(8,128)(2,1)S(1)}, bf16[512,512]{1,0:T(8,128)(2,1)S(1)}, u32[]{:S(2)}, u32[]{:S(2)}) collective-permute-start(bf16[512,512]{1,0:T(8,128)(2,1)S(1)} %get-tuple-element.183.refs_16_), channel_id=1, source_target_pairs={{0,4},{4,0},{8,12},{12,8},{16,20},{20,16},{24,28},{28,24},{1,5},{5... | collective-permute-start | bytes 1572872 | tf_op jit(solution)/shard_map/ppermute | solution.py:775
  87.3 18.9 %collective-permute-start.20 = (bf16[256,512]{1,0:T(8,128)(2,1)S(1)}, bf16[256,512]{1,0:T(8,128)(2,1)S(1)}, u32[]{:S(2)}, u32[]{:S(2)}) collective-permute-start(bf16[256,512]{1,0:T(8,128)(2,1)S(1)} %get-tuple-element.191.refs_0_), channel_id=1, source_target_pairs={{0,8},{4,12},{8,0},{12,4},{16,24},{20,28},{24,16},{28,20},{1,9},{5... | collective-permute-start | bytes 786440 | tf_op jit(solution)/shard_map/ppermute | solution.py:775
  96.6 15.8 %collective-permute-start.21 = (f32[8,768]{1,0:T(8,128)S(1)}, f32[8,768]{1,0:T(8,128)S(1)}, u32[]{:S(2)}, u32[]{:S(2)}) collective-permute-start(f32[8,768]{1,0:T(8,128)S(1)} %get-tuple-element.204), channel_id=1, source_target_pairs={{4,0},{8,4},{12,8},{16,12},{20,16},{24,20},{28,24},{5,1},{9,5},{13... | collective-permute-start | bytes 73736 | tf_op jit(solution)/shard_map/ppermute | solution.py:1426
  98.6 10.7 %collective-permute-start.22 = (bf16[256,512]{1,0:T(8,128)(2,1)S(1)}, bf16[256,512]{1,0:T(8,128)(2,1)S(1)}, u32[]{:S(2)}, u32[]{:S(2)}) collective-permute-start(bf16[256,512]{1,0:T(8,128)(2,1)S(1)} %get-tuple-element.197.refs_5_), channel_id=1, source_target_pairs={{0,8},{4,12},{8,0},{12,4},{16,24},{20,28},{24,16},{28,20},{1,9},{5... | collective-permute-start | bytes 786440 | tf_op jit(solution)/shard_map/ppermute | solution.py:775
  105.4 14.3 %collective-permute-start.19 = (bf16[512,512]{1,0:T(8,128)(2,1)S(1)}, bf16[512,512]{1,0:T(8,128)(2,1)S(1)}, u32[]{:S(2)}, u32[]{:S(2)}) collective-permute-start(bf16[512,512]{1,0:T(8,128)(2,1)S(1)} %get-tuple-element.199.refs_0_), channel_id=1, source_target_pairs={{0,4},{4,0},{8,12},{12,8},{16,20},{20,16},{24,28},{28,24},{1,5},{5... | collective-permute-start | bytes 1572872 | tf_op jit(solution)/shard_map/ppermute | solution.py:775
  106.8 11.1 %collective-permute-start.23 = (bf16[128,512]{1,0:T(8,128)(2,1)S(1)}, bf16[128,512]{1,0:T(8,128)(2,1)S(1)}, u32[]{:S(2)}, u32[]{:S(2)}) collective-permute-start(bf16[128,512]{1,0:T(8,128)(2,1)S(1)} %get-tuple-element.202.refs_6_), channel_id=1, source_target_pairs={{0,16},{4,20},{8,24},{12,28},{16,0},{20,4},{24,8},{28,12},{1,17},{... | collective-permute-start | bytes 393224 | tf_op jit(solution)/shard_map/ppermute | solution.py:775
  110.0 11.8 %collective-permute-start.27 = (bf16[128,512]{1,0:T(8,128)(2,1)S(1)}, bf16[128,512]{1,0:T(8,128)(2,1)S(1)}, u32[]{:S(2)}, u32[]{:S(2)}) collective-permute-start(bf16[128,512]{1,0:T(8,128)(2,1)S(1)} %get-tuple-element.207.refs_0_), channel_id=1, source_target_pairs={{0,16},{4,20},{8,24},{12,28},{16,0},{20,4},{24,8},{28,12},{1,17},{... | collective-permute-start | bytes 393224 | tf_op jit(solution)/shard_map/ppermute | solution.py:775
  118.0 11.1 %collective-permute-start.29 = (bf16[128,512]{1,0:T(8,128)(2,1)S(1)}, bf16[128,512]{1,0:T(8,128)(2,1)S(1)}, u32[]{:S(2)}, u32[]{:S(2)}) collective-permute-start(bf16[128,512]{1,0:T(8,128)(2,1)S(1)} %add.27.refs_2_.refs_1_), channel_id=1, source_target_pairs={{0,16},{4,20},{8,24},{12,28},{16,0},{20,4},{24,8},{28,12},{1,17},{... | collective-permute-start | bytes 393224 | tf_op jit(solution)/shard_map/ppermute | solution.py:775
  119.1 4.8 %collective-permute-start.25 = (bf16[544,256]{1,0:T(8,128)(2,1)S(1)}, bf16[544,256]{1,0:T(8,128)(2,1)S(1)}, u32[]{:S(2)}, u32[]{:S(2)}) collective-permute-start(bf16[544,256]{1,0:T(8,128)(2,1)S(1)} %lead.1.refs_0_), channel_id=1, source_target_pairs={{0,1},{1,0},{2,3},{3,2},{4,5},{5,4},{6,7},{7,6},{8,9},{9,8},{10,11... | collective-permute-start | bytes 835592 | tf_op jit(solution)/shard_map/ppermute | solution.py:775
  119.2 3.4 %collective-permute-start.26 = (bf16[256,1024]{1,0:T(8,128)(2,1)S(1)}, bf16[256,1024]{1,0:T(8,128)(2,1)S(1)}, u32[]{:S(2)}, u32[]{:S(2)}) collective-permute-start(bf16[256,1024]{1,0:T(8,128)(2,1)S(1)} %get-tuple-element.215), channel_id=1, source_target_pairs={{0,1},{1,0},{2,3},{3,2},{4,5},{5,4},{6,7},{7,6},{8,9},{9,8},{10,11... | collective-permute-start | bytes 1572872 | tf_op jit(solution)/shard_map/ppermute | solution.py:775
  119.7 4.8 %collective-permute-start.30 = (bf16[256,1024]{1,0:T(8,128)(2,1)S(1)}, bf16[256,1024]{1,0:T(8,128)(2,1)S(1)}, u32[]{:S(2)}, u32[]{:S(2)}) collective-permute-start(bf16[256,1024]{1,0:T(8,128)(2,1)S(1)} %get-tuple-element.221), channel_id=1, source_target_pairs={{0,1},{1,0},{2,3},{3,2},{4,5},{5,4},{6,7},{7,6},{8,9},{9,8},{10,11... | collective-permute-start | bytes 1572872 | tf_op jit(solution)/shard_map/ppermute | solution.py:775
  121.9 13.8 %collective-permute-start.35 = (bf16[128,512]{1,0:T(8,128)(2,1)S(1)}, bf16[128,512]{1,0:T(8,128)(2,1)S(1)}, u32[]{:S(2)}, u32[]{:S(2)}) collective-permute-start(bf16[128,512]{1,0:T(8,128)(2,1)S(1)} %add.28.refs_0_.refs_1_), channel_id=1, source_target_pairs={{0,16},{4,20},{8,24},{12,28},{16,0},{20,4},{24,8},{28,12},{1,17},{... | collective-permute-start | bytes 393224 | tf_op jit(solution)/shard_map/ppermute | solution.py:775
  122.5 11.7 %collective-permute-start.24 = (bf16[256,512]{1,0:T(8,128)(2,1)S(1)}, bf16[256,512]{1,0:T(8,128)(2,1)S(1)}, u32[]{:S(2)}, u32[]{:S(2)}) collective-permute-start(bf16[256,512]{1,0:T(8,128)(2,1)S(1)} %get-tuple-element.212.refs_0_), channel_id=1, source_target_pairs={{0,8},{4,12},{8,0},{12,4},{16,24},{20,28},{24,16},{28,20},{1,9},{5... | collective-permute-start | bytes 786440 | tf_op jit(solution)/shard_map/ppermute | solution.py:775
  124.7 6.1 %collective-permute-start.28 = (bf16[288,256]{1,0:T(8,128)(2,1)S(1)}, bf16[288,256]{1,0:T(8,128)(2,1)S(1)}, u32[]{:S(2)}, u32[]{:S(2)}) collective-permute-start(bf16[288,256]{1,0:T(8,128)(2,1)S(1)} %get-tuple-element.219), channel_id=1, source_target_pairs={{0,2},{1,3},{2,0},{3,1},{4,6},{5,7},{6,4},{7,5},{8,10},{9,11},{10,... | collective-permute-start | bytes 442376 | tf_op jit(solution)/shard_map/ppermute | solution.py:775
  129.7 12.0 %collective-permute-start.33 = (bf16[256,512]{1,0:T(8,128)(2,1)S(1)}, bf16[256,512]{1,0:T(8,128)(2,1)S(1)}, u32[]{:S(2)}, u32[]{:S(2)}) collective-permute-start(bf16[256,512]{1,0:T(8,128)(2,1)S(1)} %join.7.refs_0_.refs_1_), channel_id=1, source_target_pairs={{0,8},{4,12},{8,0},{12,4},{16,24},{20,28},{24,16},{28,20},{1,9},{5... | collective-permute-start | bytes 786440 | tf_op jit(solution)/shard_map/ppermute | solution.py:775
  129.8 15.6 %collective-permute-start.32 = (bf16[256,1024]{1,0:T(8,128)(2,1)S(1)}, bf16[256,1024]{1,0:T(8,128)(2,1)S(1)}, u32[]{:S(2)}, u32[]{:S(2)}) collective-permute-start(bf16[256,1024]{1,0:T(8,128)(2,1)S(1)} %add.30.refs_0_), channel_id=1, source_target_pairs={{0,2},{1,3},{2,0},{3,1},{4,6},{5,7},{6,4},{7,5},{8,10},{9,11},{10,... | collective-permute-start | bytes 1572872 | tf_op jit(solution)/shard_map/ppermute | solution.py:775
  130.8 7.3 %collective-permute-start.34 = (bf16[384,256]{1,0:T(8,128)(2,1)S(1)}, bf16[384,256]{1,0:T(8,128)(2,1)S(1)}, u32[]{:S(2)}, u32[]{:S(2)}) collective-permute-start(bf16[384,256]{1,0:T(8,128)(2,1)S(1)} %misc_pack.1.refs_0_), channel_id=1, source_target_pairs={{0,4},{4,0},{8,12},{12,8},{16,20},{20,16},{24,28},{28,24},{1,5},{5... | collective-permute-start | bytes 589832 | tf_op jit(solution)/shard_map/ppermute | solution.py:775
  134.9 14.5 %collective-permute-start.31 = (bf16[128,512]{1,0:T(8,128)(2,1)S(1)}, bf16[128,512]{1,0:T(8,128)(2,1)S(1)}, u32[]{:S(2)}, u32[]{:S(2)}) collective-permute-start(bf16[128,512]{1,0:T(8,128)(2,1)S(1)} %get-tuple-element.223.refs_0_), channel_id=1, source_target_pairs={{0,16},{4,20},{8,24},{12,28},{16,0},{20,4},{24,8},{28,12},{1,17},{... | collective-permute-start | bytes 393224 | tf_op jit(solution)/shard_map/ppermute | solution.py:775
  136.3 20.5 %collective-permute-start.42 = (bf16[256,512]{1,0:T(8,128)(2,1)S(1)}, bf16[256,512]{1,0:T(8,128)(2,1)S(1)}, u32[]{:S(2)}, u32[]{:S(2)}) collective-permute-start(bf16[256,512]{1,0:T(8,128)(2,1)S(1)} %join.8.refs_0_.refs_1_), channel_id=1, source_target_pairs={{0,8},{4,12},{8,0},{12,4},{16,24},{20,28},{24,16},{28,20},{1,9},{5... | collective-permute-start | bytes 786440 | tf_op jit(solution)/shard_map/ppermute | solution.py:775
  138.2 16.7 %collective-permute-start.38 = (bf16[384,256]{1,0:T(8,128)(2,1)S(1)}, bf16[384,256]{1,0:T(8,128)(2,1)S(1)}, u32[]{:S(2)}, u32[]{:S(2)}) collective-permute-start(bf16[384,256]{1,0:T(8,128)(2,1)S(1)} %misc_add.2.refs_0_), channel_id=1, source_target_pairs={{0,8},{4,12},{8,0},{12,4},{16,24},{20,28},{24,16},{28,20},{1,9},{5... | collective-permute-start | bytes 589832 | tf_op jit(solution)/shard_map/ppermute | solution.py:775
  142.3 34.3 %collective-permute-start.48 = (bf16[512,512]{1,0:T(8,128)(2,1)S(1)}, bf16[512,512]{1,0:T(8,128)(2,1)S(1)}, u32[]{:S(2)}, u32[]{:S(2)}) collective-permute-start(bf16[512,512]{1,0:T(8,128)(2,1)S(1)} %join.9.refs_0_.refs_1_), channel_id=1, source_target_pairs={{0,4},{4,0},{8,12},{12,8},{16,20},{20,16},{24,28},{28,24},{1,5},{5... | collective-permute-start | bytes 1572872 | tf_op jit(solution)/shard_map/ppermute | solution.py:775
  149.4 8.5 %collective-permute-start.41 = (bf16[128,512]{1,0:T(8,128)(2,1)S(1)}, bf16[128,512]{1,0:T(8,128)(2,1)S(1)}, u32[]{:S(2)}, u32[]{:S(2)}) collective-permute-start(bf16[128,512]{1,0:T(8,128)(2,1)S(1)} %add.31.refs_2_.refs_1_), channel_id=1, source_target_pairs={{0,16},{4,20},{8,24},{12,28},{16,0},{20,4},{24,8},{28,12},{1,17},{... | collective-permute-start | bytes 393224 | tf_op jit(solution)/shard_map/ppermute | solution.py:775
  152.7 2.0 %collective-permute-start.36 = (bf16[256,1024]{1,0:T(8,128)(2,1)S(1)}, bf16[256,1024]{1,0:T(8,128)(2,1)S(1)}, u32[]{:S(2)}, u32[]{:S(2)}) collective-permute-start(bf16[256,1024]{1,0:T(8,128)(2,1)S(1)} %get-tuple-element.225), channel_id=1, source_target_pairs={{0,1},{1,0},{2,3},{3,2},{4,5},{5,4},{6,7},{7,6},{8,9},{9,8},{10,11... | collective-permute-start | bytes 1572872 | tf_op jit(solution)/shard_map/ppermute | solution.py:775
  154.7 1.9 %collective-permute-start.37 = (bf16[256,1024]{1,0:T(8,128)(2,1)S(1)}, bf16[256,1024]{1,0:T(8,128)(2,1)S(1)}, u32[]{:S(2)}, u32[]{:S(2)}) collective-permute-start(bf16[256,1024]{1,0:T(8,128)(2,1)S(1)} %get-tuple-element.226.refs_0_), channel_id=1, source_target_pairs={{0,1},{1,0},{2,3},{3,2},{4,5},{5,4},{6,7},{7,6},{8,9},{9,8},{10,11... | collective-permute-start | bytes 1572872 | tf_op jit(solution)/shard_map/ppermute | solution.py:775
  155.0 12.5 %collective-permute-start.40 = (bf16[384,256]{1,0:T(8,128)(2,1)S(1)}, bf16[384,256]{1,0:T(8,128)(2,1)S(1)}, u32[]{:S(2)}, u32[]{:S(2)}) collective-permute-start(bf16[384,256]{1,0:T(8,128)(2,1)S(1)} %misc_add.3.refs_0_), channel_id=1, source_target_pairs={{0,16},{4,20},{8,24},{12,28},{16,0},{20,4},{24,8},{28,12},{1,17},{... | collective-permute-start | bytes 589832 | tf_op jit(solution)/shard_map/ppermute | solution.py:775
  158.4 11.5 %collective-permute-start.44 = (bf16[256,512]{1,0:T(8,128)(2,1)S(1)}, bf16[256,512]{1,0:T(8,128)(2,1)S(1)}, u32[]{:S(2)}, u32[]{:S(2)}) collective-permute-start(bf16[256,512]{1,0:T(8,128)(2,1)S(1)} %join.11.refs_0_.refs_1_), channel_id=1, source_target_pairs={{0,8},{4,12},{8,0},{12,4},{16,24},{20,28},{24,16},{28,20},{1,9},{5... | collective-permute-start | bytes 786440 | tf_op jit(solution)/shard_map/ppermute | solution.py:775
  159.4 20.8 %collective-permute-start.46 = (bf16[512,512]{1,0:T(8,128)(2,1)S(1)}, bf16[512,512]{1,0:T(8,128)(2,1)S(1)}, u32[]{:S(2)}, u32[]{:S(2)}) collective-permute-start(bf16[512,512]{1,0:T(8,128)(2,1)S(1)} %join.10.refs_0_.refs_1_), channel_id=1, source_target_pairs={{0,4},{4,0},{8,12},{12,8},{16,20},{20,16},{24,28},{28,24},{1,5},{5... | collective-permute-start | bytes 1572872 | tf_op jit(solution)/shard_map/ppermute | solution.py:775
  159.7 18.5 %collective-permute-start.39 = (bf16[256,1024]{1,0:T(8,128)(2,1)S(1)}, bf16[256,1024]{1,0:T(8,128)(2,1)S(1)}, u32[]{:S(2)}, u32[]{:S(2)}) collective-permute-start(bf16[256,1024]{1,0:T(8,128)(2,1)S(1)} %add.33.refs_0_), channel_id=1, source_target_pairs={{0,2},{1,3},{2,0},{3,1},{4,6},{5,7},{6,4},{7,5},{8,10},{9,11},{10,... | collective-permute-start | bytes 1572872 | tf_op jit(solution)/shard_map/ppermute | solution.py:775
  168.9 7.1 %collective-permute-start.43 = (bf16[256,256]{1,0:T(8,128)(2,1)S(1)}, bf16[256,256]{1,0:T(8,128)(2,1)S(1)}, u32[]{:S(2)}, u32[]{:S(2)}) collective-permute-start(bf16[256,256]{1,0:T(8,128)(2,1)S(1)} %get-tuple-element.228.refs_1_), channel_id=1, source_target_pairs={{0,2},{1,3},{2,0},{3,1},{4,6},{5,7},{6,4},{7,5},{8,10},{9,11},{10,... | collective-permute-start | bytes 393224 | tf_op jit(solution)/shard_map/ppermute | solution.py:775
  170.5 14.2 %collective-permute-start.45 = (bf16[512,512]{1,0:T(8,128)(2,1)S(1)}, bf16[512,512]{1,0:T(8,128)(2,1)S(1)}, u32[]{:S(2)}, u32[]{:S(2)}) collective-permute-start(bf16[512,512]{1,0:T(8,128)(2,1)S(1)} %join.12.refs_0_.refs_1_), channel_id=1, source_target_pairs={{0,4},{4,0},{8,12},{12,8},{16,20},{20,16},{24,28},{28,24},{1,5},{5... | collective-permute-start | bytes 1572872 | tf_op jit(solution)/shard_map/ppermute | solution.py:775
  176.5 5.3 %collective-permute-start.47 = (bf16[512,256]{1,0:T(8,128)(2,1)S(1)}, bf16[512,256]{1,0:T(8,128)(2,1)S(1)}, u32[]{:S(2)}, u32[]{:S(2)}) collective-permute-start(bf16[512,256]{1,0:T(8,128)(2,1)S(1)} %join.13.refs_0_.refs_1_), channel_id=1, source_target_pairs={{0,1},{1,0},{2,3},{3,2},{4,5},{5,4},{6,7},{7,6},{8,9},{9,8},{10,11... | collective-permute-start | bytes 786440 | tf_op jit(solution)/shard_map/ppermute | solution.py:775
  (26 other events, 146.0 us)

commit v8 on v7

--- a/solution.py
+++ b/solution.py
@@ -72,7 +72,7 @@
 LAST = []
 
 def launch(body, ins, in_specs, outs, out_specs, name, grid=(1,), meta=None, scratch=(),
-           aliases=None, vmem=8, flops=0, token=True):
+           aliases=None, vmem=8, flops=0, token=True, tick=False):
     ins, in_specs = list(ins), list(in_specs)
     lead = 0 if meta is None else 1
     at = lead + len(ins)
@@ -81,8 +81,18 @@
         ins.append(given)
         in_specs.append(pl.BlockSpec(memory_space=pl.ANY))
 
+    outs, out_specs = list(outs), list(out_specs)
+    if tick:
+        outs.append(shaped((8, L)))
+        out_specs.append(whole(outs[-1]))
+
     def run(*refs):
-        body(*(refs if given is None else refs[:at] + refs[at + 1 :]))
+        refs = refs if given is None else refs[:at] + refs[at + 1 :]
+        if tick:
+            last = lead + len(ins) - (given is not None) + len(outs) - 1
+            refs[last][...] = jnp.zeros((8, L), F32)
+            refs = refs[:last] + refs[last + 1 :]
+        body(*refs)
 
     results = pl.pallas_call(
         run,
@@ -103,7 +113,9 @@
         ),
         name=name,
     )(*([] if meta is None else [meta]), *ins)
-    if token:
+    if tick:
+        *results, LAST[:] = [*results[:-1], results[-1:]]
+    elif token:
         LAST[:] = [min(results, key=lambda a: a.size)]
     return results
 
@@ -121,7 +133,7 @@
     return jax.ShapeDtypeStruct(shape, dtype)
 
 
-def simple(body, ins, outs, name, meta=None, vmem=8, deps=()):
+def simple(body, ins, outs, name, meta=None, vmem=8, deps=(), tick=False):
     n = len(ins)
 
     def run(*refs):
@@ -131,7 +143,7 @@
     return launch(
         run, [*ins, *deps],
         [whole(a) for a in ins] + [pl.BlockSpec(memory_space=pl.ANY)] * len(deps),
-        outs, [whole(o) for o in outs], name, meta=meta, vmem=vmem,
+        outs, [whole(o) for o in outs], name, meta=meta, vmem=vmem, tick=tick,
     )
 
 
@@ -317,7 +329,7 @@
 
 def states_body(
     at, meta, cat, step, rim, vecs, hv, mats,
-    pre_o, sin_o, end_o, load_o, cum_o, pfx_o, thr_o, buf, state, prod,
+    pre_o, cb_o, sin_o, end_o, load_o, cum_o, pfx_o, thr_o, buf, state, prod,
 ):
     width = vecs.shape[1] - 2 * L
     heads = width // HD
@@ -348,6 +360,7 @@
             v = v + vecs[3 - j : 4 - j, cols] * buf[8 - j : 8 - j + L, cols]
         pre_o[:, cols] = v
         acts.append(v * sigmoid(v))
+    cb_o[...] = acts[-1].astype(BF)
     steps = softplus(step[...].astype(F32) + hv[0:1, :])
     cum = dot_r(mats[:, width:], steps * hv[1:2, :])
     cum_o[...] = cum
@@ -396,11 +409,13 @@
             gap = jnp.where(lower, cum[:, h : h + 1] - cum_t[h : h + 1, :], -1e30)
             mix = scores * jnp.exp(gap) * steps_t[h : h + 1, :]
             got.append(dot(mix.astype(BF), x))
-        y_o[:, cols] = jnp.where(first, got[0], got[1]) + far[:, cols]
+        y_o[:, cols] = (
+            jnp.where(first, got[0], got[1]) + far[:, cols] + vecs[5:6, cols] * acts[pair]
+        )
 
 
 def gate_body(
-    level, at, meta, pre, cum, pfx, y, gate, gn, before, through, load, vecs, mats,
+    level, at, meta, cb, cum, pfx, y, gate, gn, before, through, load, vecs, mats,
     mixed_o, sums_o, incoming,
 ):
     width = vecs.shape[1] - 2 * L
@@ -413,14 +428,11 @@
             incoming[...] = final_link(meta, level, False, before, through, load).astype(BF)
 
     reach = dot((jnp.exp(cum[...]) * pfx[0][0:1, :]).astype(BF), mats[:, :width])
-    cv = pre[:, width + L :]
-    cb = (cv * sigmoid(cv)).astype(BF)
-    far = reach * dot(cb, incoming[...], 1, 1)
+    far = reach * dot(cb[...], incoming[...], 1, 1)
     squares, crosses = [], []
     for x0 in range(0, width, L):
         cols = slice(x0, x0 + L)
-        v = pre[:, cols]
-        mixed = y[:, cols] + far[:, cols] + vecs[5:6, cols] * (v * sigmoid(v))
+        mixed = y[:, cols] + far[:, cols]
         mixed_o[:, cols] = mixed
         g = gate[:, cols].astype(F32)
         gated = mixed * (g * sigmoid(g))
@@ -921,7 +933,8 @@
 
 def rows_of(meta, src, mine, which, d, width, old):
     half = src.shape[0]
-    ins, specs, aliases = [src], [whole(src)], {}
+    ins, aliases = [src], {}
+    specs = [whole(src)]
     if old is not None:
         ins.append(old)
         specs.append(pl.BlockSpec(memory_space=pl.ANY))
@@ -1082,7 +1095,7 @@
     last: Any
 
 
-ORDER = "LWLFLGFWLGTIWMGTWMIGTMTWMIGMWTIBBMBGIMIMWBGMI"
+ORDER = "WLLFLGFWLGTIWMGTWMIGTMTWMIGMWTIBBMGBIIMWMBGMI"
 
 
 def run_chains(chains, done, order):
@@ -1252,12 +1265,12 @@
     state_shape = (width, L)
     load_shape = (width + 16, L)
     small = (8, L)
-    pre, sin, state, load, cum, pfx, decay = stretched(
+    pre, cb, sin, state, load, cum, pfx, decay = stretched(
         states_body,
         "states",
         [(ROWS, cat), (ROWS, step_raw), (ONE, rim), (ONE, vecs), (ONE, hv),
          (ONE, mats)],
-        [(ROWS, (tokens, wide), F32), (EACH, (count, *state_shape), BF),
+        [(ROWS, (tokens, wide), F32), (ROWS, tall, BF), (EACH, (count, *state_shape), BF),
          (ONE, state_shape, F32), (ONE, load_shape, BF), (ROWS, tall, F32),
          (EACH, (count, 8, L), F32), (ONE, small, F32)],
         [pltpu.VMEM((per, L + 8, wide), F32), pltpu.VMEM(state_shape, F32),
@@ -1305,7 +1318,7 @@
     mixed, sums, incoming = stretched(
         functools.partial(gate_body, levels - 1),
         "gated",
-        [(ROWS, pre), (ROWS, cum), (EACH, pfx), (ROWS, y), (ROWS, gate_raw),
+        [(ROWS, cb), (ROWS, cum), (EACH, pfx), (ROWS, y), (ROWS, gate_raw),
          (ROWS, gn), (ONE, befores), (ONE, throughs), (ONE, load), (ONE, vecs),
          (ONE, mats)],
         [(ROWS, (tokens, width), F32), (EACH, (count, 2, L), F32), (ONE, state_shape, BF)],
@@ -1419,7 +1432,9 @@
         yield None, False
         branch = rows_times(outproj_body, group, share, d, [normout], [weight_out], "outproj")
         parts = yield from scattered(branch)
-        (kept.layer,) = simple(layer_body, [tokens_in, *parts], [shaped((share, d), BF)], "layer")
+        (kept.layer,) = simple(
+            layer_body, [tokens_in, *parts], [shaped((share, d), BF)], "layer", tick=True
+        )
 
     def tokens_chain():
         yield "L", False
@@ -1435,7 +1450,7 @@
         parts = yield from scattered(grads)
         (kept.tokens,) = simple(
             tokens_body, [tokens_in, grad_out, *parts, gain], [shaped((share, d))], "tokens",
-            None, 12,
+            None, 12, tick=True,
         )
 
     def misc_chain():
@@ -1476,13 +1491,16 @@
         total, *kept.small = simple(
             functools.partial(misc_finish_body, rows), [load, got, mats],
             [shaped((rows, ROW), BF)] + [shaped(s) for s in outs], "misc_finish",
+            tick=True,
         )
         for level in range(len(tmasks) - 1, -1, -1):
             got = swap(total, TP, tmasks[level])
             yield None, True
             if level:
                 total = join(meta, 0, level, total, got)
-        (kept.bc,) = simple(bc_out_body, [total, got], [shaped((2, d, L))], "bc_weights", meta)
+        (kept.bc,) = simple(
+            bc_out_body, [total, got], [shaped((2, d, L))], "bc_weights", meta, tick=True
+        )
 
     run_chains(
         {

time: 187 us -> 184 us (0.984)
  local copies, waits for them, and re-layouts: 9.47 us -> 5.33 us
  starting transfers between devices: 47.9 us -> 51.4 us
    unnamed x50 -> x42, local copies, waits for them, and re-layouts: 9.45 us -> 5.31 us
    ppermute x46, starting transfers between devices: 45.3 us -> 48.8 us  [swap(): return lax.ppermute(x, axis, [(i, i ^ mask) for i in range(count)])]
  transfers between devices with their start and end apart: 49 -> 49, of which waited for: 16 -> 15; matrix products, arithmetic and copies ran while one was open for 0% -> 0% of each run, Pallas kernels for 43% -> 44%
where the time goes in v8:
time: 184 us
  Pallas kernels  90.1 us (49%)
  starting transfers between devices  51.4 us (28%)
  waiting for transfers between devices  34.5 us (19%)
  local copies, waits for them, and re-layouts  5.33 us (3%)
    pallas_call x108, Pallas kernels, launch(): pl.pallas_call(run, grid_spec=pltpu.PrefetchScalarGridSpec(num_scalar_pre...  90.1 us
    ppermute x46, starting transfers between devices, swap(): return lax.ppermute(x, axis, [(i, i ^ mask) for i in range(count)])  48.8 us
    ppermute x46, waiting for transfers between devices, swap(): return lax.ppermute(x, axis, [(i, i ^ mask) for i in range(count)])  34.5 us
    unnamed x42, local copies, waits for them, and re-layouts  5.31 us
  transfers between devices with their start and end apart: 49, of which 15 were waited for; matrix products, arithmetic and copies ran while one was open for 0% of the time, Pallas kernels for 44%

profile of v8, /device:TPU:0, one launch (start us, length us, event | category | flops | bytes accessed | tf_op | source)
XLA Modules:
  0.0 183.8 jit_solution(5674582935480596122)
XLA Ops:
  1.2 2.6 %collective-permute-start = (bf16[256,1024]{1,0:T(8,128)(2,1)}, bf16[256,1024]{1,0:T(8,128)(2,1)S(1)}, u32[]{:S(2)}, u32[]{:S(2)}) collective-permute-start(bf16[256,1024]{1,0:T(8,128)(2,1)} %refs_0_.11), channel_id=1, source_target_pairs={{0,2},{1,3},{2,0},{3,1},{4,6},{5,7},{6,4},{7,5},{8,10},{9,11},{10,... | collective-permute-start | bytes 1572872 | tf_op jit(solution)/shard_map/ppermute | solution.py:787
  8.2 1.7 copy-done
  10.1 3.1 %project.3 = (bf16[1024,1024]{1,0:T(8,128)(2,1)S(1)}, bf16[1024,512]{1,0:T(8,128)(2,1)S(1)}, bf16[1024,768]{1,0:T(8,128)(2,1)S(1)}, bf16[1024,128]{1,0:T(8,128)(2,1)S(1)}) custom-call(s32[11]{0:T(128)S(1)} %pad_add_fusion.refs_0_, bf16[256,1024]{1,0:T(8,128)(2,1)S(1)} %copy-done.5, bf16[256,1024]{1,0:T(8,128)(2,1)S(1)} %collective-permute-done.1.refs_1_.refs_2_, ...), custom_call_target="tpu_custom_call" | custom-call | tf_op jit(solution)/shard_map/project/pallas_call | solution.py:97
  13.3 3.5 %collective-permute-done.refs_0_ = bf16[256,1024]{1,0:T(8,128)(2,1)S(1)} collective-permute-done((bf16[256,1024]{1,0:T(8,128)(2,1)}, bf16[256,1024]{1,0:T(8,128)(2,1)S(1)}, u32[]{:S(2)}, u32[]{:S(2)}) %collective-permute-start) | collective-permute-done | bytes 524320 | tf_op jit(solution)/shard_map/ppermute | solution.py:787
  17.4 1.8 project.4
  19.3 2.0 %project.5 = (bf16[1024,1024]{1,0:T(8,128)(2,1)S(1)}, bf16[1024,512]{1,0:T(8,128)(2,1)S(1)}, bf16[1024,768]{1,0:T(8,128)(2,1)S(1)}, bf16[1024,128]{1,0:T(8,128)(...) custom-call(s32[11]{0:T(128)S(1)} %pad_add_fusion.refs_0_, ...), custom_call_target="tpu_custom_call", output_to_operand_aliasing={{0}: (8, {}), {1}: (9, {}), {2}: (10, {}), {3}: (11, {})} | custom-call | tf_op jit(solution)/shard_map/project/pallas_call | solution.py:97
  21.3 5.2 %states.1 = (f32[1024,768]{1,0:T(8,128)S(1)}, bf16[1024,128]{1,0:T(8,128)(2,1)S(1)}, bf16[8,512,128]{2,1,0:T(8,128)(2,1)S(1)}, f32[512,128]{1,0:T(8,128)S(1)}, b...) custom-call(s32[11]{0:T(128)S(1)} %pad_add_fusion.refs_0_, ...), custom_call_target="tpu_custom_call" | custom-call | tf_op jit(solution)/shard_map/states/pallas_call | solution.py:97
  26.5 1.6 collective-permute-start.8
  28.1 1.5 collective-permute-start.7
  29.7 3.6 %within.1.refs_0_.refs_4_ = f32[1024,512]{1,0:T(8,128)S(1)} custom-call(s32[11]{0:T(128)S(1)} %pad_add_fusion.refs_0_, f32[1024,768]{1,0:T(8,128)S(1)} %get-tuple-element.150.refs_1_.refs_3_, bf16[1024,128]{1,0:T(8,128)(2,1)S(1)} %get-tuple-element.146.refs_2_.refs_4_, f32[1024,128]{1,0:T(8,128)S(1)} %get-tuple-element.151.refs_3_.refs_2_.refs_5_, ...), custom_call_target="tpu_custom_call" | custom-call | tf_op jit(solution)/shard_map/within/pallas_call | solution.py:97
  34.1 1.6 collective-permute-start.9
  35.7 3.4 %collective-permute-done.9.refs_5_ = bf16[528,128]{1,0:T(8,128)(2,1)S(1)} collective-permute-done((bf16[528,128]{1,0:T(8,128)(2,1)S(1)}, bf16[528,128]{1,0:T(8,128)(2,1)S(1)}, u32[]{:S(2)}, u32[]{:S(2)}) %collective-permute-start.9) | collective-permute-done | bytes 135200 | tf_op jit(solution)/shard_map/ppermute | solution.py:787
  39.9 2.7 %collective-permute-start.11 = (bf16[528,128]{1,0:T(8,128)(2,1)S(1)}, bf16[528,128]{1,0:T(8,128)(2,1)S(1)}, u32[]{:S(2)}, u32[]{:S(2)}) collective-permute-start(bf16[528,128]{1,0:T(8,128)(2,1)S(1)} %get-tuple-element.167), channel_id=1, source_target_pairs={{0,16},{4,20},{8,24},{12,28},{16,0},{20,4},{24,8},{28,12},{1,17},{... | collective-permute-start | bytes 405512 | tf_op jit(solution)/shard_map/ppermute | solution.py:787
  42.7 1.9 %collective-permute-done.10.refs_3_ = bf16[256,1024]{1,0:T(8,128)(2,1)S(1)} collective-permute-done((bf16[256,1024]{1,0:T(8,128)(2,1)S(1)}, bf16[256,1024]{1,0:T(8,128)(2,1)S(1)}, u32[]{:S(2)}, u32[]{:S(2)}) %collective-permute-start.10) | collective-permute-done | bytes 524320 | tf_op jit(solution)/shard_map/ppermute | solution.py:787
  44.6 2.0 %cotangent.1 = (bf16[1024,1024]{1,0:T(8,128)(2,1)S(1)}, bf16[1024,512]{1,0:T(8,128)(2,1)S(1)}) custom-call(bf16[256,1024]{1,0:T(8,128)(2,1)S(1)} %copy-done.9, bf16[256,1024]{1,0:T(8,128)(2,1)S(1)} %collective-permute-done.6.refs_1_, bf16[256,1024]{1,0:T(8,128)(2,1)S(1)} %collective-permute-done.7.refs_0_.refs_2_, ...), custom_call_target="tpu_custom_call" | custom-call | tf_op jit(solution)/shard_map/cotangent/pallas_call | solution.py:97
  47.9 3.5 %gated.1 = (f32[1024,512]{1,0:T(8,128)S(1)}, f32[8,2,128]{2,1,0:T(2,128)S(1)}, bf16[512,128]{1,0:T(8,128)(2,1)S(1)}) custom-call(s32[11]{0:T(128)S(1)} %pad_add_fusion.refs_0_, bf16[1024,128]{1,0:T(8,128)(2,1)S(1)} %get-tuple-element.152.refs_1_, f32[1024,128]{1,0:T(8,128)S(1)} %get-tuple-element.151.refs_3_.refs_2_.refs_5_, ...), custom_call_target="tpu_custom_call" | custom-call | tf_op jit(solution)/shard_map/gated/pallas_call | solution.py:97
  52.3 2.8 %collective-permute-done.12.refs_1_ = f32[8,2,128]{2,1,0:T(2,128)S(1)} collective-permute-done((f32[8,2,128]{2,1,0:T(2,128)S(1)}, f32[8,2,128]{2,1,0:T(2,128)S(1)}, u32[]{:S(2)}, u32[]{:S(2)}) %collective-permute-start.12) | collective-permute-done | bytes 8224 | tf_op jit(solution)/shard_map/ppermute | solution.py:787
  56.3 4.4 %back_gated.1 = (bf16[1024,512]{1,0:T(8,128)(2,1)S(1)}, bf16[1024,512]{1,0:T(8,128)(2,1)S(1)}, bf16[1024,512]{1,0:T(8,128)(2,1)S(1)}, bf16[8,512,128]{2,1,0:T(8,...) custom-call(s32[11]{0:T(128)S(1)} %pad_add_fusion.refs_0_, ...), custom_call_target="tpu_custom_call" | custom-call | tf_op jit(solution)/shard_map/back_gated/pallas_call | solution.py:97
  61.2 2.3 %wgrad.3 = (bf16[512,512]{1,0:T(8,128)(2,1)S(1)}, bf16[512,512]{1,0:T(8,128)(2,1)S(1)}) custom-call(s32[11]{0:T(128)S(1)} %pad_add_fusion.refs_0_, bf16[1024,512]{1,0:T(8,128)(2,1)S(1)} %get-tuple-element.170.refs_1_.refs_0_, bf16[1024,1024]{1,0:T(8,128)(2,1)S(1)} %get-tuple-element.178.refs_2_, f32[8,512]{1,0:T(8,128)S(1)} %get-tuple-element.179.refs_3_.refs_5_), custom_call_target="tpu_custom_call" | custom-call | tf_op jit(solution)/shard_map/wgrad/pallas_call | solution.py:97
  63.6 1.6 collective-permute-start.17
  68.1 5.7 %back_within.2 = (f32[1024,512]{1,0:T(8,128)S(1)}, f32[1024,256]{1,0:T(8,128)S(1)}, f32[1024,128]{1,0:T(8,128)S(1)}, f32[1024,128]{1,0:T(8,128)S(1)}) custom-call(s32[11]{0:T(128)S(1)} %pad_add_fusion.refs_0_, f32[1024,768]{1,0:T(8,128)S(1)} %get-tuple-element.150.refs_1_.refs_3_, bf16[1024,128]{1,0:T(8,128)(2,1)S(1)} %get-tuple-element.146.refs_2_.refs_4_, ...), custom_call_target="tpu_custom_call" | custom-call | tf_op jit(solution)/shard_map/back_within/pallas_call | solution.py:97
  74.5 3.4 %collective-permute-start.16 = (bf16[528,128]{1,0:T(8,128)(2,1)S(1)}, bf16[528,128]{1,0:T(8,128)(2,1)S(1)}, u32[]{:S(2)}, u32[]{:S(2)}) collective-permute-start(bf16[528,128]{1,0:T(8,128)(2,1)S(1)} %get-tuple-element.198), channel_id=1, source_target_pairs={{0,16},{4,20},{8,24},{12,28},{16,0},{20,4},{24,8},{28,12},{1,17},{... | collective-permute-start | bytes 405512 | tf_op jit(solution)/shard_map/ppermute | solution.py:787
  78.0 2.3 %wgrad.4 = (bf16[512,512]{1,0:T(8,128)(2,1)S(1)}, bf16[512,512]{1,0:T(8,128)(2,1)S(1)}) custom-call(s32[11]{0:T(128)S(1)} %pad_add_fusion.refs_0_, bf16[1024,1024]{1,0:T(8,128)(2,1)S(1)} %get-tuple-element.171.refs_1_.refs_3_, bf16[1024,512]{1,0:T(8,128)(2,1)S(1)} %get-tuple-element.186.refs_2_.refs_0_, f32[8,128]{1,0:T(8,128)S(1)} %get-tuple-element.191.refs_3_.refs_15_), custom_call_target="tpu_custom_call" | custom-call | tf_op jit(solution)/shard_map/wgrad/pallas_call | solution.py:97
  80.6 5.5 %back_within.3 = (f32[1024,512]{1,0:T(8,128)S(1)}, f32[1024,256]{1,0:T(8,128)S(1)}, f32[1024,128]{1,0:T(8,128)S(1)}, f32[1024,128]{1,0:T(8,128)S(1)}) custom-call(s32[11]{0:T(128)S(1)} %pad_add_fusion.refs_0_, f32[1024,768]{1,0:T(8,128)S(1)} %get-tuple-element.150.refs_1_.refs_3_, ...), custom_call_target="tpu_custom_call", output_to_operand_aliasing={{0}: (12, {}), {1}: (13, {}), {2}: (14, {}), {3}: (15, {})} | custom-call | tf_op jit(solution)/shard_map/back_within/pallas_call | solution.py:97
  87.0 9.2 %back_conv.1 = (bf16[1024,768]{1,0:T(8,128)(2,1)S(1)}, bf16[1024,128]{1,0:T(8,128)(2,1)S(1)}, f32[8,768]{1,0:T(8,128)S(1)}, bf16[16,768]{1,0:T(8,128)(2,1)S(1)},...) custom-call(s32[11]{0:T(128)S(1)} %pad_add_fusion.refs_0_, bf16[1024,768]{1,0:T(8,128)(2,1)S(1)} %get-tuple-element.145.refs_1_, ...), custom_call_target="tpu_custom_call" | custom-call | tf_op jit(solution)/shard_map/back_conv/pallas_call | solution.py:97
  98.1 3.9 %collective-permute-start.22 = (bf16[256,512]{1,0:T(8,128)(2,1)S(1)}, bf16[256,512]{1,0:T(8,128)(2,1)S(1)}, u32[]{:S(2)}, u32[]{:S(2)}) collective-permute-start(bf16[256,512]{1,0:T(8,128)(2,1)S(1)} %get-tuple-element.206.refs_5_), channel_id=1, source_target_pairs={{0,8},{4,12},{8,0},{12,4},{16,24},{20,28},{24,16},{28,20},{1,9},{5... | collective-permute-start | bytes 786440 | tf_op jit(solution)/shard_map/ppermute | solution.py:787
  102.0 2.9 %wgrad.5 = (bf16[512,512]{1,0:T(8,128)(2,1)S(1)}, bf16[512,512]{1,0:T(8,128)(2,1)S(1)}) custom-call(s32[11]{0:T(128)S(1)} %pad_add_fusion.refs_0_, bf16[1024,1024]{1,0:T(8,128)(2,1)S(1)} %get-tuple-element.171.refs_1_.refs_3_, bf16[1024,768]{1,0:T(8,128)(2,1)S(1)} %get-tuple-element.201.refs_2_.refs_1_, ...), custom_call_target="tpu_custom_call" | custom-call | tf_op jit(solution)/shard_map/wgrad/pallas_call | solution.py:97
  107.1 1.7 bc_wgrad.1
  109.5 2.4 %collective-permute-start.27 = (bf16[128,512]{1,0:T(8,128)(2,1)S(1)}, bf16[128,512]{1,0:T(8,128)(2,1)S(1)}, u32[]{:S(2)}, u32[]{:S(2)}) collective-permute-start(bf16[128,512]{1,0:T(8,128)(2,1)S(1)} %get-tuple-element.216.refs_0_), channel_id=1, source_target_pairs={{0,16},{4,20},{8,24},{12,28},{16,0},{20,4},{24,8},{28,12},{1,17},{... | collective-permute-start | bytes 393224 | tf_op jit(solution)/shard_map/ppermute | solution.py:787
  112.6 4.9 %dgrad.1 = (bf16[256,1024]{1,0:T(8,128)(2,1)S(1)}, bf16[256,1024]{1,0:T(8,128)(2,1)S(1)}, bf16[256,1024]{1,0:T(8,128)(2,1)S(1)}, bf16[256,1024]{1,0:T(8,128)(2,1)S(1)}, f32[16,256]{1,0:T(8,128)S(1)}) custom-call(bf16[1024,512]{1,0:T(8,128)(2,1)S(1)} %get-tuple-element.186.refs_2_.refs_0_, bf16[1024,768]{1,0:T(8,128)(2,1)S(1)} %patch.1.refs_1_, ...), custom_call_target="tpu_custom_call" | custom-call | tf_op jit(solution)/shard_map/dgrad/pallas_call | solution.py:97
  125.3 3.4 %collective-permute-done.29.refs_2_ = bf16[128,512]{1,0:T(8,128)(2,1)S(1)} collective-permute-done((bf16[128,512]{1,0:T(8,128)(2,1)S(1)}, bf16[128,512]{1,0:T(8,128)(2,1)S(1)}, u32[]{:S(2)}, u32[]{:S(2)}) %collective-permute-start.29) | collective-permute-done | bytes 131104 | tf_op jit(solution)/shard_map/ppermute | solution.py:787
  130.4 2.3 %collective-permute-start.34 = (bf16[384,256]{1,0:T(8,128)(2,1)S(1)}, bf16[384,256]{1,0:T(8,128)(2,1)S(1)}, u32[]{:S(2)}, u32[]{:S(2)}) collective-permute-start(bf16[384,256]{1,0:T(8,128)(2,1)S(1)} %misc_pack.1.refs_0_), channel_id=1, source_target_pairs={{0,4},{4,0},{8,12},{12,8},{16,20},{20,16},{24,28},{28,24},{1,5},{5... | collective-permute-start | bytes 589832 | tf_op jit(solution)/shard_map/ppermute | solution.py:787
  135.8 1.9 %collective-permute-start.38 = (bf16[256,512]{1,0:T(8,128)(2,1)S(1)}, bf16[256,512]{1,0:T(8,128)(2,1)S(1)}, u32[]{:S(2)}, u32[]{:S(2)}) collective-permute-start(bf16[256,512]{1,0:T(8,128)(2,1)S(1)} %join.8.refs_0_.refs_1_), channel_id=1, source_target_pairs={{0,8},{4,12},{8,0},{12,4},{16,24},{20,28},{24,16},{28,20},{1,9},{5... | collective-permute-start | bytes 786440 | tf_op jit(solution)/shard_map/ppermute | solution.py:787
  138.2 3.1 %collective-permute-done.33.refs_2_ = bf16[256,512]{1,0:T(8,128)(2,1)S(1)} collective-permute-done((bf16[256,512]{1,0:T(8,128)(2,1)S(1)}, bf16[256,512]{1,0:T(8,128)(2,1)S(1)}, u32[]{:S(2)}, u32[]{:S(2)}) %collective-permute-start.33) | collective-permute-done | bytes 262176 | tf_op jit(solution)/shard_map/ppermute | solution.py:787
  143.3 1.6 out_weights.2.refs_2_
  146.1 1.5 tokens.1
  149.2 1.8 outproj.1
  151.1 1.9 %collective-permute-done.36.refs_1_ = bf16[256,1024]{1,0:T(8,128)(2,1)S(1)} collective-permute-done((bf16[256,1024]{1,0:T(8,128)(2,1)S(1)}, bf16[256,1024]{1,0:T(8,128)(2,1)S(1)}, u32[]{:S(2)}, u32[]{:S(2)}) %collective-permute-start.36) | collective-permute-done | bytes 524320 | tf_op jit(solution)/shard_map/ppermute | solution.py:787
  153.3 1.6 collective-permute-start.41
  157.3 2.2 %collective-permute-start.43 = (bf16[256,512]{1,0:T(8,128)(2,1)S(1)}, bf16[256,512]{1,0:T(8,128)(2,1)S(1)}, u32[]{:S(2)}, u32[]{:S(2)}) collective-permute-start(bf16[256,512]{1,0:T(8,128)(2,1)S(1)} %join.11.refs_0_.refs_1_), channel_id=1, source_target_pairs={{0,8},{4,12},{8,0},{12,4},{16,24},{20,28},{24,16},{28,20},{1,9},{5... | collective-permute-start | bytes 786440 | tf_op jit(solution)/shard_map/ppermute | solution.py:787
  160.3 1.6 zx_weights.4.refs_2_
  161.9 6.7 %collective-permute-done.43.refs_2_ = bf16[256,512]{1,0:T(8,128)(2,1)S(1)} collective-permute-done((bf16[256,512]{1,0:T(8,128)(2,1)S(1)}, bf16[256,512]{1,0:T(8,128)(2,1)S(1)}, u32[]{:S(2)}, u32[]{:S(2)}) %collective-permute-start.43) | collective-permute-done | bytes 262176 | tf_op jit(solution)/shard_map/ppermute | solution.py:787
  169.2 2.1 %collective-permute-start.45 = (bf16[512,512]{1,0:T(8,128)(2,1)S(1)}, bf16[512,512]{1,0:T(8,128)(2,1)S(1)}, u32[]{:S(2)}, u32[]{:S(2)}) collective-permute-start(bf16[512,512]{1,0:T(8,128)(2,1)S(1)} %join.12.refs_0_.refs_1_), channel_id=1, source_target_pairs={{0,4},{4,0},{8,12},{12,8},{16,20},{20,16},{24,28},{28,24},{1,5},{5... | collective-permute-start | bytes 1572872 | tf_op jit(solution)/shard_map/ppermute | solution.py:787
  172.9 1.6 zx_weights.5.refs_2_
  174.4 1.6 out_weights.3
  178.6 1.6 zx_weights.6.refs_2_
  180.2 1.6 bc_weights.1
  182.2 1.6 zx_weights.7
  (206 shorter events, 48.1 us)
Async XLA Ops:
  0.6 4.1 %collective-permute-start.1 = (bf16[256,1024]{1,0:T(8,128)(2,1)}, bf16[256,1024]{1,0:T(8,128)(2,1)S(1)}, u32[]{:S(2)}, u32[]{:S(2)}) collective-permute-start(bf16[256,1024]{1,0:T(8,128)(2,1)} %refs_0_.11), channel_id=1, source_target_pairs={{0,1},{1,0},{2,3},{3,2},{4,5},{5,4},{6,7},{7,6},{8,9},{9,8},{10,11... | collective-permute-start | bytes 1572872 | tf_op jit(solution)/shard_map/ppermute | solution.py:787
  1.2 15.6 %collective-permute-start = (bf16[256,1024]{1,0:T(8,128)(2,1)}, bf16[256,1024]{1,0:T(8,128)(2,1)S(1)}, u32[]{:S(2)}, u32[]{:S(2)}) collective-permute-start(bf16[256,1024]{1,0:T(8,128)(2,1)} %refs_0_.11), channel_id=1, source_target_pairs={{0,2},{1,3},{2,0},{3,1},{4,6},{5,7},{6,4},{7,5},{8,10},{9,11},{10,... | collective-permute-start | bytes 1572872 | tf_op jit(solution)/shard_map/ppermute | solution.py:787
  3.7 39.0 %collective-permute-start.6 = (bf16[256,1024]{1,0:T(8,128)(2,1)}, bf16[256,1024]{1,0:T(8,128)(2,1)S(1)}, u32[]{:S(2)}, u32[]{:S(2)}) collective-permute-start(bf16[256,1024]{1,0:T(8,128)(2,1)} %refs_1_.4), channel_id=1, source_target_pairs={{0,1},{1,0},{2,3},{3,2},{4,5},{5,4},{6,7},{7,6},{8,9},{9,8},{10,11... | collective-permute-start | bytes 1572872 | tf_op jit(solution)/shard_map/ppermute | solution.py:787
  5.8 11.1 %collective-permute-start.4 = (bf16[16,1024]{1,0:T(8,128)(2,1)S(1)}, bf16[16,1024]{1,0:T(8,128)(2,1)S(1)}, u32[]{:S(2)}, u32[]{:S(2)}) collective-permute-start(bf16[16,1024]{1,0:T(8,128)(2,1)S(1)} %last_rows.1.refs_9_), channel_id=1, source_target_pairs={{3,7},{7,11},{11,15},{15,19},{19,23},{23,27},{27,31}} | collective-permute-start | bytes 98312 | tf_op jit(solution)/shard_map/ppermute | solution.py:1180
  6.4 10.4 %collective-permute-start.3 = (bf16[16,1024]{1,0:T(8,128)(2,1)S(1)}, bf16[16,1024]{1,0:T(8,128)(2,1)S(1)}, u32[]{:S(2)}, u32[]{:S(2)}) collective-permute-start(bf16[16,1024]{1,0:T(8,128)(2,1)S(1)} %last_rows.1.refs_9_), channel_id=1, source_target_pairs={{3,5},{7,9},{11,13},{15,17},{19,21},{23,25},{27,29}} | collective-permute-start | bytes 98312 | tf_op jit(solution)/shard_map/ppermute | solution.py:1180
  16.8 2.5 %collective-permute-start.2 = (bf16[256,1024]{1,0:T(8,128)(2,1)S(1)}, bf16[256,1024]{1,0:T(8,128)(2,1)S(1)}, u32[]{:S(2)}, u32[]{:S(2)}) collective-permute-start(bf16[256,1024]{1,0:T(8,128)(2,1)S(1)} %hold.3.refs_2_.refs_1_), channel_id=1, source_target_pairs={{0,1},{1,0},{2,3},{3,2},{4,5},{5,4},{6,7},{7,6},{8,9},{9,8},{10,11... | collective-permute-start | bytes 1572872 | tf_op jit(solution)/shard_map/ppermute | solution.py:787
  16.9 2.4 %collective-permute-start.5 = (bf16[16,1024]{1,0:T(8,128)(2,1)S(1)}, bf16[16,1024]{1,0:T(8,128)(2,1)S(1)}, u32[]{:S(2)}, u32[]{:S(2)}) collective-permute-start(bf16[16,1024]{1,0:T(8,128)(2,1)S(1)} %past.1.refs_10_.refs_0_.refs_2_), channel_id=1, source_target_pairs={{0,1},{1,0},{2,3},{3,2},{4,5},{5,4},{6,7},{7,6},{8,9},{9,8},{10,11... | collective-permute-start | bytes 98312 | tf_op jit(solution)/shard_map/ppermute | solution.py:787
  26.5 6.8 %collective-permute-start.8 = (bf16[528,128]{1,0:T(8,128)(2,1)S(1)}, bf16[528,128]{1,0:T(8,128)(2,1)S(1)}, u32[]{:S(2)}, u32[]{:S(2)}) collective-permute-start(bf16[528,128]{1,0:T(8,128)(2,1)S(1)} %get-tuple-element.158), channel_id=1, source_target_pairs={{0,4},{4,0},{8,12},{12,8},{16,20},{20,16},{24,28},{28,24},{1,5},{5... | collective-permute-start | bytes 405512 | tf_op jit(solution)/shard_map/ppermute | solution.py:787
  28.1 14.4 %collective-permute-start.7 = (bf16[256,1024]{1,0:T(8,128)(2,1)S(1)}, bf16[256,1024]{1,0:T(8,128)(2,1)S(1)}, u32[]{:S(2)}, u32[]{:S(2)}) collective-permute-start(bf16[256,1024]{1,0:T(8,128)(2,1)S(1)} %hold.4.refs_8_), channel_id=1, source_target_pairs={{0,2},{1,3},{2,0},{3,1},{4,6},{5,7},{6,4},{7,5},{8,10},{9,11},{10,... | collective-permute-start | bytes 1572872 | tf_op jit(solution)/shard_map/ppermute | solution.py:787
  34.1 5.1 %collective-permute-start.9 = (bf16[528,128]{1,0:T(8,128)(2,1)S(1)}, bf16[528,128]{1,0:T(8,128)(2,1)S(1)}, u32[]{:S(2)}, u32[]{:S(2)}) collective-permute-start(bf16[528,128]{1,0:T(8,128)(2,1)S(1)} %get-tuple-element.163), channel_id=1, source_target_pairs={{0,8},{4,12},{8,0},{12,4},{16,24},{20,28},{24,16},{28,20},{1,9},{5... | collective-permute-start | bytes 405512 | tf_op jit(solution)/shard_map/ppermute | solution.py:787
  39.9 8.0 %collective-permute-start.11 = (bf16[528,128]{1,0:T(8,128)(2,1)S(1)}, bf16[528,128]{1,0:T(8,128)(2,1)S(1)}, u32[]{:S(2)}, u32[]{:S(2)}) collective-permute-start(bf16[528,128]{1,0:T(8,128)(2,1)S(1)} %get-tuple-element.167), channel_id=1, source_target_pairs={{0,16},{4,20},{8,24},{12,28},{16,0},{20,4},{24,8},{28,12},{1,17},{... | collective-permute-start | bytes 405512 | tf_op jit(solution)/shard_map/ppermute | solution.py:787
  42.6 2.0 %collective-permute-start.10 = (bf16[256,1024]{1,0:T(8,128)(2,1)S(1)}, bf16[256,1024]{1,0:T(8,128)(2,1)S(1)}, u32[]{:S(2)}, u32[]{:S(2)}) collective-permute-start(bf16[256,1024]{1,0:T(8,128)(2,1)S(1)} %hold.5.refs_0_), channel_id=1, source_target_pairs={{0,1},{1,0},{2,3},{3,2},{4,5},{5,4},{6,7},{7,6},{8,9},{9,8},{10,11... | collective-permute-start | bytes 1572872 | tf_op jit(solution)/shard_map/ppermute | solution.py:787
  51.4 3.7 %collective-permute-start.12 = (f32[8,2,128]{2,1,0:T(2,128)S(1)}, f32[8,2,128]{2,1,0:T(2,128)S(1)}, u32[]{:S(2)}, u32[]{:S(2)}) collective-permute-start(f32[8,2,128]{2,1,0:T(2,128)S(1)} %get-tuple-element.169.refs_0_), channel_id=1, source_target_pairs={{0,2},{1,3},{2,0},{3,1},{4,6},{5,7},{6,4},{7,5},{8,10},{9,11},{10,... | collective-permute-start | bytes 24584 | tf_op jit(solution)/shard_map/ppermute | solution.py:787
  60.7 6.0 %collective-permute-start.14 = (bf16[528,128]{1,0:T(8,128)(2,1)S(1)}, bf16[528,128]{1,0:T(8,128)(2,1)S(1)}, u32[]{:S(2)}, u32[]{:S(2)}) collective-permute-start(bf16[528,128]{1,0:T(8,128)(2,1)S(1)} %get-tuple-element.177), channel_id=1, source_target_pairs={{0,4},{4,0},{8,12},{12,8},{16,20},{20,16},{24,28},{28,24},{1,5},{5... | collective-permute-start | bytes 405512 | tf_op jit(solution)/shard_map/ppermute | solution.py:787
  63.6 22.6 %collective-permute-start.17 = (bf16[512,512]{1,0:T(8,128)(2,1)S(1)}, bf16[512,512]{1,0:T(8,128)(2,1)S(1)}, u32[]{:S(2)}, u32[]{:S(2)}) collective-permute-start(bf16[512,512]{1,0:T(8,128)(2,1)S(1)} %get-tuple-element.180.refs_0_), channel_id=1, source_target_pairs={{0,4},{4,0},{8,12},{12,8},{16,20},{20,16},{24,28},{28,24},{1,5},{5... | collective-permute-start | bytes 1572872 | tf_op jit(solution)/shard_map/ppermute | solution.py:787
  67.4 6.4 %collective-permute-start.15 = (bf16[528,128]{1,0:T(8,128)(2,1)S(1)}, bf16[528,128]{1,0:T(8,128)(2,1)S(1)}, u32[]{:S(2)}, u32[]{:S(2)}) collective-permute-start(bf16[528,128]{1,0:T(8,128)(2,1)S(1)} %get-tuple-element.190), channel_id=1, source_target_pairs={{0,8},{4,12},{8,0},{12,4},{16,24},{20,28},{24,16},{28,20},{1,9},{5... | collective-permute-start | bytes 405512 | tf_op jit(solution)/shard_map/ppermute | solution.py:787
  74.5 12.4 %collective-permute-start.16 = (bf16[528,128]{1,0:T(8,128)(2,1)S(1)}, bf16[528,128]{1,0:T(8,128)(2,1)S(1)}, u32[]{:S(2)}, u32[]{:S(2)}) collective-permute-start(bf16[528,128]{1,0:T(8,128)(2,1)S(1)} %get-tuple-element.198), channel_id=1, source_target_pairs={{0,16},{4,20},{8,24},{12,28},{16,0},{20,4},{24,8},{28,12},{1,17},{... | collective-permute-start | bytes 405512 | tf_op jit(solution)/shard_map/ppermute | solution.py:787
  80.3 17.2 %collective-permute-start.18 = (bf16[512,512]{1,0:T(8,128)(2,1)S(1)}, bf16[512,512]{1,0:T(8,128)(2,1)S(1)}, u32[]{:S(2)}, u32[]{:S(2)}) collective-permute-start(bf16[512,512]{1,0:T(8,128)(2,1)S(1)} %get-tuple-element.192.refs_16_), channel_id=1, source_target_pairs={{0,4},{4,0},{8,12},{12,8},{16,20},{20,16},{24,28},{28,24},{1,5},{5... | collective-permute-start | bytes 1572872 | tf_op jit(solution)/shard_map/ppermute | solution.py:787
  86.9 18.9 %collective-permute-start.20 = (bf16[256,512]{1,0:T(8,128)(2,1)S(1)}, bf16[256,512]{1,0:T(8,128)(2,1)S(1)}, u32[]{:S(2)}, u32[]{:S(2)}) collective-permute-start(bf16[256,512]{1,0:T(8,128)(2,1)S(1)} %get-tuple-element.200.refs_0_), channel_id=1, source_target_pairs={{0,8},{4,12},{8,0},{12,4},{16,24},{20,28},{24,16},{28,20},{1,9},{5... | collective-permute-start | bytes 786440 | tf_op jit(solution)/shard_map/ppermute | solution.py:787
  96.1 15.8 %collective-permute-start.21 = (f32[8,768]{1,0:T(8,128)S(1)}, f32[8,768]{1,0:T(8,128)S(1)}, u32[]{:S(2)}, u32[]{:S(2)}) collective-permute-start(f32[8,768]{1,0:T(8,128)S(1)} %get-tuple-element.213), channel_id=1, source_target_pairs={{4,0},{8,4},{12,8},{16,12},{20,16},{24,20},{28,24},{5,1},{9,5},{13... | collective-permute-start | bytes 73736 | tf_op jit(solution)/shard_map/ppermute | solution.py:1441
  98.1 10.7 %collective-permute-start.22 = (bf16[256,512]{1,0:T(8,128)(2,1)S(1)}, bf16[256,512]{1,0:T(8,128)(2,1)S(1)}, u32[]{:S(2)}, u32[]{:S(2)}) collective-permute-start(bf16[256,512]{1,0:T(8,128)(2,1)S(1)} %get-tuple-element.206.refs_5_), channel_id=1, source_target_pairs={{0,8},{4,12},{8,0},{12,4},{16,24},{20,28},{24,16},{28,20},{1,9},{5... | collective-permute-start | bytes 786440 | tf_op jit(solution)/shard_map/ppermute | solution.py:787
  104.9 14.3 %collective-permute-start.19 = (bf16[512,512]{1,0:T(8,128)(2,1)S(1)}, bf16[512,512]{1,0:T(8,128)(2,1)S(1)}, u32[]{:S(2)}, u32[]{:S(2)}) collective-permute-start(bf16[512,512]{1,0:T(8,128)(2,1)S(1)} %get-tuple-element.208.refs_0_), channel_id=1, source_target_pairs={{0,4},{4,0},{8,12},{12,8},{16,20},{20,16},{24,28},{28,24},{1,5},{5... | collective-permute-start | bytes 1572872 | tf_op jit(solution)/shard_map/ppermute | solution.py:787
  106.4 11.1 %collective-permute-start.23 = (bf16[128,512]{1,0:T(8,128)(2,1)S(1)}, bf16[128,512]{1,0:T(8,128)(2,1)S(1)}, u32[]{:S(2)}, u32[]{:S(2)}) collective-permute-start(bf16[128,512]{1,0:T(8,128)(2,1)S(1)} %get-tuple-element.211.refs_6_), channel_id=1, source_target_pairs={{0,16},{4,20},{8,24},{12,28},{16,0},{20,4},{24,8},{28,12},{1,17},{... | collective-permute-start | bytes 393224 | tf_op jit(solution)/shard_map/ppermute | solution.py:787
  109.5 11.8 %collective-permute-start.27 = (bf16[128,512]{1,0:T(8,128)(2,1)S(1)}, bf16[128,512]{1,0:T(8,128)(2,1)S(1)}, u32[]{:S(2)}, u32[]{:S(2)}) collective-permute-start(bf16[128,512]{1,0:T(8,128)(2,1)S(1)} %get-tuple-element.216.refs_0_), channel_id=1, source_target_pairs={{0,16},{4,20},{8,24},{12,28},{16,0},{20,4},{24,8},{28,12},{1,17},{... | collective-permute-start | bytes 393224 | tf_op jit(solution)/shard_map/ppermute | solution.py:787
  117.6 11.1 %collective-permute-start.29 = (bf16[128,512]{1,0:T(8,128)(2,1)S(1)}, bf16[128,512]{1,0:T(8,128)(2,1)S(1)}, u32[]{:S(2)}, u32[]{:S(2)}) collective-permute-start(bf16[128,512]{1,0:T(8,128)(2,1)S(1)} %add.27.refs_2_.refs_1_), channel_id=1, source_target_pairs={{0,16},{4,20},{8,24},{12,28},{16,0},{20,4},{24,8},{28,12},{1,17},{... | collective-permute-start | bytes 393224 | tf_op jit(solution)/shard_map/ppermute | solution.py:787
  118.6 4.8 %collective-permute-start.25 = (bf16[544,256]{1,0:T(8,128)(2,1)S(1)}, bf16[544,256]{1,0:T(8,128)(2,1)S(1)}, u32[]{:S(2)}, u32[]{:S(2)}) collective-permute-start(bf16[544,256]{1,0:T(8,128)(2,1)S(1)} %lead.1.refs_0_), channel_id=1, source_target_pairs={{0,1},{1,0},{2,3},{3,2},{4,5},{5,4},{6,7},{7,6},{8,9},{9,8},{10,11... | collective-permute-start | bytes 835592 | tf_op jit(solution)/shard_map/ppermute | solution.py:787
  118.7 3.3 %collective-permute-start.26 = (bf16[256,1024]{1,0:T(8,128)(2,1)S(1)}, bf16[256,1024]{1,0:T(8,128)(2,1)S(1)}, u32[]{:S(2)}, u32[]{:S(2)}) collective-permute-start(bf16[256,1024]{1,0:T(8,128)(2,1)S(1)} %get-tuple-element.224), channel_id=1, source_target_pairs={{0,1},{1,0},{2,3},{3,2},{4,5},{5,4},{6,7},{7,6},{8,9},{9,8},{10,11... | collective-permute-start | bytes 1572872 | tf_op jit(solution)/shard_map/ppermute | solution.py:787
  119.2 4.9 %collective-permute-start.30 = (bf16[256,1024]{1,0:T(8,128)(2,1)S(1)}, bf16[256,1024]{1,0:T(8,128)(2,1)S(1)}, u32[]{:S(2)}, u32[]{:S(2)}) collective-permute-start(bf16[256,1024]{1,0:T(8,128)(2,1)S(1)} %get-tuple-element.230), channel_id=1, source_target_pairs={{0,1},{1,0},{2,3},{3,2},{4,5},{5,4},{6,7},{7,6},{8,9},{9,8},{10,11... | collective-permute-start | bytes 1572872 | tf_op jit(solution)/shard_map/ppermute | solution.py:787
  121.4 13.9 %collective-permute-start.35 = (bf16[128,512]{1,0:T(8,128)(2,1)S(1)}, bf16[128,512]{1,0:T(8,128)(2,1)S(1)}, u32[]{:S(2)}, u32[]{:S(2)}) collective-permute-start(bf16[128,512]{1,0:T(8,128)(2,1)S(1)} %add.28.refs_0_.refs_1_), channel_id=1, source_target_pairs={{0,16},{4,20},{8,24},{12,28},{16,0},{20,4},{24,8},{28,12},{1,17},{... | collective-permute-start | bytes 393224 | tf_op jit(solution)/shard_map/ppermute | solution.py:787
  122.0 11.7 %collective-permute-start.24 = (bf16[256,512]{1,0:T(8,128)(2,1)S(1)}, bf16[256,512]{1,0:T(8,128)(2,1)S(1)}, u32[]{:S(2)}, u32[]{:S(2)}) collective-permute-start(bf16[256,512]{1,0:T(8,128)(2,1)S(1)} %get-tuple-element.221.refs_0_), channel_id=1, source_target_pairs={{0,8},{4,12},{8,0},{12,4},{16,24},{20,28},{24,16},{28,20},{1,9},{5... | collective-permute-start | bytes 786440 | tf_op jit(solution)/shard_map/ppermute | solution.py:787
  124.2 6.1 %collective-permute-start.28 = (bf16[288,256]{1,0:T(8,128)(2,1)S(1)}, bf16[288,256]{1,0:T(8,128)(2,1)S(1)}, u32[]{:S(2)}, u32[]{:S(2)}) collective-permute-start(bf16[288,256]{1,0:T(8,128)(2,1)S(1)} %get-tuple-element.228), channel_id=1, source_target_pairs={{0,2},{1,3},{2,0},{3,1},{4,6},{5,7},{6,4},{7,5},{8,10},{9,11},{10,... | collective-permute-start | bytes 442376 | tf_op jit(solution)/shard_map/ppermute | solution.py:787
  129.2 12.0 %collective-permute-start.33 = (bf16[256,512]{1,0:T(8,128)(2,1)S(1)}, bf16[256,512]{1,0:T(8,128)(2,1)S(1)}, u32[]{:S(2)}, u32[]{:S(2)}) collective-permute-start(bf16[256,512]{1,0:T(8,128)(2,1)S(1)} %join.7.refs_0_.refs_1_), channel_id=1, source_target_pairs={{0,8},{4,12},{8,0},{12,4},{16,24},{20,28},{24,16},{28,20},{1,9},{5... | collective-permute-start | bytes 786440 | tf_op jit(solution)/shard_map/ppermute | solution.py:787
  129.3 15.6 %collective-permute-start.32 = (bf16[256,1024]{1,0:T(8,128)(2,1)S(1)}, bf16[256,1024]{1,0:T(8,128)(2,1)S(1)}, u32[]{:S(2)}, u32[]{:S(2)}) collective-permute-start(bf16[256,1024]{1,0:T(8,128)(2,1)S(1)} %add.30.refs_0_), channel_id=1, source_target_pairs={{0,2},{1,3},{2,0},{3,1},{4,6},{5,7},{6,4},{7,5},{8,10},{9,11},{10,... | collective-permute-start | bytes 1572872 | tf_op jit(solution)/shard_map/ppermute | solution.py:787
  130.4 7.3 %collective-permute-start.34 = (bf16[384,256]{1,0:T(8,128)(2,1)S(1)}, bf16[384,256]{1,0:T(8,128)(2,1)S(1)}, u32[]{:S(2)}, u32[]{:S(2)}) collective-permute-start(bf16[384,256]{1,0:T(8,128)(2,1)S(1)} %misc_pack.1.refs_0_), channel_id=1, source_target_pairs={{0,4},{4,0},{8,12},{12,8},{16,20},{20,16},{24,28},{28,24},{1,5},{5... | collective-permute-start | bytes 589832 | tf_op jit(solution)/shard_map/ppermute | solution.py:787
  134.4 13.3 %collective-permute-start.31 = (bf16[128,512]{1,0:T(8,128)(2,1)S(1)}, bf16[128,512]{1,0:T(8,128)(2,1)S(1)}, u32[]{:S(2)}, u32[]{:S(2)}) collective-permute-start(bf16[128,512]{1,0:T(8,128)(2,1)S(1)} %get-tuple-element.232.refs_0_), channel_id=1, source_target_pairs={{0,16},{4,20},{8,24},{12,28},{16,0},{20,4},{24,8},{28,12},{1,17},{... | collective-permute-start | bytes 393224 | tf_op jit(solution)/shard_map/ppermute | solution.py:787
  135.8 19.1 %collective-permute-start.38 = (bf16[256,512]{1,0:T(8,128)(2,1)S(1)}, bf16[256,512]{1,0:T(8,128)(2,1)S(1)}, u32[]{:S(2)}, u32[]{:S(2)}) collective-permute-start(bf16[256,512]{1,0:T(8,128)(2,1)S(1)} %join.8.refs_0_.refs_1_), channel_id=1, source_target_pairs={{0,8},{4,12},{8,0},{12,4},{16,24},{20,28},{24,16},{28,20},{1,9},{5... | collective-permute-start | bytes 786440 | tf_op jit(solution)/shard_map/ppermute | solution.py:787
  137.8 15.5 %collective-permute-start.39 = (bf16[384,256]{1,0:T(8,128)(2,1)S(1)}, bf16[384,256]{1,0:T(8,128)(2,1)S(1)}, u32[]{:S(2)}, u32[]{:S(2)}) collective-permute-start(bf16[384,256]{1,0:T(8,128)(2,1)S(1)} %misc_add.2.refs_0_), channel_id=1, source_target_pairs={{0,8},{4,12},{8,0},{12,4},{16,24},{20,28},{24,16},{28,20},{1,9},{5... | collective-permute-start | bytes 589832 | tf_op jit(solution)/shard_map/ppermute | solution.py:787
  141.8 32.6 %collective-permute-start.48 = (bf16[512,512]{1,0:T(8,128)(2,1)S(1)}, bf16[512,512]{1,0:T(8,128)(2,1)S(1)}, u32[]{:S(2)}, u32[]{:S(2)}) collective-permute-start(bf16[512,512]{1,0:T(8,128)(2,1)S(1)} %join.9.refs_0_.refs_1_), channel_id=1, source_target_pairs={{0,4},{4,0},{8,12},{12,8},{16,20},{20,16},{24,28},{28,24},{1,5},{5... | collective-permute-start | bytes 1572872 | tf_op jit(solution)/shard_map/ppermute | solution.py:787
  147.7 9.0 %collective-permute-start.42 = (bf16[128,512]{1,0:T(8,128)(2,1)S(1)}, bf16[128,512]{1,0:T(8,128)(2,1)S(1)}, u32[]{:S(2)}, u32[]{:S(2)}) collective-permute-start(bf16[128,512]{1,0:T(8,128)(2,1)S(1)} %add.31.refs_2_.refs_1_), channel_id=1, source_target_pairs={{0,16},{4,20},{8,24},{12,28},{16,0},{20,4},{24,8},{28,12},{1,17},{... | collective-permute-start | bytes 393224 | tf_op jit(solution)/shard_map/ppermute | solution.py:787
  151.0 2.0 %collective-permute-start.36 = (bf16[256,1024]{1,0:T(8,128)(2,1)S(1)}, bf16[256,1024]{1,0:T(8,128)(2,1)S(1)}, u32[]{:S(2)}, u32[]{:S(2)}) collective-permute-start(bf16[256,1024]{1,0:T(8,128)(2,1)S(1)} %get-tuple-element.235), channel_id=1, source_target_pairs={{0,1},{1,0},{2,3},{3,2},{4,5},{5,4},{6,7},{7,6},{8,9},{9,8},{10,11... | collective-permute-start | bytes 1572872 | tf_op jit(solution)/shard_map/ppermute | solution.py:787
  153.0 3.5 %collective-permute-start.37 = (bf16[256,1024]{1,0:T(8,128)(2,1)S(1)}, bf16[256,1024]{1,0:T(8,128)(2,1)S(1)}, u32[]{:S(2)}, u32[]{:S(2)}) collective-permute-start(bf16[256,1024]{1,0:T(8,128)(2,1)S(1)} %get-tuple-element.236.refs_0_), channel_id=1, source_target_pairs={{0,1},{1,0},{2,3},{3,2},{4,5},{5,4},{6,7},{7,6},{8,9},{9,8},{10,11... | collective-permute-start | bytes 1572872 | tf_op jit(solution)/shard_map/ppermute | solution.py:787
  153.3 17.9 %collective-permute-start.41 = (bf16[384,256]{1,0:T(8,128)(2,1)S(1)}, bf16[384,256]{1,0:T(8,128)(2,1)S(1)}, u32[]{:S(2)}, u32[]{:S(2)}) collective-permute-start(bf16[384,256]{1,0:T(8,128)(2,1)S(1)} %misc_add.3.refs_0_), channel_id=1, source_target_pairs={{0,16},{4,20},{8,24},{12,28},{16,0},{20,4},{24,8},{28,12},{1,17},{... | collective-permute-start | bytes 589832 | tf_op jit(solution)/shard_map/ppermute | solution.py:787
  155.5 23.1 %collective-permute-start.46 = (bf16[512,512]{1,0:T(8,128)(2,1)S(1)}, bf16[512,512]{1,0:T(8,128)(2,1)S(1)}, u32[]{:S(2)}, u32[]{:S(2)}) collective-permute-start(bf16[512,512]{1,0:T(8,128)(2,1)S(1)} %join.10.refs_0_.refs_1_), channel_id=1, source_target_pairs={{0,4},{4,0},{8,12},{12,8},{16,20},{20,16},{24,28},{28,24},{1,5},{5... | collective-permute-start | bytes 1572872 | tf_op jit(solution)/shard_map/ppermute | solution.py:787
  157.3 11.3 %collective-permute-start.43 = (bf16[256,512]{1,0:T(8,128)(2,1)S(1)}, bf16[256,512]{1,0:T(8,128)(2,1)S(1)}, u32[]{:S(2)}, u32[]{:S(2)}) collective-permute-start(bf16[256,512]{1,0:T(8,128)(2,1)S(1)} %join.11.refs_0_.refs_1_), channel_id=1, source_target_pairs={{0,8},{4,12},{8,0},{12,4},{16,24},{20,28},{24,16},{28,20},{1,9},{5... | collective-permute-start | bytes 786440 | tf_op jit(solution)/shard_map/ppermute | solution.py:787
  159.5 18.2 %collective-permute-start.40 = (bf16[256,1024]{1,0:T(8,128)(2,1)S(1)}, bf16[256,1024]{1,0:T(8,128)(2,1)S(1)}, u32[]{:S(2)}, u32[]{:S(2)}) collective-permute-start(bf16[256,1024]{1,0:T(8,128)(2,1)S(1)} %add.33.refs_0_), channel_id=1, source_target_pairs={{0,2},{1,3},{2,0},{3,1},{4,6},{5,7},{6,4},{7,5},{8,10},{9,11},{10,... | collective-permute-start | bytes 1572872 | tf_op jit(solution)/shard_map/ppermute | solution.py:787
  169.2 13.1 %collective-permute-start.45 = (bf16[512,512]{1,0:T(8,128)(2,1)S(1)}, bf16[512,512]{1,0:T(8,128)(2,1)S(1)}, u32[]{:S(2)}, u32[]{:S(2)}) collective-permute-start(bf16[512,512]{1,0:T(8,128)(2,1)S(1)} %join.12.refs_0_.refs_1_), channel_id=1, source_target_pairs={{0,4},{4,0},{8,12},{12,8},{16,20},{20,16},{24,28},{28,24},{1,5},{5... | collective-permute-start | bytes 1572872 | tf_op jit(solution)/shard_map/ppermute | solution.py:787
  171.9 5.0 %collective-permute-start.44 = (bf16[256,256]{1,0:T(8,128)(2,1)S(1)}, bf16[256,256]{1,0:T(8,128)(2,1)S(1)}, u32[]{:S(2)}, u32[]{:S(2)}) collective-permute-start(bf16[256,256]{1,0:T(8,128)(2,1)S(1)} %get-tuple-element.238.refs_1_), channel_id=1, source_target_pairs={{0,2},{1,3},{2,0},{3,1},{4,6},{5,7},{6,4},{7,5},{8,10},{9,11},{10,... | collective-permute-start | bytes 393224 | tf_op jit(solution)/shard_map/ppermute | solution.py:787
  177.5 2.7 %collective-permute-start.47 = (bf16[512,256]{1,0:T(8,128)(2,1)S(1)}, bf16[512,256]{1,0:T(8,128)(2,1)S(1)}, u32[]{:S(2)}, u32[]{:S(2)}) collective-permute-start(bf16[512,256]{1,0:T(8,128)(2,1)S(1)} %join.13.refs_0_.refs_1_), channel_id=1, source_target_pairs={{0,1},{1,0},{2,3},{3,2},{4,5},{5,4},{6,7},{7,6},{8,9},{9,8},{10,11... | collective-permute-start | bytes 786440 | tf_op jit(solution)/shard_map/ppermute | solution.py:787
  (22 other events, 134.6 us)

commit v9 on v8

--- a/solution.py
+++ b/solution.py
@@ -702,8 +702,8 @@
             )
 
 
-def dgrad_body(k, ggr, gcat, gsr, normed, wzx, wbc, wst, gain, conv, *refs):
-    outs, shared_o, acc = refs[:k], refs[k], refs[k + 1]
+def dgrad_body(half, ggr, gcat, gsr, normed, wzx, wbc, wst, gain, conv, *refs):
+    send_o, keep_o, shared_o, acc = refs
     width, d = wzx.shape[2], gain.shape[1]
     i = pl.program_id(0)
 
@@ -717,15 +717,9 @@
     r = r + dot(gcat[:, width + L :], wbc[1], 1, 1)
     r = r + dot(gsr[...], wst[...])
     acc[...] += eights(r * normed[...].astype(F32))
-    rounded = r.astype(BF)
-
-    def into(out):
-        out[...] = rounded
-
-    for j in range(k):
-        pl.when(i == j)(functools.partial(into, outs[j]))
-
-    @pl.when(i == k - 1)
+    into_two(half, r.astype(BF), send_o, keep_o)
+
+    @pl.when(i == 2 * half - 1)
     def _():
         shared_o[...] = jnp.zeros_like(shared_o)
         sums = jnp.sum(acc[...], axis=0, keepdims=True) / gain[...]
@@ -734,29 +728,58 @@
         shared_o[d // ROW : d // ROW + 5, :] = conv[0:5, conv.shape[1] - ROW :]
 
 
-def outproj_body(k, normout, wout, *outs):
-    def one(out):
-        out[...] = dot(normout[...], wout[...]).astype(BF)
-
-    for j in range(k):
-        pl.when(pl.program_id(0) == j)(functools.partial(one, outs[j]))
-
-
-def rows_times(body, frames_n, share, d, rows, consts, name, more=(), scratch=()):
-    k = frames_n
-    outs = launch(
-        functools.partial(body, k),
+def outproj_body(half, normout, wout, send_o, keep_o):
+    into_two(half, dot(normout[...], wout[...]).astype(BF), send_o, keep_o)
+
+
+def exchange_order(count):
+    if count == 1:
+        return [0]
+    inner = exchange_order(count // 2)
+    return [2 * f + 1 for f in inner] + [2 * f for f in inner]
+
+
+def rows_times(body, count, share, d, rows, consts, name, more=(), scratch=()):
+    half = count // 2
+    frames = [2 * f + odd for odd in (1, 0) for f in reversed(exchange_order(half))]
+
+    def frame(i):
+        return sum(jnp.where(i == k, f, 0) for k, f in enumerate(frames))
+
+    return launch(
+        functools.partial(body, half),
         [*rows, *consts],
-        [pl.BlockSpec((share, r.shape[1]), lambda i: (k - 1 - i, 0)) for r in rows]
+        [pl.BlockSpec((share, r.shape[1]), lambda i: (frame(i), 0)) for r in rows]
         + [whole(a) for a in consts],
-        [shaped((share, d), BF)] * k + list(more),
-        [pl.BlockSpec((share, d), lambda i: (0, 0))] * k + [whole(o) for o in more],
+        [shaped((half * share, d), BF)] * 2 + list(more),
+        [
+            pl.BlockSpec((share, d), lambda i: (jnp.minimum(i, half - 1), 0)),
+            pl.BlockSpec((share, d), lambda i: (jnp.maximum(i - half, 0), 0)),
+            *[whole(o) for o in more],
+        ],
         name,
-        grid=(k,),
+        grid=(count,),
         scratch=scratch,
         vmem=20,
     )
-    return [*outs[:k][::-1], *outs[k:]]
+
+
+def into_two(half, value, send_o, keep_o):
+    i = pl.program_id(0)
+
+    @pl.when(i < half)
+    def _():
+        send_o[...] = value
+
+    @pl.when(i >= half)
+    def _():
+        keep_o[...] = value
+
+
+def part_body(kept, got, keep_o, send_o):
+    half = keep_o.shape[0]
+    for o, rows in ((keep_o, slice(0, half)), (send_o, slice(half, 2 * half))):
+        o[...] = (kept[rows, :].astype(F32) + got[rows, :].astype(F32)).astype(BF)
 
 
 def total_body(*refs):
@@ -1095,7 +1118,7 @@
     last: Any
 
 
-ORDER = "WLLFLGFWLGTIWMGTWMIGTMTWMIGMWTIBBMGBIIMWMBGMI"
+ORDER = "WLLFLGFWLGTIWMGTWMIGTMWMIGMWTIBMGBIIMWMBGMI"
 
 
 def run_chains(chains, done, order):
@@ -1412,26 +1435,20 @@
                 [], True, 16, (begin, half), kept.within,
             )
 
-    def scattered(frames_in):
-        sums_in = []
-        for first in (0, half):
-            part = dict(enumerate(frames_in[first : first + half]))
-            mask = 1
-            while mask < half:
-                for f in [f for f in part if f & mask]:
-                    got = swap(part.pop(f), TP, mask)
-                    yield None, True
-                    part[f ^ mask] = add(part[f ^ mask], got)
-                mask *= 2
-            sums_in.append(part[0])
-        got = swap(sums_in[1], TP, half)
+    def scattered(send, keep):
+        for mask in tmasks[:-1]:
+            got = swap(send, TP, mask)
+            yield None, True
+            shape = shaped((keep.shape[0] // 2, d), BF)
+            keep, send = simple(part_body, [keep, got], [shape, shape], "part")
+        got = swap(send, TP, half)
         yield None, True
-        return sums_in[0], got
+        return keep, got
 
     def branch_chain():
         yield None, False
         branch = rows_times(outproj_body, group, share, d, [normout], [weight_out], "outproj")
-        parts = yield from scattered(branch)
+        parts = yield from scattered(*branch)
         (kept.layer,) = simple(
             layer_body, [tokens_in, *parts], [shaped((share, d), BF)], "layer", tick=True
         )
@@ -1447,7 +1464,7 @@
             "dgrad", [shaped((16, ROW))], [pltpu.VMEM((8, d), F32)],
         )
         done.add("dgrad")
-        parts = yield from scattered(grads)
+        parts = yield from scattered(*grads)
         (kept.tokens,) = simple(
             tokens_body, [tokens_in, grad_out, *parts, gain], [shaped((share, d))], "tokens",
             None, 12, tick=True,

time: 184 us -> 186 us (1.011)
  starting transfers between devices: 51.4 us -> 53.4 us
    ppermute x46 -> x44, starting transfers between devices: 48.8 us -> 50.7 us  [swap(): return lax.ppermute(x, axis, [(i, i ^ mask) for i in range(count)])]
    ppermute x46 -> x44, waiting for transfers between devices: 34.5 us -> 34 us  [swap(): return lax.ppermute(x, axis, [(i, i ^ mask) for i in range(count)])]
    pallas_call x108 -> x104, Pallas kernels: 90.1 us -> 90.3 us  [launch(): pl.pallas_call(run, grid_spec=pltpu.PrefetchScalarGridSpec(num_scalar_pre...]
  transfers between devices with their start and end apart: 49 -> 47, of which waited for: 15 -> 14; matrix products, arithmetic and copies ran while one was open for 0% -> 0% of each run, Pallas kernels for 44% -> 44%
where the time goes in v9:
time: 186 us; the launch traced here: 185 us
  Pallas kernels  90.3 us (49%)
  starting transfers between devices  53.4 us (29%)
  waiting for transfers between devices  34 us (18%)
  local copies, waits for them, and re-layouts  5.33 us (3%)
    pallas_call x104, Pallas kernels, launch(): pl.pallas_call(run, grid_spec=pltpu.PrefetchScalarGridSpec(num_scalar_pre...  90.3 us
    ppermute x44, starting transfers between devices, swap(): return lax.ppermute(x, axis, [(i, i ^ mask) for i in range(count)])  50.7 us
    ppermute x44, waiting for transfers between devices, swap(): return lax.ppermute(x, axis, [(i, i ^ mask) for i in range(count)])  34 us
    unnamed x42, local copies, waits for them, and re-layouts  5.31 us
  transfers between devices with their start and end apart: 47, of which 14 were waited for; matrix products, arithmetic and copies ran while one was open for 0% of the time, Pallas kernels for 44%

profile of v9, /device:TPU:0, one launch (start us, length us, event | category | flops | bytes accessed | tf_op | source)
XLA Modules:
  0.0 185.4 jit_solution(1189393169091027683)
XLA Ops:
  1.2 2.6 %collective-permute-start = (bf16[256,1024]{1,0:T(8,128)(2,1)}, bf16[256,1024]{1,0:T(8,128)(2,1)S(1)}, u32[]{:S(2)}, u32[]{:S(2)}) collective-permute-start(bf16[256,1024]{1,0:T(8,128)(2,1)} %refs_0_.11), channel_id=1, source_target_pairs={{0,2},{1,3},{2,0},{3,1},{4,6},{5,7},{6,4},{7,5},{8,10},{9,11},{10,... | collective-permute-start | bytes 1572872 | tf_op jit(solution)/shard_map/ppermute | solution.py:810
  8.2 1.7 copy-done
  10.1 3.1 %project.3 = (bf16[1024,1024]{1,0:T(8,128)(2,1)S(1)}, bf16[1024,512]{1,0:T(8,128)(2,1)S(1)}, bf16[1024,768]{1,0:T(8,128)(2,1)S(1)}, bf16[1024,128]{1,0:T(8,128)(2,1)S(1)}) custom-call(s32[11]{0:T(128)S(1)} %pad_add_fusion.refs_0_, bf16[256,1024]{1,0:T(8,128)(2,1)S(1)} %copy-done.5, bf16[256,1024]{1,0:T(8,128)(2,1)S(1)} %collective-permute-done.1.refs_1_.refs_2_, ...), custom_call_target="tpu_custom_call" | custom-call | tf_op jit(solution)/shard_map/project/pallas_call | solution.py:97
  13.3 3.5 %collective-permute-done.refs_0_ = bf16[256,1024]{1,0:T(8,128)(2,1)S(1)} collective-permute-done((bf16[256,1024]{1,0:T(8,128)(2,1)}, bf16[256,1024]{1,0:T(8,128)(2,1)S(1)}, u32[]{:S(2)}, u32[]{:S(2)}) %collective-permute-start) | collective-permute-done | bytes 524320 | tf_op jit(solution)/shard_map/ppermute | solution.py:810
  17.4 1.8 project.4
  19.3 2.0 %project.5 = (bf16[1024,1024]{1,0:T(8,128)(2,1)S(1)}, bf16[1024,512]{1,0:T(8,128)(2,1)S(1)}, bf16[1024,768]{1,0:T(8,128)(2,1)S(1)}, bf16[1024,128]{1,0:T(8,128)(...) custom-call(s32[11]{0:T(128)S(1)} %pad_add_fusion.refs_0_, ...), custom_call_target="tpu_custom_call", output_to_operand_aliasing={{0}: (8, {}), {1}: (9, {}), {2}: (10, {}), {3}: (11, {})} | custom-call | tf_op jit(solution)/shard_map/project/pallas_call | solution.py:97
  21.3 5.2 %states.1 = (f32[1024,768]{1,0:T(8,128)S(1)}, bf16[1024,128]{1,0:T(8,128)(2,1)S(1)}, bf16[8,512,128]{2,1,0:T(8,128)(2,1)S(1)}, f32[512,128]{1,0:T(8,128)S(1)}, b...) custom-call(s32[11]{0:T(128)S(1)} %pad_add_fusion.refs_0_, ...), custom_call_target="tpu_custom_call" | custom-call | tf_op jit(solution)/shard_map/states/pallas_call | solution.py:97
  26.5 1.6 collective-permute-start.8
  28.1 1.5 collective-permute-start.7
  29.7 3.6 %within.1.refs_0_.refs_4_ = f32[1024,512]{1,0:T(8,128)S(1)} custom-call(s32[11]{0:T(128)S(1)} %pad_add_fusion.refs_0_, f32[1024,768]{1,0:T(8,128)S(1)} %get-tuple-element.150.refs_1_.refs_3_, bf16[1024,128]{1,0:T(8,128)(2,1)S(1)} %get-tuple-element.146.refs_2_.refs_4_, f32[1024,128]{1,0:T(8,128)S(1)} %get-tuple-element.151.refs_3_.refs_2_.refs_5_, ...), custom_call_target="tpu_custom_call" | custom-call | tf_op jit(solution)/shard_map/within/pallas_call | solution.py:97
  34.1 1.6 collective-permute-start.9
  35.7 3.4 %collective-permute-done.9.refs_5_ = bf16[528,128]{1,0:T(8,128)(2,1)S(1)} collective-permute-done((bf16[528,128]{1,0:T(8,128)(2,1)S(1)}, bf16[528,128]{1,0:T(8,128)(2,1)S(1)}, u32[]{:S(2)}, u32[]{:S(2)}) %collective-permute-start.9) | collective-permute-done | bytes 135200 | tf_op jit(solution)/shard_map/ppermute | solution.py:810
  39.9 2.7 %collective-permute-start.11 = (bf16[528,128]{1,0:T(8,128)(2,1)S(1)}, bf16[528,128]{1,0:T(8,128)(2,1)S(1)}, u32[]{:S(2)}, u32[]{:S(2)}) collective-permute-start(bf16[528,128]{1,0:T(8,128)(2,1)S(1)} %get-tuple-element.167), channel_id=1, source_target_pairs={{0,16},{4,20},{8,24},{12,28},{16,0},{20,4},{24,8},{28,12},{1,17},{... | collective-permute-start | bytes 405512 | tf_op jit(solution)/shard_map/ppermute | solution.py:810
  42.7 1.9 %collective-permute-done.10.refs_3_ = bf16[256,1024]{1,0:T(8,128)(2,1)S(1)} collective-permute-done((bf16[256,1024]{1,0:T(8,128)(2,1)S(1)}, bf16[256,1024]{1,0:T(8,128)(2,1)S(1)}, u32[]{:S(2)}, u32[]{:S(2)}) %collective-permute-start.10) | collective-permute-done | bytes 524320 | tf_op jit(solution)/shard_map/ppermute | solution.py:810
  44.6 2.0 %cotangent.1 = (bf16[1024,1024]{1,0:T(8,128)(2,1)S(1)}, bf16[1024,512]{1,0:T(8,128)(2,1)S(1)}) custom-call(bf16[256,1024]{1,0:T(8,128)(2,1)S(1)} %copy-done.9, bf16[256,1024]{1,0:T(8,128)(2,1)S(1)} %collective-permute-done.6.refs_1_, bf16[256,1024]{1,0:T(8,128)(2,1)S(1)} %collective-permute-done.7.refs_0_.refs_2_, ...), custom_call_target="tpu_custom_call" | custom-call | tf_op jit(solution)/shard_map/cotangent/pallas_call | solution.py:97
  47.9 3.5 %gated.1 = (f32[1024,512]{1,0:T(8,128)S(1)}, f32[8,2,128]{2,1,0:T(2,128)S(1)}, bf16[512,128]{1,0:T(8,128)(2,1)S(1)}) custom-call(s32[11]{0:T(128)S(1)} %pad_add_fusion.refs_0_, bf16[1024,128]{1,0:T(8,128)(2,1)S(1)} %get-tuple-element.152.refs_1_, f32[1024,128]{1,0:T(8,128)S(1)} %get-tuple-element.151.refs_3_.refs_2_.refs_5_, ...), custom_call_target="tpu_custom_call" | custom-call | tf_op jit(solution)/shard_map/gated/pallas_call | solution.py:97
  52.3 2.8 %collective-permute-done.12.refs_1_ = f32[8,2,128]{2,1,0:T(2,128)S(1)} collective-permute-done((f32[8,2,128]{2,1,0:T(2,128)S(1)}, f32[8,2,128]{2,1,0:T(2,128)S(1)}, u32[]{:S(2)}, u32[]{:S(2)}) %collective-permute-start.12) | collective-permute-done | bytes 8224 | tf_op jit(solution)/shard_map/ppermute | solution.py:810
  56.3 4.4 %back_gated.1 = (bf16[1024,512]{1,0:T(8,128)(2,1)S(1)}, bf16[1024,512]{1,0:T(8,128)(2,1)S(1)}, bf16[1024,512]{1,0:T(8,128)(2,1)S(1)}, bf16[8,512,128]{2,1,0:T(8,...) custom-call(s32[11]{0:T(128)S(1)} %pad_add_fusion.refs_0_, ...), custom_call_target="tpu_custom_call" | custom-call | tf_op jit(solution)/shard_map/back_gated/pallas_call | solution.py:97
  61.2 2.3 %wgrad.3 = (bf16[512,512]{1,0:T(8,128)(2,1)S(1)}, bf16[512,512]{1,0:T(8,128)(2,1)S(1)}) custom-call(s32[11]{0:T(128)S(1)} %pad_add_fusion.refs_0_, bf16[1024,512]{1,0:T(8,128)(2,1)S(1)} %get-tuple-element.170.refs_1_.refs_0_, bf16[1024,1024]{1,0:T(8,128)(2,1)S(1)} %get-tuple-element.178.refs_2_, f32[8,512]{1,0:T(8,128)S(1)} %get-tuple-element.179.refs_3_.refs_5_), custom_call_target="tpu_custom_call" | custom-call | tf_op jit(solution)/shard_map/wgrad/pallas_call | solution.py:97
  63.6 1.6 collective-permute-start.17
  68.1 5.7 %back_within.2 = (f32[1024,512]{1,0:T(8,128)S(1)}, f32[1024,256]{1,0:T(8,128)S(1)}, f32[1024,128]{1,0:T(8,128)S(1)}, f32[1024,128]{1,0:T(8,128)S(1)}) custom-call(s32[11]{0:T(128)S(1)} %pad_add_fusion.refs_0_, f32[1024,768]{1,0:T(8,128)S(1)} %get-tuple-element.150.refs_1_.refs_3_, bf16[1024,128]{1,0:T(8,128)(2,1)S(1)} %get-tuple-element.146.refs_2_.refs_4_, ...), custom_call_target="tpu_custom_call" | custom-call | tf_op jit(solution)/shard_map/back_within/pallas_call | solution.py:97
  74.5 3.4 %collective-permute-start.16 = (bf16[528,128]{1,0:T(8,128)(2,1)S(1)}, bf16[528,128]{1,0:T(8,128)(2,1)S(1)}, u32[]{:S(2)}, u32[]{:S(2)}) collective-permute-start(bf16[528,128]{1,0:T(8,128)(2,1)S(1)} %get-tuple-element.198), channel_id=1, source_target_pairs={{0,16},{4,20},{8,24},{12,28},{16,0},{20,4},{24,8},{28,12},{1,17},{... | collective-permute-start | bytes 405512 | tf_op jit(solution)/shard_map/ppermute | solution.py:810
  78.0 2.3 %wgrad.4 = (bf16[512,512]{1,0:T(8,128)(2,1)S(1)}, bf16[512,512]{1,0:T(8,128)(2,1)S(1)}) custom-call(s32[11]{0:T(128)S(1)} %pad_add_fusion.refs_0_, bf16[1024,1024]{1,0:T(8,128)(2,1)S(1)} %get-tuple-element.171.refs_1_.refs_3_, bf16[1024,512]{1,0:T(8,128)(2,1)S(1)} %get-tuple-element.186.refs_2_.refs_0_, f32[8,128]{1,0:T(8,128)S(1)} %get-tuple-element.191.refs_3_.refs_15_), custom_call_target="tpu_custom_call" | custom-call | tf_op jit(solution)/shard_map/wgrad/pallas_call | solution.py:97
  80.6 5.5 %back_within.3 = (f32[1024,512]{1,0:T(8,128)S(1)}, f32[1024,256]{1,0:T(8,128)S(1)}, f32[1024,128]{1,0:T(8,128)S(1)}, f32[1024,128]{1,0:T(8,128)S(1)}) custom-call(s32[11]{0:T(128)S(1)} %pad_add_fusion.refs_0_, f32[1024,768]{1,0:T(8,128)S(1)} %get-tuple-element.150.refs_1_.refs_3_, ...), custom_call_target="tpu_custom_call", output_to_operand_aliasing={{0}: (12, {}), {1}: (13, {}), {2}: (14, {}), {3}: (15, {})} | custom-call | tf_op jit(solution)/shard_map/back_within/pallas_call | solution.py:97
  86.9 9.2 %back_conv.1 = (bf16[1024,768]{1,0:T(8,128)(2,1)S(1)}, bf16[1024,128]{1,0:T(8,128)(2,1)S(1)}, f32[8,768]{1,0:T(8,128)S(1)}, bf16[16,768]{1,0:T(8,128)(2,1)S(1)},...) custom-call(s32[11]{0:T(128)S(1)} %pad_add_fusion.refs_0_, bf16[1024,768]{1,0:T(8,128)(2,1)S(1)} %get-tuple-element.145.refs_1_, ...), custom_call_target="tpu_custom_call" | custom-call | tf_op jit(solution)/shard_map/back_conv/pallas_call | solution.py:97
  98.1 3.9 %collective-permute-start.22 = (bf16[256,512]{1,0:T(8,128)(2,1)S(1)}, bf16[256,512]{1,0:T(8,128)(2,1)S(1)}, u32[]{:S(2)}, u32[]{:S(2)}) collective-permute-start(bf16[256,512]{1,0:T(8,128)(2,1)S(1)} %get-tuple-element.206.refs_5_), channel_id=1, source_target_pairs={{0,8},{4,12},{8,0},{12,4},{16,24},{20,28},{24,16},{28,20},{1,9},{5... | collective-permute-start | bytes 786440 | tf_op jit(solution)/shard_map/ppermute | solution.py:810
  102.0 2.9 %wgrad.5 = (bf16[512,512]{1,0:T(8,128)(2,1)S(1)}, bf16[512,512]{1,0:T(8,128)(2,1)S(1)}) custom-call(s32[11]{0:T(128)S(1)} %pad_add_fusion.refs_0_, bf16[1024,1024]{1,0:T(8,128)(2,1)S(1)} %get-tuple-element.171.refs_1_.refs_3_, bf16[1024,768]{1,0:T(8,128)(2,1)S(1)} %get-tuple-element.201.refs_2_.refs_1_, ...), custom_call_target="tpu_custom_call" | custom-call | tf_op jit(solution)/shard_map/wgrad/pallas_call | solution.py:97
  107.1 1.7 bc_wgrad.1
  109.5 2.4 %collective-permute-start.27 = (bf16[128,512]{1,0:T(8,128)(2,1)S(1)}, bf16[128,512]{1,0:T(8,128)(2,1)S(1)}, u32[]{:S(2)}, u32[]{:S(2)}) collective-permute-start(bf16[128,512]{1,0:T(8,128)(2,1)S(1)} %get-tuple-element.216.refs_0_), channel_id=1, source_target_pairs={{0,16},{4,20},{8,24},{12,28},{16,0},{20,4},{24,8},{28,12},{1,17},{... | collective-permute-start | bytes 393224 | tf_op jit(solution)/shard_map/ppermute | solution.py:810
  112.6 4.9 %dgrad.1 = (bf16[512,1024]{1,0:T(8,128)(2,1)S(1)}, bf16[512,1024]{1,0:T(8,128)(2,1)S(1)}, f32[16,256]{1,0:T(8,128)S(1)}) custom-call(bf16[1024,512]{1,0:T(8,128)(2,1)S(1)} %get-tuple-element.186.refs_2_.refs_0_, bf16[1024,768]{1,0:T(8,128)(2,1)S(1)} %patch.1.refs_1_, bf16[1024,128]{1,0:T(8,128)(2,1)S(1)} %get-tuple-element.209.refs_3_.refs_2_, ...), custom_call_target="tpu_custom_call" | custom-call | tf_op jit(solution)/shard_map/dgrad/pallas_call | solution.py:97
  119.9 1.7 collective-permute-start.24
  127.7 2.0 %collective-permute-done.28.refs_2_ = bf16[288,256]{1,0:T(8,128)(2,1)S(1)} collective-permute-done((bf16[288,256]{1,0:T(8,128)(2,1)S(1)}, bf16[288,256]{1,0:T(8,128)(2,1)S(1)}, u32[]{:S(2)}, u32[]{:S(2)}) %collective-permute-start.28) | collective-permute-done | bytes 147488 | tf_op jit(solution)/shard_map/ppermute | solution.py:810
  129.7 3.5 %collective-permute-done.24.refs_2_ = bf16[256,512]{1,0:T(8,128)(2,1)S(1)} collective-permute-done((bf16[256,512]{1,0:T(8,128)(2,1)S(1)}, bf16[256,512]{1,0:T(8,128)(2,1)S(1)}, u32[]{:S(2)}, u32[]{:S(2)}) %collective-permute-start.24) | collective-permute-done | bytes 262176 | tf_op jit(solution)/shard_map/ppermute | solution.py:810
  134.0 1.6 collective-permute-start.33
  136.2 2.5 %collective-permute-start.36 = (bf16[256,512]{1,0:T(8,128)(2,1)S(1)}, bf16[256,512]{1,0:T(8,128)(2,1)S(1)}, u32[]{:S(2)}, u32[]{:S(2)}) collective-permute-start(bf16[256,512]{1,0:T(8,128)(2,1)S(1)} %join.8.refs_0_.refs_1_), channel_id=1, source_target_pairs={{0,8},{4,12},{8,0},{12,4},{16,24},{20,28},{24,16},{28,20},{1,9},{5... | collective-permute-start | bytes 786440 | tf_op jit(solution)/shard_map/ppermute | solution.py:810
  139.8 2.5 %collective-permute-start.37 = (bf16[384,256]{1,0:T(8,128)(2,1)S(1)}, bf16[384,256]{1,0:T(8,128)(2,1)S(1)}, u32[]{:S(2)}, u32[]{:S(2)}) collective-permute-start(bf16[384,256]{1,0:T(8,128)(2,1)S(1)} %misc_add.2.refs_0_), channel_id=1, source_target_pairs={{0,8},{4,12},{8,0},{12,4},{16,24},{20,28},{24,16},{28,20},{1,9},{5... | collective-permute-start | bytes 589832 | tf_op jit(solution)/shard_map/ppermute | solution.py:810
  142.9 1.8 collective-permute-start.46
  144.7 1.6 out_weights.2.refs_2_
  150.5 2.0 %outproj.1 = (bf16[512,1024]{1,0:T(8,128)(2,1)S(1)}, bf16[512,1024]{1,0:T(8,128)(2,1)S(1)}) custom-call(bf16[1024,512]{1,0:T(8,128)(2,1)S(1)} %copy-done.16, bf16[512,1024]{1,0:T(8,128)(2,1)S(1)} %copy-done.14, bf16[128,512]{1,0:T(8,128)(2,1)S(1)} %add.25.refs_2_.refs_1_), custom_call_target="tpu_custom_call" | custom-call | tf_op jit(solution)/shard_map/outproj/pallas_call | solution.py:97
  152.7 1.6 collective-permute-start.39
  155.2 1.6 zx_weights.4.refs_2_
  157.6 2.4 %collective-permute-start.41 = (bf16[256,512]{1,0:T(8,128)(2,1)S(1)}, bf16[256,512]{1,0:T(8,128)(2,1)S(1)}, u32[]{:S(2)}, u32[]{:S(2)}) collective-permute-start(bf16[256,512]{1,0:T(8,128)(2,1)S(1)} %join.11.refs_0_.refs_1_), channel_id=1, source_target_pairs={{0,8},{4,12},{8,0},{12,4},{16,24},{20,28},{24,16},{28,20},{1,9},{5... | collective-permute-start | bytes 786440 | tf_op jit(solution)/shard_map/ppermute | solution.py:810
  160.8 9.1 %collective-permute-done.41.refs_2_ = bf16[256,512]{1,0:T(8,128)(2,1)S(1)} collective-permute-done((bf16[256,512]{1,0:T(8,128)(2,1)S(1)}, bf16[256,512]{1,0:T(8,128)(2,1)S(1)}, u32[]{:S(2)}, u32[]{:S(2)}) %collective-permute-start.41) | collective-permute-done | bytes 262176 | tf_op jit(solution)/shard_map/ppermute | solution.py:810
  173.4 1.6 zx_weights.5.refs_2_
  175.0 1.6 out_weights.3
  179.3 1.6 zx_weights.6.refs_2_
  180.9 1.6 bc_weights.1
  183.8 1.6 zx_weights.7
  (198 shorter events, 47.4 us)
Async XLA Ops:
  0.6 4.1 %collective-permute-start.1 = (bf16[256,1024]{1,0:T(8,128)(2,1)}, bf16[256,1024]{1,0:T(8,128)(2,1)S(1)}, u32[]{:S(2)}, u32[]{:S(2)}) collective-permute-start(bf16[256,1024]{1,0:T(8,128)(2,1)} %refs_0_.11), channel_id=1, source_target_pairs={{0,1},{1,0},{2,3},{3,2},{4,5},{5,4},{6,7},{7,6},{8,9},{9,8},{10,11... | collective-permute-start | bytes 1572872 | tf_op jit(solution)/shard_map/ppermute | solution.py:810
  1.2 15.6 %collective-permute-start = (bf16[256,1024]{1,0:T(8,128)(2,1)}, bf16[256,1024]{1,0:T(8,128)(2,1)S(1)}, u32[]{:S(2)}, u32[]{:S(2)}) collective-permute-start(bf16[256,1024]{1,0:T(8,128)(2,1)} %refs_0_.11), channel_id=1, source_target_pairs={{0,2},{1,3},{2,0},{3,1},{4,6},{5,7},{6,4},{7,5},{8,10},{9,11},{10,... | collective-permute-start | bytes 1572872 | tf_op jit(solution)/shard_map/ppermute | solution.py:810
  3.7 39.0 %collective-permute-start.6 = (bf16[256,1024]{1,0:T(8,128)(2,1)}, bf16[256,1024]{1,0:T(8,128)(2,1)S(1)}, u32[]{:S(2)}, u32[]{:S(2)}) collective-permute-start(bf16[256,1024]{1,0:T(8,128)(2,1)} %refs_1_.4), channel_id=1, source_target_pairs={{0,1},{1,0},{2,3},{3,2},{4,5},{5,4},{6,7},{7,6},{8,9},{9,8},{10,11... | collective-permute-start | bytes 1572872 | tf_op jit(solution)/shard_map/ppermute | solution.py:810
  5.8 11.1 %collective-permute-start.4 = (bf16[16,1024]{1,0:T(8,128)(2,1)S(1)}, bf16[16,1024]{1,0:T(8,128)(2,1)S(1)}, u32[]{:S(2)}, u32[]{:S(2)}) collective-permute-start(bf16[16,1024]{1,0:T(8,128)(2,1)S(1)} %last_rows.1.refs_9_), channel_id=1, source_target_pairs={{3,7},{7,11},{11,15},{15,19},{19,23},{23,27},{27,31}} | collective-permute-start | bytes 98312 | tf_op jit(solution)/shard_map/ppermute | solution.py:1203
  6.4 10.4 %collective-permute-start.3 = (bf16[16,1024]{1,0:T(8,128)(2,1)S(1)}, bf16[16,1024]{1,0:T(8,128)(2,1)S(1)}, u32[]{:S(2)}, u32[]{:S(2)}) collective-permute-start(bf16[16,1024]{1,0:T(8,128)(2,1)S(1)} %last_rows.1.refs_9_), channel_id=1, source_target_pairs={{3,5},{7,9},{11,13},{15,17},{19,21},{23,25},{27,29}} | collective-permute-start | bytes 98312 | tf_op jit(solution)/shard_map/ppermute | solution.py:1203
  8.1 78.8 %copy-start.2 = (bf16[128,640]{1,0:T(8,128)(2,1)}, bf16[128,640]{1,0:T(8,128)(2,1)S(1)}, u32[]{:S(2)}) copy-start(bf16[128,640]{1,0:T(8,128)(2,1)S(1)} %get-tuple-element.149.refs_6_.refs_7_.refs_11_.refs_10_.refs_19_.refs_2_) | copy-start | bytes 491524
  16.8 2.5 %collective-permute-start.2 = (bf16[256,1024]{1,0:T(8,128)(2,1)S(1)}, bf16[256,1024]{1,0:T(8,128)(2,1)S(1)}, u32[]{:S(2)}, u32[]{:S(2)}) collective-permute-start(bf16[256,1024]{1,0:T(8,128)(2,1)S(1)} %hold.3.refs_2_.refs_1_), channel_id=1, source_target_pairs={{0,1},{1,0},{2,3},{3,2},{4,5},{5,4},{6,7},{7,6},{8,9},{9,8},{10,11... | collective-permute-start | bytes 1572872 | tf_op jit(solution)/shard_map/ppermute | solution.py:810
  16.9 2.4 %collective-permute-start.5 = (bf16[16,1024]{1,0:T(8,128)(2,1)S(1)}, bf16[16,1024]{1,0:T(8,128)(2,1)S(1)}, u32[]{:S(2)}, u32[]{:S(2)}) collective-permute-start(bf16[16,1024]{1,0:T(8,128)(2,1)S(1)} %past.1.refs_10_.refs_0_.refs_2_), channel_id=1, source_target_pairs={{0,1},{1,0},{2,3},{3,2},{4,5},{5,4},{6,7},{7,6},{8,9},{9,8},{10,11... | collective-permute-start | bytes 98312 | tf_op jit(solution)/shard_map/ppermute | solution.py:810
  26.5 6.8 %collective-permute-start.8 = (bf16[528,128]{1,0:T(8,128)(2,1)S(1)}, bf16[528,128]{1,0:T(8,128)(2,1)S(1)}, u32[]{:S(2)}, u32[]{:S(2)}) collective-permute-start(bf16[528,128]{1,0:T(8,128)(2,1)S(1)} %get-tuple-element.158), channel_id=1, source_target_pairs={{0,4},{4,0},{8,12},{12,8},{16,20},{20,16},{24,28},{28,24},{1,5},{5... | collective-permute-start | bytes 405512 | tf_op jit(solution)/shard_map/ppermute | solution.py:810
  28.1 14.4 %collective-permute-start.7 = (bf16[256,1024]{1,0:T(8,128)(2,1)S(1)}, bf16[256,1024]{1,0:T(8,128)(2,1)S(1)}, u32[]{:S(2)}, u32[]{:S(2)}) collective-permute-start(bf16[256,1024]{1,0:T(8,128)(2,1)S(1)} %hold.4.refs_8_), channel_id=1, source_target_pairs={{0,2},{1,3},{2,0},{3,1},{4,6},{5,7},{6,4},{7,5},{8,10},{9,11},{10,... | collective-permute-start | bytes 1572872 | tf_op jit(solution)/shard_map/ppermute | solution.py:810
  34.1 5.1 %collective-permute-start.9 = (bf16[528,128]{1,0:T(8,128)(2,1)S(1)}, bf16[528,128]{1,0:T(8,128)(2,1)S(1)}, u32[]{:S(2)}, u32[]{:S(2)}) collective-permute-start(bf16[528,128]{1,0:T(8,128)(2,1)S(1)} %get-tuple-element.163), channel_id=1, source_target_pairs={{0,8},{4,12},{8,0},{12,4},{16,24},{20,28},{24,16},{28,20},{1,9},{5... | collective-permute-start | bytes 405512 | tf_op jit(solution)/shard_map/ppermute | solution.py:810
  39.9 8.0 %collective-permute-start.11 = (bf16[528,128]{1,0:T(8,128)(2,1)S(1)}, bf16[528,128]{1,0:T(8,128)(2,1)S(1)}, u32[]{:S(2)}, u32[]{:S(2)}) collective-permute-start(bf16[528,128]{1,0:T(8,128)(2,1)S(1)} %get-tuple-element.167), channel_id=1, source_target_pairs={{0,16},{4,20},{8,24},{12,28},{16,0},{20,4},{24,8},{28,12},{1,17},{... | collective-permute-start | bytes 405512 | tf_op jit(solution)/shard_map/ppermute | solution.py:810
  42.6 2.0 %collective-permute-start.10 = (bf16[256,1024]{1,0:T(8,128)(2,1)S(1)}, bf16[256,1024]{1,0:T(8,128)(2,1)S(1)}, u32[]{:S(2)}, u32[]{:S(2)}) collective-permute-start(bf16[256,1024]{1,0:T(8,128)(2,1)S(1)} %hold.5.refs_0_), channel_id=1, source_target_pairs={{0,1},{1,0},{2,3},{3,2},{4,5},{5,4},{6,7},{7,6},{8,9},{9,8},{10,11... | collective-permute-start | bytes 1572872 | tf_op jit(solution)/shard_map/ppermute | solution.py:810
  51.4 3.7 %collective-permute-start.12 = (f32[8,2,128]{2,1,0:T(2,128)S(1)}, f32[8,2,128]{2,1,0:T(2,128)S(1)}, u32[]{:S(2)}, u32[]{:S(2)}) collective-permute-start(f32[8,2,128]{2,1,0:T(2,128)S(1)} %get-tuple-element.169.refs_0_), channel_id=1, source_target_pairs={{0,2},{1,3},{2,0},{3,1},{4,6},{5,7},{6,4},{7,5},{8,10},{9,11},{10,... | collective-permute-start | bytes 24584 | tf_op jit(solution)/shard_map/ppermute | solution.py:810
  55.1 1.2 collective-permute-start.13
  60.7 5.9 %collective-permute-start.14 = (bf16[528,128]{1,0:T(8,128)(2,1)S(1)}, bf16[528,128]{1,0:T(8,128)(2,1)S(1)}, u32[]{:S(2)}, u32[]{:S(2)}) collective-permute-start(bf16[528,128]{1,0:T(8,128)(2,1)S(1)} %get-tuple-element.177), channel_id=1, source_target_pairs={{0,4},{4,0},{8,12},{12,8},{16,20},{20,16},{24,28},{28,24},{1,5},{5... | collective-permute-start | bytes 405512 | tf_op jit(solution)/shard_map/ppermute | solution.py:810
  63.6 22.6 %collective-permute-start.17 = (bf16[512,512]{1,0:T(8,128)(2,1)S(1)}, bf16[512,512]{1,0:T(8,128)(2,1)S(1)}, u32[]{:S(2)}, u32[]{:S(2)}) collective-permute-start(bf16[512,512]{1,0:T(8,128)(2,1)S(1)} %get-tuple-element.180.refs_0_), channel_id=1, source_target_pairs={{0,4},{4,0},{8,12},{12,8},{16,20},{20,16},{24,28},{28,24},{1,5},{5... | collective-permute-start | bytes 1572872 | tf_op jit(solution)/shard_map/ppermute | solution.py:810
  67.3 6.4 %collective-permute-start.15 = (bf16[528,128]{1,0:T(8,128)(2,1)S(1)}, bf16[528,128]{1,0:T(8,128)(2,1)S(1)}, u32[]{:S(2)}, u32[]{:S(2)}) collective-permute-start(bf16[528,128]{1,0:T(8,128)(2,1)S(1)} %get-tuple-element.190), channel_id=1, source_target_pairs={{0,8},{4,12},{8,0},{12,4},{16,24},{20,28},{24,16},{28,20},{1,9},{5... | collective-permute-start | bytes 405512 | tf_op jit(solution)/shard_map/ppermute | solution.py:810
  74.5 12.4 %collective-permute-start.16 = (bf16[528,128]{1,0:T(8,128)(2,1)S(1)}, bf16[528,128]{1,0:T(8,128)(2,1)S(1)}, u32[]{:S(2)}, u32[]{:S(2)}) collective-permute-start(bf16[528,128]{1,0:T(8,128)(2,1)S(1)} %get-tuple-element.198), channel_id=1, source_target_pairs={{0,16},{4,20},{8,24},{12,28},{16,0},{20,4},{24,8},{28,12},{1,17},{... | collective-permute-start | bytes 405512 | tf_op jit(solution)/shard_map/ppermute | solution.py:810
  80.2 17.2 %collective-permute-start.18 = (bf16[512,512]{1,0:T(8,128)(2,1)S(1)}, bf16[512,512]{1,0:T(8,128)(2,1)S(1)}, u32[]{:S(2)}, u32[]{:S(2)}) collective-permute-start(bf16[512,512]{1,0:T(8,128)(2,1)S(1)} %get-tuple-element.192.refs_16_), channel_id=1, source_target_pairs={{0,4},{4,0},{8,12},{12,8},{16,20},{20,16},{24,28},{28,24},{1,5},{5... | collective-permute-start | bytes 1572872 | tf_op jit(solution)/shard_map/ppermute | solution.py:810
  86.8 18.9 %collective-permute-start.20 = (bf16[256,512]{1,0:T(8,128)(2,1)S(1)}, bf16[256,512]{1,0:T(8,128)(2,1)S(1)}, u32[]{:S(2)}, u32[]{:S(2)}) collective-permute-start(bf16[256,512]{1,0:T(8,128)(2,1)S(1)} %get-tuple-element.200.refs_0_), channel_id=1, source_target_pairs={{0,8},{4,12},{8,0},{12,4},{16,24},{20,28},{24,16},{28,20},{1,9},{5... | collective-permute-start | bytes 786440 | tf_op jit(solution)/shard_map/ppermute | solution.py:810
  96.1 15.8 %collective-permute-start.21 = (f32[8,768]{1,0:T(8,128)S(1)}, f32[8,768]{1,0:T(8,128)S(1)}, u32[]{:S(2)}, u32[]{:S(2)}) collective-permute-start(f32[8,768]{1,0:T(8,128)S(1)} %get-tuple-element.213), channel_id=1, source_target_pairs={{4,0},{8,4},{12,8},{16,12},{20,16},{24,20},{28,24},{5,1},{9,5},{13... | collective-permute-start | bytes 73736 | tf_op jit(solution)/shard_map/ppermute | solution.py:1458
  98.1 10.7 %collective-permute-start.22 = (bf16[256,512]{1,0:T(8,128)(2,1)S(1)}, bf16[256,512]{1,0:T(8,128)(2,1)S(1)}, u32[]{:S(2)}, u32[]{:S(2)}) collective-permute-start(bf16[256,512]{1,0:T(8,128)(2,1)S(1)} %get-tuple-element.206.refs_5_), channel_id=1, source_target_pairs={{0,8},{4,12},{8,0},{12,4},{16,24},{20,28},{24,16},{28,20},{1,9},{5... | collective-permute-start | bytes 786440 | tf_op jit(solution)/shard_map/ppermute | solution.py:810
  104.9 14.3 %collective-permute-start.19 = (bf16[512,512]{1,0:T(8,128)(2,1)S(1)}, bf16[512,512]{1,0:T(8,128)(2,1)S(1)}, u32[]{:S(2)}, u32[]{:S(2)}) collective-permute-start(bf16[512,512]{1,0:T(8,128)(2,1)S(1)} %get-tuple-element.208.refs_0_), channel_id=1, source_target_pairs={{0,4},{4,0},{8,12},{12,8},{16,20},{20,16},{24,28},{28,24},{1,5},{5... | collective-permute-start | bytes 1572872 | tf_op jit(solution)/shard_map/ppermute | solution.py:810
  106.4 11.1 %collective-permute-start.23 = (bf16[128,512]{1,0:T(8,128)(2,1)S(1)}, bf16[128,512]{1,0:T(8,128)(2,1)S(1)}, u32[]{:S(2)}, u32[]{:S(2)}) collective-permute-start(bf16[128,512]{1,0:T(8,128)(2,1)S(1)} %get-tuple-element.211.refs_6_), channel_id=1, source_target_pairs={{0,16},{4,20},{8,24},{12,28},{16,0},{20,4},{24,8},{28,12},{1,17},{... | collective-permute-start | bytes 393224 | tf_op jit(solution)/shard_map/ppermute | solution.py:810
  109.5 12.0 %collective-permute-start.27 = (bf16[128,512]{1,0:T(8,128)(2,1)S(1)}, bf16[128,512]{1,0:T(8,128)(2,1)S(1)}, u32[]{:S(2)}, u32[]{:S(2)}) collective-permute-start(bf16[128,512]{1,0:T(8,128)(2,1)S(1)} %get-tuple-element.216.refs_0_), channel_id=1, source_target_pairs={{0,16},{4,20},{8,24},{12,28},{16,0},{20,4},{24,8},{28,12},{1,17},{... | collective-permute-start | bytes 393224 | tf_op jit(solution)/shard_map/ppermute | solution.py:810
  117.6 7.4 %collective-permute-start.29 = (bf16[128,512]{1,0:T(8,128)(2,1)S(1)}, bf16[128,512]{1,0:T(8,128)(2,1)S(1)}, u32[]{:S(2)}, u32[]{:S(2)}) collective-permute-start(bf16[128,512]{1,0:T(8,128)(2,1)S(1)} %add.23.refs_2_.refs_1_), channel_id=1, source_target_pairs={{0,16},{4,20},{8,24},{12,28},{16,0},{20,4},{24,8},{28,12},{1,17},{... | collective-permute-start | bytes 393224 | tf_op jit(solution)/shard_map/ppermute | solution.py:810
  118.6 4.3 %collective-permute-start.25 = (bf16[544,256]{1,0:T(8,128)(2,1)S(1)}, bf16[544,256]{1,0:T(8,128)(2,1)S(1)}, u32[]{:S(2)}, u32[]{:S(2)}) collective-permute-start(bf16[544,256]{1,0:T(8,128)(2,1)S(1)} %lead.1.refs_0_), channel_id=1, source_target_pairs={{0,1},{1,0},{2,3},{3,2},{4,5},{5,4},{6,7},{7,6},{8,9},{9,8},{10,11... | collective-permute-start | bytes 835592 | tf_op jit(solution)/shard_map/ppermute | solution.py:810
  118.7 3.9 %collective-permute-start.26 = (bf16[512,1024]{1,0:T(8,128)(2,1)S(1)}, bf16[512,1024]{1,0:T(8,128)(2,1)S(1)}, u32[]{:S(2)}, u32[]{:S(2)}) collective-permute-start(bf16[512,1024]{1,0:T(8,128)(2,1)S(1)} %get-tuple-element.224), channel_id=1, source_target_pairs={{0,1},{1,0},{2,3},{3,2},{4,5},{5,4},{6,7},{7,6},{8,9},{9,8},{10,11... | collective-permute-start | bytes 3145736 | tf_op jit(solution)/shard_map/ppermute | solution.py:810
  119.9 13.3 %collective-permute-start.24 = (bf16[256,512]{1,0:T(8,128)(2,1)S(1)}, bf16[256,512]{1,0:T(8,128)(2,1)S(1)}, u32[]{:S(2)}, u32[]{:S(2)}) collective-permute-start(bf16[256,512]{1,0:T(8,128)(2,1)S(1)} %get-tuple-element.221.refs_0_), channel_id=1, source_target_pairs={{0,8},{4,12},{8,0},{12,4},{16,24},{20,28},{24,16},{28,20},{1,9},{5... | collective-permute-start | bytes 786440 | tf_op jit(solution)/shard_map/ppermute | solution.py:810
  121.6 14.0 %collective-permute-start.34 = (bf16[128,512]{1,0:T(8,128)(2,1)S(1)}, bf16[128,512]{1,0:T(8,128)(2,1)S(1)}, u32[]{:S(2)}, u32[]{:S(2)}) collective-permute-start(bf16[128,512]{1,0:T(8,128)(2,1)S(1)} %add.24.refs_0_.refs_1_), channel_id=1, source_target_pairs={{0,16},{4,20},{8,24},{12,28},{16,0},{20,4},{24,8},{28,12},{1,17},{... | collective-permute-start | bytes 393224 | tf_op jit(solution)/shard_map/ppermute | solution.py:810
  123.5 6.1 %collective-permute-start.28 = (bf16[288,256]{1,0:T(8,128)(2,1)S(1)}, bf16[288,256]{1,0:T(8,128)(2,1)S(1)}, u32[]{:S(2)}, u32[]{:S(2)}) collective-permute-start(bf16[288,256]{1,0:T(8,128)(2,1)S(1)} %get-tuple-element.229), channel_id=1, source_target_pairs={{0,2},{1,3},{2,0},{3,1},{4,6},{5,7},{6,4},{7,5},{8,10},{9,11},{10,... | collective-permute-start | bytes 442376 | tf_op jit(solution)/shard_map/ppermute | solution.py:810
  125.6 16.7 %collective-permute-start.32 = (bf16[256,512]{1,0:T(8,128)(2,1)S(1)}, bf16[256,512]{1,0:T(8,128)(2,1)S(1)}, u32[]{:S(2)}, u32[]{:S(2)}) collective-permute-start(bf16[256,512]{1,0:T(8,128)(2,1)S(1)} %join.7.refs_0_.refs_1_), channel_id=1, source_target_pairs={{0,8},{4,12},{8,0},{12,4},{16,24},{20,28},{24,16},{28,20},{1,9},{5... | collective-permute-start | bytes 786440 | tf_op jit(solution)/shard_map/ppermute | solution.py:810
  126.6 19.7 %collective-permute-start.31 = (bf16[256,1024]{1,0:T(8,128)(2,1)S(1)}, bf16[256,1024]{1,0:T(8,128)(2,1)S(1)}, u32[]{:S(2)}, u32[]{:S(2)}) collective-permute-start(bf16[256,1024]{1,0:T(8,128)(2,1)S(1)} %get-tuple-element.232), channel_id=1, source_target_pairs={{0,2},{1,3},{2,0},{3,1},{4,6},{5,7},{6,4},{7,5},{8,10},{9,11},{10,... | collective-permute-start | bytes 1572872 | tf_op jit(solution)/shard_map/ppermute | solution.py:810
  133.8 15.2 %collective-permute-start.30 = (bf16[128,512]{1,0:T(8,128)(2,1)S(1)}, bf16[128,512]{1,0:T(8,128)(2,1)S(1)}, u32[]{:S(2)}, u32[]{:S(2)}) collective-permute-start(bf16[128,512]{1,0:T(8,128)(2,1)S(1)} %get-tuple-element.231.refs_0_), channel_id=1, source_target_pairs={{0,16},{4,20},{8,24},{12,28},{16,0},{20,4},{24,8},{28,12},{1,17},{... | collective-permute-start | bytes 393224 | tf_op jit(solution)/shard_map/ppermute | solution.py:810
  134.0 5.7 %collective-permute-start.33 = (bf16[384,256]{1,0:T(8,128)(2,1)S(1)}, bf16[384,256]{1,0:T(8,128)(2,1)S(1)}, u32[]{:S(2)}, u32[]{:S(2)}) collective-permute-start(bf16[384,256]{1,0:T(8,128)(2,1)S(1)} %misc_pack.1.refs_0_), channel_id=1, source_target_pairs={{0,4},{4,0},{8,12},{12,8},{16,20},{20,16},{24,28},{28,24},{1,5},{5... | collective-permute-start | bytes 589832 | tf_op jit(solution)/shard_map/ppermute | solution.py:810
  136.2 18.0 %collective-permute-start.36 = (bf16[256,512]{1,0:T(8,128)(2,1)S(1)}, bf16[256,512]{1,0:T(8,128)(2,1)S(1)}, u32[]{:S(2)}, u32[]{:S(2)}) collective-permute-start(bf16[256,512]{1,0:T(8,128)(2,1)S(1)} %join.8.refs_0_.refs_1_), channel_id=1, source_target_pairs={{0,8},{4,12},{8,0},{12,4},{16,24},{20,28},{24,16},{28,20},{1,9},{5... | collective-permute-start | bytes 786440 | tf_op jit(solution)/shard_map/ppermute | solution.py:810
  139.8 12.8 %collective-permute-start.37 = (bf16[384,256]{1,0:T(8,128)(2,1)S(1)}, bf16[384,256]{1,0:T(8,128)(2,1)S(1)}, u32[]{:S(2)}, u32[]{:S(2)}) collective-permute-start(bf16[384,256]{1,0:T(8,128)(2,1)S(1)} %misc_add.2.refs_0_), channel_id=1, source_target_pairs={{0,8},{4,12},{8,0},{12,4},{16,24},{20,28},{24,16},{28,20},{1,9},{5... | collective-permute-start | bytes 589832 | tf_op jit(solution)/shard_map/ppermute | solution.py:810
  142.9 32.1 %collective-permute-start.46 = (bf16[512,512]{1,0:T(8,128)(2,1)S(1)}, bf16[512,512]{1,0:T(8,128)(2,1)S(1)}, u32[]{:S(2)}, u32[]{:S(2)}) collective-permute-start(bf16[512,512]{1,0:T(8,128)(2,1)S(1)} %join.9.refs_0_.refs_1_), channel_id=1, source_target_pairs={{0,4},{4,0},{8,12},{12,8},{16,20},{20,16},{24,28},{28,24},{1,5},{5... | collective-permute-start | bytes 1572872 | tf_op jit(solution)/shard_map/ppermute | solution.py:810
  149.0 8.0 %collective-permute-start.40 = (bf16[128,512]{1,0:T(8,128)(2,1)S(1)}, bf16[128,512]{1,0:T(8,128)(2,1)S(1)}, u32[]{:S(2)}, u32[]{:S(2)}) collective-permute-start(bf16[128,512]{1,0:T(8,128)(2,1)S(1)} %add.25.refs_2_.refs_1_), channel_id=1, source_target_pairs={{0,16},{4,20},{8,24},{12,28},{16,0},{20,4},{24,8},{28,12},{1,17},{... | collective-permute-start | bytes 393224 | tf_op jit(solution)/shard_map/ppermute | solution.py:810
  152.5 4.3 %collective-permute-start.35 = (bf16[512,1024]{1,0:T(8,128)(2,1)S(1)}, bf16[512,1024]{1,0:T(8,128)(2,1)S(1)}, u32[]{:S(2)}, u32[]{:S(2)}) collective-permute-start(bf16[512,1024]{1,0:T(8,128)(2,1)S(1)} %get-tuple-element.235.refs_0_), channel_id=1, source_target_pairs={{0,1},{1,0},{2,3},{3,2},{4,5},{5,4},{6,7},{7,6},{8,9},{9,8},{10,11... | collective-permute-start | bytes 3145736 | tf_op jit(solution)/shard_map/ppermute | solution.py:810
  152.7 19.1 %collective-permute-start.39 = (bf16[384,256]{1,0:T(8,128)(2,1)S(1)}, bf16[384,256]{1,0:T(8,128)(2,1)S(1)}, u32[]{:S(2)}, u32[]{:S(2)}) collective-permute-start(bf16[384,256]{1,0:T(8,128)(2,1)S(1)} %misc_add.3.refs_0_), channel_id=1, source_target_pairs={{0,16},{4,20},{8,24},{12,28},{16,0},{20,4},{24,8},{28,12},{1,17},{... | collective-permute-start | bytes 589832 | tf_op jit(solution)/shard_map/ppermute | solution.py:810
  154.8 24.5 %collective-permute-start.44 = (bf16[512,512]{1,0:T(8,128)(2,1)S(1)}, bf16[512,512]{1,0:T(8,128)(2,1)S(1)}, u32[]{:S(2)}, u32[]{:S(2)}) collective-permute-start(bf16[512,512]{1,0:T(8,128)(2,1)S(1)} %join.10.refs_0_.refs_1_), channel_id=1, source_target_pairs={{0,4},{4,0},{8,12},{12,8},{16,20},{20,16},{24,28},{28,24},{1,5},{5... | collective-permute-start | bytes 1572872 | tf_op jit(solution)/shard_map/ppermute | solution.py:810
  157.6 12.3 %collective-permute-start.41 = (bf16[256,512]{1,0:T(8,128)(2,1)S(1)}, bf16[256,512]{1,0:T(8,128)(2,1)S(1)}, u32[]{:S(2)}, u32[]{:S(2)}) collective-permute-start(bf16[256,512]{1,0:T(8,128)(2,1)S(1)} %join.11.refs_0_.refs_1_), channel_id=1, source_target_pairs={{0,8},{4,12},{8,0},{12,4},{16,24},{20,28},{24,16},{28,20},{1,9},{5... | collective-permute-start | bytes 786440 | tf_op jit(solution)/shard_map/ppermute | solution.py:810
  160.1 18.3 %collective-permute-start.38 = (bf16[256,1024]{1,0:T(8,128)(2,1)S(1)}, bf16[256,1024]{1,0:T(8,128)(2,1)S(1)}, u32[]{:S(2)}, u32[]{:S(2)}) collective-permute-start(bf16[256,1024]{1,0:T(8,128)(2,1)S(1)} %get-tuple-element.237), channel_id=1, source_target_pairs={{0,2},{1,3},{2,0},{3,1},{4,6},{5,7},{6,4},{7,5},{8,10},{9,11},{10,... | collective-permute-start | bytes 1572872 | tf_op jit(solution)/shard_map/ppermute | solution.py:810
  170.5 13.3 %collective-permute-start.43 = (bf16[512,512]{1,0:T(8,128)(2,1)S(1)}, bf16[512,512]{1,0:T(8,128)(2,1)S(1)}, u32[]{:S(2)}, u32[]{:S(2)}) collective-permute-start(bf16[512,512]{1,0:T(8,128)(2,1)S(1)} %join.12.refs_0_.refs_1_), channel_id=1, source_target_pairs={{0,4},{4,0},{8,12},{12,8},{16,20},{20,16},{24,28},{28,24},{1,5},{5... | collective-permute-start | bytes 1572872 | tf_op jit(solution)/shard_map/ppermute | solution.py:810
  172.5 5.2 %collective-permute-start.42 = (bf16[256,256]{1,0:T(8,128)(2,1)S(1)}, bf16[256,256]{1,0:T(8,128)(2,1)S(1)}, u32[]{:S(2)}, u32[]{:S(2)}) collective-permute-start(bf16[256,256]{1,0:T(8,128)(2,1)S(1)} %get-tuple-element.238.refs_1_), channel_id=1, source_target_pairs={{0,2},{1,3},{2,0},{3,1},{4,6},{5,7},{6,4},{7,5},{8,10},{9,11},{10,... | collective-permute-start | bytes 393224 | tf_op jit(solution)/shard_map/ppermute | solution.py:810
  178.2 2.7 %collective-permute-start.45 = (bf16[512,256]{1,0:T(8,128)(2,1)S(1)}, bf16[512,256]{1,0:T(8,128)(2,1)S(1)}, u32[]{:S(2)}, u32[]{:S(2)}) collective-permute-start(bf16[512,256]{1,0:T(8,128)(2,1)S(1)} %join.13.refs_0_.refs_1_), channel_id=1, source_target_pairs={{0,1},{1,0},{2,3},{3,2},{4,5},{5,4},{6,7},{7,6},{8,9},{9,8},{10,11... | collective-permute-start | bytes 786440 | tf_op jit(solution)/shard_map/ppermute | solution.py:810
  (20 other events, 56.7 us)
